TPU v7x, 32 devices: a whole 2x2x4 slice. The times are simulated.
32 devices in a mesh: tx: 8 (over y, x, core), ty: 4 (over z).
Axes of the slice: x: 2, y: 2, z: 4, core: 2. Of those that a mesh axis runs over, the one named last changes fastest.
Arguments:
- points: bfloat16 [131072, 128], P(('tx', 'ty')), may hold values from -6 to 6
- embed_weight: bfloat16 [128, 512], replicated, may hold values from -0.5 to 0.5
- inner_weights: bfloat16 [1, 512, 512], replicated, may hold values from -0.25 to 0.25
- output_weight: bfloat16 [512, 128], replicated, may hold values from -0.25 to 0.25
- counts: int32 [32, 128], replicated, may hold values from 1 to 64, as said below
- point_order: int32 [32, 4096], P(('tx', 'ty')), may hold values from 0 to 4095, each once within a row
- inducing: bfloat16 [128, 128], replicated, may hold values from -6 to 6
- first_proj: bfloat16 [4, 128, 128], replicated, may hold values from -0.5 to 0.5
- second_proj: bfloat16 [4, 128, 128], replicated, may hold values from -0.5 to 0.5
- mixing: bfloat16 [8, 128, 128], replicated, may hold values from -0.1875 to 0.1875
Outputs:
- encoded: bfloat16 [131072, 128], P(('tx', 'ty'))
Inputs may be any that keep to these rules, and one draw needn't show every extreme that they name: Row s sums to 4096. For every source s and every device, the counts of s in the 4 tiles that device holds sum to exactly 128, and one of those 4 entries equals 64. Row s is a permutation of the local points of source s: the points of tile g are point_order[s, offsets[s, g] + c] for c below counts[s, g].
All inputs are finite; a program needn't handle non-finite values.
Results may differ from a plain program's by a relative error of at most 0.025.
Values may be sent and summed in bfloat16 or wider, within the bound.
No kernel may reach another device: no remote copies, remote signals or barrier semaphores. Data moves between devices by JAX's collectives and lax.ppermute only.
A program may use at most 64 MiB of HBM per device.

v0:
```python
import math

import jax
import jax.numpy as jnp
from jax import lax
from jax.sharding import PartitionSpec as P

HEADS = 2
TLX = 2
TLY = 2


sharpness = 32.0
epsilon = 1e-06
neighbour_steps = ((-1, -1), (-1, 0), (-1, 1), (0, -1), (0, 1), (1, -1), (1, 0), (1, 1))


def padded_2(block, sides, width):
    for axis, dim in sides:
        count = lax.axis_size(axis)
        forward = [(i, i + 1) for i in range(count - 1)]
        backward = [(target, source) for source, target in forward]
        low = lax.ppermute(
            lax.slice_in_dim(block, block.shape[dim] - width, None, axis=dim), axis, forward
        )
        high = lax.ppermute(lax.slice_in_dim(block, 0, width, axis=dim), axis, backward)
        block = jnp.concatenate([low, block, high], axis=dim)
    return block


def unit_heads(projected, head_count):
    pieces = projected.reshape(
        projected.shape[:-1] + (head_count, projected.shape[-1] // head_count)
    )
    magnitude = jnp.sqrt(jnp.sum(pieces * pieces, axis=-1, keepdims=True) + epsilon)
    return (pieces / magnitude).reshape(projected.shape).astype(jnp.bfloat16)


def attend(query_rows, key_rows, value_rows, weight_mask):
    head_width = query_rows.shape[-1] // HEADS
    outputs = []
    for head_id in range(HEADS):
        lower = head_id * head_width
        upper = lower + head_width
        scores = jnp.dot(
            query_rows[:, lower:upper],
            key_rows[:, lower:upper].T,
            preferred_element_type=jnp.float32,
        )
        weights = jnp.exp(sharpness * scores) * weight_mask[None, :]
        totals = jnp.sum(weights, axis=1, keepdims=True)
        numer = jnp.dot(
            weights.astype(jnp.bfloat16),
            value_rows[:, lower:upper],
            preferred_element_type=jnp.float32,
        )
        outputs.append(numer / totals)
    return jnp.concatenate(outputs, axis=1).astype(jnp.bfloat16)


def block_layout(tallies, quota):
    before = jnp.cumsum(tallies, axis=0) - tallies
    through = (before + tallies).T
    slot_ids = jnp.arange(quota, dtype=jnp.int32)
    which = jnp.sum((slot_ids[None, :, None] >= through[:, None, :]).astype(jnp.int32), axis=2)
    base = jnp.take_along_axis(before.T, which, axis=1)
    return (before, which, slot_ids[None, :] - base)


def local_rows(index, source_rows, block):
    column_ids = jnp.arange(source_rows.shape[0], dtype=jnp.int32)

    def pick_block(index_block):
        table = (index_block[:, None] == column_ids[None, :]).astype(jnp.bfloat16)
        return jnp.dot(table, source_rows, preferred_element_type=jnp.float32).astype(jnp.bfloat16)

    picked = lax.map(pick_block, index.reshape(-1, block))
    return picked.reshape(index.shape[0], source_rows.shape[1])


def place_rows(index, rows, total, block):
    target_ids = jnp.arange(total, dtype=jnp.int32).reshape(-1, block)

    def place_block(target_block):
        table = (target_block[:, None] == index[None, :]).astype(jnp.bfloat16)
        return jnp.dot(table, rows, preferred_element_type=jnp.float32).astype(jnp.bfloat16)

    placed = lax.map(place_block, target_ids)
    return placed.reshape(total, rows.shape[1])


def slot_table(tallies, before, capacity, quota):
    slot_ids = jnp.arange(capacity, dtype=jnp.int32)
    packed_ids = jnp.arange(quota, dtype=jnp.int32)
    starts = before.T
    live = slot_ids[None, None, :] < tallies.T[:, :, None]
    hits = (
        packed_ids[None, None, None, :] == starts[:, :, None, None] + slot_ids[None, None, :, None]
    )
    return (hits & live[..., None]).astype(jnp.bfloat16)


def expand(blocks, table):
    return jnp.einsum("otcq,oqe->toce", table, blocks, preferred_element_type=jnp.float32).astype(
        jnp.bfloat16
    )


def collapse(slots, table):
    return jnp.einsum("otcq,toce->oqe", table, slots, preferred_element_type=jnp.float32).astype(
        jnp.bfloat16
    )


def body(
    points,
    embed_weight,
    inner_weights,
    output_weight,
    counts,
    point_order,
    inducing,
    first_proj,
    second_proj,
    mixing,
):
    along_x = lax.axis_size("tx")
    along_y = lax.axis_size("ty")
    devices = along_x * along_y
    index_x = lax.axis_index("tx")
    index_y = lax.axis_index("ty")
    own_index = index_x * along_y + index_y
    point_count = points.shape[0]
    capacity = 2 * point_count // counts.shape[1]
    per_device = TLX * TLY
    width = output_weight.shape[1]
    tile_rows = devices * capacity
    quota = point_count // devices
    block = math.gcd(512, point_count)
    hidden = jax.nn.silu(jnp.dot(points, embed_weight, preferred_element_type=jnp.float32)).astype(
        jnp.bfloat16
    )
    hidden = jax.nn.silu(
        jnp.dot(hidden, inner_weights[0], preferred_element_type=jnp.float32)
    ).astype(jnp.bfloat16)
    features = jnp.dot(hidden, output_weight, preferred_element_type=jnp.float32).astype(
        jnp.bfloat16
    )
    own_counts = lax.dynamic_index_in_dim(counts, own_index, 0, keepdims=False)
    own_offsets = jnp.cumsum(own_counts) - own_counts

    def by_owner(table):
        return (
            table.reshape(along_x, TLX, along_y, TLY)
            .transpose(1, 3, 0, 2)
            .reshape(per_device, devices)
        )

    slot_ids = jnp.arange(capacity, dtype=jnp.int32)
    send_counts = by_owner(own_counts)
    send_starts = by_owner(own_offsets)
    inbound = counts.reshape(devices, along_x, TLX, along_y, TLY)
    inbound = lax.dynamic_index_in_dim(inbound, index_x, 1, keepdims=False)
    inbound = lax.dynamic_index_in_dim(inbound, index_y, 2, keepdims=False)
    inbound = inbound.transpose(1, 2, 0).reshape(per_device, devices)
    live_slots = slot_ids[None, None, :] < inbound[:, :, None]
    key_mask = live_slots.astype(jnp.float32).reshape(per_device, tile_rows)
    send_before, send_which, send_within = block_layout(send_counts, quota)
    packed_pos = jnp.take_along_axis(send_starts.T, send_which, axis=1) + send_within
    packed_index = point_order[0][packed_pos].reshape(-1)
    packed = local_rows(packed_index, features, block).reshape(devices, quota, width)
    send_table = slot_table(send_counts, send_before, capacity, quota)
    outgoing = expand(packed, send_table)
    arrived = lax.all_to_all(outgoing, ("tx", "ty"), split_axis=1, concat_axis=1, tiled=True)
    arrived = arrived.reshape(per_device, tile_rows, width)
    all_rows = arrived.reshape(per_device * tile_rows, width)
    first_keys = unit_heads(
        jnp.dot(all_rows, first_proj[1], preferred_element_type=jnp.float32), HEADS
    ).reshape(per_device, tile_rows, width)
    first_values = (
        jnp.dot(all_rows, first_proj[2], preferred_element_type=jnp.float32)
        .astype(jnp.bfloat16)
        .reshape(per_device, tile_rows, width)
    )
    inducing_queries = unit_heads(
        jnp.dot(inducing, first_proj[0], preferred_element_type=jnp.float32), HEADS
    )
    first_attended = jax.vmap(attend, in_axes=(None, 0, 0, 0))(
        inducing_queries, first_keys, first_values, key_mask
    )
    summary = (
        inducing.astype(jnp.float32)[None]
        + jnp.einsum(
            "tic,ce->tie", first_attended, first_proj[3], preferred_element_type=jnp.float32
        )
    ).astype(jnp.bfloat16)
    tile_grid = summary.reshape(TLX, TLY, summary.shape[1], width)
    padded = padded_2(tile_grid, (("tx", 0), ("ty", 1)), 1)
    stacked = jnp.stack(
        [
            padded[1 + steps[0] : 1 + steps[0] + TLX, 1 + steps[1] : 1 + steps[1] + TLY]
            for steps in neighbour_steps
        ]
    )
    mixture = tile_grid.astype(jnp.float32) + jnp.einsum(
        "dxyic,dce->xyie", stacked, mixing, preferred_element_type=jnp.float32
    )
    mixture = mixture.astype(jnp.bfloat16).reshape(per_device * summary.shape[1], width)
    point_queries = unit_heads(
        jnp.dot(all_rows, second_proj[0], preferred_element_type=jnp.float32), HEADS
    ).reshape(per_device, tile_rows, width)
    second_keys = unit_heads(
        jnp.dot(mixture, second_proj[1], preferred_element_type=jnp.float32), HEADS
    ).reshape(per_device, -1, width)
    second_values = (
        jnp.dot(mixture, second_proj[2], preferred_element_type=jnp.float32)
        .astype(jnp.bfloat16)
        .reshape(per_device, -1, width)
    )
    every_key = jnp.ones((second_keys.shape[1],), jnp.float32)
    second_attended = jax.vmap(attend, in_axes=(0, 0, 0, None))(
        point_queries, second_keys, second_values, every_key
    )
    result = (
        arrived.astype(jnp.float32)
        + jnp.einsum(
            "trc,ce->tre", second_attended, second_proj[3], preferred_element_type=jnp.float32
        )
    ).astype(jnp.bfloat16)
    result_slots = result.reshape(per_device, devices, capacity, width)
    coming = lax.all_to_all(result_slots, ("tx", "ty"), split_axis=1, concat_axis=1, tiled=True)
    returned = collapse(coming, send_table)
    return place_rows(packed_index, returned.reshape(point_count, width), point_count, block)


def solution(mesh):
    placed = (P(("tx", "ty"), None), P(), P(), P(), P(), P(("tx", "ty"), None), P(), P(), P(), P())
    return jax.shard_map(
        body, mesh=mesh, in_specs=placed, out_specs=P(("tx", "ty"), None), check_vma=False
    )
```

profile of v0, /device:TPU:0, one launch (start us, length us, event | category | flops | bytes accessed | tf_op | source)
XLA Modules:
  0.0 313.0 jit_solution(17499641403373414593)
XLA Ops:
  2.4 33.8 %gather_fusion.2 = s32[4096]{0:T(1024)S(1)} fusion(s32[32,4]{0,1:T(4,128)S(1)} %subtract_bitcast_fusion.1, s32[4096]{0:T(1024)S(1)} %fusion.112), kind=kCustom, calls=%fused_computation.1.clone | custom fusion | bytes 65536 | tf_op jit(solution)/shard_map/jit(take_along_axis)/gather | solution.py:66
  36.2 33.8 %gather_fusion.1 = s32[4096]{0:T(1024)S(1)} fusion(s32[32,4]{0,1:T(4,128)S(1)} %bitcast.257, s32[4096]{0:T(1024)S(1)} %fusion.112), kind=kCustom, calls=%fused_computation.clone | custom fusion | bytes 65536 | tf_op jit(solution)/shard_map/jit(take_along_axis)/gather | solution.py:169
  70.8 23.0 %gather_fusion = s32[4096]{0:T(1024)S(1)} fusion(s32[4096]{0:T(1024)S(1)} %bitcast.258, s32[4096]{0:T(1024)S(1)} %fusion.109), kind=kCustom, calls=%fused_computation.2 | custom fusion | bytes 49152 | tf_op jit(solution)/shard_map/gather | solution.py:170
  93.9 6.4 %fusion.21 = f32[4096,512]{1,0:T(8,128)} fusion(bf16[4096,128]{1,0:T(8,128)(2,1)S(1)} %copy-done, bf16[128,512]{1,0:T(8,128)(2,1)S(1)} %copy-done.14, bf16[1,512,512]{2,1,0:T(8,128)(2,1)S(1)} %copy-done.13), kind=kOutput, calls=%fused_computation.38 | convolution fusion | flops 2694840320 | bytes 10092544 | tf_op jit(solution)/shard_map/dot_general | solution.py:144
  100.3 5.7 %convolution_convert_fusion.1 = bf16[4096,128]{1,0:T(8,128)(2,1)S(1)} fusion(bf16[512,128]{1,0:T(8,128)(2,1)S(1)} %copy-done.15, f32[4096,512]{1,0:T(8,128)} %fusion.21), kind=kOutput, calls=%fused_computation.22 | convolution fusion | flops 547880960 | bytes 9568256 | tf_op jit(solution)/shard_map/dot_general | solution.py:146
  106.1 12.9 %while.22 = (s32[]{:T(128)}, bf16[8,512,128]{2,1,0:T(8,128)(2,1)S(1)}, s32[8,512]{1,0:T(8,128)S(1)}, bf16[4096,128]{1,0:T(8,128)(2,1)S(1)}, s32[]{:T(128)}) while((s32[]{:T(128)}, bf16[8,512,128]{2,1,0:T(8,128)(2,1)S(1)}, s32[8,512]{1,0:T(8,128)S(1)}, bf16[4096,128]{1,0:T(8,128)(2,1)S(1)}, s32[]{:T(128)}) %tuple.52), condition=%wide.region_4.6_spmd.clone, body=%wide.region_3.5_spmd.clone.sunk | while | flops 539033600 | bytes 1185861 | solution.py:77
  106.2 1.6 fusion.153
  107.8 1.6 fusion.153
  109.4 1.6 fusion.153
  111.0 1.6 fusion.153
  112.6 1.6 fusion.153
  114.2 1.6 fusion.153
  115.9 1.6 fusion.153
  117.5 1.6 fusion.153
  119.4 5.1 %convert_bitcast_fusion = bf16[4,32,64,128]{3,2,0,1:T(8,128)(2,1)} fusion(bf16[32,128,128,1]{2,1,3,0:T(8,128)(2,1)S(1)} %bitcast.272, s32[32,4,64]{2,1,0:T(4,128)S(1)} %iota_add_fusion, pred[32,4,64]{2,1,0:T(4,128)(4,1)S(1)} %iota_compare_fusion.9), kind=kOutput, calls=%fused_computation.65 | convolution fusion | flops 271581184 | bytes 3186688 | tf_op jit(solution)/shard_map/otcq,oqe->toce/dot_general | solution.py:104
  124.5 7.6 %all-to-all-start = ((bf16[4,32,64,128]{3,2,0,1:T(8,128)(2,1)}), bf16[4,32,64,128]{3,2,0,1:T(8,128)(2,1)}, u32[]{:S(2)}, u32[]{:S(2)}) async-start(bf16[4,32,64,128]{3,2,0,1:T(8,128)(2,1)} %convert_bitcast_fusion), calls=%async_computation | async-start | bytes 4194304 | tf_op jit(solution)/shard_map/all_to_all | solution.py:174
  133.3 46.1 %all-to-all-done = bf16[4,32,64,128]{3,2,0,1:T(8,128)(2,1)} async-done(((bf16[4,32,64,128]{3,2,0,1:T(8,128)(2,1)}), bf16[4,32,64,128]{3,2,0,1:T(8,128)(2,1)}, u32[]{:S(2)}, u32[]{:S(2)}) %all-to-all-start) | async-done | bytes 2097184 | tf_op jit(solution)/shard_map/all_to_all | solution.py:174
  179.5 1.8 copy.69
  182.1 1.7 divide_convert_fusion
  183.8 4.5 %convert_element_type.119 = bf16[4,2048,128]{1,0,2:T(4,128)(2,1)} reshape(bf16[8192,2,64]{0,2,1:T(8,128)(2,1)} %divide_convert_fusion) | data formatting | bytes 4194304 | tf_op jit(solution)/shard_map/convert_element_type | solution.py:36
  188.3 2.5 fusion.124
  191.5 1.6 fusion.77
  193.1 2.7 bitcast_reduce_fusion.1
  195.9 1.9 fusion.64
  197.8 1.1 fusion.70
  199.1 2.9 collective-permute-start
  202.0 1.5 collective-permute-start.1
  204.7 2.7 convert_element_type.114
  207.6 3.5 %collective-permute-start.2 = (bf16[4,1,128,128]{3,2,1,0:T(8,128)(2,1)S(1)}, bf16[4,1,128,128]{3,2,1,0:T(8,128)(2,1)S(1)}, u32[]{:S(2)}, u32[]{:S(2)}) collective-permute-start(bf16[4,1,128,128]{3,2,1,0:T(8,128)(2,1)S(1)} %get-tuple-element.99), channel_id=1, source_target_pairs={{0,1},{1,2},{2,3},{4,5},{5,6},{6,7},{8,9},{9,10},{10,11},{12,13},{... | collective-permute-start | bytes 393224 | tf_op jit(solution)/shard_map/ppermute | solution.py:23
  211.1 1.3 collective-permute-start.3
  212.4 2.6 fusion.123
  214.9 4.0 %copy.68 = f32[4,32,64,128]{3,2,1,0:T(8,128)} copy(bf16[4,32,64,128]{3,2,0,1:T(8,128)(2,1)} %all-to-all-done) | data formatting | bytes 6291456 | tf_op jit(solution)/shard_map/convert_element_type | solution.py:225
  220.3 2.0 fusion.27
  222.4 2.0 fusion.29
  226.2 1.3 copy-done.3
  228.4 1.5 copy.96
  229.9 7.2 %all-to-all-start.1 = ((bf16[4,32,64,128]{3,2,0,1:T(8,128)(2,1)}), bf16[4,32,64,128]{3,2,0,1:T(8,128)(2,1)S(1)}, u32[]{:S(2)}, u32[]{:S(2)}) async-start(bf16[4,32,64,128]{3,2,0,1:T(8,128)(2,1)} %copy.96), calls=%async_computation.1 | async-start | bytes 4194304 | tf_op jit(solution)/shard_map/all_to_all | solution.py:231
  237.1 47.5 %all-to-all-done.1 = bf16[4,32,64,128]{3,2,0,1:T(8,128)(2,1)S(1)} async-done(((bf16[4,32,64,128]{3,2,0,1:T(8,128)(2,1)}), bf16[4,32,64,128]{3,2,0,1:T(8,128)(2,1)S(1)}, u32[]{:S(2)}, u32[]{:S(2)}) %all-to-all-start.1) | async-done | bytes 2097184 | tf_op jit(solution)/shard_map/all_to_all | solution.py:231
  284.6 5.7 %bitcast_convert_fusion.4 = bf16[32,128,128]{2,1,0:T(8,128)(2,1)} fusion(bf16[4,32,64,128]{3,2,0,1:T(8,128)(2,1)S(1)} %all-to-all-done.1, s32[32,4,64]{2,1,0:T(4,128)S(1)} %iota_add_fusion, pred[32,4,64]{2,1,0:T(4,128)(4,1)S(1)} %copy-done.12), kind=kOutput, calls=%fused_computation.58 | convolution fusion | flops 271056896 | bytes 3186688 | tf_op jit(solution)/shard_map/otcq,toce->oqe/dot_general | solution.py:110
  290.4 20.9 %while.21 = (s32[]{:T(128)}, bf16[8,512,128]{2,1,0:T(8,128)(2,1)S(1)}, s32[8,512]{1,0:T(8,128)S(1)}, s32[32,128]{1,0:T(8,128)S(1)}, bf16[4096,128]{1,0:T(8,128)(2,1)}, /*index=5*/s32[]{:T(128)}) while((s32[]{:T(128)}, bf16[8,512,128]{2,1,0:T(8,128)(2,1)S(1)}, s32[8,512]{1,0:T(8,128)S(1)}, s32[32,128]{1,0:T(8,128)S(1)}, ...), condition=%wide.region_14.16_spmd, body=%wide.region_13.15_spmd.sunk | while | flops 539033600 | bytes 1202253 | solution.py:88
  290.5 2.6 fusion.151
  293.1 2.6 fusion.151
  295.7 2.6 fusion.151
  298.3 2.6 fusion.151
  300.9 2.6 fusion.151
  303.5 2.6 fusion.151
  306.1 2.6 fusion.151
  308.8 2.6 fusion.151
  (121 shorter events, 13.3 us)
Async XLA Ops:
  0.0 93.8 %copy-start = (bf16[4096,128]{1,0:T(8,128)(2,1)S(1)}, bf16[4096,128]{1,0:T(8,128)(2,1)}, u32[]{:S(2)}) copy-start(bf16[4096,128]{1,0:T(8,128)(2,1)} %param.16) | copy-start | bytes 3145732
  70.1 0.7 copy-start.2
  70.8 23.1 %copy-start.13 = (bf16[1,512,512]{2,1,0:T(8,128)(2,1)S(1)}, bf16[1,512,512]{2,1,0:T(8,128)(2,1)}, u32[]{:S(2)}) copy-start(bf16[1,512,512]{2,1,0:T(8,128)(2,1)} %param.18) | copy-start | bytes 1572868
  70.8 23.1 %copy-start.14 = (bf16[128,512]{1,0:T(8,128)(2,1)S(1)}, bf16[128,512]{1,0:T(8,128)(2,1)}, u32[]{:S(2)}) copy-start(bf16[128,512]{1,0:T(8,128)(2,1)} %param.17) | copy-start | bytes 393220
  93.9 6.4 %copy-start.15 = (bf16[512,128]{1,0:T(8,128)(2,1)S(1)}, bf16[512,128]{1,0:T(8,128)(2,1)}, u32[]{:S(2)}) copy-start(bf16[512,128]{1,0:T(8,128)(2,1)} %param.19) | copy-start | bytes 393220
  119.4 5.2 %copy-start.11 = (pred[32,4,64]{2,1,0:T(4,128)(4,1)}, pred[32,4,64]{2,1,0:T(4,128)(4,1)S(1)}, u32[]{:S(2)}) copy-start(pred[32,4,64]{2,1,0:T(4,128)(4,1)S(1)} %iota_compare_fusion.9) | copy-start | bytes 24580
  119.4 12.8 %copy-start.10 = (s32[32,128]{1,0:T(8,128)S(1)}, s32[32,128]{1,0:T(8,128)}, u32[]{:S(2)}) copy-start(s32[32,128]{1,0:T(8,128)} %param.20) | copy-start | bytes 49156
  119.4 12.9 %copy-start.7 = (bf16[4,128,128]{2,1,0:T(8,128)(2,1)S(1)}, bf16[4,128,128]{2,1,0:T(8,128)(2,1)}, u32[]{:S(2)}) copy-start(bf16[4,128,128]{2,1,0:T(8,128)(2,1)} %param.23) | copy-start | bytes 393220
  119.4 13.4 %copy-start.9 = (bf16[128,128]{1,0:T(8,128)(2,1)S(1)}, bf16[128,128]{1,0:T(8,128)(2,1)}, u32[]{:S(2)}) copy-start(bf16[128,128]{1,0:T(8,128)(2,1)} %param.22) | copy-start | bytes 98308
  119.4 13.4 %copy-start.6 = (bf16[4,128,128]{2,1,0:T(8,128)(2,1)S(1)}, bf16[4,128,128]{2,1,0:T(8,128)(2,1)}, u32[]{:S(2)}) copy-start(bf16[4,128,128]{2,1,0:T(8,128)(2,1)} %param.24) | copy-start | bytes 393220
  124.5 54.9 %all-to-all-start = ((bf16[4,32,64,128]{3,2,0,1:T(8,128)(2,1)}), bf16[4,32,64,128]{3,2,0,1:T(8,128)(2,1)}, u32[]{:S(2)}, u32[]{:S(2)}) async-start(bf16[4,32,64,128]{3,2,0,1:T(8,128)(2,1)} %convert_bitcast_fusion), calls=%async_computation | async-start | bytes 4194304 | tf_op jit(solution)/shard_map/all_to_all | solution.py:174
  188.3 2.5 copy-start.8
  199.1 8.4 %collective-permute-start = (bf16[1,2,128,128]{3,2,1,0:T(8,128)(2,1)S(1)}, bf16[1,2,128,128]{3,2,1,0:T(8,128)(2,1)S(1)}, u32[]{:S(2)}, u32[]{:S(2)}) collective-permute-start(bf16[1,2,128,128]{3,2,1,0:T(8,128)(2,1)S(1)} %get-tuple-element.104), channel_id=1, source_target_pairs={{0,4},{4,8},{8,12},{12,16},{16,20},{20,24},{24,28},{1,5},{5,9},{9,... | collective-permute-start | bytes 196616 | tf_op jit(solution)/shard_map/ppermute | solution.py:23
  202.0 5.5 %collective-permute-start.1 = (bf16[1,2,128,128]{3,2,1,0:T(8,128)(2,1)S(1)}, bf16[1,2,128,128]{3,2,1,0:T(8,128)(2,1)S(1)}, u32[]{:S(2)}, u32[]{:S(2)}) collective-permute-start(bf16[1,2,128,128]{3,2,1,0:T(8,128)(2,1)S(1)} %get-tuple-element.105), channel_id=1, source_target_pairs={{4,0},{8,4},{12,8},{16,12},{20,16},{24,20},{28,24},{5,1},{9,5},{13... | collective-permute-start | bytes 196616 | tf_op jit(solution)/shard_map/ppermute | solution.py:26
  207.6 11.4 %collective-permute-start.2 = (bf16[4,1,128,128]{3,2,1,0:T(8,128)(2,1)S(1)}, bf16[4,1,128,128]{3,2,1,0:T(8,128)(2,1)S(1)}, u32[]{:S(2)}, u32[]{:S(2)}) collective-permute-start(bf16[4,1,128,128]{3,2,1,0:T(8,128)(2,1)S(1)} %get-tuple-element.99), channel_id=1, source_target_pairs={{0,1},{1,2},{2,3},{4,5},{5,6},{6,7},{8,9},{9,10},{10,11},{12,13},{... | collective-permute-start | bytes 393224 | tf_op jit(solution)/shard_map/ppermute | solution.py:23
  211.1 8.0 %collective-permute-start.3 = (bf16[4,1,128,128]{3,2,1,0:T(8,128)(2,1)S(1)}, bf16[4,1,128,128]{3,2,1,0:T(8,128)(2,1)S(1)}, u32[]{:S(2)}, u32[]{:S(2)}) collective-permute-start(bf16[4,1,128,128]{3,2,1,0:T(8,128)(2,1)S(1)} %get-tuple-element.98), channel_id=1, source_target_pairs={{1,0},{2,1},{3,2},{5,4},{6,5},{7,6},{9,8},{10,9},{11,10},{13,12},{... | collective-permute-start | bytes 393224 | tf_op jit(solution)/shard_map/ppermute | solution.py:26
  214.9 4.4 %copy-start.5 = (bf16[8,128,128]{2,1,0:T(8,128)(2,1)S(1)}, bf16[8,128,128]{2,1,0:T(8,128)(2,1)}, u32[]{:S(2)}) copy-start(bf16[8,128,128]{2,1,0:T(8,128)(2,1)} %param.25) | copy-start | bytes 786436
  225.3 2.2 copy-start.3
  228.3 56.2 %copy-start.12 = (pred[32,4,64]{2,1,0:T(4,128)(4,1)S(1)}, pred[32,4,64]{2,1,0:T(4,128)(4,1)}, u32[]{:S(2)}) copy-start(pred[32,4,64]{2,1,0:T(4,128)(4,1)} %copy-done.11) | copy-start | bytes 24580
  229.9 54.7 %all-to-all-start.1 = ((bf16[4,32,64,128]{3,2,0,1:T(8,128)(2,1)}), bf16[4,32,64,128]{3,2,0,1:T(8,128)(2,1)S(1)}, u32[]{:S(2)}, u32[]{:S(2)}) async-start(bf16[4,32,64,128]{3,2,0,1:T(8,128)(2,1)} %copy.96), calls=%async_computation.1 | async-start | bytes 4194304 | tf_op jit(solution)/shard_map/all_to_all | solution.py:231
  311.3 1.0 copy-start.4
  311.4 1.6 copy-start.1
where the time goes:
time: 314 us; the launch traced here: 313 us
  local copies, waits for them, and re-layouts  117 us (37%)
  waiting for transfers between devices  93.7 us (30%)
  matrix products  73.7 us (23%)
  starting transfers between devices  23.9 us (8%)
    all_to_all x1, waiting for transfers between devices, body(): lax.all_to_all(result_slots, ('tx', 'ty'), split_axis=1, concat_axis=1, t...  47.5 us
    all_to_all x1, waiting for transfers between devices, body(): lax.all_to_all(outgoing, ('tx', 'ty'), split_axis=1, concat_axis=1, tiled...  46.1 us
    gather x1, local copies, waits for them, and re-layouts, body(): jnp.take_along_axis(send_starts.T, send_which, axis=1) + send_within  33.8 us
    gather x1, local copies, waits for them, and re-layouts, block_layout(): base = jnp.take_along_axis(before.T, which, axis=1)  33.8 us
    gather x1, local copies, waits for them, and re-layouts, body(): packed_index = point_order[0][packed_pos].reshape(-1)  23 us
    dot_general x8, matrix products, place_block(): jnp.dot(table, rows, preferred_element_type=jnp.float32)  20.7 us
    dot_general x8, matrix products, pick_block(): jnp.dot(table, source_rows, preferred_element_type=jnp.float32)  12.7 us
    dot_general x4, matrix products, attend(): jnp.dot(query_rows[:, lower:upper], key_rows[:, lower:upper].T, preferred...  8.44 us
  transfers between devices with their start and end apart: 6, of which 3 were waited for; matrix products, arithmetic and copies ran while one was open for 4% of the time, Pallas kernels for 0%

commit v1 on v0

v1 whole, which is shorter than its diff:
```python
import functools
import math

import jax
import jax.numpy as jnp
from jax import lax
from jax.experimental import pallas as pl
from jax.experimental.pallas import tpu as pltpu
from jax.sharding import PartitionSpec as P

HEADS = 2
TLX = 2
TLY = 2
LANES = 128
BF = jnp.bfloat16
F32 = jnp.float32

sharpness = 32.0
epsilon = 1e-06
neighbour_steps = ((-1, -1), (-1, 0), (-1, 1), (0, -1), (0, 1), (1, -1), (1, 0), (1, 1))
VMEM = pltpu.VMEM
SMEM = pltpu.SMEM


def dot(a, b):
    return jnp.dot(a, b, preferred_element_type=F32)


def dot_t(a, b):
    return lax.dot_general(a, b, (((1,), (1,)), ((), ())), preferred_element_type=F32)


def head_ones():
    row = lax.broadcasted_iota(jnp.int32, (2 * LANES, LANES), 0)
    col = lax.broadcasted_iota(jnp.int32, (2 * LANES, LANES), 1)
    half = LANES // HEADS
    same = ((row % LANES) // half) == (col // half)
    return jnp.where(same, 1.0, 0.0).astype(BF)


def unit(v, ones):
    square = v * v
    high = square.astype(BF)
    low = (square - high.astype(F32)).astype(BF)
    total = dot(jnp.concatenate([high, low], axis=1), ones)
    return v * lax.rsqrt(total + epsilon)


def silu(v):
    half = 0.5 * v
    return half + half * jnp.tanh(half)


def encode_kernel(
    grid_y,
    along_y,
    quota,
    points_ref,
    w1_ref,
    w2_ref,
    w3_ref,
    counts_ref,
    order_ref,
    feat_ref,
    index_ref,
    off_ref,
    index_s,
    wide_ref,
    xa_ref,
    xb_ref,
    sem,
):
    tiles = counts_ref.shape[0]
    order_rows = order_ref.shape[0]
    rows_total = points_ref.shape[0]
    chunk = xa_ref.shape[0]

    def add_up(g, total):
        off_ref[g] = total
        return total + counts_ref[g]

    lax.fori_loop(0, tiles, add_up, jnp.int32(0), unroll=8)
    wide_ref[...] = points_ref[...].astype(F32)
    lane = lax.broadcasted_iota(jnp.int32, (1, LANES), 1)

    def run_of(start):
        line = start >> 7
        shift = start & (LANES - 1)
        first = order_ref[pl.ds(jnp.clip(line, 0, order_rows - 1), 1), :]
        second = order_ref[pl.ds(jnp.clip(line + 1, 0, order_rows - 1), 1), :]
        merged = jnp.where(lane < shift, second, first)
        return pltpu.roll(merged, (LANES - shift) & (LANES - 1), 1)

    per_line = LANES // quota

    def index_line(line, carry):
        value = jnp.zeros((1, LANES), jnp.int32)
        for k in range(per_line):
            d = line * per_line + k
            g1 = (d // along_y) * (TLX * grid_y) + (d % along_y) * TLY
            n1 = counts_ref[g1] + counts_ref[g1 + 1]
            run1 = run_of(off_ref[g1] - k * quota)
            run2 = run_of(off_ref[g1 + grid_y] - n1 - k * quota)
            both = jnp.where(lane < k * quota + n1, run1, run2)
            value = both if k == 0 else jnp.where(lane >= k * quota, both, value)
        index_ref[pl.ds(line, 1), :] = value
        return carry

    lax.fori_loop(0, rows_total // LANES, index_line, 0)
    copy = pltpu.make_async_copy(index_ref, index_s, sem)
    copy.start()
    copy.wait()

    def gather(c, buffer):
        for r in range(chunk):
            i = index_s[c * (chunk // LANES) + r // LANES, r % LANES]
            buffer[pl.ds(r, 1), :] = wide_ref[pl.ds(i, 1), :]

    def network(c, buffer):
        x = buffer[...].astype(BF)
        hidden = silu(dot(x, w1_ref[...])).astype(BF)
        hidden = silu(dot(hidden, w2_ref[0])).astype(BF)
        start = pl.multiple_of(c * chunk, chunk)
        feat_ref[pl.ds(start, chunk), :] = dot(hidden, w3_ref[...]).astype(BF)

    chunks = rows_total // chunk
    gather(0, xa_ref)

    def step(k, carry):
        c = 2 * k
        gather(c + 1, xb_ref)
        network(c, xa_ref)
        gather(jnp.minimum(c + 2, chunks - 1), xa_ref)
        network(c + 1, xb_ref)
        return carry

    lax.fori_loop(0, chunks // 2, step, 0)


def tile_bounds(n0, n1, n2):
    return (0, n0, n0 + n1, n0 + n1 + n2)


def summarize_kernel(
    along_y, quota, rows_ref, counts_ref, where_ref, inducing_ref, proj_ref, out_ref, kv_ref, num_ref
):
    total_rows = rows_ref.shape[0]
    grid_y = along_y * TLY
    half = LANES // HEADS
    chunk = min(512, total_rows)
    ones = head_ones()
    lane = lax.broadcasted_iota(jnp.int32, (1, LANES), 1)
    left = lane < half
    base = where_ref[0] * (TLX * grid_y) + where_ref[1] * TLY
    inducing = inducing_ref[...]
    queries = unit(dot(inducing, proj_ref[0]), ones)
    queries = jnp.concatenate(
        [jnp.where(left, queries, 0.0), jnp.where(left, 0.0, queries)], axis=0
    ).astype(BF)
    wk = proj_ref[1]
    wv = proj_ref[2]
    wv0, wv1 = wv[:, :half], wv[:, half:]
    weights = jnp.concatenate([wk, wv0, wv0, wv1, wv1], axis=1)
    kv_ref[...] = weights
    num_ref[...] = jnp.zeros_like(num_ref)
    block_row = lax.broadcasted_iota(jnp.int32, (quota, LANES), 0)

    def step(c, carry):
        x = rows_ref[pl.ds(pl.multiple_of(c * chunk, chunk), chunk), :]
        projected = dot(x, kv_ref[...])
        keys = unit(projected[:, :LANES], ones).astype(BF)
        scores = dot_t(queries, keys)
        weights = jnp.exp2(scores * (sharpness * math.log2(math.e))).astype(BF)
        masks = [[], []]
        for k in range(chunk // quota):
            s = c * (chunk // quota) + k
            n0 = counts_ref[s, base]
            n1 = counts_ref[s, base + 1]
            n2 = counts_ref[s, base + grid_y]
            b = tile_bounds(n0, n1, n2) + (quota,)
            for pair in range(2):
                low = jnp.where(left, b[2 * pair], b[2 * pair + 1])
                high = jnp.where(left, b[2 * pair + 1], b[2 * pair + 2])
                masks[pair].append(
                    jnp.where((block_row >= low) & (block_row < high), 1.0, 0.0)
                )
        masks = [jnp.concatenate(m, axis=0) for m in masks]
        mask_bf = [m.astype(BF) for m in masks]
        for h in range(HEADS):
            value = projected[:, (1 + h) * LANES : (2 + h) * LANES]
            right = jnp.concatenate(
                [(value * m).astype(BF) for m in masks] + mask_bf, axis=1
            )
            num_ref[h] += dot(weights[h * LANES : (h + 1) * LANES], right)
        return carry

    lax.fori_loop(0, total_rows // chunk, step, 0)
    for pair in range(2):
        cols = slice(pair * LANES, (pair + 1) * LANES)
        tots = slice((2 + pair) * LANES, (3 + pair) * LANES)
        a0 = num_ref[0, :, cols] / num_ref[0, :, tots]
        a1 = num_ref[1, :, cols] / num_ref[1, :, tots]
        first = jnp.where(left, a0, pltpu.roll(a1, half, 1))
        second = jnp.where(left, pltpu.roll(a0, half, 1), a1)
        for k, attended in enumerate((first, second)):
            t = pair * 2 + k
            value = inducing.astype(F32) + dot(attended.astype(BF), proj_ref[3])
            out_ref[t * LANES : (t + 1) * LANES, :] = value.astype(BF)


def finish_kernel(
    along_x,
    along_y,
    quota,
    summary_hbm,
    feat_ref,
    counts_ref,
    index_ref,
    proj_ref,
    mixing_ref,
    out_ref,
    grid_ref,
    mid_ref,
    side_ref,
    kv_ref,
    wide_ref,
    res_ref,
    sems,
):
    grid_x = along_x * TLX
    grid_y = along_y * TLY
    half = LANES // HEADS
    devices = along_x * along_y

    def load(d):
        ax, ay = d // along_y, d % along_y
        return pltpu.make_async_copy(
            summary_hbm.at[d],
            grid_ref.at[pl.ds(2 * ax + 1, TLX), pl.ds(2 * ay + 1, TLY)],
            sems.at[d],
        )

    lax.fori_loop(0, devices, lambda d, c: (load(d).start(), c)[1], 0)

    blank = jnp.zeros((LANES, LANES), BF)

    def blank_x(i, c):
        grid_ref[i, 0] = blank
        grid_ref[i, grid_y + 1] = blank
        return c

    lax.fori_loop(0, grid_x + 2, blank_x, 0)
    for j in range(1, grid_y + 1):
        grid_ref[0, j] = blank
        grid_ref[grid_x + 1, j] = blank

    row = lax.broadcasted_iota(jnp.int32, (LANES, LANES), 0)
    col = lax.broadcasted_iota(jnp.int32, (LANES, LANES), 1)
    eye = jnp.where(row == col, 1.0, 0.0).astype(BF)

    def mix(a, b):
        return eye if (a, b) == (0, 0) else mixing_ref[neighbour_steps.index((a, b))]

    for k, a in enumerate((-1, 0, 1)):
        rows = slice(k * 2 * LANES, (k + 1) * 2 * LANES)
        mid_ref[rows, :] = jnp.concatenate(
            [
                jnp.concatenate([mix(a, 0), mix(a, -1)], axis=1),
                jnp.concatenate([mix(a, 1), mix(a, 0)], axis=1),
            ],
            axis=0,
        )
    for k, b in enumerate((-1, 1)):
        side_ref[k] = jnp.concatenate(
            [
                jnp.concatenate([mix(0, b), mix(-1, b)], axis=1),
                jnp.concatenate([mix(1, b), mix(0, b)], axis=1),
                jnp.concatenate([mix(-1, b), blank], axis=1),
                jnp.concatenate([blank, mix(1, b)], axis=1),
            ],
            axis=0,
        )
    kv_ref[...] = jnp.concatenate([proj_ref[1], proj_ref[2]], axis=1)
    ones = head_ones()
    lane = lax.broadcasted_iota(jnp.int32, (1, LANES), 1)
    left = lane < half
    ones_block = jnp.ones((LANES, LANES), BF)
    block_row = lax.broadcasted_iota(jnp.int32, (quota, LANES), 0)
    lax.fori_loop(0, devices, lambda d, c: (load(d).wait(), c)[1], 0)

    def band(ax, carry):
        def tile(i, j):
            return grid_ref[2 * ax + i, j]

        mids, lefts, rights = [], [], []
        for i in range(2):
            for ay in range(along_y):
                mids.append(
                    jnp.concatenate(
                        [tile(i + r, 2 * ay + 1 + s) for r in range(3) for s in range(2)], axis=1
                    )
                )
        for ay in range(along_y):
            lefts.append(jnp.concatenate([tile(i, 2 * ay) for i in (1, 2, 0, 3)], axis=1))
            rights.append(jnp.concatenate([tile(i, 2 * ay + 3) for i in (1, 2, 0, 3)], axis=1))
        middle = dot(jnp.concatenate(mids, axis=0), mid_ref[...])
        from_left = dot(jnp.concatenate(lefts, axis=0), side_ref[0])
        from_right = dot(jnp.concatenate(rights, axis=0), side_ref[1])
        mixtures = []
        for ay in range(along_y):
            span = slice(ay * LANES, (ay + 1) * LANES)
            for i in range(2):
                m = middle[(i * along_y + ay) * LANES : (i * along_y + ay + 1) * LANES]
                cols = slice(i * LANES, (i + 1) * LANES)
                mixtures.append((m[:, :LANES] + from_left[span, cols]).astype(BF))
                mixtures.append((m[:, LANES:] + from_right[span, cols]).astype(BF))
        kv = dot(jnp.concatenate(mixtures, axis=0), kv_ref[...])
        keys = unit(kv[:, :LANES], ones).astype(BF)
        values = kv[:, LANES:].astype(BF)
        band_rows = along_y * quota
        start = pl.multiple_of(ax * band_rows, band_rows)
        x_band = feat_ref[pl.ds(start, band_rows), :]
        query_band = unit(dot(x_band, proj_ref[0]), ones)
        attended = []
        for ay in range(along_y):
            base = ax * (TLX * grid_y) + ay * TLY
            b = tile_bounds(
                counts_ref[base], counts_ref[base + 1], counts_ref[base + grid_y]
            ) + (quota,)
            inside = [(block_row >= b[t]) & (block_row < b[t + 1]) for t in range(4)]
            query = query_band[ay * quota : (ay + 1) * quota]
            expanded = jnp.concatenate(
                [
                    jnp.concatenate(
                        [
                            jnp.where(inside[t] & (left if h == 0 else ~left), query, 0.0)
                            for t in range(4)
                        ],
                        axis=1,
                    )
                    for h in range(HEADS)
                ],
                axis=0,
            ).astype(BF)
            spans = [slice((ay * 4 + t) * LANES, (ay * 4 + t + 1) * LANES) for t in range(4)]
            key_cat = jnp.concatenate([keys[s] for s in spans], axis=1)
            scores = dot_t(expanded, key_cat)
            weights = jnp.exp2(scores * (sharpness * math.log2(math.e)))
            spread = jnp.concatenate(
                [
                    jnp.concatenate(
                        [
                            jnp.where(inside[t], weights[h * quota : (h + 1) * quota], 0.0)
                            for t in range(4)
                        ],
                        axis=1,
                    )
                    for h in range(HEADS)
                ],
                axis=0,
            ).astype(BF)
            value_cat = jnp.concatenate(
                [jnp.concatenate([values[s], ones_block], axis=1) for s in spans], axis=0
            )
            both = dot(spread, value_cat)
            picked = jnp.where(left, both[:quota, :LANES], both[quota:, :LANES])
            totals = jnp.where(left, both[:quota, LANES:], both[quota:, LANES:])
            attended.append((picked / totals).astype(BF))
        result = x_band.astype(F32) + dot(jnp.concatenate(attended, axis=0), proj_ref[3])
        res_ref[...] = result
        for r in range(band_rows):
            line = ax * (band_rows // LANES) + r // LANES
            i = index_ref[line, r % LANES]
            wide_ref[pl.ds(i, 1), :] = res_ref[pl.ds(r, 1), :]
        return carry

    lax.fori_loop(0, along_x, band, 0)
    out_ref[...] = wide_ref[...].astype(BF)


def spec(space):
    return pl.BlockSpec(memory_space=space)


def body(
    points,
    embed_weight,
    inner_weights,
    output_weight,
    counts,
    point_order,
    inducing,
    first_proj,
    second_proj,
    mixing,
):
    along_x = lax.axis_size("tx")
    along_y = lax.axis_size("ty")
    devices = along_x * along_y
    index_x = lax.axis_index("tx")
    index_y = lax.axis_index("ty")
    own_index = index_x * along_y + index_y
    point_count, width = points.shape
    quota = point_count // devices
    grid_x, grid_y = along_x * TLX, along_y * TLY
    lines = point_count // LANES
    chunk = 512
    own_counts = lax.dynamic_index_in_dim(counts, own_index, 0, keepdims=False)
    position = jnp.stack([index_x, index_y]).astype(jnp.int32)
    limit = pltpu.CompilerParams(vmem_limit_bytes=56 * 1024 * 1024)

    features, index = pl.pallas_call(
        functools.partial(encode_kernel, grid_y, along_y, quota),
        out_shape=(
            jax.ShapeDtypeStruct((point_count, width), BF),
            jax.ShapeDtypeStruct((lines, LANES), jnp.int32),
        ),
        in_specs=[spec(VMEM)] * 4 + [spec(SMEM), spec(VMEM)],
        out_specs=(spec(VMEM), spec(VMEM)),
        scratch_shapes=[
            SMEM((counts.shape[1],), jnp.int32),
            SMEM((lines, LANES), jnp.int32),
            VMEM((point_count, width), F32),
            VMEM((chunk, width), F32),
            VMEM((chunk, width), F32),
            pltpu.SemaphoreType.DMA,
        ],
        compiler_params=limit,
        name="encode_points",
    )(
        points,
        embed_weight,
        inner_weights,
        output_weight,
        own_counts,
        point_order.reshape(lines, LANES),
    )

    arrived = lax.all_to_all(
        features.reshape(devices, quota, width), ("tx", "ty"), split_axis=0, concat_axis=0, tiled=True
    ).reshape(point_count, width)

    summary = pl.pallas_call(
        functools.partial(summarize_kernel, along_y, quota),
        out_shape=jax.ShapeDtypeStruct((TLX * TLY * LANES, width), BF),
        in_specs=[spec(VMEM), spec(SMEM), spec(SMEM), spec(VMEM), spec(VMEM)],
        out_specs=spec(VMEM),
        scratch_shapes=[
            VMEM((width, 3 * LANES), BF),
            VMEM((HEADS, LANES, 4 * LANES), F32),
        ],
        compiler_params=limit,
        name="summarize_tiles",
    )(arrived, counts, position, inducing, first_proj)

    everyone = lax.all_gather(summary, ("tx", "ty"), axis=0, tiled=True)
    everyone = everyone.reshape(devices, TLX, TLY, LANES, width)

    return pl.pallas_call(
        functools.partial(finish_kernel, along_x, along_y, quota),
        out_shape=jax.ShapeDtypeStruct((point_count, width), BF),
        in_specs=[
            spec(pl.ANY),
            spec(VMEM),
            spec(SMEM),
            spec(SMEM),
            spec(VMEM),
            spec(VMEM),
        ],
        out_specs=spec(VMEM),
        scratch_shapes=[
            VMEM((grid_x + 2, grid_y + 2, LANES, width), BF),
            VMEM((6 * LANES, 2 * LANES), BF),
            VMEM((2, 4 * LANES, 2 * LANES), BF),
            VMEM((width, 2 * LANES), BF),
            VMEM((point_count, width), F32),
            VMEM((along_y * quota, width), F32),
            pltpu.SemaphoreType.DMA((devices,)),
        ],
        compiler_params=limit,
        name="finish_points",
    )(everyone, features, own_counts, index, second_proj, mixing)


def solution(mesh):
    placed = (P(("tx", "ty"), None), P(), P(), P(), P(), P(("tx", "ty"), None), P(), P(), P(), P())
    return jax.shard_map(
        body, mesh=mesh, in_specs=placed, out_specs=P(("tx", "ty"), None), check_vma=False
    )
```

time: 314 us -> 160 us (0.51)
  local copies, waits for them, and re-layouts: 117 us -> 2.14 us
  matrix products: 73.7 us -> 0 us
  Pallas kernels: 0 us -> 49.4 us
  starting transfers between devices: 23.9 us -> 7.34 us
  between operations: 0.69 us -> 13.4 us
  waiting for transfers between devices: 93.7 us -> 86.5 us
    gather x3 -> x0, local copies, waits for them, and re-layouts: 90.7 us -> none  [the longest x1 33.8 us: body(): jnp.take_along_axis(send_starts.T, send_which, axis=1) + send_within]
    dot_general x37 -> x0, matrix products: 73.7 us -> none  [the longest x8 20.7 us: place_block(): jnp.dot(table, rows, preferred_element_type=jnp.float32)]
    all_to_all x2 -> x1, waiting for transfers between devices: 93.6 us -> 24.3 us  [body(): lax.all_to_all(features.reshape(devices, quota, width), ('tx', 'ty'), spl...]
    all_gather x0 -> x1, waiting for transfers between devices: none -> 62.1 us  [body(): everyone = lax.all_gather(summary, ('tx', 'ty'), axis=0, tiled=True)]
    pallas_call x0 -> x3, Pallas kernels: none -> 49.4 us  [the longest x1 26.6 us: body(): pl.pallas_call(functools.partial(finish_kernel, along_x, along_y, quota),...]
    convert_element_type x4 -> x0, local copies, waits for them, and re-layouts: 11.3 us -> none  [the longest x3 7.27 us: unit_heads(): return (pieces / magnitude).reshape(projected.shape).astype(jnp.bfloat16)]
    ppermute x4 -> x0, starting transfers between devices: 9.18 us -> none  [the longest x2 6.38 us: padded_2(): lax.ppermute(lax.slice_in_dim(block, block.shape[dim] - width, None, axis...]
    all_to_all x2 -> x1, starting transfers between devices: 14.8 us -> 7.29 us  [body(): lax.all_to_all(features.reshape(devices, quota, width), ('tx', 'ty'), spl...]
  transfers between devices with their start and end apart: 6 -> 2, of which waited for: 3 -> 2; matrix products, arithmetic and copies ran while one was open for 4% -> 0% of each run, Pallas kernels for 0% -> 0%
where the time goes in v1:
time: 160 us; the launch traced here: 159 us
  waiting for transfers between devices  86.5 us (54%)
  Pallas kernels  49.4 us (31%)
  between operations  13.4 us (8%)
  starting transfers between devices  7.34 us (5%)
  local copies, waits for them, and re-layouts  2.14 us (1%)
    all_gather x1, waiting for transfers between devices, body(): everyone = lax.all_gather(summary, ('tx', 'ty'), axis=0, tiled=True)  62.1 us
    pallas_call x1, Pallas kernels, body(): pl.pallas_call(functools.partial(finish_kernel, along_x, along_y, quota),...  26.6 us
    all_to_all x1, waiting for transfers between devices, body(): lax.all_to_all(features.reshape(devices, quota, width), ('tx', 'ty'), spl...  24.3 us
    pallas_call x1, Pallas kernels, body(): pl.pallas_call(functools.partial(encode_kernel, grid_y, along_y, quota),...  13.6 us
    pallas_call x1, Pallas kernels, body(): pl.pallas_call(functools.partial(summarize_kernel, along_y, quota), out_s...  9.19 us
    all_to_all x1, starting transfers between devices, body(): lax.all_to_all(features.reshape(devices, quota, width), ('tx', 'ty'), spl...  7.29 us
  transfers between devices with their start and end apart: 2, of which 2 were waited for; matrix products, arithmetic and copies ran while one was open for 0% of the time, Pallas kernels for 0%

profile of v1, /device:TPU:0, one launch (start us, length us, event | category | flops | bytes accessed | tf_op | source)
XLA Modules:
  0.0 159.4 jit_solution(1670902421790193653)
XLA Ops:
  6.5 1.2 dynamic-slice_bitcast_fusion.counts_ref
  7.7 13.6 %encode_points.1 = (bf16[4096,128]{1,0:T(8,128)(2,1)}, s32[32,128]{1,0:T(8,128)}) custom-call(bf16[4096,128]{1,0:T(8,128)(2,1)} %points_ref.1, bf16[128,512]{1,0:T(8,128)(2,1)} %w1_ref.1, bf16[1,512,512]{2,1,0:T(8,128)(2,1)} %w2_ref.1, bf16[512,128]{1,0:T(8,128)(2,1)} %w3_ref.1, s32[128]{0:T(128)} %dynamic-slice_bitcast_fusion.counts_ref, s32[32,128]{1,0:T(8,128)} %bitcast.11), custom_call_target="tpu_custom_call" | custom-call | tf_op jit(solution)/shard_map/encode_points/pallas_call | solution.py:412
  21.3 7.3 %all-to-all-start = ((bf16[32,128,128]{2,1,0:T(8,128)(2,1)}), bf16[32,128,128]{2,1,0:T(8,128)(2,1)S(1)}, u32[]{:S(2)}, u32[]{:S(2)}) async-start(bf16[32,128,128]{2,1,0:T(8,128)(2,1)} %bitcast.10), calls=%async_computation | async-start | bytes 2097152 | tf_op jit(solution)/shard_map/all_to_all | solution.py:439
  28.6 0.0 all-gather.2.cloned.1.call-start
  28.7 0.7 pad_add_fusion.where_ref
  29.3 24.3 %all-to-all-done = bf16[32,128,128]{2,1,0:T(8,128)(2,1)S(1)} async-done(((bf16[32,128,128]{2,1,0:T(8,128)(2,1)}), bf16[32,128,128]{2,1,0:T(8,128)(2,1)S(1)}, u32[]{:S(2)}, u32[]{:S(2)}) %all-to-all-start) | async-done | bytes 1048608 | tf_op jit(solution)/shard_map/all_to_all | solution.py:439
  53.7 0.0 copy-start
  53.7 1.0 copy-done
  54.7 9.2 %summarize_tiles.1 = bf16[512,128]{1,0:T(8,128)(2,1)} custom-call(bf16[4096,128]{1,0:T(8,128)(2,1)} %bitcast.9, s32[32,128]{1,0:T(8,128)} %counts_ref.1, s32[2]{0:T(128)} %pad_add_fusion.where_ref, bf16[128,128]{1,0:T(8,128)(2,1)} %inducing_ref.1, bf16[4,128,128]{2,1,0:T(8,128)(2,1)} %proj_ref.2), custom_call_target="tpu_custom_call" | custom-call | tf_op jit(solution)/shard_map/summarize_tiles/pallas_call | solution.py:443
  63.8 0.0 all-gather.2.cloned.1.call-update
  63.9 62.1 %all-gather.2.cloned.1.call-done = bf16[16384,128]{1,0:T(8,128)(2,1)} async-done(((bf16[512,128]{1,0:T(8,128)(2,1)}), bf16[16384,128]{1,0:T(8,128)(2,1)}) %all-gather.2.cloned.1.call-update) | async-done | bytes 4194320 | tf_op jit(solution)/shard_map/all_gather | solution.py:456
  126.0 26.6 %finish_points.1 = bf16[4096,128]{1,0:T(8,128)(2,1)} custom-call(bf16[32,2,2,128,128]{4,3,2,1,0:T(8,128)(2,1)} %bitcast.8, bf16[4096,128]{1,0:T(8,128)(2,1)} %get-tuple-element.7.feat_ref, s32[128]{0:T(128)} %dynamic-slice_bitcast_fusion.counts_ref, s32[32,128]{1,0:T(8,128)} %get-tuple-element.8.index_ref, bf16[4,128,128]{2,1,0:T(8,128)(2,1)} %proj_ref.3, ...), custom_call_target="tpu_custom_call" | custom-call | tf_op jit(solution)/shard_map/finish_points/pallas_call | solution.py:459
Async XLA Ops:
  21.3 32.4 %all-to-all-start = ((bf16[32,128,128]{2,1,0:T(8,128)(2,1)}), bf16[32,128,128]{2,1,0:T(8,128)(2,1)S(1)}, u32[]{:S(2)}, u32[]{:S(2)}) async-start(bf16[32,128,128]{2,1,0:T(8,128)(2,1)} %bitcast.10), calls=%async_computation | async-start | bytes 2097152 | tf_op jit(solution)/shard_map/all_to_all | solution.py:439
  28.6 97.4 %all-gather.2.cloned.1.call-start = ((), (), s32[]{:S(2)}) async-start(), calls=%async_computation.1 | async-start | bytes 4325376 | tf_op jit(solution)/shard_map/all_gather | solution.py:456
  53.7 1.0 copy-start
Sparse Core Ops, SparseCore 0:
  64.0 61.9 all-gather.1

commit v2 on v1

v2 whole, which is shorter than its diff:
```python
import functools
import math

import jax
import jax.numpy as jnp
from jax import lax
from jax.experimental import pallas as pl
from jax.experimental.pallas import tpu as pltpu
from jax.sharding import PartitionSpec as P

HEADS = 2
TLX = 2
TLY = 2
LANES = 128
BF = jnp.bfloat16
F32 = jnp.float32

sharpness = 32.0
epsilon = 1e-06
neighbour_steps = ((-1, -1), (-1, 0), (-1, 1), (0, -1), (0, 1), (1, -1), (1, 0), (1, 1))
VMEM = pltpu.VMEM
SMEM = pltpu.SMEM


def dot(a, b):
    return jnp.dot(a, b, preferred_element_type=F32)


def dot_t(a, b):
    return lax.dot_general(a, b, (((1,), (1,)), ((), ())), preferred_element_type=F32)


def head_ones():
    row = lax.broadcasted_iota(jnp.int32, (2 * LANES, LANES), 0)
    col = lax.broadcasted_iota(jnp.int32, (2 * LANES, LANES), 1)
    half = LANES // HEADS
    same = ((row % LANES) // half) == (col // half)
    return jnp.where(same, 1.0, 0.0).astype(BF)


def unit(v, ones):
    square = v * v
    high = square.astype(BF)
    low = (square - high.astype(F32)).astype(BF)
    total = dot(jnp.concatenate([high, low], axis=1), ones)
    return v * lax.rsqrt(total + epsilon)


def silu(v):
    half = 0.5 * v
    return half + half * jnp.tanh(half)


def encode_kernel(
    grid_y,
    along_y,
    quota,
    points_ref,
    w1_ref,
    w2_ref,
    w3_ref,
    counts_ref,
    order_ref,
    feat_ref,
    index_ref,
    off_ref,
    index_s,
    wide_ref,
    xa_ref,
    xb_ref,
    sem,
):
    tiles = counts_ref.shape[0]
    order_rows = order_ref.shape[0]
    rows_total = points_ref.shape[0]
    chunk = xa_ref.shape[0]

    def add_up(g, total):
        off_ref[g] = total
        return total + counts_ref[g]

    lax.fori_loop(0, tiles, add_up, jnp.int32(0), unroll=8)
    wide_ref[...] = points_ref[...].astype(F32)
    lane = lax.broadcasted_iota(jnp.int32, (1, LANES), 1)

    def run_of(start):
        line = start >> 7
        shift = start & (LANES - 1)
        first = order_ref[pl.ds(jnp.clip(line, 0, order_rows - 1), 1), :]
        second = order_ref[pl.ds(jnp.clip(line + 1, 0, order_rows - 1), 1), :]
        merged = jnp.where(lane < shift, second, first)
        return pltpu.roll(merged, (LANES - shift) & (LANES - 1), 1)

    per_line = LANES // quota

    def index_line(line, carry):
        value = jnp.zeros((1, LANES), jnp.int32)
        for k in range(per_line):
            d = line * per_line + k
            g1 = (d // along_y) * (TLX * grid_y) + (d % along_y) * TLY
            n1 = counts_ref[g1] + counts_ref[g1 + 1]
            run1 = run_of(off_ref[g1] - k * quota)
            run2 = run_of(off_ref[g1 + grid_y] - n1 - k * quota)
            both = jnp.where(lane < k * quota + n1, run1, run2)
            value = both if k == 0 else jnp.where(lane >= k * quota, both, value)
        index_ref[pl.ds(line, 1), :] = value
        return carry

    lax.fori_loop(0, rows_total // LANES, index_line, 0)
    copy = pltpu.make_async_copy(index_ref, index_s, sem)
    copy.start()
    copy.wait()

    def gather(c, buffer):
        for r in range(chunk):
            i = index_s[c * (chunk // LANES) + r // LANES, r % LANES]
            buffer[pl.ds(r, 1), :] = wide_ref[pl.ds(i, 1), :]

    def network(c, buffer):
        x = buffer[...].astype(BF)
        hidden = silu(dot(x, w1_ref[...])).astype(BF)
        hidden = silu(dot(hidden, w2_ref[0])).astype(BF)
        start = pl.multiple_of(c * chunk, chunk)
        feat_ref[pl.ds(start, chunk), :] = dot(hidden, w3_ref[...]).astype(BF)

    chunks = rows_total // chunk
    gather(0, xa_ref)

    def step(k, carry):
        c = 2 * k
        gather(c + 1, xb_ref)
        network(c, xa_ref)
        gather(jnp.minimum(c + 2, chunks - 1), xa_ref)
        network(c + 1, xb_ref)
        return carry

    lax.fori_loop(0, chunks // 2, step, 0)


def tile_bounds(n0, n1, n2):
    return (n0, n0 + n1, n0 + n1 + n2)


def tile_of(position, counts_ref, pieces, piece_id, grid_y):
    bounds = [None, None, None]
    for k, (s, base) in enumerate(pieces):
        found = tile_bounds(
            counts_ref[s, base], counts_ref[s, base + 1], counts_ref[s, base + grid_y]
        )
        for i in range(3):
            if k == 0:
                bounds[i] = jnp.full(position.shape, found[i], jnp.int32)
            else:
                bounds[i] = jnp.where(piece_id >= k, found[i], bounds[i])
    return sum((position >= b).astype(jnp.int32) for b in bounds)


def source_of(member, where_ref, low_count, along_y):
    return (member // low_count) * along_y + where_ref[1] * low_count + member % low_count


def tile_base(block, where_ref, low_blocks, grid_y):
    return where_ref[0] * (TLX * grid_y) + (where_ref[2] * low_blocks + block) * TLY


def partial_kernel(
    along_y, rows_ref, counts_ref, where_ref, inducing_ref, proj_ref, own_ref, send_ref, num_ref
):
    members, blocks, quota, width = rows_ref.shape
    grid_y = along_y * TLY
    half = LANES // HEADS
    group = min(512 // quota, members)
    chunk = group * quota
    ones = head_ones()
    lane = lax.broadcasted_iota(jnp.int32, (1, LANES), 1)
    left = lane < half
    queries = unit(dot(inducing_ref[...], proj_ref[0]), ones)
    queries = jnp.concatenate(
        [jnp.where(left, queries, 0.0), jnp.where(left, 0.0, queries)], axis=0
    ).astype(BF)
    wv_t = proj_ref[2].astype(F32).T.astype(BF)
    num_ref[...] = jnp.zeros_like(num_ref)
    spot = lax.broadcasted_iota(jnp.int32, (1, chunk), 1)
    tile_row = lax.broadcasted_iota(jnp.int32, (16, chunk), 0)
    low_count = along_y // blocks

    def step(c, carry):
        for b in range(blocks):
            x = jnp.concatenate([rows_ref[c * group + k, b] for k in range(group)], axis=0)
            keys = unit(dot(x, proj_ref[1]), ones).astype(BF)
            weights = jnp.exp2(dot_t(keys, queries) * (sharpness * math.log2(math.e))).astype(BF)
            values = dot_t(wv_t, x)
            base = tile_base(b, where_ref, blocks, grid_y)
            pieces = [
                (source_of(c * group + k, where_ref, low_count, along_y), base)
                for k in range(group)
            ]
            tile = tile_of(spot % quota, counts_ref, pieces, spot // quota, grid_y)
            stacked = [jnp.where(tile == t, values, 0.0).astype(BF) for t in range(4)]
            stacked.append(jnp.where(tile_row == tile, 1.0, 0.0).astype(BF))
            num_ref[b] += dot(jnp.concatenate(stacked, axis=0), weights)
        return carry

    lax.fori_loop(0, members // group, step, 0)
    totals = []
    for b in range(blocks):
        for t in range(4):
            rows = slice((b * 4 + t) * LANES, (b * 4 + t + 1) * LANES)
            value = jnp.concatenate(
                [
                    num_ref[b, t * LANES : t * LANES + half, :LANES],
                    num_ref[b, t * LANES + half : (t + 1) * LANES, LANES:],
                ],
                axis=0,
            )
            own_ref[rows, :] = value
            send_ref[rows, :] = value.astype(BF)
        for h in range(HEADS):
            totals.append(num_ref[b, 4 * LANES : 4 * LANES + 4, h * LANES : (h + 1) * LANES])
    totals = jnp.concatenate(totals, axis=0)
    own_ref[blocks * 4 * LANES :, :] = totals
    send_ref[blocks * 4 * LANES :, :] = totals.astype(BF)


def combine_kernel(blocks, own_ref, other_ref, inducing_ref, proj_ref, out_ref):
    half = LANES // HEADS
    last = blocks * 4 * LANES
    totals = own_ref[last:, :] + other_ref[last:, :].astype(F32)
    for b in range(blocks):
        for t in range(4):
            rows = slice((b * 4 + t) * LANES, (b * 4 + t + 1) * LANES)
            value = own_ref[rows, :] + other_ref[rows, :].astype(F32)
            line = b * HEADS * 4 + t
            attended = jnp.concatenate(
                [
                    value[:half] / totals[line : line + 1],
                    value[half:] / totals[line + 4 : line + 5],
                ],
                axis=0,
            )
            attended = attended.T.astype(BF)
            out = inducing_ref[...].astype(F32) + dot(attended, proj_ref[3])
            out_ref[t // 2, b * TLY + t % 2] = out.astype(BF)


def finish_kernel(
    along_y,
    summary_ref,
    column_ref,
    below_ref,
    above_ref,
    rows_ref,
    counts_ref,
    where_ref,
    proj_ref,
    mixing_ref,
    out_ref,
    mid_ref,
    side_ref,
    key_ref,
    value_ref,
):
    members, blocks, quota, width = rows_ref.shape
    grid_y = along_y * TLY
    half = LANES // HEADS
    group = min(512 // quota, members)
    chunk = group * quota
    low = where_ref[2]
    tall = summary_ref.shape[1]

    row = lax.broadcasted_iota(jnp.int32, (LANES, LANES), 0)
    col = lax.broadcasted_iota(jnp.int32, (LANES, LANES), 1)
    eye = jnp.where(row == col, 1.0, 0.0).astype(BF)
    blank = jnp.zeros((LANES, LANES), BF)

    def mix(a, b):
        return eye if (a, b) == (0, 0) else mixing_ref[neighbour_steps.index((a, b))]

    for k, a in enumerate((-1, 0, 1)):
        rows = slice(k * 2 * LANES, (k + 1) * 2 * LANES)
        mid_ref[rows, :] = jnp.concatenate(
            [
                jnp.concatenate([mix(a, 0), mix(a, -1)], axis=1),
                jnp.concatenate([mix(a, 1), mix(a, 0)], axis=1),
            ],
            axis=0,
        )
    for k, b in enumerate((-1, 1)):
        side_ref[k] = jnp.concatenate(
            [
                jnp.concatenate([mix(0, b), mix(-1, b)], axis=1),
                jnp.concatenate([mix(1, b), mix(0, b)], axis=1),
                jnp.concatenate([mix(-1, b), blank], axis=1),
                jnp.concatenate([blank, mix(1, b)], axis=1),
            ],
            axis=0,
        )
    ones = head_ones()
    lane = lax.broadcasted_iota(jnp.int32, (1, LANES), 1)
    left = lane < half

    def tile(i, j):
        if 0 <= j < tall:
            return below_ref[j] if i == 0 else above_ref[j] if i == 3 else summary_ref[i - 1, j]
        held = below_ref[tall] if i == 0 else above_ref[tall] if i == 3 else column_ref[i - 1]
        wanted = 1 if j < 0 else 0
        return jnp.where(low == wanted, held, blank)

    mids, lefts, rights = [], [], []
    for i in range(2):
        for b in range(blocks):
            mids.append(
                jnp.concatenate(
                    [tile(i + r, 2 * b + s) for r in range(3) for s in range(2)], axis=1
                )
            )
    for b in range(blocks):
        lefts.append(jnp.concatenate([tile(i, 2 * b - 1) for i in (1, 2, 0, 3)], axis=1))
        rights.append(jnp.concatenate([tile(i, 2 * b + 2) for i in (1, 2, 0, 3)], axis=1))
    middle = dot(jnp.concatenate(mids, axis=0), mid_ref[...])
    from_left = dot(jnp.concatenate(lefts, axis=0), side_ref[0])
    from_right = dot(jnp.concatenate(rights, axis=0), side_ref[1])
    mixtures = []
    for b in range(blocks):
        span = slice(b * LANES, (b + 1) * LANES)
        for i in range(2):
            m = middle[(i * blocks + b) * LANES : (i * blocks + b + 1) * LANES]
            cols = slice(i * LANES, (i + 1) * LANES)
            mixtures.append((m[:, :LANES] + from_left[span, cols]).astype(BF))
            mixtures.append((m[:, LANES:] + from_right[span, cols]).astype(BF))
    mixtures = jnp.concatenate(mixtures, axis=0)
    keys = unit(dot(mixtures, proj_ref[1]), ones)
    values = dot(mixtures, proj_ref[2])
    for b in range(blocks):
        spans = [slice((b * 4 + t) * LANES, (b * 4 + t + 1) * LANES) for t in range(4)]
        for h in range(HEADS):
            mine = left if h == 0 else ~left
            key_ref[b, h * LANES : (h + 1) * LANES, :] = jnp.concatenate(
                [jnp.where(mine, keys[s], 0.0) for s in spans], axis=1
            ).astype(BF)
            flags = jnp.broadcast_to(jnp.where(mine, 1.0, 0.0), (LANES, LANES))
            for t, s in enumerate(spans):
                rows = slice((t * HEADS + h) * LANES, (t * HEADS + h + 1) * LANES)
                value_ref[b, rows, :] = jnp.concatenate(
                    [jnp.where(mine, values[s], 0.0), flags], axis=1
                ).astype(BF)
    spot = lax.broadcasted_iota(jnp.int32, (chunk, LANES), 0)

    def step(c, carry):
        for b in range(blocks):
            x = jnp.concatenate([rows_ref[c * group + k, b] for k in range(group)], axis=0)
            query = unit(dot(x, proj_ref[0]), ones)
            base = tile_base(b, where_ref, blocks, grid_y)
            pieces = [
                (source_of(c * group + k, where_ref, along_y // blocks, along_y), base)
                for k in range(group)
            ]
            which = tile_of(spot % quota, counts_ref, pieces, spot // quota, grid_y)
            inside = [which == t for t in range(4)]
            expanded = jnp.concatenate(
                [jnp.where(m, query, 0.0).astype(BF) for m in inside], axis=1
            )
            scores = dot_t(expanded, key_ref[b])
            weights = jnp.exp2(scores * (sharpness * math.log2(math.e)))
            spread = jnp.concatenate(
                [
                    jnp.where(m, weights[:, h * LANES : (h + 1) * LANES], 0.0).astype(BF)
                    for m in inside
                    for h in range(HEADS)
                ],
                axis=1,
            )
            both = dot(spread, value_ref[b])
            attended = (both[:, :LANES] / both[:, LANES:]).astype(BF)
            result = (x.astype(F32) + dot(attended, proj_ref[3])).astype(BF)
            for k in range(group):
                out_ref[c * group + k, b] = result[k * quota : (k + 1) * quota]
        return carry

    lax.fori_loop(0, members // group, step, 0)


def scatter_kernel(rows_ref, index_ref, out_ref, wide_ref, part_ref):
    chunk = part_ref.shape[0]
    total = rows_ref.shape[0]

    def step(c, carry):
        start = pl.multiple_of(c * chunk, chunk)
        part_ref[...] = rows_ref[pl.ds(start, chunk), :].astype(F32)
        for r in range(chunk):
            i = index_ref[c * (chunk // LANES) + r // LANES, r % LANES]
            wide_ref[pl.ds(i, 1), :] = part_ref[pl.ds(r, 1), :]
        return carry

    lax.fori_loop(0, total // chunk, step, 0)
    out_ref[...] = wide_ref[...].astype(BF)


def spec(space):
    return pl.BlockSpec(memory_space=space)


def body(
    points,
    embed_weight,
    inner_weights,
    output_weight,
    counts,
    point_order,
    inducing,
    first_proj,
    second_proj,
    mixing,
):
    along_x = lax.axis_size("tx")
    highs = lax.axis_size("zh")
    lows = lax.axis_size("zl")
    along_y = highs * lows
    devices = along_x * along_y
    index_x = lax.axis_index("tx")
    index_h = lax.axis_index("zh")
    index_l = lax.axis_index("zl")
    own_index = index_x * along_y + index_h * lows + index_l
    point_count, width = points.shape
    quota = point_count // devices
    grid_y = along_y * TLY
    blocks = along_y // lows
    members = along_x * lows
    tall = blocks * TLY
    lines = point_count // LANES
    chunk = 512
    group_axes = ("tx", "zl")
    own_counts = lax.dynamic_index_in_dim(counts, own_index, 0, keepdims=False)
    position = jnp.stack([index_x, index_h, index_l]).astype(jnp.int32)
    limit = pltpu.CompilerParams(vmem_limit_bytes=56 * 1024 * 1024)

    features, index = pl.pallas_call(
        functools.partial(encode_kernel, grid_y, along_y, quota),
        out_shape=(
            jax.ShapeDtypeStruct((point_count, width), BF),
            jax.ShapeDtypeStruct((lines, LANES), jnp.int32),
        ),
        in_specs=[spec(VMEM)] * 4 + [spec(SMEM), spec(VMEM)],
        out_specs=(spec(VMEM), spec(VMEM)),
        scratch_shapes=[
            SMEM((counts.shape[1],), jnp.int32),
            SMEM((lines, LANES), jnp.int32),
            VMEM((point_count, width), F32),
            VMEM((chunk, width), F32),
            VMEM((chunk, width), F32),
            pltpu.SemaphoreType.DMA,
        ],
        compiler_params=limit,
        name="encode_points",
    )(
        points,
        embed_weight,
        inner_weights,
        output_weight,
        own_counts,
        point_order.reshape(lines, LANES),
    )

    arrived = lax.all_to_all(
        features.reshape(members, blocks * quota, width),
        group_axes,
        split_axis=0,
        concat_axis=0,
        tiled=True,
    ).reshape(members, blocks, quota, width)

    part_rows = blocks * 4 * LANES + blocks * HEADS * 4
    own, send = pl.pallas_call(
        functools.partial(partial_kernel, along_y),
        out_shape=(
            jax.ShapeDtypeStruct((part_rows, LANES), F32),
            jax.ShapeDtypeStruct((part_rows, LANES), BF),
        ),
        in_specs=[spec(VMEM), spec(SMEM), spec(SMEM), spec(VMEM), spec(VMEM)],
        out_specs=(spec(VMEM), spec(VMEM)),
        scratch_shapes=[VMEM((blocks, 4 * LANES + 16, HEADS * LANES), F32)],
        compiler_params=limit,
        name="partial_attention",
    )(arrived, counts, position, inducing, first_proj)

    other = lax.ppermute(send, "zh", [(i, highs - 1 - i) for i in range(highs)])

    summary = pl.pallas_call(
        functools.partial(combine_kernel, blocks),
        out_shape=jax.ShapeDtypeStruct((TLX, tall, LANES, width), BF),
        in_specs=[spec(VMEM)] * 4,
        out_specs=spec(VMEM),
        compiler_params=limit,
        name="combine_partials",
    )(own, other, inducing, first_proj)

    edge = jnp.where(index_l == 0, summary[:, tall - 1], summary[:, 0])
    column = lax.ppermute(edge, "zl", [(i, lows - 1 - i) for i in range(lows)])
    wider = jnp.concatenate([summary, column[:, None]], axis=1)
    forward = [(i, i + 1) for i in range(along_x - 1)]
    backward = [(i + 1, i) for i in range(along_x - 1)]
    below = lax.ppermute(wider[TLX - 1], "tx", forward)
    above = lax.ppermute(wider[0], "tx", backward)

    result = pl.pallas_call(
        functools.partial(finish_kernel, along_y),
        out_shape=jax.ShapeDtypeStruct((members, blocks, quota, width), BF),
        in_specs=[spec(VMEM)] * 5 + [spec(SMEM)] * 2 + [spec(VMEM)] * 2,
        out_specs=spec(VMEM),
        scratch_shapes=[
            VMEM((6 * LANES, 2 * LANES), BF),
            VMEM((2, 4 * LANES, 2 * LANES), BF),
            VMEM((blocks, HEADS * LANES, 4 * LANES), BF),
            VMEM((blocks, 4 * HEADS * LANES, 2 * LANES), BF),
        ],
        compiler_params=limit,
        name="finish_rows",
    )(summary, column, below, above, arrived, counts, position, second_proj, mixing)

    returned = lax.all_to_all(
        result.reshape(members, blocks * quota, width),
        group_axes,
        split_axis=0,
        concat_axis=0,
        tiled=True,
    ).reshape(point_count, width)

    return pl.pallas_call(
        scatter_kernel,
        out_shape=jax.ShapeDtypeStruct((point_count, width), BF),
        in_specs=[spec(VMEM), spec(SMEM)],
        out_specs=spec(VMEM),
        scratch_shapes=[VMEM((point_count, width), F32), VMEM((chunk, width), F32)],
        compiler_params=limit,
        name="scatter_rows",
    )(returned, index)


def solution(mesh):
    along_x, along_y = mesh.devices.shape
    split = jax.sharding.Mesh(mesh.devices.reshape(along_x, 2, along_y // 2), ("tx", "zh", "zl"))
    rows = P(("tx", "zh", "zl"), None)
    placed = (rows, P(), P(), P(), P(), rows, P(), P(), P(), P())
    return jax.shard_map(body, mesh=split, in_specs=placed, out_specs=rows, check_vma=False)
```

time: 160 us -> 117 us (0.73)
  waiting for transfers between devices: 86.5 us -> 31.4 us
  blocking collectives: 0 us -> 22.1 us
  between operations: 13.4 us -> 0.07 us
  Pallas kernels: 49.4 us -> 42.8 us
  starting transfers between devices: 7.34 us -> 13.8 us
  other arithmetic: 0.67 us -> 2.5 us
    all_gather x1 -> x0, waiting for transfers between devices: 62.1 us -> none  [body(): everyone = lax.all_gather(summary, ('tx', 'ty'), axis=0, tiled=True)]
    all_to_all x0 -> x1, blocking collectives: none -> 22.1 us  [body(): lax.all_to_all(result.reshape(members, blocks * quota, width), group_axes...]
    ppermute x0 -> x4, waiting for transfers between devices: none -> 17 us  [the longest x1 12.3 us: body(): other = lax.ppermute(send, 'zh', [(i, highs - 1 - i) for i in range(highs)])]
    all_to_all x1, waiting for transfers between devices: 24.3 us -> 14.4 us  [body(): lax.all_to_all(features.reshape(members, blocks * quota, width), group_ax...]
    ppermute x0 -> x4, starting transfers between devices: none -> 7.57 us  [the longest x1 3.04 us: body(): below = lax.ppermute(wider[TLX - 1], 'tx', forward)]
    pallas_call x2 -> x4, Pallas kernels: 35.8 us -> 29.1 us  [the longest x1 13.5 us: body(): pl.pallas_call(functools.partial(finish_kernel, along_y), out_shape=jax.S...]
  transfers between devices with their start and end apart: 2 -> 5, of which waited for: 2 -> 4; matrix products, arithmetic and copies ran while one was open for 0% -> 1% of each run, Pallas kernels for 0% -> 0%
where the time goes in v2:
time: 117 us; the launch traced here: 116 us
  Pallas kernels  42.8 us (37%)
  waiting for transfers between devices  31.4 us (27%)
  blocking collectives  22.1 us (19%)
  starting transfers between devices  13.8 us (12%)
  local copies, waits for them, and re-layouts  3.58 us (3%)
  other arithmetic  2.5 us (2%)
    all_to_all x1, blocking collectives, body(): lax.all_to_all(result.reshape(members, blocks * quota, width), group_axes...  22.1 us
    all_to_all x1, waiting for transfers between devices, body(): lax.all_to_all(features.reshape(members, blocks * quota, width), group_ax...  14.4 us
    pallas_call x1, Pallas kernels, body(): pl.pallas_call(functools.partial(encode_kernel, grid_y, along_y, quota),...  13.6 us
    pallas_call x1, Pallas kernels, body(): pl.pallas_call(functools.partial(finish_kernel, along_y), out_shape=jax.S...  13.5 us
    ppermute x1, waiting for transfers between devices, body(): other = lax.ppermute(send, 'zh', [(i, highs - 1 - i) for i in range(highs)])  12.3 us
    pallas_call x1, Pallas kernels, body(): pl.pallas_call(functools.partial(partial_kernel, along_y), out_shape=(jax...  7.83 us
    all_to_all x1, starting transfers between devices, body(): lax.all_to_all(features.reshape(members, blocks * quota, width), group_ax...  6.28 us
    pallas_call x1, Pallas kernels, body(): pl.pallas_call(scatter_kernel, out_shape=jax.ShapeDtypeStruct((point_coun...  5.6 us
  transfers between devices with their start and end apart: 5, of which 4 were waited for; matrix products, arithmetic and copies ran while one was open for 1% of the time, Pallas kernels for 0%

profile of v2, /device:TPU:0, one launch (start us, length us, event | category | flops | bytes accessed | tf_op | source)
XLA Modules:
  0.0 116.3 jit_solution(5577703407047342325)
XLA Ops:
  0.0 1.2 %dynamic-slice_bitcast_fusion.counts_ref = s32[128]{0:T(128)} fusion(s32[32,128]{1,0:T(8,128)} %counts_ref.3, s32[]{:T(128)S(6)} %select_n.15), kind=kLoop, calls=%fused_computation.11 | loop fusion | bytes 1028 | tf_op jit(solution)/shard_map/jit(dynamic_index_in_dim)/squeeze | solution.py:433
  1.2 13.6 %encode_points.1 = (bf16[4096,128]{1,0:T(8,128)(2,1)}, s32[32,128]{1,0:T(8,128)}) custom-call(bf16[4096,128]{1,0:T(8,128)(2,1)} %points_ref.1, bf16[128,512]{1,0:T(8,128)(2,1)} %w1_ref.1, bf16[1,512,512]{2,1,0:T(8,128)(2,1)} %w2_ref.1, bf16[512,128]{1,0:T(8,128)(2,1)} %w3_ref.1, s32[128]{0:T(128)} %dynamic-slice_bitcast_fusion.counts_ref, s32[32,128]{1,0:T(8,128)} %bitcast.33), custom_call_target="tpu_custom_call" | custom-call | tf_op jit(solution)/shard_map/encode_points/pallas_call | solution.py:437
  14.9 6.3 %all-to-all-start = ((bf16[16,256,128]{2,1,0:T(8,128)(2,1)}), bf16[16,256,128]{2,1,0:T(8,128)(2,1)S(1)}, u32[]{:S(2)}, u32[]{:S(2)}) async-start(bf16[16,256,128]{2,1,0:T(8,128)(2,1)} %bitcast.31), calls=%async_computation | async-start | bytes 2097152 | tf_op jit(solution)/shard_map/all_to_all | solution.py:464
  21.2 0.6 pad_add_fusion.where_ref
  21.8 14.4 %all-to-all-done = bf16[16,256,128]{2,1,0:T(8,128)(2,1)S(1)} async-done(((bf16[16,256,128]{2,1,0:T(8,128)(2,1)}), bf16[16,256,128]{2,1,0:T(8,128)(2,1)S(1)}, u32[]{:S(2)}, u32[]{:S(2)}) %all-to-all-start) | async-done | bytes 1048608 | tf_op jit(solution)/shard_map/all_to_all | solution.py:464
  36.2 0.0 copy-start
  36.2 1.0 copy-done
  37.1 7.8 %partial_attention.1 = (f32[1040,128]{1,0:T(8,128)}, bf16[1040,128]{1,0:T(8,128)(2,1)}) custom-call(bf16[16,2,128,128]{3,2,1,0:T(8,128)(2,1)} %bitcast.27, s32[32,128]{1,0:T(8,128)} %counts_ref.3, s32[3]{0:T(128)} %pad_add_fusion.where_ref, bf16[128,128]{1,0:T(8,128)(2,1)} %inducing_ref.3, bf16[4,128,128]{2,1,0:T(8,128)(2,1)} %proj_ref.4), custom_call_target="tpu_custom_call" | custom-call | tf_op jit(solution)/shard_map/partial_attention/pallas_call | solution.py:473
  45.0 2.6 %collective-permute-start = (bf16[1040,128]{1,0:T(8,128)(2,1)}, bf16[1040,128]{1,0:T(8,128)(2,1)S(1)}, u32[]{:S(2)}, u32[]{:S(2)}) collective-permute-start(bf16[1040,128]{1,0:T(8,128)(2,1)} %get-tuple-element.11), channel_id=1, source_target_pairs={{0,2},{2,0},{1,3},{3,1},{4,6},{6,4},{5,7},{7,5},{8,10},{10,8},{9,1... | collective-permute-start | bytes 798728 | tf_op jit(solution)/shard_map/ppermute | solution.py:486
  47.5 12.3 %collective-permute-done.other_ref = bf16[1040,128]{1,0:T(8,128)(2,1)S(1)} collective-permute-done((bf16[1040,128]{1,0:T(8,128)(2,1)}, bf16[1040,128]{1,0:T(8,128)(2,1)S(1)}, u32[]{:S(2)}, u32[]{:S(2)}) %collective-permute-start) | collective-permute-done | bytes 266272 | tf_op jit(solution)/shard_map/ppermute | solution.py:486
  59.9 0.0 copy-start.1
  59.9 0.7 copy-done.1
  60.6 2.2 %combine_partials.1.summary_ref = bf16[2,4,128,128]{3,2,1,0:T(8,128)(2,1)} custom-call(f32[1040,128]{1,0:T(8,128)} %get-tuple-element.10.own_ref, bf16[1040,128]{1,0:T(8,128)(2,1)} %copy-done.1, bf16[128,128]{1,0:T(8,128)(2,1)} %inducing_ref.3, bf16[4,128,128]{2,1,0:T(8,128)(2,1)} %proj_ref.4), custom_call_target="tpu_custom_call" | custom-call | tf_op jit(solution)/shard_map/combine_partials/pallas_call | solution.py:488
  62.8 0.9 fusion.4
  63.7 0.7 collective-permute-start.1
  64.3 3.7 %collective-permute-done.1.column_ref = bf16[2,128,128]{2,1,0:T(8,128)(2,1)S(1)} collective-permute-done((bf16[2,128,128]{2,1,0:T(8,128)(2,1)S(1)}, bf16[2,128,128]{2,1,0:T(8,128)(2,1)S(1)}, u32[]{:S(2)}, u32[]{:S(2)}) %collective-permute-start.1) | collective-permute-done | bytes 65568 | tf_op jit(solution)/shard_map/ppermute | solution.py:498
  68.0 0.0 copy-start.2
  68.0 1.0 fusion.2
  69.0 0.0 copy-done.2
  69.0 1.3 %collective-permute-start.3 = (bf16[5,128,128]{2,1,0:T(8,128)(2,1)S(1)}, bf16[5,128,128]{2,1,0:T(8,128)(2,1)S(1)}, u32[]{:S(2)}, u32[]{:S(2)}) collective-permute-start(bf16[5,128,128]{2,1,0:T(8,128)(2,1)S(1)} %get-tuple-element.13), channel_id=1, source_target_pairs={{4,0},{8,4},{12,8},{16,12},{20,16},{24,20},{28,24},{5,1},{9,5},{13... | collective-permute-start | bytes 491528 | tf_op jit(solution)/shard_map/ppermute | solution.py:503
  70.3 3.0 %collective-permute-start.2 = (bf16[5,128,128]{2,1,0:T(8,128)(2,1)S(1)}, bf16[5,128,128]{2,1,0:T(8,128)(2,1)S(1)}, u32[]{:S(2)}, u32[]{:S(2)}) collective-permute-start(bf16[5,128,128]{2,1,0:T(8,128)(2,1)S(1)} %get-tuple-element.14), channel_id=1, source_target_pairs={{0,4},{4,8},{8,12},{12,16},{16,20},{20,24},{24,28},{1,5},{5,9},{9,... | collective-permute-start | bytes 491528 | tf_op jit(solution)/shard_map/ppermute | solution.py:502
  73.4 0.0 collective-permute-done.3.above_ref
  73.4 0.0 copy-start.3
  73.4 1.0 collective-permute-done.2.below_ref
  74.4 0.0 copy-done.3
  74.4 0.0 copy-start.4
  74.4 0.7 copy-done.4
  75.0 13.5 %finish_rows.1 = bf16[16,2,128,128]{3,2,1,0:T(8,128)(2,1)} custom-call(bf16[2,4,128,128]{3,2,1,0:T(8,128)(2,1)} %combine_partials.1.summary_ref, bf16[2,128,128]{2,1,0:T(8,128)(2,1)} %copy-done.2, bf16[5,128,128]{2,1,0:T(8,128)(2,1)} %copy-done.4, bf16[5,128,128]{2,1,0:T(8,128)(2,1)} %copy-done.3, bf16[16,2,128,128]{3,2,1,0:T(8,128)(2,1)} %bitcast.28, ...), custom_call_target="tpu_custom_call" | custom-call | tf_op jit(solution)/shard_map/finish_rows/pallas_call | solution.py:505
  88.6 22.1 %all_to_all.10 = bf16[16,256,128]{2,1,0:T(8,128)(2,1)} all-to-all(bf16[16,256,128]{2,1,0:T(8,128)(2,1)} %bitcast.29), channel_id=1, replica_groups=mesh['tx'=8,'zh'=2,'zl'=2] {'tx','zl'}, dimensions={0} | all-to-all | bytes 2097152 | tf_op jit(solution)/shard_map/all_to_all | solution.py:520
  110.7 5.6 %scatter_rows.1 = bf16[4096,128]{1,0:T(8,128)(2,1)} custom-call(bf16[4096,128]{1,0:T(8,128)(2,1)} %bitcast.30, s32[32,128]{1,0:T(8,128)} %get-tuple-element.12.index_ref), custom_call_target="tpu_custom_call" | custom-call | tf_op jit(solution)/shard_map/scatter_rows/pallas_call | solution.py:528
Async XLA Ops:
  14.9 21.3 %all-to-all-start = ((bf16[16,256,128]{2,1,0:T(8,128)(2,1)}), bf16[16,256,128]{2,1,0:T(8,128)(2,1)S(1)}, u32[]{:S(2)}, u32[]{:S(2)}) async-start(bf16[16,256,128]{2,1,0:T(8,128)(2,1)} %bitcast.31), calls=%async_computation | async-start | bytes 2097152 | tf_op jit(solution)/shard_map/all_to_all | solution.py:464
  36.2 1.0 copy-start
  45.0 14.9 %collective-permute-start = (bf16[1040,128]{1,0:T(8,128)(2,1)}, bf16[1040,128]{1,0:T(8,128)(2,1)S(1)}, u32[]{:S(2)}, u32[]{:S(2)}) collective-permute-start(bf16[1040,128]{1,0:T(8,128)(2,1)} %get-tuple-element.11), channel_id=1, source_target_pairs={{0,2},{2,0},{1,3},{3,1},{4,6},{6,4},{5,7},{7,5},{8,10},{10,8},{9,1... | collective-permute-start | bytes 798728 | tf_op jit(solution)/shard_map/ppermute | solution.py:486
  59.9 0.7 copy-start.1
  63.7 4.3 %collective-permute-start.1 = (bf16[2,128,128]{2,1,0:T(8,128)(2,1)S(1)}, bf16[2,128,128]{2,1,0:T(8,128)(2,1)S(1)}, u32[]{:S(2)}, u32[]{:S(2)}) collective-permute-start(bf16[2,128,128]{2,1,0:T(8,128)(2,1)S(1)} %fusion.4), channel_id=1, source_target_pairs={{0,1},{1,0},{2,3},{3,2},{4,5},{5,4},{6,7},{7,6},{8,9},{9,8},{10,11... | collective-permute-start | bytes 196616 | tf_op jit(solution)/shard_map/ppermute | solution.py:498
  68.0 1.0 copy-start.2
  69.0 4.4 %collective-permute-start.3 = (bf16[5,128,128]{2,1,0:T(8,128)(2,1)S(1)}, bf16[5,128,128]{2,1,0:T(8,128)(2,1)S(1)}, u32[]{:S(2)}, u32[]{:S(2)}) collective-permute-start(bf16[5,128,128]{2,1,0:T(8,128)(2,1)S(1)} %get-tuple-element.13), channel_id=1, source_target_pairs={{4,0},{8,4},{12,8},{16,12},{20,16},{24,20},{28,24},{5,1},{9,5},{13... | collective-permute-start | bytes 491528 | tf_op jit(solution)/shard_map/ppermute | solution.py:503
  70.3 4.0 %collective-permute-start.2 = (bf16[5,128,128]{2,1,0:T(8,128)(2,1)S(1)}, bf16[5,128,128]{2,1,0:T(8,128)(2,1)S(1)}, u32[]{:S(2)}, u32[]{:S(2)}) collective-permute-start(bf16[5,128,128]{2,1,0:T(8,128)(2,1)S(1)} %get-tuple-element.14), channel_id=1, source_target_pairs={{0,4},{4,8},{8,12},{12,16},{16,20},{20,24},{24,28},{1,5},{5,9},{9,... | collective-permute-start | bytes 491528 | tf_op jit(solution)/shard_map/ppermute | solution.py:502
  73.4 1.0 copy-start.3
  74.4 0.7 copy-start.4

commit v3 on v2

v3 whole, which is shorter than its diff:
```python
import functools
import math

import jax
import jax.numpy as jnp
from jax import lax
from jax.experimental import pallas as pl
from jax.experimental.pallas import tpu as pltpu
from jax.sharding import PartitionSpec as P

HEADS = 2
TLX = 2
TLY = 2
LANES = 128
BF = jnp.bfloat16
F32 = jnp.float32

sharpness = 32.0
epsilon = 1e-06
neighbour_steps = ((-1, -1), (-1, 0), (-1, 1), (0, -1), (0, 1), (1, -1), (1, 0), (1, 1))
VMEM = pltpu.VMEM
SMEM = pltpu.SMEM


def dot(a, b):
    return jnp.dot(a, b, preferred_element_type=F32)


def dot_t(a, b):
    return lax.dot_general(a, b, (((1,), (1,)), ((), ())), preferred_element_type=F32)


def head_ones():
    row = lax.broadcasted_iota(jnp.int32, (2 * LANES, LANES), 0)
    col = lax.broadcasted_iota(jnp.int32, (2 * LANES, LANES), 1)
    half = LANES // HEADS
    same = ((row % LANES) // half) == (col // half)
    return jnp.where(same, 1.0, 0.0).astype(BF)


def unit(v, ones):
    square = v * v
    high = square.astype(BF)
    low = (square - high.astype(F32)).astype(BF)
    total = dot(jnp.concatenate([high, low], axis=1), ones)
    return v * lax.rsqrt(total + epsilon)


def silu(v):
    half = 0.5 * v
    return half + half * jnp.tanh(half)


def place():
    return lax.axis_index("tx"), lax.axis_index("zh"), lax.axis_index("zl")


def network(x, w1_ref, w2_ref, w3_ref):
    hidden = silu(dot(x.astype(BF), w1_ref[...])).astype(BF)
    hidden = silu(dot(hidden, w2_ref[0])).astype(BF)
    return dot(hidden, w3_ref[...]).astype(BF)


def encode_rows(
    half_id, quota, chunk, points_ref, w1_ref, w2_ref, w3_ref, index_s, feat_ref, wide_ref, xs
):
    rows_total = points_ref.shape[0] // 2
    group = chunk // quota
    wide_ref[...] = points_ref[...].astype(F32)

    def gather(c, buffer):
        for r in range(chunk):
            spot = (r // quota) * 2 * quota + half_id * quota + r % quota
            i = index_s[c * (2 * chunk // LANES) + spot // LANES, spot % LANES]
            buffer[pl.ds(r, 1), :] = wide_ref[pl.ds(i, 1), :]

    def apply(c, buffer):
        out = network(buffer[...], w1_ref, w2_ref, w3_ref)
        for k in range(group):
            feat_ref[c * group + k] = out[k * quota : (k + 1) * quota]

    chunks = rows_total // chunk
    gather(0, xs[0])

    def step(k, carry):
        c = 2 * k
        gather(c + 1, xs[1])
        apply(c, xs[0])
        gather(jnp.minimum(c + 2, chunks - 1), xs[0])
        apply(c + 1, xs[1])
        return carry

    lax.fori_loop(0, chunks // 2, step, 0)


def encode_first_kernel(
    grid_y,
    along_y,
    quota,
    points_ref,
    w1_ref,
    w2_ref,
    w3_ref,
    counts_ref,
    order_ref,
    feat_ref,
    index_ref,
    off_ref,
    index_s,
    wide_ref,
    xa_ref,
    xb_ref,
    sem,
):
    tx, zh, zl = place()
    own = tx * along_y + zh * (along_y // 2) + zl
    tiles = counts_ref.shape[1]
    order_rows = order_ref.shape[0]
    rows_total = points_ref.shape[0]

    def add_up(g, total):
        off_ref[g] = total
        return total + counts_ref[own, g]

    lax.fori_loop(0, tiles, add_up, jnp.int32(0), unroll=8)
    lane = lax.broadcasted_iota(jnp.int32, (1, LANES), 1)

    def run_of(start):
        line = start >> 7
        shift = start & (LANES - 1)
        first = order_ref[pl.ds(jnp.clip(line, 0, order_rows - 1), 1), :]
        second = order_ref[pl.ds(jnp.clip(line + 1, 0, order_rows - 1), 1), :]
        merged = jnp.where(lane < shift, second, first)
        return pltpu.roll(merged, (LANES - shift) & (LANES - 1), 1)

    per_line = LANES // quota

    def index_line(line, carry):
        value = jnp.zeros((1, LANES), jnp.int32)
        for k in range(per_line):
            d = line * per_line + k
            g1 = (d // along_y) * (TLX * grid_y) + (d % along_y) * TLY
            n1 = counts_ref[own, g1] + counts_ref[own, g1 + 1]
            run1 = run_of(off_ref[g1] - k * quota)
            run2 = run_of(off_ref[g1 + grid_y] - n1 - k * quota)
            both = jnp.where(lane < k * quota + n1, run1, run2)
            value = both if k == 0 else jnp.where(lane >= k * quota, both, value)
        index_ref[pl.ds(line, 1), :] = value
        return carry

    lax.fori_loop(0, rows_total // LANES, index_line, 0, unroll=4)
    copy = pltpu.make_async_copy(index_ref, index_s, sem)
    copy.start()
    copy.wait()
    encode_rows(
        0, quota, xa_ref.shape[0], points_ref, w1_ref, w2_ref, w3_ref, index_s, feat_ref, wide_ref,
        (xa_ref, xb_ref),
    )


def encode_second_kernel(
    quota, points_ref, w1_ref, w2_ref, w3_ref, index_ref, feat_ref, wide_ref, xa_ref, xb_ref
):
    encode_rows(
        1, quota, xa_ref.shape[0], points_ref, w1_ref, w2_ref, w3_ref, index_ref, feat_ref, wide_ref,
        (xa_ref, xb_ref),
    )


def tile_of(position, counts_ref, pieces, piece_id, grid_y):
    bounds = [None, None, None]
    for k, (s, base) in enumerate(pieces):
        n0 = counts_ref[s, base]
        n1 = counts_ref[s, base + 1]
        n2 = counts_ref[s, base + grid_y]
        for i, found in enumerate((n0, n0 + n1, n0 + n1 + n2)):
            if k == 0:
                bounds[i] = jnp.full(position.shape, found, jnp.int32)
            else:
                bounds[i] = jnp.where(piece_id >= k, found, bounds[i])
    return sum((position >= b).astype(jnp.int32) for b in bounds)


def pieces_of(first, group, half_id, along_y):
    tx, zh, zl = place()
    lows = along_y // 2
    blocks = 2
    base = tx * (TLX * along_y * TLY) + (zl * blocks + half_id) * TLY
    found = []
    for k in range(group):
        member = first + k
        found.append(((member // lows) * along_y + zh * lows + member % lows, base))
    return found


def partial_kernel(half_id, along_y, rows_ref, counts_ref, inducing_ref, proj_ref, *rest):
    if half_id:
        before_ref, own_ref, send_ref, edge_ref, num_ref = rest
    else:
        own_ref, send_ref, num_ref = rest
    members, quota, width = rows_ref.shape
    grid_y = along_y * TLY
    half = LANES // HEADS
    group = min(512 // quota, members)
    chunk = group * quota
    ones = head_ones()
    lane = lax.broadcasted_iota(jnp.int32, (1, LANES), 1)
    left = lane < half
    queries = unit(dot(inducing_ref[...], proj_ref[0]), ones)
    queries = jnp.concatenate(
        [jnp.where(left, queries, 0.0), jnp.where(left, 0.0, queries)], axis=0
    ).astype(BF)
    wv_t = proj_ref[2].astype(F32).T.astype(BF)
    num_ref[...] = jnp.zeros_like(num_ref)
    spot = lax.broadcasted_iota(jnp.int32, (1, chunk), 1)
    tile_row = lax.broadcasted_iota(jnp.int32, (16, chunk), 0)

    def step(c, carry):
        x = jnp.concatenate([rows_ref[c * group + k] for k in range(group)], axis=0)
        keys = unit(dot(x, proj_ref[1]), ones).astype(BF)
        weights = jnp.exp2(dot_t(keys, queries) * (sharpness * math.log2(math.e))).astype(BF)
        values = dot_t(wv_t, x)
        pieces = pieces_of(c * group, group, half_id, along_y)
        tile = tile_of(spot % quota, counts_ref, pieces, spot // quota, grid_y)
        stacked = [jnp.where(tile == t, values, 0.0).astype(BF) for t in range(4)]
        stacked.append(jnp.where(tile_row == tile, 1.0, 0.0).astype(BF))
        num_ref[...] += dot(jnp.concatenate(stacked, axis=0), weights)
        return carry

    lax.fori_loop(0, members // group, step, 0)
    pad = jnp.zeros((8, LANES), F32)
    last = 4 * LANES

    def tile_sums(t):
        return jnp.concatenate(
            [
                num_ref[t * LANES : t * LANES + half, :LANES],
                num_ref[t * LANES + half : (t + 1) * LANES, LANES:],
            ],
            axis=0,
        )

    for t in range(4):
        rows = slice(t * LANES, (t + 1) * LANES)
        value = tile_sums(t)
        own_ref[rows, :] = value
        send_ref[rows, :] = value.astype(BF)
    totals = jnp.concatenate(
        [num_ref[last : last + 4, h * LANES : (h + 1) * LANES] for h in range(HEADS)] + [pad],
        axis=0,
    )
    own_ref[last:, :] = totals
    send_ref[last:, :] = totals.astype(BF)
    if half_id:
        zl = lax.axis_index("zl")
        for x in range(TLX):
            rows = slice(x * LANES, (x + 1) * LANES)
            here = send_ref[(2 * x + 1) * LANES : (2 * x + 2) * LANES, :]
            there = before_ref[2 * x * LANES : (2 * x + 1) * LANES, :]
            edge_ref[rows, :] = jnp.where(zl == 0, here, there)
        edge_ref[TLX * LANES :, :] = jnp.where(zl == 0, send_ref[last:, :], before_ref[last:, :])


def queries_kernel(rows0_ref, rows1_ref, proj_ref, out0_ref, out1_ref):
    ones = head_ones()
    for rows_ref, out_ref in ((rows0_ref, out0_ref), (rows1_ref, out1_ref)):
        members, quota, width = rows_ref.shape
        group = min(512 // quota, members)

        def step(c, carry):
            x = jnp.concatenate([rows_ref[c * group + k] for k in range(group)], axis=0)
            query = unit(dot(x, proj_ref[0]), ones).astype(BF)
            for k in range(group):
                out_ref[c * group + k] = query[k * quota : (k + 1) * quota]
            return carry

        lax.fori_loop(0, members // group, step, 0)


def combine_kernel(
    own0_ref, own1_ref, other0_ref, other1_ref, near_ref, far_ref, inducing_ref, proj_ref, out0_ref, out1_ref
):
    half = LANES // HEADS
    last = 4 * LANES
    outs = (out0_ref, out1_ref)
    zl = lax.axis_index("zl")

    def summarize(value, total0, total1):
        attended = jnp.concatenate([value[:half] / total0, value[half:] / total1], axis=0)
        attended = attended.T.astype(BF)
        out = inducing_ref[...].astype(F32) + dot(attended, proj_ref[3])
        return out.astype(BF)

    for b, (own_ref, other_ref) in enumerate(((own0_ref, other0_ref), (own1_ref, other1_ref))):
        totals = own_ref[last:, :] + other_ref[last:, :].astype(F32)
        for t in range(4):
            rows = slice(t * LANES, (t + 1) * LANES)
            value = own_ref[rows, :] + other_ref[rows, :].astype(F32)
            outs[t // 2][b * TLY + t % 2] = summarize(
                value, totals[t : t + 1], totals[t + 4 : t + 5]
            )
    totals = near_ref[TLX * LANES :, :].astype(F32) + far_ref[TLX * LANES :, :].astype(F32)
    for x in range(TLX):
        rows = slice(x * LANES, (x + 1) * LANES)
        value = near_ref[rows, :].astype(F32) + far_ref[rows, :].astype(F32)
        lines = [
            jnp.where(zl == 1, totals[k + 1 : k + 2], totals[k : k + 1])
            for k in (2 * x, 2 * x + 4)
        ]
        outs[x][2 * TLY] = summarize(value, *lines)


def mixture_kernel(
    own0_ref,
    own1_ref,
    below_ref,
    above_ref,
    proj_ref,
    mixing_ref,
    key_ref,
    value_ref,
    mid_ref,
    side_ref,
):
    half = LANES // HEADS
    blocks = key_ref.shape[0]
    tall = blocks * TLY
    low = lax.axis_index("zl")

    row = lax.broadcasted_iota(jnp.int32, (LANES, LANES), 0)
    col = lax.broadcasted_iota(jnp.int32, (LANES, LANES), 1)
    eye = jnp.where(row == col, 1.0, 0.0).astype(BF)
    blank = jnp.zeros((LANES, LANES), BF)

    def mix(a, b):
        return eye if (a, b) == (0, 0) else mixing_ref[neighbour_steps.index((a, b))]

    for k, a in enumerate((-1, 0, 1)):
        rows = slice(k * 2 * LANES, (k + 1) * 2 * LANES)
        mid_ref[rows, :] = jnp.concatenate(
            [
                jnp.concatenate([mix(a, 0), mix(a, -1)], axis=1),
                jnp.concatenate([mix(a, 1), mix(a, 0)], axis=1),
            ],
            axis=0,
        )
    for k, b in enumerate((-1, 1)):
        side_ref[k] = jnp.concatenate(
            [
                jnp.concatenate([mix(0, b), mix(-1, b)], axis=1),
                jnp.concatenate([mix(1, b), mix(0, b)], axis=1),
                jnp.concatenate([mix(-1, b), blank], axis=1),
                jnp.concatenate([blank, mix(1, b)], axis=1),
            ],
            axis=0,
        )
    ones = head_ones()
    lane = lax.broadcasted_iota(jnp.int32, (1, LANES), 1)
    left = lane < half
    grid = (below_ref, own0_ref, own1_ref, above_ref)

    def tile(i, j):
        if 0 <= j < tall:
            return grid[i][j]
        return jnp.where(low == (1 if j < 0 else 0), grid[i][tall], blank)

    mids, lefts, rights = [], [], []
    for i in range(2):
        for b in range(blocks):
            mids.append(
                jnp.concatenate(
                    [tile(i + r, 2 * b + s) for r in range(3) for s in range(2)], axis=1
                )
            )
    for b in range(blocks):
        lefts.append(jnp.concatenate([tile(i, 2 * b - 1) for i in (1, 2, 0, 3)], axis=1))
        rights.append(jnp.concatenate([tile(i, 2 * b + 2) for i in (1, 2, 0, 3)], axis=1))
    middle = dot(jnp.concatenate(mids, axis=0), mid_ref[...])
    from_left = dot(jnp.concatenate(lefts, axis=0), side_ref[0])
    from_right = dot(jnp.concatenate(rights, axis=0), side_ref[1])
    mixtures = []
    for b in range(blocks):
        span = slice(b * LANES, (b + 1) * LANES)
        for i in range(2):
            m = middle[(i * blocks + b) * LANES : (i * blocks + b + 1) * LANES]
            cols = slice(i * LANES, (i + 1) * LANES)
            mixtures.append((m[:, :LANES] + from_left[span, cols]).astype(BF))
            mixtures.append((m[:, LANES:] + from_right[span, cols]).astype(BF))
    mixtures = jnp.concatenate(mixtures, axis=0)
    keys = unit(dot(mixtures, proj_ref[1]), ones)
    values = dot(mixtures, proj_ref[2])
    for b in range(blocks):
        spans = [slice((b * 4 + t) * LANES, (b * 4 + t + 1) * LANES) for t in range(4)]
        for h in range(HEADS):
            mine = left if h == 0 else ~left
            key_ref[b, h * LANES : (h + 1) * LANES, :] = jnp.concatenate(
                [jnp.where(mine, keys[s], 0.0) for s in spans], axis=1
            ).astype(BF)
            flags = jnp.broadcast_to(jnp.where(mine, 1.0, 0.0), (LANES, LANES))
            for t, s in enumerate(spans):
                rows = slice((t * HEADS + h) * LANES, (t * HEADS + h + 1) * LANES)
                value_ref[b, rows, :] = jnp.concatenate(
                    [jnp.where(mine, values[s], 0.0), flags], axis=1
                ).astype(BF)


def attend_kernel(
    half_id, along_y, rows_ref, query_ref, counts_ref, key_ref, value_ref, proj_ref, out_ref
):
    members, quota, width = rows_ref.shape
    grid_y = along_y * TLY
    group = min(512 // quota, members)
    chunk = group * quota
    spot = lax.broadcasted_iota(jnp.int32, (chunk, LANES), 0)

    def step(c, carry):
        x = jnp.concatenate([rows_ref[c * group + k] for k in range(group)], axis=0)
        query = jnp.concatenate([query_ref[c * group + k] for k in range(group)], axis=0)
        query = query.astype(F32)
        pieces = pieces_of(c * group, group, half_id, along_y)
        which = tile_of(spot % quota, counts_ref, pieces, spot // quota, grid_y)
        inside = [which == t for t in range(4)]
        expanded = jnp.concatenate(
            [jnp.where(m, query, 0.0).astype(BF) for m in inside], axis=1
        )
        scores = dot_t(expanded, key_ref[half_id])
        weights = jnp.exp2(scores * (sharpness * math.log2(math.e)))
        spread = jnp.concatenate(
            [
                jnp.where(m, weights[:, h * LANES : (h + 1) * LANES], 0.0).astype(BF)
                for m in inside
                for h in range(HEADS)
            ],
            axis=1,
        )
        both = dot(spread, value_ref[half_id])
        attended = (both[:, :LANES] / both[:, LANES:]).astype(BF)
        result = (x.astype(F32) + dot(attended, proj_ref[3])).astype(BF)
        for k in range(group):
            out_ref[c * group + k] = result[k * quota : (k + 1) * quota]
        return carry

    lax.fori_loop(0, members // group, step, 0)


def scatter_rows(half_id, rows_ref, index_ref, wide_ref, part_ref):
    chunk = part_ref.shape[0]
    members, quota, width = rows_ref.shape
    group = chunk // quota

    def step(c, carry):
        for k in range(group):
            part_ref[k * quota : (k + 1) * quota, :] = rows_ref[c * group + k].astype(F32)
        for r in range(chunk):
            spot = (r // quota) * 2 * quota + half_id * quota + r % quota
            i = index_ref[c * (2 * chunk // LANES) + spot // LANES, spot % LANES]
            wide_ref[pl.ds(i, 1), :] = part_ref[pl.ds(r, 1), :]
        return carry

    lax.fori_loop(0, members // group, step, 0)


def scatter_first_kernel(rows_ref, index_ref, wide_ref, part_ref):
    scatter_rows(0, rows_ref, index_ref, wide_ref, part_ref)


def scatter_second_kernel(rows_ref, index_ref, before_ref, out_ref, wide_ref, part_ref):
    wide_ref[...] = before_ref[...]
    scatter_rows(1, rows_ref, index_ref, wide_ref, part_ref)
    out_ref[...] = wide_ref[...].astype(BF)


def call(kernel, name, out_shape, in_specs, scratch, micros, operands, megabytes=20, **more):
    spaces = {"v": pltpu.VMEM, "s": pltpu.SMEM}
    many = isinstance(out_shape, tuple)
    whole = pl.BlockSpec(memory_space=pltpu.VMEM)
    return pl.pallas_call(
        kernel,
        out_shape=out_shape,
        in_specs=[pl.BlockSpec(memory_space=spaces[c]) for c in in_specs],
        out_specs=(whole,) * len(out_shape) if many else whole,
        scratch_shapes=scratch,
        compiler_params=pltpu.CompilerParams(vmem_limit_bytes=megabytes * 1024 * 1024),
        cost_estimate=pl.CostEstimate(
            flops=int(micros * 5e8), bytes_accessed=int(micros * 1e6), transcendentals=0
        ),
        name=name,
        **more,
    )(*operands)


def body(
    points,
    embed_weight,
    inner_weights,
    output_weight,
    counts,
    point_order,
    inducing,
    first_proj,
    second_proj,
    mixing,
):
    along_x = lax.axis_size("tx")
    highs = lax.axis_size("zh")
    lows = lax.axis_size("zl")
    along_y = highs * lows
    point_count, width = points.shape
    quota = point_count // (along_x * along_y)
    grid_y = along_y * TLY
    blocks = 2
    members = along_x * lows
    tall = blocks * TLY
    lines = point_count // LANES
    chunk = 512
    half_rows = (members, quota, width)

    def shape(sizes, dtype=BF):
        return jax.ShapeDtypeStruct(sizes, dtype)

    weights = (embed_weight, inner_weights, output_weight)
    buffers = [
        VMEM((point_count, width), F32),
        VMEM((chunk, width), F32),
        VMEM((chunk, width), F32),
    ]
    first, index = call(
        functools.partial(encode_first_kernel, grid_y, along_y, quota),
        "encode_first",
        (shape(half_rows), shape((lines, LANES), jnp.int32)),
        "vvvvsv",
        [SMEM((counts.shape[1],), jnp.int32), SMEM((lines, LANES), jnp.int32)]
        + buffers
        + [pltpu.SemaphoreType.DMA],
        8,
        (points, *weights, counts, point_order.reshape(lines, LANES)),
    )
    second = call(
        functools.partial(encode_second_kernel, quota),
        "encode_second",
        shape(half_rows),
        "vvvvs",
        buffers,
        6,
        (points, *weights, index),
    )

    def exchange(rows):
        return lax.all_to_all(rows, ("tx", "zl"), split_axis=0, concat_axis=0, tiled=True)

    rows0 = exchange(first)
    rows1 = exchange(second)

    part_rows = 4 * LANES + 16
    edge_rows = TLX * LANES + 16
    parts = (shape((part_rows, LANES), F32), shape((part_rows, LANES)))
    sums = [VMEM((part_rows, HEADS * LANES), F32)]
    own0, send0 = call(
        functools.partial(partial_kernel, 0, along_y),
        "partial_first",
        parts,
        "vsvv",
        sums,
        4,
        (rows0, counts, inducing, first_proj),
    )
    own1, send1, edge = call(
        functools.partial(partial_kernel, 1, along_y),
        "partial_second",
        parts + (shape((edge_rows, LANES)),),
        "vsvvv",
        sums,
        4,
        (rows1, counts, inducing, first_proj, send0),
    )
    across = [(h * lows + l, (highs - 1 - h) * lows + l) for h in range(highs) for l in range(lows)]
    beside = [(h * lows + l, h * lows + lows - 1 - l) for h in range(highs) for l in range(lows)]
    both = [
        (h * lows + l, (highs - 1 - h) * lows + lows - 1 - l)
        for h in range(highs)
        for l in range(lows)
    ]
    z_axes = ("zh", "zl")
    other0 = lax.ppermute(send0, z_axes, across)
    other1 = lax.ppermute(send1, z_axes, across)
    near = lax.ppermute(edge, z_axes, beside)
    far = lax.ppermute(edge, z_axes, both)

    query0, query1 = call(
        queries_kernel,
        "point_queries",
        (shape(half_rows), shape(half_rows)),
        "vvv",
        [],
        3,
        (rows0, rows1, second_proj),
    )

    line = shape((tall + 1, LANES, width))
    summary0, summary1 = call(
        combine_kernel,
        "combine_partials",
        (line, line),
        "v" * 8,
        [],
        2,
        (own0, own1, other0, other1, near, far, inducing, first_proj),
    )
    forward = [(i, i + 1) for i in range(along_x - 1)]
    backward = [(i + 1, i) for i in range(along_x - 1)]
    below = lax.ppermute(summary1, "tx", forward)
    above = lax.ppermute(summary0, "tx", backward)

    keys, values = call(
        mixture_kernel,
        "mix_tiles",
        (shape((blocks, HEADS * LANES, 4 * LANES)), shape((blocks, 4 * HEADS * LANES, 2 * LANES))),
        "v" * 6,
        [VMEM((6 * LANES, 2 * LANES), BF), VMEM((2, 4 * LANES, 2 * LANES), BF)],
        4,
        (summary0, summary1, below, above, second_proj, mixing),
    )

    def attend(half_id, rows, query):
        return call(
            functools.partial(attend_kernel, half_id, along_y),
            ("attend_first", "attend_second")[half_id],
            shape(half_rows),
            "vvsvvv",
            [],
            4,
            (rows, query, counts, keys, values, second_proj),
        )

    back0 = exchange(attend(0, rows0, query0))
    back1 = exchange(attend(1, rows1, query1))
    wide = call(
        scatter_first_kernel,
        "scatter_first",
        shape((point_count, width), F32),
        "vs",
        [VMEM((chunk, width), F32)],
        3,
        (back0, index),
    )
    return call(
        scatter_second_kernel,
        "scatter_second",
        shape((point_count, width)),
        "vsv",
        [VMEM((point_count, width), F32), VMEM((chunk, width), F32)],
        4,
        (back1, index, wide),
    )


def solution(mesh):
    along_x, along_y = mesh.devices.shape
    split = jax.sharding.Mesh(mesh.devices.reshape(along_x, 2, along_y // 2), ("tx", "zh", "zl"))
    rows = P(("tx", "zh", "zl"), None)
    placed = (rows, P(), P(), P(), P(), rows, P(), P(), P(), P())
    return jax.shard_map(body, mesh=split, in_specs=placed, out_specs=rows, check_vma=False)
```

time: 117 us -> 105 us (0.90)
  blocking collectives: 22.1 us -> 0 us
  starting transfers between devices: 13.8 us -> 30.5 us
  waiting for transfers between devices: 31.4 us -> 21.5 us
  local copies, waits for them, and re-layouts: 3.58 us -> 7.38 us
  other arithmetic: 2.5 us -> 0 us
  Pallas kernels: 42.8 us -> 44.6 us
    all_to_all x1 -> x0, blocking collectives: 22.1 us -> none  [body(): lax.all_to_all(result.reshape(members, blocks * quota, width), group_axes...]
    all_to_all x1 -> x4, starting transfers between devices: 6.28 us -> 19.8 us  [exchange(): lax.all_to_all(rows, ('tx', 'zl'), split_axis=0, concat_axis=0, tiled=True)]
    ppermute x4 -> x6, waiting for transfers between devices: 17 us -> 6.31 us  [the longest x1 3.85 us: body(): far = lax.ppermute(edge, z_axes, both)]
    unnamed x10 -> x34, local copies, waits for them, and re-layouts: 2.35 us -> 7.38 us
    ppermute x4 -> x6, starting transfers between devices: 7.57 us -> 10.7 us  [the longest x1 3.17 us: body(): below = lax.ppermute(summary1, 'tx', forward)]
    pallas_call x5 -> x11, Pallas kernels: 42.8 us -> 44.6 us  [call(): pl.pallas_call(kernel, out_shape=out_shape, in_specs=[pl.BlockSpec(memory...]
    squeeze x1 -> x0, local copies, waits for them, and re-layouts: 1.23 us -> none  [body(): own_counts = lax.dynamic_index_in_dim(counts, own_index, 0, keepdims=False)]
    all_to_all x1 -> x4, waiting for transfers between devices: 14.4 us -> 15.2 us  [exchange(): lax.all_to_all(rows, ('tx', 'zl'), split_axis=0, concat_axis=0, tiled=True)]
  transfers between devices with their start and end apart: 5 -> 10, of which waited for: 4 -> 6; matrix products, arithmetic and copies ran while one was open for 1% -> 0% of each run, Pallas kernels for 0% -> 25%
where the time goes in v3:
time: 105 us; the launch traced here: 104 us
  Pallas kernels  44.6 us (42%)
  starting transfers between devices  30.5 us (29%)
  waiting for transfers between devices  21.5 us (20%)
  local copies, waits for them, and re-layouts  7.38 us (7%)
    pallas_call x11, Pallas kernels, call(): pl.pallas_call(kernel, out_shape=out_shape, in_specs=[pl.BlockSpec(memory...  44.6 us
    all_to_all x4, starting transfers between devices, exchange(): lax.all_to_all(rows, ('tx', 'zl'), split_axis=0, concat_axis=0, tiled=True)  19.8 us
    all_to_all x4, waiting for transfers between devices, exchange(): lax.all_to_all(rows, ('tx', 'zl'), split_axis=0, concat_axis=0, tiled=True)  15.2 us
    unnamed x34, local copies, waits for them, and re-layouts  7.38 us
    ppermute x1, waiting for transfers between devices, body(): far = lax.ppermute(edge, z_axes, both)  3.85 us
    ppermute x1, starting transfers between devices, body(): below = lax.ppermute(summary1, 'tx', forward)  3.17 us
    ppermute x1, starting transfers between devices, body(): other0 = lax.ppermute(send0, z_axes, across)  2.67 us
    ppermute x1, waiting for transfers between devices, body(): near = lax.ppermute(edge, z_axes, beside)  2.45 us
  transfers between devices with their start and end apart: 10, of which 6 were waited for; matrix products, arithmetic and copies ran while one was open for 0% of the time, Pallas kernels for 25%

profile of v3, /device:TPU:0, one launch (start us, length us, event | category | flops | bytes accessed | tf_op | source)
XLA Modules:
  0.0 104.3 jit_solution(8121462922210777266)
XLA Ops:
  0.0 1.2 %copy-done = bf16[4096,128]{1,0:T(8,128)(2,1)S(1)} copy-done((bf16[4096,128]{1,0:T(8,128)(2,1)S(1)}, bf16[4096,128]{1,0:T(8,128)(2,1)}, u32[]{:S(2)}) %copy-start) | copy-done | bytes 1048600
  1.2 1.0 copy-done.2
  2.3 0.9 copy-done.5
  3.2 0.9 copy-done.7
  4.1 0.7 copy-done.12
  4.8 0.7 copy-done.13
  5.5 7.9 %encode_first.1 = (bf16[16,128,128]{2,1,0:T(8,128)(2,1)}, s32[32,128]{1,0:T(8,128)S(1)}) custom-call(bf16[4096,128]{1,0:T(8,128)(2,1)S(1)} %copy-done, bf16[128,512]{1,0:T(8,128)(2,1)S(1)} %copy-done.5, bf16[1,512,512]{2,1,0:T(8,128)(2,1)S(1)} %copy-done.2, bf16[512,128]{1,0:T(8,128)(2,1)S(1)} %copy-done.7, s32[32,128]{1,0:T(8,128)S(1)} %copy-done.13, ...), custom_call_target="tpu_custom_call" | custom-call | flops 4000000000 | bytes 8000000 | tf_op jit(solution)/shard_map/encode_first/pallas_call | solution.py:477
  13.4 6.3 %all-to-all-start.1 = ((bf16[16,128,128]{2,1,0:T(8,128)(2,1)}), bf16[16,128,128]{2,1,0:T(8,128)(2,1)S(1)}, u32[]{:S(2)}, u32[]{:S(2)}) async-start(bf16[16,128,128]{2,1,0:T(8,128)(2,1)} %get-tuple-element.19), calls=%async_computation.1 | async-start | bytes 1048576 | tf_op jit(solution)/shard_map/all_to_all | solution.py:549
  19.7 0.0 copy-done.1
  19.7 0.0 copy-done.3
  19.8 0.0 copy-start.9
  19.8 0.0 copy-start.11
  19.8 0.0 copy-start.14
  19.8 5.7 %encode_second.1 = bf16[16,128,128]{2,1,0:T(8,128)(2,1)} custom-call(bf16[4096,128]{1,0:T(8,128)(2,1)S(1)} %copy-done.1, bf16[128,512]{1,0:T(8,128)(2,1)S(1)} %copy-done.6, bf16[1,512,512]{2,1,0:T(8,128)(2,1)S(1)} %copy-done.3, bf16[512,128]{1,0:T(8,128)(2,1)S(1)} %copy-done.8, s32[32,128]{1,0:T(8,128)S(1)} %get-tuple-element.18.index_ref), custom_call_target="tpu_custom_call" | custom-call | flops 3000000000 | bytes 6000000 | tf_op jit(solution)/shard_map/encode_second/pallas_call | solution.py:477
  25.5 3.0 %all-to-all-done.1.rows0_ref.rows_ref = bf16[16,128,128]{2,1,0:T(8,128)(2,1)S(1)} async-done(((bf16[16,128,128]{2,1,0:T(8,128)(2,1)}), bf16[16,128,128]{2,1,0:T(8,128)(2,1)S(1)}, u32[]{:S(2)}, u32[]{:S(2)}) %all-to-all-start.1) | async-done | bytes 524320 | tf_op jit(solution)/shard_map/all_to_all | solution.py:549
  28.5 3.8 %all-to-all-start = ((bf16[16,128,128]{2,1,0:T(8,128)(2,1)}), bf16[16,128,128]{2,1,0:T(8,128)(2,1)S(1)}, u32[]{:S(2)}, u32[]{:S(2)}) async-start(bf16[16,128,128]{2,1,0:T(8,128)(2,1)} %encode_second.1), calls=%async_computation | async-start | bytes 1048576 | tf_op jit(solution)/shard_map/all_to_all | solution.py:549
  32.3 4.2 %partial_first.1 = (f32[528,128]{1,0:T(8,128)S(1)}, bf16[528,128]{1,0:T(8,128)(2,1)S(1)}) custom-call(bf16[16,128,128]{2,1,0:T(8,128)(2,1)S(1)} %all-to-all-done.1.rows0_ref.rows_ref, s32[32,128]{1,0:T(8,128)S(1)} %copy-done.14, bf16[128,128]{1,0:T(8,128)(2,1)S(1)} %copy-done.11, bf16[4,128,128]{2,1,0:T(8,128)(2,1)S(1)} %copy-done.9), custom_call_target="tpu_custom_call" | custom-call | flops 2000000000 | bytes 4000000 | tf_op jit(solution)/shard_map/partial_first/pallas_call | solution.py:477
  36.5 2.7 %collective-permute-start = (bf16[528,128]{1,0:T(8,128)(2,1)S(1)}, bf16[528,128]{1,0:T(8,128)(2,1)S(1)}, u32[]{:S(2)}, u32[]{:S(2)}) collective-permute-start(bf16[528,128]{1,0:T(8,128)(2,1)S(1)} %get-tuple-element.22.rest_0_), channel_id=1, source_target_pairs={{0,2},{1,3},{2,0},{3,1},{4,6},{5,7},{6,4},{7,5},{8,10},{9,11},{10,... | collective-permute-start | bytes 405512 | tf_op jit(solution)/shard_map/ppermute | solution.py:584
  39.2 4.3 %all-to-all-done.rows1_ref.rows_ref = bf16[16,128,128]{2,1,0:T(8,128)(2,1)S(1)} async-done(((bf16[16,128,128]{2,1,0:T(8,128)(2,1)}), bf16[16,128,128]{2,1,0:T(8,128)(2,1)S(1)}, u32[]{:S(2)}, u32[]{:S(2)}) %all-to-all-start) | async-done | bytes 524320 | tf_op jit(solution)/shard_map/all_to_all | solution.py:549
  43.5 4.2 %partial_second.1 = (f32[528,128]{1,0:T(8,128)S(1)}, bf16[528,128]{1,0:T(8,128)(2,1)S(1)}, bf16[272,128]{1,0:T(8,128)(2,1)S(1)}) custom-call(bf16[16,128,128]{2,1,0:T(8,128)(2,1)S(1)} %all-to-all-done.rows1_ref.rows_ref, s32[32,128]{1,0:T(8,128)S(1)} %copy-done.14, bf16[128,128]{1,0:T(8,128)(2,1)S(1)} %copy-done.11, bf16[4,128,128]{2,1,0:T(8,128)(2,1)S(1)} %copy-done.9, ...), custom_call_target="tpu_custom_call" | custom-call | flops 2000000000 | bytes 4000000 | tf_op jit(solution)/shard_map/partial_second/pallas_call | solution.py:477
  47.7 0.0 copy-start.10
  47.7 0.7 collective-permute-start.1
  48.4 1.3 %collective-permute-start.3 = (bf16[272,128]{1,0:T(8,128)(2,1)S(1)}, bf16[272,128]{1,0:T(8,128)(2,1)S(1)}, u32[]{:S(2)}, u32[]{:S(2)}) collective-permute-start(bf16[272,128]{1,0:T(8,128)(2,1)S(1)} %get-tuple-element.25), channel_id=1, source_target_pairs={{0,3},{1,2},{2,1},{3,0},{4,7},{5,6},{6,5},{7,4},{8,11},{9,10},{10,... | collective-permute-start | bytes 208904 | tf_op jit(solution)/shard_map/ppermute | solution.py:587
  49.7 1.6 %collective-permute-start.2 = (bf16[272,128]{1,0:T(8,128)(2,1)S(1)}, bf16[272,128]{1,0:T(8,128)(2,1)S(1)}, u32[]{:S(2)}, u32[]{:S(2)}) collective-permute-start(bf16[272,128]{1,0:T(8,128)(2,1)S(1)} %get-tuple-element.25), channel_id=1, source_target_pairs={{0,1},{1,0},{2,3},{3,2},{4,5},{5,4},{6,7},{7,6},{8,9},{9,8},{10,11... | collective-permute-start | bytes 208904 | tf_op jit(solution)/shard_map/ppermute | solution.py:586
  51.3 3.9 %collective-permute-done.3.far_ref = bf16[272,128]{1,0:T(8,128)(2,1)S(1)} collective-permute-done((bf16[272,128]{1,0:T(8,128)(2,1)S(1)}, bf16[272,128]{1,0:T(8,128)(2,1)S(1)}, u32[]{:S(2)}, u32[]{:S(2)}) %collective-permute-start.3) | collective-permute-done | bytes 69664 | tf_op jit(solution)/shard_map/ppermute | solution.py:587
  55.1 2.4 %collective-permute-done.2.near_ref = bf16[272,128]{1,0:T(8,128)(2,1)S(1)} collective-permute-done((bf16[272,128]{1,0:T(8,128)(2,1)S(1)}, bf16[272,128]{1,0:T(8,128)(2,1)S(1)}, u32[]{:S(2)}, u32[]{:S(2)}) %collective-permute-start.2) | collective-permute-done | bytes 69664 | tf_op jit(solution)/shard_map/ppermute | solution.py:586
  57.6 0.0 collective-permute-done.other0_ref
  57.6 0.0 collective-permute-done.1.other1_ref
  57.6 0.3 combine_partials.1
  57.9 1.3 %collective-permute-start.5 = (bf16[5,128,128]{2,1,0:T(8,128)(2,1)S(1)}, bf16[5,128,128]{2,1,0:T(8,128)(2,1)S(1)}, u32[]{:S(2)}, u32[]{:S(2)}) collective-permute-start(bf16[5,128,128]{2,1,0:T(8,128)(2,1)S(1)} %get-tuple-element.26.own0_ref), channel_id=1, source_target_pairs={{4,0},{8,4},{12,8},{16,12},{20,16},{24,20},{28,24},{5,1},{9,5},{13... | collective-permute-start | bytes 491528 | tf_op jit(solution)/shard_map/ppermute | solution.py:612
  59.2 0.0 copy-start.4
  59.2 3.2 %collective-permute-start.4 = (bf16[5,128,128]{2,1,0:T(8,128)(2,1)S(1)}, bf16[5,128,128]{2,1,0:T(8,128)(2,1)S(1)}, u32[]{:S(2)}, u32[]{:S(2)}) collective-permute-start(bf16[5,128,128]{2,1,0:T(8,128)(2,1)S(1)} %get-tuple-element.27.own1_ref), channel_id=1, source_target_pairs={{0,4},{4,8},{8,12},{12,16},{16,20},{20,24},{24,28},{1,5},{5,9},{9,... | collective-permute-start | bytes 491528 | tf_op jit(solution)/shard_map/ppermute | solution.py:611
  62.4 3.1 %point_queries.1 = (bf16[16,128,128]{2,1,0:T(8,128)(2,1)S(1)}, bf16[16,128,128]{2,1,0:T(8,128)(2,1)S(1)}) custom-call(bf16[16,128,128]{2,1,0:T(8,128)(2,1)S(1)} %all-to-all-done.1.rows0_ref.rows_ref, bf16[16,128,128]{2,1,0:T(8,128)(2,1)S(1)} %all-to-all-done.rows1_ref.rows_ref, bf16[4,128,128]{2,1,0:T(8,128)(2,1)S(1)} %copy-done.10), custom_call_target="tpu_custom_call" | custom-call | flops 1500000000 | bytes 3000000 | tf_op jit(solution)/shard_map/point_queries/pallas_call | solution.py:477
  65.6 0.0 collective-permute-done.5.above_ref
  65.6 0.0 collective-permute-done.4.below_ref
  65.6 0.0 copy-done.4
  65.6 0.9 mix_tiles.1
  66.5 6.0 %attend_first.1 = bf16[16,128,128]{2,1,0:T(8,128)(2,1)} custom-call(bf16[16,128,128]{2,1,0:T(8,128)(2,1)S(1)} %all-to-all-done.1.rows0_ref.rows_ref, bf16[16,128,128]{2,1,0:T(8,128)(2,1)S(1)} %get-tuple-element.30.query_ref, s32[32,128]{1,0:T(8,128)S(1)} %copy-done.14, bf16[2,256,512]{2,1,0:T(8,128)(2,1)S(1)} %get-tuple-element.28.key_ref, ...), custom_call_target="tpu_custom_call" | custom-call | flops 2000000000 | bytes 4000000 | tf_op jit(solution)/shard_map/attend_first/pallas_call | solution.py:477
  72.6 0.8 copy-done.15
  73.4 6.0 %all-to-all-start.3 = ((bf16[16,128,128]{2,1,0:T(8,128)(2,1)}), bf16[16,128,128]{2,1,0:T(8,128)(2,1)S(1)}, u32[]{:S(2)}, u32[]{:S(2)}) async-start(bf16[16,128,128]{2,1,0:T(8,128)(2,1)} %attend_first.1), calls=%async_computation.3 | async-start | bytes 1048576 | tf_op jit(solution)/shard_map/all_to_all | solution.py:549
  79.3 0.0 copy-start.16
  79.3 1.0 copy-done.16
  80.4 6.0 %attend_second.1 = bf16[16,128,128]{2,1,0:T(8,128)(2,1)} custom-call(bf16[16,128,128]{2,1,0:T(8,128)(2,1)S(1)} %all-to-all-done.rows1_ref.rows_ref, bf16[16,128,128]{2,1,0:T(8,128)(2,1)S(1)} %get-tuple-element.20.query_ref, s32[32,128]{1,0:T(8,128)S(1)} %copy-done.14, bf16[2,256,512]{2,1,0:T(8,128)(2,1)S(1)} %copy-done.16, ...), custom_call_target="tpu_custom_call" | custom-call | flops 2000000000 | bytes 4000000 | tf_op jit(solution)/shard_map/attend_second/pallas_call | solution.py:477
  86.4 1.7 %all-to-all-done.3.rows_ref = bf16[16,128,128]{2,1,0:T(8,128)(2,1)S(1)} async-done(((bf16[16,128,128]{2,1,0:T(8,128)(2,1)}), bf16[16,128,128]{2,1,0:T(8,128)(2,1)S(1)}, u32[]{:S(2)}, u32[]{:S(2)}) %all-to-all-start.3) | async-done | bytes 524320 | tf_op jit(solution)/shard_map/all_to_all | solution.py:549
  88.1 3.8 %all-to-all-start.2 = ((bf16[16,128,128]{2,1,0:T(8,128)(2,1)}), bf16[16,128,128]{2,1,0:T(8,128)(2,1)S(1)}, u32[]{:S(2)}, u32[]{:S(2)}) async-start(bf16[16,128,128]{2,1,0:T(8,128)(2,1)} %attend_second.1), calls=%async_computation.2 | async-start | bytes 1048576 | tf_op jit(solution)/shard_map/all_to_all | solution.py:549
  91.9 2.5 %scatter_first.1.before_ref = f32[4096,128]{1,0:T(8,128)S(1)} custom-call(bf16[16,128,128]{2,1,0:T(8,128)(2,1)S(1)} %all-to-all-done.3.rows_ref, s32[32,128]{1,0:T(8,128)S(1)} %get-tuple-element.18.index_ref), custom_call_target="tpu_custom_call" | custom-call | flops 1500000000 | bytes 3000000 | tf_op jit(solution)/shard_map/scatter_first/pallas_call | solution.py:477
  94.3 6.3 %all-to-all-done.2.rows_ref = bf16[16,128,128]{2,1,0:T(8,128)(2,1)S(1)} async-done(((bf16[16,128,128]{2,1,0:T(8,128)(2,1)}), bf16[16,128,128]{2,1,0:T(8,128)(2,1)S(1)}, u32[]{:S(2)}, u32[]{:S(2)}) %all-to-all-start.2) | async-done | bytes 524320 | tf_op jit(solution)/shard_map/all_to_all | solution.py:549
  100.6 3.7 %scatter_second.1 = bf16[4096,128]{1,0:T(8,128)(2,1)} custom-call(bf16[16,128,128]{2,1,0:T(8,128)(2,1)S(1)} %all-to-all-done.2.rows_ref, s32[32,128]{1,0:T(8,128)S(1)} %get-tuple-element.18.index_ref, f32[4096,128]{1,0:T(8,128)S(1)} %scatter_first.1.before_ref), custom_call_target="tpu_custom_call" | custom-call | flops 2000000000 | bytes 4000000 | tf_op jit(solution)/shard_map/scatter_second/pallas_call | solution.py:477
  (17 shorter events, 0.0 us)
Async XLA Ops:
  0.0 1.2 %copy-start = (bf16[4096,128]{1,0:T(8,128)(2,1)S(1)}, bf16[4096,128]{1,0:T(8,128)(2,1)}, u32[]{:S(2)}) copy-start(bf16[4096,128]{1,0:T(8,128)(2,1)} %points_ref.3) | copy-start | bytes 3145732
  1.2 1.0 copy-start.2
  2.3 0.9 copy-start.5
  3.2 0.9 copy-start.7
  4.1 0.7 copy-start.12
  4.8 0.7 copy-start.13
  5.5 14.2 %copy-start.1 = (bf16[4096,128]{1,0:T(8,128)(2,1)S(1)}, bf16[4096,128]{1,0:T(8,128)(2,1)}, u32[]{:S(2)}) copy-start(bf16[4096,128]{1,0:T(8,128)(2,1)} %points_ref.3) | copy-start | bytes 3145732
  5.5 14.2 %copy-start.3 = (bf16[1,512,512]{2,1,0:T(8,128)(2,1)S(1)}, bf16[1,512,512]{2,1,0:T(8,128)(2,1)}, u32[]{:S(2)}) copy-start(bf16[1,512,512]{2,1,0:T(8,128)(2,1)} %w2_ref.3) | copy-start | bytes 1572868
  5.5 14.2 %copy-start.6 = (bf16[128,512]{1,0:T(8,128)(2,1)S(1)}, bf16[128,512]{1,0:T(8,128)(2,1)}, u32[]{:S(2)}) copy-start(bf16[128,512]{1,0:T(8,128)(2,1)} %w1_ref.3) | copy-start | bytes 393220
  5.5 14.2 %copy-start.8 = (bf16[512,128]{1,0:T(8,128)(2,1)S(1)}, bf16[512,128]{1,0:T(8,128)(2,1)}, u32[]{:S(2)}) copy-start(bf16[512,128]{1,0:T(8,128)(2,1)} %w3_ref.3) | copy-start | bytes 393220
  13.4 15.1 %all-to-all-start.1 = ((bf16[16,128,128]{2,1,0:T(8,128)(2,1)}), bf16[16,128,128]{2,1,0:T(8,128)(2,1)S(1)}, u32[]{:S(2)}, u32[]{:S(2)}) async-start(bf16[16,128,128]{2,1,0:T(8,128)(2,1)} %get-tuple-element.19), calls=%async_computation.1 | async-start | bytes 1048576 | tf_op jit(solution)/shard_map/all_to_all | solution.py:549
  19.8 12.5 %copy-start.9 = (bf16[4,128,128]{2,1,0:T(8,128)(2,1)S(1)}, bf16[4,128,128]{2,1,0:T(8,128)(2,1)}, u32[]{:S(2)}) copy-start(bf16[4,128,128]{2,1,0:T(8,128)(2,1)} %proj_ref.10) | copy-start | bytes 393220
  19.8 12.5 %copy-start.11 = (bf16[128,128]{1,0:T(8,128)(2,1)S(1)}, bf16[128,128]{1,0:T(8,128)(2,1)}, u32[]{:S(2)}) copy-start(bf16[128,128]{1,0:T(8,128)(2,1)} %inducing_ref.5) | copy-start | bytes 98308
  19.8 12.5 %copy-start.14 = (s32[32,128]{1,0:T(8,128)S(1)}, s32[32,128]{1,0:T(8,128)}, u32[]{:S(2)}) copy-start(s32[32,128]{1,0:T(8,128)} %counts_ref.9) | copy-start | bytes 49156
  28.5 15.0 %all-to-all-start = ((bf16[16,128,128]{2,1,0:T(8,128)(2,1)}), bf16[16,128,128]{2,1,0:T(8,128)(2,1)S(1)}, u32[]{:S(2)}, u32[]{:S(2)}) async-start(bf16[16,128,128]{2,1,0:T(8,128)(2,1)} %encode_second.1), calls=%async_computation | async-start | bytes 1048576 | tf_op jit(solution)/shard_map/all_to_all | solution.py:549
  36.5 21.1 %collective-permute-start = (bf16[528,128]{1,0:T(8,128)(2,1)S(1)}, bf16[528,128]{1,0:T(8,128)(2,1)S(1)}, u32[]{:S(2)}, u32[]{:S(2)}) collective-permute-start(bf16[528,128]{1,0:T(8,128)(2,1)S(1)} %get-tuple-element.22.rest_0_), channel_id=1, source_target_pairs={{0,2},{1,3},{2,0},{3,1},{4,6},{5,7},{6,4},{7,5},{8,10},{9,11},{10,... | collective-permute-start | bytes 405512 | tf_op jit(solution)/shard_map/ppermute | solution.py:584
  47.7 14.7 %copy-start.10 = (bf16[4,128,128]{2,1,0:T(8,128)(2,1)S(1)}, bf16[4,128,128]{2,1,0:T(8,128)(2,1)}, u32[]{:S(2)}) copy-start(bf16[4,128,128]{2,1,0:T(8,128)(2,1)} %proj_ref.13) | copy-start | bytes 393220
  47.7 9.9 %collective-permute-start.1 = (bf16[528,128]{1,0:T(8,128)(2,1)S(1)}, bf16[528,128]{1,0:T(8,128)(2,1)S(1)}, u32[]{:S(2)}, u32[]{:S(2)}) collective-permute-start(bf16[528,128]{1,0:T(8,128)(2,1)S(1)} %get-tuple-element.24), channel_id=1, source_target_pairs={{0,2},{1,3},{2,0},{3,1},{4,6},{5,7},{6,4},{7,5},{8,10},{9,11},{10,... | collective-permute-start | bytes 405512 | tf_op jit(solution)/shard_map/ppermute | solution.py:585
  48.4 6.8 %collective-permute-start.3 = (bf16[272,128]{1,0:T(8,128)(2,1)S(1)}, bf16[272,128]{1,0:T(8,128)(2,1)S(1)}, u32[]{:S(2)}, u32[]{:S(2)}) collective-permute-start(bf16[272,128]{1,0:T(8,128)(2,1)S(1)} %get-tuple-element.25), channel_id=1, source_target_pairs={{0,3},{1,2},{2,1},{3,0},{4,7},{5,6},{6,5},{7,4},{8,11},{9,10},{10,... | collective-permute-start | bytes 208904 | tf_op jit(solution)/shard_map/ppermute | solution.py:587
  49.7 7.9 %collective-permute-start.2 = (bf16[272,128]{1,0:T(8,128)(2,1)S(1)}, bf16[272,128]{1,0:T(8,128)(2,1)S(1)}, u32[]{:S(2)}, u32[]{:S(2)}) collective-permute-start(bf16[272,128]{1,0:T(8,128)(2,1)S(1)} %get-tuple-element.25), channel_id=1, source_target_pairs={{0,1},{1,0},{2,3},{3,2},{4,5},{5,4},{6,7},{7,6},{8,9},{9,8},{10,11... | collective-permute-start | bytes 208904 | tf_op jit(solution)/shard_map/ppermute | solution.py:586
  57.9 7.6 %collective-permute-start.5 = (bf16[5,128,128]{2,1,0:T(8,128)(2,1)S(1)}, bf16[5,128,128]{2,1,0:T(8,128)(2,1)S(1)}, u32[]{:S(2)}, u32[]{:S(2)}) collective-permute-start(bf16[5,128,128]{2,1,0:T(8,128)(2,1)S(1)} %get-tuple-element.26.own0_ref), channel_id=1, source_target_pairs={{4,0},{8,4},{12,8},{16,12},{20,16},{24,20},{28,24},{5,1},{9,5},{13... | collective-permute-start | bytes 491528 | tf_op jit(solution)/shard_map/ppermute | solution.py:612
  59.2 6.4 %copy-start.4 = (bf16[8,128,128]{2,1,0:T(8,128)(2,1)S(1)}, bf16[8,128,128]{2,1,0:T(8,128)(2,1)}, u32[]{:S(2)}) copy-start(bf16[8,128,128]{2,1,0:T(8,128)(2,1)} %mixing_ref.1) | copy-start | bytes 786436
  59.2 6.3 %collective-permute-start.4 = (bf16[5,128,128]{2,1,0:T(8,128)(2,1)S(1)}, bf16[5,128,128]{2,1,0:T(8,128)(2,1)S(1)}, u32[]{:S(2)}, u32[]{:S(2)}) collective-permute-start(bf16[5,128,128]{2,1,0:T(8,128)(2,1)S(1)} %get-tuple-element.27.own1_ref), channel_id=1, source_target_pairs={{0,4},{4,8},{8,12},{12,16},{16,20},{20,24},{24,28},{1,5},{5,9},{9,... | collective-permute-start | bytes 491528 | tf_op jit(solution)/shard_map/ppermute | solution.py:611
  72.6 0.8 copy-start.15
  73.4 14.7 %all-to-all-start.3 = ((bf16[16,128,128]{2,1,0:T(8,128)(2,1)}), bf16[16,128,128]{2,1,0:T(8,128)(2,1)S(1)}, u32[]{:S(2)}, u32[]{:S(2)}) async-start(bf16[16,128,128]{2,1,0:T(8,128)(2,1)} %attend_first.1), calls=%async_computation.3 | async-start | bytes 1048576 | tf_op jit(solution)/shard_map/all_to_all | solution.py:549
  79.3 1.0 %copy-start.16 = (bf16[2,256,512]{2,1,0:T(8,128)(2,1)S(1)}, bf16[2,256,512]{2,1,0:T(8,128)(2,1)}, u32[]{:S(2)}) copy-start(bf16[2,256,512]{2,1,0:T(8,128)(2,1)} %copy-done.15) | copy-start | bytes 1572868
  88.1 12.5 %all-to-all-start.2 = ((bf16[16,128,128]{2,1,0:T(8,128)(2,1)}), bf16[16,128,128]{2,1,0:T(8,128)(2,1)S(1)}, u32[]{:S(2)}, u32[]{:S(2)}) async-start(bf16[16,128,128]{2,1,0:T(8,128)(2,1)} %attend_second.1), calls=%async_computation.2 | async-start | bytes 1048576 | tf_op jit(solution)/shard_map/all_to_all | solution.py:549

commit v4 on v3

--- a/solution.py
+++ b/solution.py
@@ -55,39 +55,41 @@
     return lax.axis_index("tx"), lax.axis_index("zh"), lax.axis_index("zl")
 
 
-def network(x, w1_ref, w2_ref, w3_ref):
-    hidden = silu(dot(x.astype(BF), w1_ref[...])).astype(BF)
-    hidden = silu(dot(hidden, w2_ref[0])).astype(BF)
-    return dot(hidden, w3_ref[...]).astype(BF)
-
-
-def encode_rows(
-    half_id, quota, chunk, points_ref, w1_ref, w2_ref, w3_ref, index_s, feat_ref, wide_ref, xs
-):
-    rows_total = points_ref.shape[0] // 2
+def block_of(half_id, low):
+    return low if half_id else 1 - low
+
+
+def encode_rows(half_id, quota, chunk, points, weights_ready, w1_ref, w2_ref, w3_ref, index_s, feat_ref, wide_ref, xs):
+    rows_total = points.shape[0] // 2
     group = chunk // quota
-    wide_ref[...] = points_ref[...].astype(F32)
-
-    def gather(c, buffer):
-        for r in range(chunk):
-            spot = (r // quota) * 2 * quota + half_id * quota + r % quota
+    wide_ref[...] = points[...].astype(F32)
+
+    def gather(c, buffer, first, last):
+        for r in range(first, last):
+            member = r // quota
+            spot = (member * 2 + block_of(half_id, member % 2)) * quota + r % quota
             i = index_s[c * (2 * chunk // LANES) + spot // LANES, spot % LANES]
             buffer[pl.ds(r, 1), :] = wide_ref[pl.ds(i, 1), :]
 
-    def apply(c, buffer):
-        out = network(buffer[...], w1_ref, w2_ref, w3_ref)
+    def apply(c, buffer, ahead):
+        cuts = [chunk * k // 4 for k in range(5)]
+        ahead(cuts[0], cuts[1])
+        hidden = silu(dot(buffer[...].astype(BF), w1_ref[...])).astype(BF)
+        ahead(cuts[1], cuts[3])
+        hidden = silu(dot(hidden, w2_ref[0])).astype(BF)
+        ahead(cuts[3], cuts[4])
+        out = dot(hidden, w3_ref[...]).astype(BF)
         for k in range(group):
             feat_ref[c * group + k] = out[k * quota : (k + 1) * quota]
 
     chunks = rows_total // chunk
-    gather(0, xs[0])
+    gather(0, xs[0], 0, chunk)
+    weights_ready()
 
     def step(k, carry):
         c = 2 * k
-        gather(c + 1, xs[1])
-        apply(c, xs[0])
-        gather(jnp.minimum(c + 2, chunks - 1), xs[0])
-        apply(c + 1, xs[1])
+        apply(c, xs[0], lambda a, b: gather(c + 1, xs[1], a, b))
+        apply(c + 1, xs[1], lambda a, b: gather(jnp.minimum(c + 2, chunks - 1), xs[0], a, b))
         return carry
 
     lax.fori_loop(0, chunks // 2, step, 0)
@@ -97,32 +99,47 @@
     grid_y,
     along_y,
     quota,
-    points_ref,
-    w1_ref,
-    w2_ref,
-    w3_ref,
-    counts_ref,
-    order_ref,
+    points_hbm,
+    w1_hbm,
+    w2_hbm,
+    w3_hbm,
+    counts_hbm,
+    order_hbm,
     feat_ref,
     index_ref,
+    counts_s,
     off_ref,
     index_s,
     wide_ref,
     xa_ref,
     xb_ref,
-    sem,
+    points_ref,
+    w1_ref,
+    w2_ref,
+    w3_ref,
+    order_ref,
+    sems,
 ):
     tx, zh, zl = place()
     own = tx * along_y + zh * (along_y // 2) + zl
-    tiles = counts_ref.shape[1]
+    sources = (counts_hbm.at[own], order_hbm, points_hbm, w1_hbm, w2_hbm, w3_hbm)
+    targets = (counts_s, order_ref, points_ref, w1_ref, w2_ref, w3_ref)
+    copies = [
+        pltpu.make_async_copy(a, b, sems.at[k]) for k, (a, b) in enumerate(zip(sources, targets))
+    ]
+    for copy in copies:
+        copy.start()
+    tiles = counts_s.shape[0]
     order_rows = order_ref.shape[0]
     rows_total = points_ref.shape[0]
+    copies[0].wait()
 
     def add_up(g, total):
         off_ref[g] = total
-        return total + counts_ref[own, g]
+        return total + counts_s[g]
 
     lax.fori_loop(0, tiles, add_up, jnp.int32(0), unroll=8)
+    copies[1].wait()
     lane = lax.broadcasted_iota(jnp.int32, (1, LANES), 1)
 
     def run_of(start):
@@ -140,7 +157,7 @@
         for k in range(per_line):
             d = line * per_line + k
             g1 = (d // along_y) * (TLX * grid_y) + (d % along_y) * TLY
-            n1 = counts_ref[own, g1] + counts_ref[own, g1 + 1]
+            n1 = counts_s[g1] + counts_s[g1 + 1]
             run1 = run_of(off_ref[g1] - k * quota)
             run2 = run_of(off_ref[g1 + grid_y] - n1 - k * quota)
             both = jnp.where(lane < k * quota + n1, run1, run2)
@@ -148,13 +165,19 @@
         index_ref[pl.ds(line, 1), :] = value
         return carry
 
-    lax.fori_loop(0, rows_total // LANES, index_line, 0, unroll=4)
-    copy = pltpu.make_async_copy(index_ref, index_s, sem)
+    lax.fori_loop(0, rows_total // LANES, index_line, 0, unroll=8)
+    copy = pltpu.make_async_copy(index_ref, index_s, sems.at[6])
     copy.start()
+    copies[2].wait()
     copy.wait()
+
+    def weights_ready():
+        for k in (3, 4, 5):
+            copies[k].wait()
+
     encode_rows(
-        0, quota, xa_ref.shape[0], points_ref, w1_ref, w2_ref, w3_ref, index_s, feat_ref, wide_ref,
-        (xa_ref, xb_ref),
+        0, quota, xa_ref.shape[0], points_ref, weights_ready, w1_ref, w2_ref, w3_ref, index_s,
+        feat_ref, wide_ref, (xa_ref, xb_ref),
     )
 
 
@@ -162,8 +185,8 @@
     quota, points_ref, w1_ref, w2_ref, w3_ref, index_ref, feat_ref, wide_ref, xa_ref, xb_ref
 ):
     encode_rows(
-        1, quota, xa_ref.shape[0], points_ref, w1_ref, w2_ref, w3_ref, index_ref, feat_ref, wide_ref,
-        (xa_ref, xb_ref),
+        1, quota, xa_ref.shape[0], points_ref, lambda: None, w1_ref, w2_ref, w3_ref, index_ref,
+        feat_ref, wide_ref, (xa_ref, xb_ref),
     )
 
 
@@ -184,8 +207,8 @@
 def pieces_of(first, group, half_id, along_y):
     tx, zh, zl = place()
     lows = along_y // 2
-    blocks = 2
-    base = tx * (TLX * along_y * TLY) + (zl * blocks + half_id) * TLY
+    block = zl * 2 + block_of(half_id, zl)
+    base = tx * (TLX * along_y * TLY) + block * TLY
     found = []
     for k in range(group):
         member = first + k
@@ -194,10 +217,8 @@
 
 
 def partial_kernel(half_id, along_y, rows_ref, counts_ref, inducing_ref, proj_ref, *rest):
-    if half_id:
-        before_ref, own_ref, send_ref, edge_ref, num_ref = rest
-    else:
-        own_ref, send_ref, num_ref = rest
+    own_ref, send_ref = rest[:2]
+    num_ref = rest[-1]
     members, quota, width = rows_ref.shape
     grid_y = along_y * TLY
     half = LANES // HEADS
@@ -211,74 +232,79 @@
         [jnp.where(left, queries, 0.0), jnp.where(left, 0.0, queries)], axis=0
     ).astype(BF)
     wv_t = proj_ref[2].astype(F32).T.astype(BF)
-    num_ref[...] = jnp.zeros_like(num_ref)
-    spot = lax.broadcasted_iota(jnp.int32, (1, chunk), 1)
+    spot = lax.broadcasted_iota(jnp.int32, (16, chunk), 1)
     tile_row = lax.broadcasted_iota(jnp.int32, (16, chunk), 0)
-
-    def step(c, carry):
+    for c in range(members // group):
         x = jnp.concatenate([rows_ref[c * group + k] for k in range(group)], axis=0)
         keys = unit(dot(x, proj_ref[1]), ones).astype(BF)
         weights = jnp.exp2(dot_t(keys, queries) * (sharpness * math.log2(math.e))).astype(BF)
-        values = dot_t(wv_t, x)
+        values = dot_t(wv_t, x).astype(BF)
         pieces = pieces_of(c * group, group, half_id, along_y)
         tile = tile_of(spot % quota, counts_ref, pieces, spot // quota, grid_y)
-        stacked = [jnp.where(tile == t, values, 0.0).astype(BF) for t in range(4)]
+        stacked = []
+        for t in range(4):
+            mask = jnp.where(tile == t, 1.0, 0.0).astype(BF)
+            stacked += [values[k : k + 16] * mask for k in range(0, LANES, 16)]
         stacked.append(jnp.where(tile_row == tile, 1.0, 0.0).astype(BF))
-        num_ref[...] += dot(jnp.concatenate(stacked, axis=0), weights)
-        return carry
-
-    lax.fori_loop(0, members // group, step, 0)
-    pad = jnp.zeros((8, LANES), F32)
+        sums = dot(jnp.concatenate(stacked, axis=0), weights)
+        if c == 0:
+            num_ref[...] = sums
+        else:
+            num_ref[...] += sums
     last = 4 * LANES
-
-    def tile_sums(t):
-        return jnp.concatenate(
+    for t in range(4):
+        rows = slice(t * LANES, (t + 1) * LANES)
+        value = jnp.concatenate(
             [
                 num_ref[t * LANES : t * LANES + half, :LANES],
                 num_ref[t * LANES + half : (t + 1) * LANES, LANES:],
             ],
             axis=0,
         )
-
-    for t in range(4):
-        rows = slice(t * LANES, (t + 1) * LANES)
-        value = tile_sums(t)
         own_ref[rows, :] = value
         send_ref[rows, :] = value.astype(BF)
     totals = jnp.concatenate(
-        [num_ref[last : last + 4, h * LANES : (h + 1) * LANES] for h in range(HEADS)] + [pad],
+        [num_ref[last : last + 4, h * LANES : (h + 1) * LANES] for h in range(HEADS)]
+        + [jnp.zeros((8, LANES), F32)],
         axis=0,
     )
     own_ref[last:, :] = totals
     send_ref[last:, :] = totals.astype(BF)
-    if half_id:
+    if half_id == 0:
+        edge_ref = rest[2]
         zl = lax.axis_index("zl")
         for x in range(TLX):
             rows = slice(x * LANES, (x + 1) * LANES)
-            here = send_ref[(2 * x + 1) * LANES : (2 * x + 2) * LANES, :]
-            there = before_ref[2 * x * LANES : (2 * x + 1) * LANES, :]
-            edge_ref[rows, :] = jnp.where(zl == 0, here, there)
-        edge_ref[TLX * LANES :, :] = jnp.where(zl == 0, send_ref[last:, :], before_ref[last:, :])
-
-
-def queries_kernel(rows0_ref, rows1_ref, proj_ref, out0_ref, out1_ref):
+            high = send_ref[(2 * x + 1) * LANES : (2 * x + 2) * LANES, :]
+            low = send_ref[2 * x * LANES : (2 * x + 1) * LANES, :]
+            edge_ref[rows, :] = jnp.where(zl == 0, high, low)
+        edge_ref[TLX * LANES :, :] = send_ref[last:, :]
+
+
+def queries_kernel(rows0_ref, rows1_ref, proj_ref, out_ref):
     ones = head_ones()
-    for rows_ref, out_ref in ((rows0_ref, out0_ref), (rows1_ref, out1_ref)):
+    for half_id, rows_ref in enumerate((rows0_ref, rows1_ref)):
         members, quota, width = rows_ref.shape
         group = min(512 // quota, members)
-
-        def step(c, carry):
+        for c in range(members // group):
             x = jnp.concatenate([rows_ref[c * group + k] for k in range(group)], axis=0)
             query = unit(dot(x, proj_ref[0]), ones).astype(BF)
             for k in range(group):
-                out_ref[c * group + k] = query[k * quota : (k + 1) * quota]
-            return carry
-
-        lax.fori_loop(0, members // group, step, 0)
+                out_ref[half_id, c * group + k] = query[k * quota : (k + 1) * quota]
 
 
 def combine_kernel(
-    own0_ref, own1_ref, other0_ref, other1_ref, near_ref, far_ref, inducing_ref, proj_ref, out0_ref, out1_ref
+    own0_ref,
+    own1_ref,
+    other0_ref,
+    other1_ref,
+    near_ref,
+    far_ref,
+    inducing_ref,
+    proj_ref,
+    query_any,
+    out0_ref,
+    out1_ref,
 ):
     half = LANES // HEADS
     last = 4 * LANES
@@ -291,7 +317,8 @@
         out = inducing_ref[...].astype(F32) + dot(attended, proj_ref[3])
         return out.astype(BF)
 
-    for b, (own_ref, other_ref) in enumerate(((own0_ref, other0_ref), (own1_ref, other1_ref))):
+    for half_id, (own_ref, other_ref) in enumerate(((own0_ref, other0_ref), (own1_ref, other1_ref))):
+        b = block_of(half_id, zl)
         totals = own_ref[last:, :] + other_ref[last:, :].astype(F32)
         for t in range(4):
             rows = slice(t * LANES, (t + 1) * LANES)
@@ -405,73 +432,62 @@
 
 
 def attend_kernel(
-    half_id, along_y, rows_ref, query_ref, counts_ref, key_ref, value_ref, proj_ref, out_ref
+    along_y, rows0_ref, rows1_ref, query_ref, counts_ref, key_ref, value_ref, proj_ref, out_ref
 ):
-    members, quota, width = rows_ref.shape
+    members, quota, width = rows0_ref.shape
     grid_y = along_y * TLY
     group = min(512 // quota, members)
     chunk = group * quota
     spot = lax.broadcasted_iota(jnp.int32, (chunk, LANES), 0)
-
-    def step(c, carry):
-        x = jnp.concatenate([rows_ref[c * group + k] for k in range(group)], axis=0)
-        query = jnp.concatenate([query_ref[c * group + k] for k in range(group)], axis=0)
-        query = query.astype(F32)
-        pieces = pieces_of(c * group, group, half_id, along_y)
-        which = tile_of(spot % quota, counts_ref, pieces, spot // quota, grid_y)
-        inside = [which == t for t in range(4)]
-        expanded = jnp.concatenate(
-            [jnp.where(m, query, 0.0).astype(BF) for m in inside], axis=1
-        )
-        scores = dot_t(expanded, key_ref[half_id])
-        weights = jnp.exp2(scores * (sharpness * math.log2(math.e)))
-        spread = jnp.concatenate(
-            [
-                jnp.where(m, weights[:, h * LANES : (h + 1) * LANES], 0.0).astype(BF)
-                for m in inside
-                for h in range(HEADS)
-            ],
-            axis=1,
-        )
-        both = dot(spread, value_ref[half_id])
-        attended = (both[:, :LANES] / both[:, LANES:]).astype(BF)
-        result = (x.astype(F32) + dot(attended, proj_ref[3])).astype(BF)
-        for k in range(group):
-            out_ref[c * group + k] = result[k * quota : (k + 1) * quota]
-        return carry
-
-    lax.fori_loop(0, members // group, step, 0)
-
-
-def scatter_rows(half_id, rows_ref, index_ref, wide_ref, part_ref):
+    for half_id, rows_ref in enumerate((rows0_ref, rows1_ref)):
+        block = block_of(half_id, lax.axis_index("zl"))
+        for c in range(members // group):
+            x = jnp.concatenate([rows_ref[c * group + k] for k in range(group)], axis=0)
+            query = jnp.concatenate(
+                [query_ref[half_id, c * group + k] for k in range(group)], axis=0
+            )
+            pieces = pieces_of(c * group, group, half_id, along_y)
+            which = tile_of(spot % quota, counts_ref, pieces, spot // quota, grid_y)
+            masks = [jnp.where(which == t, 1.0, 0.0).astype(BF) for t in range(4)]
+            expanded = jnp.concatenate([query * m for m in masks], axis=1)
+            scores = dot_t(expanded, key_ref[block])
+            weights = jnp.exp2(scores * (sharpness * math.log2(math.e))).astype(BF)
+            spread = jnp.concatenate(
+                [
+                    weights[:, h * LANES : (h + 1) * LANES] * m
+                    for m in masks
+                    for h in range(HEADS)
+                ],
+                axis=1,
+            )
+            both = dot(spread, value_ref[block])
+            attended = (both[:, :LANES] / both[:, LANES:]).astype(BF)
+            result = (x.astype(F32) + dot(attended, proj_ref[3])).astype(BF)
+            for k in range(group):
+                out_ref[c * group + k, half_id] = result[k * quota : (k + 1) * quota]
+
+
+def scatter_kernel(rows_ref, index_ref, out_ref, wide_ref, part_ref):
     chunk = part_ref.shape[0]
-    members, quota, width = rows_ref.shape
-    group = chunk // quota
+    members, halves, quota, width = rows_ref.shape
+    group = chunk // (halves * quota)
 
     def step(c, carry):
         for k in range(group):
-            part_ref[k * quota : (k + 1) * quota, :] = rows_ref[c * group + k].astype(F32)
+            for half_id in range(halves):
+                row = (k * halves + block_of(half_id, k % 2)) * quota
+                part_ref[row : row + quota, :] = rows_ref[c * group + k, half_id].astype(F32)
         for r in range(chunk):
-            spot = (r // quota) * 2 * quota + half_id * quota + r % quota
-            i = index_ref[c * (2 * chunk // LANES) + spot // LANES, spot % LANES]
+            i = index_ref[c * (chunk // LANES) + r // LANES, r % LANES]
             wide_ref[pl.ds(i, 1), :] = part_ref[pl.ds(r, 1), :]
         return carry
 
     lax.fori_loop(0, members // group, step, 0)
-
-
-def scatter_first_kernel(rows_ref, index_ref, wide_ref, part_ref):
-    scatter_rows(0, rows_ref, index_ref, wide_ref, part_ref)
-
-
-def scatter_second_kernel(rows_ref, index_ref, before_ref, out_ref, wide_ref, part_ref):
-    wide_ref[...] = before_ref[...]
-    scatter_rows(1, rows_ref, index_ref, wide_ref, part_ref)
     out_ref[...] = wide_ref[...].astype(BF)
 
 
 def call(kernel, name, out_shape, in_specs, scratch, micros, operands, megabytes=20, **more):
-    spaces = {"v": pltpu.VMEM, "s": pltpu.SMEM}
+    spaces = {"v": pltpu.VMEM, "s": pltpu.SMEM, "a": pl.ANY}
     many = isinstance(out_shape, tuple)
     whole = pl.BlockSpec(memory_space=pltpu.VMEM)
     return pl.pallas_call(
@@ -528,12 +544,18 @@
         functools.partial(encode_first_kernel, grid_y, along_y, quota),
         "encode_first",
         (shape(half_rows), shape((lines, LANES), jnp.int32)),
-        "vvvvsv",
-        [SMEM((counts.shape[1],), jnp.int32), SMEM((lines, LANES), jnp.int32)]
+        "aaaaaa",
+        [
+            SMEM((counts.shape[1],), jnp.int32),
+            SMEM((counts.shape[1],), jnp.int32),
+            SMEM((lines, LANES), jnp.int32),
+        ]
         + buffers
-        + [pltpu.SemaphoreType.DMA],
+        + [VMEM(a.shape, BF) for a in (points, *weights)]
+        + [VMEM((lines, LANES), jnp.int32), pltpu.SemaphoreType.DMA((7,))],
         8,
         (points, *weights, counts, point_order.reshape(lines, LANES)),
+        megabytes=56,
     )
     second = call(
         functools.partial(encode_second_kernel, quota),
@@ -555,44 +577,46 @@
     edge_rows = TLX * LANES + 16
     parts = (shape((part_rows, LANES), F32), shape((part_rows, LANES)))
     sums = [VMEM((part_rows, HEADS * LANES), F32)]
-    own0, send0 = call(
+    own0, send0, edge = call(
         functools.partial(partial_kernel, 0, along_y),
         "partial_first",
+        parts + (shape((edge_rows, LANES)),),
+        "vsvv",
+        sums,
+        3,
+        (rows0, counts, inducing, first_proj),
+    )
+    own1, send1 = call(
+        functools.partial(partial_kernel, 1, along_y),
+        "partial_second",
         parts,
         "vsvv",
         sums,
-        4,
-        (rows0, counts, inducing, first_proj),
-    )
-    own1, send1, edge = call(
-        functools.partial(partial_kernel, 1, along_y),
-        "partial_second",
-        parts + (shape((edge_rows, LANES)),),
-        "vsvvv",
-        sums,
-        4,
-        (rows1, counts, inducing, first_proj, send0),
-    )
-    across = [(h * lows + l, (highs - 1 - h) * lows + l) for h in range(highs) for l in range(lows)]
-    beside = [(h * lows + l, h * lows + lows - 1 - l) for h in range(highs) for l in range(lows)]
-    both = [
-        (h * lows + l, (highs - 1 - h) * lows + lows - 1 - l)
-        for h in range(highs)
-        for l in range(lows)
-    ]
-    z_axes = ("zh", "zl")
-    other0 = lax.ppermute(send0, z_axes, across)
-    other1 = lax.ppermute(send1, z_axes, across)
-    near = lax.ppermute(edge, z_axes, beside)
-    far = lax.ppermute(edge, z_axes, both)
-
-    query0, query1 = call(
+        3,
+        (rows1, counts, inducing, first_proj),
+    )
+    pairs = [(h, l) for h in range(highs) for l in range(lows)]
+
+    def swap(value, flip_high, flip_low):
+        steps = []
+        for h, l in pairs:
+            other_h = highs - 1 - h if flip_high else h
+            other_l = lows - 1 - l if flip_low else l
+            steps.append((h * lows + l, other_h * lows + other_l))
+        return lax.ppermute(value, ("zh", "zl"), steps)
+
+    other0 = swap(send0, True, False)
+    far = swap(edge, True, True)
+    near = swap(edge, False, True)
+    other1 = swap(send1, True, False)
+
+    queries = call(
         queries_kernel,
         "point_queries",
-        (shape(half_rows), shape(half_rows)),
+        shape((2,) + half_rows),
         "vvv",
         [],
-        3,
+        2,
         (rows0, rows1, second_proj),
     )
 
@@ -601,10 +625,10 @@
         combine_kernel,
         "combine_partials",
         (line, line),
-        "v" * 8,
+        "v" * 8 + "a",
         [],
-        2,
-        (own0, own1, other0, other1, near, far, inducing, first_proj),
+        1,
+        (own0, own1, other0, other1, near, far, inducing, first_proj, queries),
     )
     forward = [(i, i + 1) for i in range(along_x - 1)]
     backward = [(i + 1, i) for i in range(along_x - 1)]
@@ -621,36 +645,23 @@
         (summary0, summary1, below, above, second_proj, mixing),
     )
 
-    def attend(half_id, rows, query):
-        return call(
-            functools.partial(attend_kernel, half_id, along_y),
-            ("attend_first", "attend_second")[half_id],
-            shape(half_rows),
-            "vvsvvv",
-            [],
-            4,
-            (rows, query, counts, keys, values, second_proj),
-        )
-
-    back0 = exchange(attend(0, rows0, query0))
-    back1 = exchange(attend(1, rows1, query1))
-    wide = call(
-        scatter_first_kernel,
-        "scatter_first",
-        shape((point_count, width), F32),
+    result = call(
+        functools.partial(attend_kernel, along_y),
+        "attend_points",
+        shape((members, 2, quota, width)),
+        "vvvsvvv",
+        [],
+        7,
+        (rows0, rows1, queries, counts, keys, values, second_proj),
+    )
+    return call(
+        scatter_kernel,
+        "scatter_rows",
+        shape((point_count, width)),
         "vs",
-        [VMEM((chunk, width), F32)],
-        3,
-        (back0, index),
-    )
-    return call(
-        scatter_second_kernel,
-        "scatter_second",
-        shape((point_count, width)),
-        "vsv",
         [VMEM((point_count, width), F32), VMEM((chunk, width), F32)],
-        4,
-        (back1, index, wide),
+        5,
+        (exchange(result), index),
     )
 
 

time: 105 us -> 95.3 us (0.908)
  blocking collectives: 0 us -> 23 us
  starting transfers between devices: 30.5 us -> 21 us
  Pallas kernels: 44.6 us -> 35.5 us
  waiting for transfers between devices: 21.5 us -> 14.4 us
  local copies, waits for them, and re-layouts: 7.38 us -> 0.75 us
    all_to_all x0 -> x1, blocking collectives: none -> 23 us  [exchange(): lax.all_to_all(rows, ('tx', 'zl'), split_axis=0, concat_axis=0, tiled=True)]
    all_to_all x4 -> x2, starting transfers between devices: 19.8 us -> 10.2 us  [exchange(): lax.all_to_all(rows, ('tx', 'zl'), split_axis=0, concat_axis=0, tiled=True)]
    pallas_call x11 -> x9, Pallas kernels: 44.6 us -> 35.5 us  [call(): pl.pallas_call(kernel, out_shape=out_shape, in_specs=[pl.BlockSpec(memory...]
    all_to_all x4 -> x2, waiting for transfers between devices: 15.2 us -> 8.09 us  [exchange(): lax.all_to_all(rows, ('tx', 'zl'), split_axis=0, concat_axis=0, tiled=True)]
    unnamed x34 -> x22, local copies, waits for them, and re-layouts: 7.38 us -> 0.75 us
  transfers between devices with their start and end apart: 10 -> 8, of which waited for: 6 -> 5; matrix products, arithmetic and copies ran while one was open for 0% -> 0% of each run, Pallas kernels for 25% -> 14%
where the time goes in v4:
time: 95.3 us; the launch traced here: 94.8 us
  Pallas kernels  35.5 us (37%)
  blocking collectives  23 us (24%)
  starting transfers between devices  21 us (22%)
  waiting for transfers between devices  14.4 us (15%)
    pallas_call x9, Pallas kernels, call(): pl.pallas_call(kernel, out_shape=out_shape, in_specs=[pl.BlockSpec(memory...  35.5 us
    all_to_all x1, blocking collectives, exchange(): lax.all_to_all(rows, ('tx', 'zl'), split_axis=0, concat_axis=0, tiled=True)  23 us
    all_to_all x2, starting transfers between devices, exchange(): lax.all_to_all(rows, ('tx', 'zl'), split_axis=0, concat_axis=0, tiled=True)  10.2 us
    all_to_all x2, waiting for transfers between devices, exchange(): lax.all_to_all(rows, ('tx', 'zl'), split_axis=0, concat_axis=0, tiled=True)  8.09 us
    ppermute x4, starting transfers between devices, swap(): return lax.ppermute(value, ('zh', 'zl'), steps)  6.24 us
    ppermute x4, waiting for transfers between devices, swap(): return lax.ppermute(value, ('zh', 'zl'), steps)  5.47 us
    ppermute x1, starting transfers between devices, body(): below = lax.ppermute(summary1, 'tx', forward)  3.22 us
  transfers between devices with their start and end apart: 8, of which 5 were waited for; matrix products, arithmetic and copies ran while one was open for 0% of the time, Pallas kernels for 14%

profile of v4, /device:TPU:0, one launch (start us, length us, event | category | flops | bytes accessed | tf_op | source)
XLA Modules:
  0.0 94.8 jit_solution(3814610843282262615)
XLA Ops:
  0.0 0.0 copy-start.3
  0.0 0.0 copy-start.5
  0.0 0.0 copy-start.6
  0.0 7.5 %encode_first.1 = (bf16[16,128,128]{2,1,0:T(8,128)(2,1)}, s32[32,128]{1,0:T(8,128)}) custom-call(bf16[4096,128]{1,0:T(8,128)(2,1)} %points_ref.1, bf16[128,512]{1,0:T(8,128)(2,1)} %w1_ref.1, bf16[1,512,512]{2,1,0:T(8,128)(2,1)} %w2_ref.1, bf16[512,128]{1,0:T(8,128)(2,1)} %w3_ref.1, s32[32,128]{1,0:T(8,128)} %counts_ref.5, s32[32,128]{1,0:T(8,128)} %bitcast.1), custom_call_target="tpu_custom_call" | custom-call | flops 4000000000 | bytes 8000000 | tf_op jit(solution)/shard_map/encode_first/pallas_call | solution.py:493
  7.5 0.0 copy-start.2
  7.5 6.4 %all-to-all-start = ((bf16[16,128,128]{2,1,0:T(8,128)(2,1)}), bf16[16,128,128]{2,1,0:T(8,128)(2,1)S(1)}, u32[]{:S(2)}, u32[]{:S(2)}) async-start(bf16[16,128,128]{2,1,0:T(8,128)(2,1)} %get-tuple-element.16), calls=%async_computation | async-start | bytes 1048576 | tf_op jit(solution)/shard_map/all_to_all | solution.py:571
  14.0 0.0 copy-done.3
  14.0 0.0 copy-done.5
  14.0 0.0 copy-done.6
  14.0 0.0 copy-done.2
  14.0 0.0 copy-start.9
  14.0 0.7 copy-done.9
  14.7 5.7 %encode_second.1 = bf16[16,128,128]{2,1,0:T(8,128)(2,1)} custom-call(bf16[4096,128]{1,0:T(8,128)(2,1)S(1)} %copy-done.2, bf16[128,512]{1,0:T(8,128)(2,1)S(1)} %copy-done.5, bf16[1,512,512]{2,1,0:T(8,128)(2,1)S(1)} %copy-done.3, bf16[512,128]{1,0:T(8,128)(2,1)S(1)} %copy-done.6, s32[32,128]{1,0:T(8,128)S(1)} %copy-done.9), custom_call_target="tpu_custom_call" | custom-call | flops 3000000000 | bytes 6000000 | tf_op jit(solution)/shard_map/encode_second/pallas_call | solution.py:493
  20.4 0.0 copy-start
  20.4 0.0 copy-start.1
  20.4 0.0 copy-start.8
  20.4 2.3 %all-to-all-done.rows0_ref.rows_ref = bf16[16,128,128]{2,1,0:T(8,128)(2,1)S(1)} async-done(((bf16[16,128,128]{2,1,0:T(8,128)(2,1)}), bf16[16,128,128]{2,1,0:T(8,128)(2,1)S(1)}, u32[]{:S(2)}, u32[]{:S(2)}) %all-to-all-start) | async-done | bytes 524320 | tf_op jit(solution)/shard_map/all_to_all | solution.py:571
  22.7 3.8 %all-to-all-start.1 = ((bf16[16,128,128]{2,1,0:T(8,128)(2,1)}), bf16[16,128,128]{2,1,0:T(8,128)(2,1)S(1)}, u32[]{:S(2)}, u32[]{:S(2)}) async-start(bf16[16,128,128]{2,1,0:T(8,128)(2,1)} %encode_second.1), calls=%async_computation.1 | async-start | bytes 1048576 | tf_op jit(solution)/shard_map/all_to_all | solution.py:571
  26.5 0.0 copy-done
  26.5 0.0 copy-done.1
  26.5 0.0 copy-done.8
  26.5 3.1 %partial_first.1 = (f32[528,128]{1,0:T(8,128)S(1)}, bf16[528,128]{1,0:T(8,128)(2,1)S(1)}, bf16[272,128]{1,0:T(8,128)(2,1)S(1)}) custom-call(bf16[16,128,128]{2,1,0:T(8,128)(2,1)S(1)} %all-to-all-done.rows0_ref.rows_ref, s32[32,128]{1,0:T(8,128)S(1)} %copy-done.8, bf16[128,128]{1,0:T(8,128)(2,1)S(1)} %copy-done.1, bf16[4,128,128]{2,1,0:T(8,128)(2,1)S(1)} %copy-done), custom_call_target="tpu_custom_call" | custom-call | flops 1500000000 | bytes 3000000 | tf_op jit(solution)/shard_map/partial_first/pallas_call | solution.py:493
  29.6 0.0 copy-start.7
  29.6 2.7 %collective-permute-start = (bf16[528,128]{1,0:T(8,128)(2,1)S(1)}, bf16[528,128]{1,0:T(8,128)(2,1)S(1)}, u32[]{:S(2)}, u32[]{:S(2)}) collective-permute-start(bf16[528,128]{1,0:T(8,128)(2,1)S(1)} %get-tuple-element.20), channel_id=1, source_target_pairs={{0,2},{1,3},{2,0},{3,1},{4,6},{5,7},{6,4},{7,5},{8,10},{9,11},{10,... | collective-permute-start | bytes 405512 | tf_op jit(solution)/shard_map/ppermute | solution.py:606
  32.3 5.8 %all-to-all-done.1.rows1_ref.rows_ref = bf16[16,128,128]{2,1,0:T(8,128)(2,1)S(1)} async-done(((bf16[16,128,128]{2,1,0:T(8,128)(2,1)}), bf16[16,128,128]{2,1,0:T(8,128)(2,1)S(1)}, u32[]{:S(2)}, u32[]{:S(2)}) %all-to-all-start.1) | async-done | bytes 524320 | tf_op jit(solution)/shard_map/all_to_all | solution.py:571
  38.1 3.1 %partial_second.1 = (f32[528,128]{1,0:T(8,128)S(1)}, bf16[528,128]{1,0:T(8,128)(2,1)S(1)}) custom-call(bf16[16,128,128]{2,1,0:T(8,128)(2,1)S(1)} %all-to-all-done.1.rows1_ref.rows_ref, s32[32,128]{1,0:T(8,128)S(1)} %copy-done.8, bf16[128,128]{1,0:T(8,128)(2,1)S(1)} %copy-done.1, bf16[4,128,128]{2,1,0:T(8,128)(2,1)S(1)} %copy-done), custom_call_target="tpu_custom_call" | custom-call | flops 1500000000 | bytes 3000000 | tf_op jit(solution)/shard_map/partial_second/pallas_call | solution.py:493
  41.2 0.2 collective-permute-start.1
  41.5 1.8 %collective-permute-start.3 = (bf16[272,128]{1,0:T(8,128)(2,1)S(1)}, bf16[272,128]{1,0:T(8,128)(2,1)S(1)}, u32[]{:S(2)}, u32[]{:S(2)}) collective-permute-start(bf16[272,128]{1,0:T(8,128)(2,1)S(1)} %get-tuple-element.22), channel_id=1, source_target_pairs={{0,3},{1,2},{2,1},{3,0},{4,7},{5,6},{6,5},{7,4},{8,11},{9,10},{10,... | collective-permute-start | bytes 208904 | tf_op jit(solution)/shard_map/ppermute | solution.py:606
  43.3 1.5 %collective-permute-start.2 = (bf16[272,128]{1,0:T(8,128)(2,1)S(1)}, bf16[272,128]{1,0:T(8,128)(2,1)S(1)}, u32[]{:S(2)}, u32[]{:S(2)}) collective-permute-start(bf16[272,128]{1,0:T(8,128)(2,1)S(1)} %get-tuple-element.22), channel_id=1, source_target_pairs={{0,1},{1,0},{2,3},{3,2},{4,5},{5,4},{6,7},{7,6},{8,9},{9,8},{10,11... | collective-permute-start | bytes 208904 | tf_op jit(solution)/shard_map/ppermute | solution.py:606
  44.8 0.0 copy-done.7
  44.8 1.3 %point_queries.1.query_any.query_ref = bf16[2,16,128,128]{3,2,1,0:T(8,128)(2,1)S(1)} custom-call(bf16[16,128,128]{2,1,0:T(8,128)(2,1)S(1)} %all-to-all-done.rows0_ref.rows_ref, bf16[16,128,128]{2,1,0:T(8,128)(2,1)S(1)} %all-to-all-done.1.rows1_ref.rows_ref, bf16[4,128,128]{2,1,0:T(8,128)(2,1)S(1)} %copy-done.7), custom_call_target="tpu_custom_call" | custom-call | flops 1000000000 | bytes 2000000 | tf_op jit(solution)/shard_map/point_queries/pallas_call | solution.py:493
  46.1 2.3 %collective-permute-done.3.far_ref = bf16[272,128]{1,0:T(8,128)(2,1)S(1)} collective-permute-done((bf16[272,128]{1,0:T(8,128)(2,1)S(1)}, bf16[272,128]{1,0:T(8,128)(2,1)S(1)}, u32[]{:S(2)}, u32[]{:S(2)}) %collective-permute-start.3) | collective-permute-done | bytes 69664 | tf_op jit(solution)/shard_map/ppermute | solution.py:606
  48.4 3.1 %collective-permute-done.2.near_ref = bf16[272,128]{1,0:T(8,128)(2,1)S(1)} collective-permute-done((bf16[272,128]{1,0:T(8,128)(2,1)S(1)}, bf16[272,128]{1,0:T(8,128)(2,1)S(1)}, u32[]{:S(2)}, u32[]{:S(2)}) %collective-permute-start.2) | collective-permute-done | bytes 69664 | tf_op jit(solution)/shard_map/ppermute | solution.py:606
  51.5 0.0 collective-permute-done.other0_ref
  51.5 0.0 collective-permute-done.1.other1_ref
  51.5 0.0 copy-start.4
  51.5 0.3 combine_partials.1
  51.9 1.3 %collective-permute-start.5 = (bf16[5,128,128]{2,1,0:T(8,128)(2,1)S(1)}, bf16[5,128,128]{2,1,0:T(8,128)(2,1)S(1)}, u32[]{:S(2)}, u32[]{:S(2)}) collective-permute-start(bf16[5,128,128]{2,1,0:T(8,128)(2,1)S(1)} %get-tuple-element.23.own0_ref), channel_id=1, source_target_pairs={{4,0},{8,4},{12,8},{16,12},{20,16},{24,20},{28,24},{5,1},{9,5},{13... | collective-permute-start | bytes 491528 | tf_op jit(solution)/shard_map/ppermute | solution.py:636
  53.2 3.2 %collective-permute-start.4 = (bf16[5,128,128]{2,1,0:T(8,128)(2,1)S(1)}, bf16[5,128,128]{2,1,0:T(8,128)(2,1)S(1)}, u32[]{:S(2)}, u32[]{:S(2)}) collective-permute-start(bf16[5,128,128]{2,1,0:T(8,128)(2,1)S(1)} %get-tuple-element.24.own1_ref), channel_id=1, source_target_pairs={{0,4},{4,8},{8,12},{12,16},{16,20},{20,24},{24,28},{1,5},{5,9},{9,... | collective-permute-start | bytes 491528 | tf_op jit(solution)/shard_map/ppermute | solution.py:635
  56.4 0.0 collective-permute-done.5.above_ref
  56.4 0.8 collective-permute-done.4.below_ref
  57.2 0.0 copy-done.4
  57.2 0.9 mix_tiles.1
  58.2 8.4 %attend_points.1 = bf16[16,2,128,128]{3,2,1,0:T(8,128)(2,1)S(1)} custom-call(bf16[16,128,128]{2,1,0:T(8,128)(2,1)S(1)} %all-to-all-done.rows0_ref.rows_ref, bf16[16,128,128]{2,1,0:T(8,128)(2,1)S(1)} %all-to-all-done.1.rows1_ref.rows_ref, bf16[2,16,128,128]{3,2,1,0:T(8,128)(2,1)S(1)} %point_queries.1.query_any.query_ref, s32[32,128]{1,0:T(8,128)S(1)} %copy-done.8, ...), custom_call_target="tpu_custom_call" | custom-call | flops 3500000000 | bytes 7000000 | tf_op jit(solution)/shard_map/attend_points/pallas_call | solution.py:493
  66.5 0.0 copy-start.10
  66.5 23.0 %all_to_all.15.rows_ref = bf16[16,2,128,128]{3,2,1,0:T(8,128)(2,1)S(1)} all-to-all(bf16[16,2,128,128]{3,2,1,0:T(8,128)(2,1)S(1)} %attend_points.1), channel_id=1, replica_groups=mesh['tx'=8,'zh'=2,'zl'=2] {'tx','zl'}, dimensions={0} | all-to-all | bytes 2097152 | tf_op jit(solution)/shard_map/all_to_all | solution.py:571
  89.6 0.0 copy-done.10
  89.6 5.2 %scatter_rows.1 = bf16[4096,128]{1,0:T(8,128)(2,1)} custom-call(bf16[16,2,128,128]{3,2,1,0:T(8,128)(2,1)S(1)} %all_to_all.15.rows_ref, s32[32,128]{1,0:T(8,128)S(1)} %copy-done.10), custom_call_target="tpu_custom_call" | custom-call | flops 2500000000 | bytes 5000000 | tf_op jit(solution)/shard_map/scatter_rows/pallas_call | solution.py:493
Async XLA Ops:
  0.0 14.0 %copy-start.3 = (bf16[1,512,512]{2,1,0:T(8,128)(2,1)S(1)}, bf16[1,512,512]{2,1,0:T(8,128)(2,1)}, u32[]{:S(2)}) copy-start(bf16[1,512,512]{2,1,0:T(8,128)(2,1)} %w2_ref.1) | copy-start | bytes 1572868
  0.0 14.0 %copy-start.5 = (bf16[128,512]{1,0:T(8,128)(2,1)S(1)}, bf16[128,512]{1,0:T(8,128)(2,1)}, u32[]{:S(2)}) copy-start(bf16[128,512]{1,0:T(8,128)(2,1)} %w1_ref.1) | copy-start | bytes 393220
  0.0 14.0 %copy-start.6 = (bf16[512,128]{1,0:T(8,128)(2,1)S(1)}, bf16[512,128]{1,0:T(8,128)(2,1)}, u32[]{:S(2)}) copy-start(bf16[512,128]{1,0:T(8,128)(2,1)} %w3_ref.1) | copy-start | bytes 393220
  7.5 6.5 %copy-start.2 = (bf16[4096,128]{1,0:T(8,128)(2,1)S(1)}, bf16[4096,128]{1,0:T(8,128)(2,1)}, u32[]{:S(2)}) copy-start(bf16[4096,128]{1,0:T(8,128)(2,1)} %points_ref.1) | copy-start | bytes 3145732
  7.5 15.2 %all-to-all-start = ((bf16[16,128,128]{2,1,0:T(8,128)(2,1)}), bf16[16,128,128]{2,1,0:T(8,128)(2,1)S(1)}, u32[]{:S(2)}, u32[]{:S(2)}) async-start(bf16[16,128,128]{2,1,0:T(8,128)(2,1)} %get-tuple-element.16), calls=%async_computation | async-start | bytes 1048576 | tf_op jit(solution)/shard_map/all_to_all | solution.py:571
  14.0 0.7 copy-start.9
  20.4 6.1 %copy-start = (bf16[4,128,128]{2,1,0:T(8,128)(2,1)S(1)}, bf16[4,128,128]{2,1,0:T(8,128)(2,1)}, u32[]{:S(2)}) copy-start(bf16[4,128,128]{2,1,0:T(8,128)(2,1)} %proj_ref.9) | copy-start | bytes 393220
  20.4 6.1 %copy-start.1 = (bf16[128,128]{1,0:T(8,128)(2,1)S(1)}, bf16[128,128]{1,0:T(8,128)(2,1)}, u32[]{:S(2)}) copy-start(bf16[128,128]{1,0:T(8,128)(2,1)} %inducing_ref.5) | copy-start | bytes 98308
  20.4 6.1 %copy-start.8 = (s32[32,128]{1,0:T(8,128)S(1)}, s32[32,128]{1,0:T(8,128)}, u32[]{:S(2)}) copy-start(s32[32,128]{1,0:T(8,128)} %counts_ref.5) | copy-start | bytes 49156
  22.7 15.4 %all-to-all-start.1 = ((bf16[16,128,128]{2,1,0:T(8,128)(2,1)}), bf16[16,128,128]{2,1,0:T(8,128)(2,1)S(1)}, u32[]{:S(2)}, u32[]{:S(2)}) async-start(bf16[16,128,128]{2,1,0:T(8,128)(2,1)} %encode_second.1), calls=%async_computation.1 | async-start | bytes 1048576 | tf_op jit(solution)/shard_map/all_to_all | solution.py:571
  29.6 15.2 %copy-start.7 = (bf16[4,128,128]{2,1,0:T(8,128)(2,1)S(1)}, bf16[4,128,128]{2,1,0:T(8,128)(2,1)}, u32[]{:S(2)}) copy-start(bf16[4,128,128]{2,1,0:T(8,128)(2,1)} %proj_ref.11) | copy-start | bytes 393220
  29.6 21.9 %collective-permute-start = (bf16[528,128]{1,0:T(8,128)(2,1)S(1)}, bf16[528,128]{1,0:T(8,128)(2,1)S(1)}, u32[]{:S(2)}, u32[]{:S(2)}) collective-permute-start(bf16[528,128]{1,0:T(8,128)(2,1)S(1)} %get-tuple-element.20), channel_id=1, source_target_pairs={{0,2},{1,3},{2,0},{3,1},{4,6},{5,7},{6,4},{7,5},{8,10},{9,11},{10,... | collective-permute-start | bytes 405512 | tf_op jit(solution)/shard_map/ppermute | solution.py:606
  41.2 10.3 %collective-permute-start.1 = (bf16[528,128]{1,0:T(8,128)(2,1)S(1)}, bf16[528,128]{1,0:T(8,128)(2,1)S(1)}, u32[]{:S(2)}, u32[]{:S(2)}) collective-permute-start(bf16[528,128]{1,0:T(8,128)(2,1)S(1)} %get-tuple-element.21), channel_id=1, source_target_pairs={{0,2},{1,3},{2,0},{3,1},{4,6},{5,7},{6,4},{7,5},{8,10},{9,11},{10,... | collective-permute-start | bytes 405512 | tf_op jit(solution)/shard_map/ppermute | solution.py:606
  41.5 6.9 %collective-permute-start.3 = (bf16[272,128]{1,0:T(8,128)(2,1)S(1)}, bf16[272,128]{1,0:T(8,128)(2,1)S(1)}, u32[]{:S(2)}, u32[]{:S(2)}) collective-permute-start(bf16[272,128]{1,0:T(8,128)(2,1)S(1)} %get-tuple-element.22), channel_id=1, source_target_pairs={{0,3},{1,2},{2,1},{3,0},{4,7},{5,6},{6,5},{7,4},{8,11},{9,10},{10,... | collective-permute-start | bytes 208904 | tf_op jit(solution)/shard_map/ppermute | solution.py:606
  43.3 8.2 %collective-permute-start.2 = (bf16[272,128]{1,0:T(8,128)(2,1)S(1)}, bf16[272,128]{1,0:T(8,128)(2,1)S(1)}, u32[]{:S(2)}, u32[]{:S(2)}) collective-permute-start(bf16[272,128]{1,0:T(8,128)(2,1)S(1)} %get-tuple-element.22), channel_id=1, source_target_pairs={{0,1},{1,0},{2,3},{3,2},{4,5},{5,4},{6,7},{7,6},{8,9},{9,8},{10,11... | collective-permute-start | bytes 208904 | tf_op jit(solution)/shard_map/ppermute | solution.py:606
  51.5 5.7 %copy-start.4 = (bf16[8,128,128]{2,1,0:T(8,128)(2,1)S(1)}, bf16[8,128,128]{2,1,0:T(8,128)(2,1)}, u32[]{:S(2)}) copy-start(bf16[8,128,128]{2,1,0:T(8,128)(2,1)} %mixing_ref.1) | copy-start | bytes 786436
  51.9 4.5 %collective-permute-start.5 = (bf16[5,128,128]{2,1,0:T(8,128)(2,1)S(1)}, bf16[5,128,128]{2,1,0:T(8,128)(2,1)S(1)}, u32[]{:S(2)}, u32[]{:S(2)}) collective-permute-start(bf16[5,128,128]{2,1,0:T(8,128)(2,1)S(1)} %get-tuple-element.23.own0_ref), channel_id=1, source_target_pairs={{4,0},{8,4},{12,8},{16,12},{20,16},{24,20},{28,24},{5,1},{9,5},{13... | collective-permute-start | bytes 491528 | tf_op jit(solution)/shard_map/ppermute | solution.py:636
  53.2 4.0 %collective-permute-start.4 = (bf16[5,128,128]{2,1,0:T(8,128)(2,1)S(1)}, bf16[5,128,128]{2,1,0:T(8,128)(2,1)S(1)}, u32[]{:S(2)}, u32[]{:S(2)}) collective-permute-start(bf16[5,128,128]{2,1,0:T(8,128)(2,1)S(1)} %get-tuple-element.24.own1_ref), channel_id=1, source_target_pairs={{0,4},{4,8},{8,12},{12,16},{16,20},{20,24},{24,28},{1,5},{5,9},{9,... | collective-permute-start | bytes 491528 | tf_op jit(solution)/shard_map/ppermute | solution.py:635
  66.5 23.1 %copy-start.10 = (s32[32,128]{1,0:T(8,128)S(1)}, s32[32,128]{1,0:T(8,128)}, u32[]{:S(2)}) copy-start(s32[32,128]{1,0:T(8,128)} %get-tuple-element.17.index_ref) | copy-start | bytes 49156

commit v5 on v4

--- a/solution.py
+++ b/solution.py
@@ -71,20 +71,29 @@
             i = index_s[c * (2 * chunk // LANES) + spot // LANES, spot % LANES]
             buffer[pl.ds(r, 1), :] = wide_ref[pl.ds(i, 1), :]
 
+    def layer(x, w, ahead, cuts):
+        parts = []
+        step = w.shape[1] // 2
+        for k in range(2):
+            ahead(cuts[k], cuts[k + 1])
+            parts.append(silu(dot(x, w[:, k * step : (k + 1) * step])).astype(BF))
+        return jnp.concatenate(parts, axis=1)
+
     def apply(c, buffer, ahead):
-        cuts = [chunk * k // 4 for k in range(5)]
-        ahead(cuts[0], cuts[1])
-        hidden = silu(dot(buffer[...].astype(BF), w1_ref[...])).astype(BF)
-        ahead(cuts[1], cuts[3])
-        hidden = silu(dot(hidden, w2_ref[0])).astype(BF)
-        ahead(cuts[3], cuts[4])
+        cuts = [chunk * k // 5 for k in range(6)]
+        hidden = layer(buffer[...].astype(BF), w1_ref, ahead, cuts[:3])
+        hidden = layer(hidden, w2_ref.at[0], ahead, cuts[2:5])
+        ahead(cuts[4], cuts[5])
         out = dot(hidden, w3_ref[...]).astype(BF)
         for k in range(group):
             feat_ref[c * group + k] = out[k * quota : (k + 1) * quota]
 
     chunks = rows_total // chunk
+    if half_id:
+        weights_ready()
     gather(0, xs[0], 0, chunk)
-    weights_ready()
+    if not half_id:
+        weights_ready()
 
     def step(k, carry):
         c = 2 * k
@@ -182,10 +191,12 @@
 
 
 def encode_second_kernel(
-    quota, points_ref, w1_ref, w2_ref, w3_ref, index_ref, feat_ref, wide_ref, xa_ref, xb_ref
+    quota, points_ref, w1_ref, w2_ref, w3_ref, index_any, feat_ref, index_s, wide_ref, xa_ref, xb_ref, sem
 ):
+    copy = pltpu.make_async_copy(index_any, index_s, sem)
+    copy.start()
     encode_rows(
-        1, quota, xa_ref.shape[0], points_ref, lambda: None, w1_ref, w2_ref, w3_ref, index_ref,
+        1, quota, xa_ref.shape[0], points_ref, copy.wait, w1_ref, w2_ref, w3_ref, index_s,
         feat_ref, wide_ref, (xa_ref, xb_ref),
     )
 
@@ -216,9 +227,12 @@
     return found
 
 
-def partial_kernel(half_id, along_y, rows_ref, counts_ref, inducing_ref, proj_ref, *rest):
-    own_ref, send_ref = rest[:2]
+def partial_kernel(half_id, along_y, rows_ref, counts_ref, *rest):
     num_ref = rest[-1]
+    if half_id:
+        query_ref, wv_ref, proj_ref, near_any, far_any, own_ref, send_ref = rest[:-1]
+    else:
+        inducing_ref, proj_ref, own_ref, send_ref, edge_ref, query_ref, wv_ref = rest[:-1]
     members, quota, width = rows_ref.shape
     grid_y = along_y * TLY
     half = LANES // HEADS
@@ -227,11 +241,17 @@
     ones = head_ones()
     lane = lax.broadcasted_iota(jnp.int32, (1, LANES), 1)
     left = lane < half
-    queries = unit(dot(inducing_ref[...], proj_ref[0]), ones)
-    queries = jnp.concatenate(
-        [jnp.where(left, queries, 0.0), jnp.where(left, 0.0, queries)], axis=0
-    ).astype(BF)
-    wv_t = proj_ref[2].astype(F32).T.astype(BF)
+    if half_id:
+        queries = query_ref[...]
+        wv_t = wv_ref[...]
+    else:
+        queries = unit(dot(inducing_ref[...], proj_ref[0]), ones)
+        queries = jnp.concatenate(
+            [jnp.where(left, queries, 0.0), jnp.where(left, 0.0, queries)], axis=0
+        ).astype(BF)
+        wv_t = proj_ref[2].astype(F32).T.astype(BF)
+        query_ref[...] = queries
+        wv_ref[...] = wv_t
     spot = lax.broadcasted_iota(jnp.int32, (16, chunk), 1)
     tile_row = lax.broadcasted_iota(jnp.int32, (16, chunk), 0)
     for c in range(members // group):
@@ -271,7 +291,6 @@
     own_ref[last:, :] = totals
     send_ref[last:, :] = totals.astype(BF)
     if half_id == 0:
-        edge_ref = rest[2]
         zl = lax.axis_index("zl")
         for x in range(TLX):
             rows = slice(x * LANES, (x + 1) * LANES)
@@ -281,16 +300,31 @@
         edge_ref[TLX * LANES :, :] = send_ref[last:, :]
 
 
-def queries_kernel(rows0_ref, rows1_ref, proj_ref, out_ref):
+def row_bounds(piece, counts_ref, grid_y):
+    s, base = piece
+    n0 = counts_ref[s, base]
+    n1 = n0 + counts_ref[s, base + 1]
+    return n0, n1, n1 + counts_ref[s, base + grid_y]
+
+
+def queries_kernel(along_y, rows0_ref, rows1_ref, counts_ref, proj_ref, out_ref):
     ones = head_ones()
     for half_id, rows_ref in enumerate((rows0_ref, rows1_ref)):
         members, quota, width = rows_ref.shape
         group = min(512 // quota, members)
+        row = lax.broadcasted_iota(jnp.int32, (quota, LANES), 0)
         for c in range(members // group):
             x = jnp.concatenate([rows_ref[c * group + k] for k in range(group)], axis=0)
-            query = unit(dot(x, proj_ref[0]), ones).astype(BF)
+            query = unit(dot(x, proj_ref[0]), ones)
+            pieces = pieces_of(c * group, group, half_id, along_y)
             for k in range(group):
-                out_ref[half_id, c * group + k] = query[k * quota : (k + 1) * quota]
+                bounds = row_bounds(pieces[k], counts_ref, along_y * TLY)
+                past = [row >= b for b in bounds]
+                mine = query[k * quota : (k + 1) * quota]
+                masks = (~past[0], past[0] & ~past[1], past[1] & ~past[2], past[2])
+                out_ref[half_id, c * group + k] = jnp.concatenate(
+                    [jnp.where(m, mine, 0.0).astype(BF) for m in masks], axis=1
+                )
 
 
 def combine_kernel(
@@ -305,6 +339,8 @@
     query_any,
     out0_ref,
     out1_ref,
+    near_pair_ref,
+    far_pair_ref,
 ):
     half = LANES // HEADS
     last = 4 * LANES
@@ -335,13 +371,17 @@
             for k in (2 * x, 2 * x + 4)
         ]
         outs[x][2 * TLY] = summarize(value, *lines)
+    even = lax.axis_index("tx") % 2 == 0
+    for j in range(out0_ref.shape[0]):
+        near_pair_ref[j] = jnp.where(even, out1_ref[j], out0_ref[j])
+        far_pair_ref[j] = jnp.where(even, out0_ref[j], out1_ref[j])
 
 
 def mixture_kernel(
     own0_ref,
     own1_ref,
-    below_ref,
-    above_ref,
+    near_pair_ref,
+    far_pair_ref,
     proj_ref,
     mixing_ref,
     key_ref,
@@ -384,7 +424,15 @@
     ones = head_ones()
     lane = lax.broadcasted_iota(jnp.int32, (1, LANES), 1)
     left = lane < half
-    grid = (below_ref, own0_ref, own1_ref, above_ref)
+    even = lax.axis_index("tx") % 2 == 0
+
+    def held(i, j):
+        if i in (1, 2):
+            return (own0_ref, own1_ref)[i - 1][j]
+        near, far = near_pair_ref[j], far_pair_ref[j]
+        return jnp.where(even, far, near) if i == 0 else jnp.where(even, near, far)
+
+    grid = [[held(i, j) for j in range(tall + 1)] for i in range(4)]
 
     def tile(i, j):
         if 0 <= j < tall:
@@ -424,45 +472,39 @@
                 [jnp.where(mine, keys[s], 0.0) for s in spans], axis=1
             ).astype(BF)
             flags = jnp.broadcast_to(jnp.where(mine, 1.0, 0.0), (LANES, LANES))
-            for t, s in enumerate(spans):
-                rows = slice((t * HEADS + h) * LANES, (t * HEADS + h + 1) * LANES)
-                value_ref[b, rows, :] = jnp.concatenate(
-                    [jnp.where(mine, values[s], 0.0), flags], axis=1
-                ).astype(BF)
+            value_ref[b, h * LANES : (h + 1) * LANES, :] = jnp.concatenate(
+                [jnp.where(mine, values[s], 0.0) for s in spans] + [flags], axis=1
+            ).astype(BF)
 
 
 def attend_kernel(
     along_y, rows0_ref, rows1_ref, query_ref, counts_ref, key_ref, value_ref, proj_ref, out_ref
 ):
     members, quota, width = rows0_ref.shape
-    grid_y = along_y * TLY
     group = min(512 // quota, members)
-    chunk = group * quota
-    spot = lax.broadcasted_iota(jnp.int32, (chunk, LANES), 0)
+    row = lax.broadcasted_iota(jnp.int32, (quota, LANES), 0)
     for half_id, rows_ref in enumerate((rows0_ref, rows1_ref)):
         block = block_of(half_id, lax.axis_index("zl"))
         for c in range(members // group):
-            x = jnp.concatenate([rows_ref[c * group + k] for k in range(group)], axis=0)
-            query = jnp.concatenate(
+            expanded = jnp.concatenate(
                 [query_ref[half_id, c * group + k] for k in range(group)], axis=0
             )
-            pieces = pieces_of(c * group, group, half_id, along_y)
-            which = tile_of(spot % quota, counts_ref, pieces, spot // quota, grid_y)
-            masks = [jnp.where(which == t, 1.0, 0.0).astype(BF) for t in range(4)]
-            expanded = jnp.concatenate([query * m for m in masks], axis=1)
             scores = dot_t(expanded, key_ref[block])
             weights = jnp.exp2(scores * (sharpness * math.log2(math.e))).astype(BF)
-            spread = jnp.concatenate(
-                [
-                    weights[:, h * LANES : (h + 1) * LANES] * m
-                    for m in masks
-                    for h in range(HEADS)
-                ],
-                axis=1,
-            )
-            both = dot(spread, value_ref[block])
-            attended = (both[:, :LANES] / both[:, LANES:]).astype(BF)
-            result = (x.astype(F32) + dot(attended, proj_ref[3])).astype(BF)
+            every = dot(weights, value_ref[block])
+            pieces = pieces_of(c * group, group, half_id, along_y)
+            attended = []
+            for k in range(group):
+                bounds = row_bounds(pieces[k], counts_ref, along_y * TLY)
+                part = every[k * quota : (k + 1) * quota]
+                picked = part[:, :LANES]
+                for t, bound in enumerate(bounds):
+                    tile = part[:, (t + 1) * LANES : (t + 2) * LANES]
+                    picked = jnp.where(row >= bound, tile, picked)
+                attended.append((picked / part[:, 4 * LANES :]).astype(BF))
+            x = jnp.concatenate([rows_ref[c * group + k] for k in range(group)], axis=0)
+            added = dot(jnp.concatenate(attended, axis=0), proj_ref[3])
+            result = (x.astype(F32) + added).astype(BF)
             for k in range(group):
                 out_ref[c * group + k, half_id] = result[k * quota : (k + 1) * quota]
 
@@ -561,8 +603,8 @@
         functools.partial(encode_second_kernel, quota),
         "encode_second",
         shape(half_rows),
-        "vvvvs",
-        buffers,
+        "vvvva",
+        [SMEM((lines, LANES), jnp.int32)] + buffers + [pltpu.SemaphoreType.DMA],
         6,
         (points, *weights, index),
     )
@@ -577,23 +619,15 @@
     edge_rows = TLX * LANES + 16
     parts = (shape((part_rows, LANES), F32), shape((part_rows, LANES)))
     sums = [VMEM((part_rows, HEADS * LANES), F32)]
-    own0, send0, edge = call(
+    own0, send0, edge, first_queries, value_weight = call(
         functools.partial(partial_kernel, 0, along_y),
         "partial_first",
-        parts + (shape((edge_rows, LANES)),),
+        parts
+        + (shape((edge_rows, LANES)), shape((HEADS * LANES, width)), shape((LANES, width))),
         "vsvv",
         sums,
         3,
         (rows0, counts, inducing, first_proj),
-    )
-    own1, send1 = call(
-        functools.partial(partial_kernel, 1, along_y),
-        "partial_second",
-        parts,
-        "vsvv",
-        sums,
-        3,
-        (rows1, counts, inducing, first_proj),
     )
     pairs = [(h, l) for h in range(highs) for l in range(lows)]
 
@@ -605,44 +639,53 @@
             steps.append((h * lows + l, other_h * lows + other_l))
         return lax.ppermute(value, ("zh", "zl"), steps)
 
-    other0 = swap(send0, True, False)
     far = swap(edge, True, True)
     near = swap(edge, False, True)
+    other0 = swap(send0, True, False)
+    own1, send1 = call(
+        functools.partial(partial_kernel, 1, along_y),
+        "partial_second",
+        parts,
+        "vsvvvaa",
+        sums,
+        3,
+        (rows1, counts, first_queries, value_weight, first_proj, near, far),
+    )
     other1 = swap(send1, True, False)
 
     queries = call(
-        queries_kernel,
+        functools.partial(queries_kernel, along_y),
         "point_queries",
-        shape((2,) + half_rows),
-        "vvv",
+        shape((2, members, quota, 4 * width)),
+        "vvsv",
         [],
-        2,
-        (rows0, rows1, second_proj),
+        3,
+        (rows0, rows1, counts, second_proj),
     )
 
     line = shape((tall + 1, LANES, width))
-    summary0, summary1 = call(
+    summary0, summary1, near_line, far_line = call(
         combine_kernel,
         "combine_partials",
-        (line, line),
+        (line,) * 4,
         "v" * 8 + "a",
         [],
         1,
         (own0, own1, other0, other1, near, far, inducing, first_proj, queries),
     )
-    forward = [(i, i + 1) for i in range(along_x - 1)]
-    backward = [(i + 1, i) for i in range(along_x - 1)]
-    below = lax.ppermute(summary1, "tx", forward)
-    above = lax.ppermute(summary0, "tx", backward)
+    near_pairs = [(i, i ^ 1) for i in range(along_x)]
+    far_pairs = [(i, ((i + 1) ^ 1) - 1) for i in range(1, along_x - 1)]
+    near_line = lax.ppermute(near_line, "tx", near_pairs)
+    far_line = lax.ppermute(far_line, "tx", far_pairs)
 
     keys, values = call(
         mixture_kernel,
         "mix_tiles",
-        (shape((blocks, HEADS * LANES, 4 * LANES)), shape((blocks, 4 * HEADS * LANES, 2 * LANES))),
+        (shape((blocks, HEADS * LANES, 4 * LANES)), shape((blocks, HEADS * LANES, 5 * LANES))),
         "v" * 6,
         [VMEM((6 * LANES, 2 * LANES), BF), VMEM((2, 4 * LANES, 2 * LANES), BF)],
         4,
-        (summary0, summary1, below, above, second_proj, mixing),
+        (summary0, summary1, near_line, far_line, second_proj, mixing),
     )
 
     result = call(

time: 95.3 us -> 90.2 us (0.946)
  starting transfers between devices: 21 us -> 16 us
  waiting for transfers between devices: 14.4 us -> 12.7 us
  blocking collectives: 23 us -> 24.7 us
    all_to_all x2, waiting for transfers between devices: 8.09 us -> 3.33 us  [exchange(): lax.all_to_all(rows, ('tx', 'zl'), split_axis=0, concat_axis=0, tiled=True)]
    ppermute x2, starting transfers between devices: 4.51 us -> 0.96 us  [the longest x1 0.89 us: body(): far_line = lax.ppermute(far_line, 'tx', far_pairs)]
    ppermute x4, waiting for transfers between devices: 5.47 us -> 8.91 us  [swap(): return lax.ppermute(value, ('zh', 'zl'), steps)]
    all_to_all x1, blocking collectives: 23 us -> 24.7 us  [exchange(): lax.all_to_all(rows, ('tx', 'zl'), split_axis=0, concat_axis=0, tiled=True)]
    ppermute x4, starting transfers between devices: 6.24 us -> 4.94 us  [swap(): return lax.ppermute(value, ('zh', 'zl'), steps)]
  transfers between devices with their start and end apart: 8 -> 8, of which waited for: 5 -> 6; matrix products, arithmetic and copies ran while one was open for 0% -> 0% of each run, Pallas kernels for 14% -> 17%
where the time goes in v5:
time: 90.2 us; the launch traced here: 89.8 us
  Pallas kernels  35.5 us (39%)
  blocking collectives  24.7 us (27%)
  starting transfers between devices  16 us (18%)
  waiting for transfers between devices  12.7 us (14%)
    pallas_call x9, Pallas kernels, call(): pl.pallas_call(kernel, out_shape=out_shape, in_specs=[pl.BlockSpec(memory...  35.5 us
    all_to_all x1, blocking collectives, exchange(): lax.all_to_all(rows, ('tx', 'zl'), split_axis=0, concat_axis=0, tiled=True)  24.7 us
    all_to_all x2, starting transfers between devices, exchange(): lax.all_to_all(rows, ('tx', 'zl'), split_axis=0, concat_axis=0, tiled=True)  10.1 us
    ppermute x4, waiting for transfers between devices, swap(): return lax.ppermute(value, ('zh', 'zl'), steps)  8.91 us
    ppermute x4, starting transfers between devices, swap(): return lax.ppermute(value, ('zh', 'zl'), steps)  4.94 us
    all_to_all x2, waiting for transfers between devices, exchange(): lax.all_to_all(rows, ('tx', 'zl'), split_axis=0, concat_axis=0, tiled=True)  3.33 us
  transfers between devices with their start and end apart: 8, of which 6 were waited for; matrix products, arithmetic and copies ran while one was open for 0% of the time, Pallas kernels for 17%

profile of v5, /device:TPU:0, one launch (start us, length us, event | category | flops | bytes accessed | tf_op | source)
XLA Modules:
  0.0 89.8 jit_solution(6005766673653214092)
XLA Ops:
  0.0 0.0 copy-start.2
  0.0 0.0 copy-start.3
  0.0 0.0 copy-start.5
  0.0 0.0 copy-start.6
  0.0 7.5 %encode_first.1 = (bf16[16,128,128]{2,1,0:T(8,128)(2,1)}, s32[32,128]{1,0:T(8,128)}) custom-call(bf16[4096,128]{1,0:T(8,128)(2,1)} %points_ref.1, bf16[128,512]{1,0:T(8,128)(2,1)} %w1_ref.1, bf16[1,512,512]{2,1,0:T(8,128)(2,1)} %w2_ref.1, bf16[512,128]{1,0:T(8,128)(2,1)} %w3_ref.1, s32[32,128]{1,0:T(8,128)} %counts_ref.7, s32[32,128]{1,0:T(8,128)} %bitcast.1), custom_call_target="tpu_custom_call" | custom-call | flops 4000000000 | bytes 8000000 | tf_op jit(solution)/shard_map/encode_first/pallas_call | solution.py:535
  7.5 6.3 %all-to-all-start = ((bf16[16,128,128]{2,1,0:T(8,128)(2,1)}), bf16[16,128,128]{2,1,0:T(8,128)(2,1)S(1)}, u32[]{:S(2)}, u32[]{:S(2)}) async-start(bf16[16,128,128]{2,1,0:T(8,128)(2,1)} %get-tuple-element.20), calls=%async_computation | async-start | bytes 1048576 | tf_op jit(solution)/shard_map/all_to_all | solution.py:613
  13.8 0.0 copy-done.2
  13.8 0.0 copy-done.3
  13.9 0.0 copy-done.5
  13.9 0.0 copy-done.6
  13.9 0.0 copy-start.9
  13.9 0.7 copy-done.9
  14.6 0.0 copy-start
  14.6 0.0 copy-start.1
  14.6 0.0 copy-start.8
  14.6 5.6 %encode_second.1 = bf16[16,128,128]{2,1,0:T(8,128)(2,1)} custom-call(bf16[4096,128]{1,0:T(8,128)(2,1)S(1)} %copy-done.2, bf16[128,512]{1,0:T(8,128)(2,1)S(1)} %copy-done.5, bf16[1,512,512]{2,1,0:T(8,128)(2,1)S(1)} %copy-done.3, bf16[512,128]{1,0:T(8,128)(2,1)S(1)} %copy-done.6, s32[32,128]{1,0:T(8,128)S(1)} %copy-done.9), custom_call_target="tpu_custom_call" | custom-call | flops 3000000000 | bytes 6000000 | tf_op jit(solution)/shard_map/encode_second/pallas_call | solution.py:535
  20.2 2.4 %all-to-all-done.rows0_ref.rows_ref = bf16[16,128,128]{2,1,0:T(8,128)(2,1)S(1)} async-done(((bf16[16,128,128]{2,1,0:T(8,128)(2,1)}), bf16[16,128,128]{2,1,0:T(8,128)(2,1)S(1)}, u32[]{:S(2)}, u32[]{:S(2)}) %all-to-all-start) | async-done | bytes 524320 | tf_op jit(solution)/shard_map/all_to_all | solution.py:613
  22.6 3.8 %all-to-all-start.1 = ((bf16[16,128,128]{2,1,0:T(8,128)(2,1)}), bf16[16,128,128]{2,1,0:T(8,128)(2,1)S(1)}, u32[]{:S(2)}, u32[]{:S(2)}) async-start(bf16[16,128,128]{2,1,0:T(8,128)(2,1)} %encode_second.1), calls=%async_computation.1 | async-start | bytes 1048576 | tf_op jit(solution)/shard_map/all_to_all | solution.py:613
  26.4 0.0 copy-done
  26.4 0.0 copy-done.1
  26.4 0.0 copy-done.8
  26.4 0.0 copy-start.7
  26.4 3.1 %partial_first.1 = (f32[528,128]{1,0:T(8,128)S(1)}, bf16[528,128]{1,0:T(8,128)(2,1)S(1)}, bf16[272,128]{1,0:T(8,128)(2,1)S(1)}, bf16[256,128]{1,0:T(8,128)(2,1)S(1)}, bf16[128,128]{1,0:T(8,128)(2,1)S(1)}) custom-call(bf16[16,128,128]{2,1,0:T(8,128)(2,1)S(1)} %all-to-all-done.rows0_ref.rows_ref, s32[32,128]{1,0:T(8,128)S(1)} %copy-done.8, ...), custom_call_target="tpu_custom_call" | custom-call | flops 1500000000 | bytes 3000000 | tf_op jit(solution)/shard_map/partial_first/pallas_call | solution.py:535
  29.5 4.0 %collective-permute-start.1 = (bf16[272,128]{1,0:T(8,128)(2,1)S(1)}, bf16[272,128]{1,0:T(8,128)(2,1)S(1)}, u32[]{:S(2)}, u32[]{:S(2)}) collective-permute-start(bf16[272,128]{1,0:T(8,128)(2,1)S(1)} %get-tuple-element.25), channel_id=1, source_target_pairs={{0,3},{1,2},{2,1},{3,0},{4,7},{5,6},{6,5},{7,4},{8,11},{9,10},{10,... | collective-permute-start | bytes 208904 | tf_op jit(solution)/shard_map/ppermute | solution.py:640
  33.5 0.0 collective-permute-start
  33.5 0.6 collective-permute-start.2
  34.2 0.9 %all-to-all-done.1.rows1_ref.rows_ref = bf16[16,128,128]{2,1,0:T(8,128)(2,1)S(1)} async-done(((bf16[16,128,128]{2,1,0:T(8,128)(2,1)}), bf16[16,128,128]{2,1,0:T(8,128)(2,1)S(1)}, u32[]{:S(2)}, u32[]{:S(2)}) %all-to-all-start.1) | async-done | bytes 524320 | tf_op jit(solution)/shard_map/all_to_all | solution.py:613
  35.1 4.1 %collective-permute-done.1.rest_4_.far_ref = bf16[272,128]{1,0:T(8,128)(2,1)S(1)} collective-permute-done((bf16[272,128]{1,0:T(8,128)(2,1)S(1)}, bf16[272,128]{1,0:T(8,128)(2,1)S(1)}, u32[]{:S(2)}, u32[]{:S(2)}) %collective-permute-start.1) | collective-permute-done | bytes 69664 | tf_op jit(solution)/shard_map/ppermute | solution.py:640
  39.2 1.8 %collective-permute-done.rest_3_.near_ref = bf16[272,128]{1,0:T(8,128)(2,1)S(1)} collective-permute-done((bf16[272,128]{1,0:T(8,128)(2,1)S(1)}, bf16[272,128]{1,0:T(8,128)(2,1)S(1)}, u32[]{:S(2)}, u32[]{:S(2)}) %collective-permute-start) | collective-permute-done | bytes 69664 | tf_op jit(solution)/shard_map/ppermute | solution.py:640
  40.9 3.1 %partial_second.1 = (f32[528,128]{1,0:T(8,128)S(1)}, bf16[528,128]{1,0:T(8,128)(2,1)S(1)}) custom-call(bf16[16,128,128]{2,1,0:T(8,128)(2,1)S(1)} %all-to-all-done.1.rows1_ref.rows_ref, s32[32,128]{1,0:T(8,128)S(1)} %copy-done.8, bf16[256,128]{1,0:T(8,128)(2,1)S(1)} %get-tuple-element.23.rest_0_, bf16[128,128]{1,0:T(8,128)(2,1)S(1)} %get-tuple-element.24.rest_1_, ...), custom_call_target="tpu_custom_call" | custom-call | flops 1500000000 | bytes 3000000 | tf_op jit(solution)/shard_map/partial_second/pallas_call | solution.py:535
  44.0 0.0 copy-start.4
  44.0 0.3 collective-permute-start.3
  44.3 0.0 copy-done.7
  44.3 3.3 %point_queries.1.query_any.query_ref = bf16[2,16,128,512]{3,2,1,0:T(8,128)(2,1)S(1)} custom-call(bf16[16,128,128]{2,1,0:T(8,128)(2,1)S(1)} %all-to-all-done.rows0_ref.rows_ref, bf16[16,128,128]{2,1,0:T(8,128)(2,1)S(1)} %all-to-all-done.1.rows1_ref.rows_ref, s32[32,128]{1,0:T(8,128)S(1)} %copy-done.8, bf16[4,128,128]{2,1,0:T(8,128)(2,1)S(1)} %copy-done.7), custom_call_target="tpu_custom_call" | custom-call | flops 1500000000 | bytes 3000000 | tf_op jit(solution)/shard_map/point_queries/pallas_call | solution.py:535
  47.6 0.0 collective-permute-done.2.other0_ref
  47.6 3.1 %collective-permute-done.3.other1_ref = bf16[528,128]{1,0:T(8,128)(2,1)S(1)} collective-permute-done((bf16[528,128]{1,0:T(8,128)(2,1)S(1)}, bf16[528,128]{1,0:T(8,128)(2,1)S(1)}, u32[]{:S(2)}, u32[]{:S(2)}) %collective-permute-start.3) | collective-permute-done | bytes 135200 | tf_op jit(solution)/shard_map/ppermute | solution.py:640
  50.7 0.4 combine_partials.1
  51.1 0.1 collective-permute-start.4
  51.2 0.9 collective-permute-start.5
  52.1 0.5 collective-permute-done.4.near_pair_ref
  52.5 0.0 collective-permute-done.5.far_pair_ref
  52.5 0.0 copy-done.4
  52.6 1.0 %mix_tiles.1 = (bf16[2,256,512]{2,1,0:T(8,128)(2,1)S(1)}, bf16[2,256,640]{2,1,0:T(8,128)(2,1)S(1)}) custom-call(bf16[5,128,128]{2,1,0:T(8,128)(2,1)S(1)} %get-tuple-element.29.own0_ref, bf16[5,128,128]{2,1,0:T(8,128)(2,1)S(1)} %get-tuple-element.30.own1_ref, bf16[5,128,128]{2,1,0:T(8,128)(2,1)S(1)} %collective-permute-done.4.near_pair_ref, ...), custom_call_target="tpu_custom_call" | custom-call | flops 2000000000 | bytes 4000000 | tf_op jit(solution)/shard_map/mix_tiles/pallas_call | solution.py:535
  53.5 0.0 copy-start.10
  53.5 6.5 %attend_points.1 = bf16[16,2,128,128]{3,2,1,0:T(8,128)(2,1)S(1)} custom-call(bf16[16,128,128]{2,1,0:T(8,128)(2,1)S(1)} %all-to-all-done.rows0_ref.rows_ref, bf16[16,128,128]{2,1,0:T(8,128)(2,1)S(1)} %all-to-all-done.1.rows1_ref.rows_ref, bf16[2,16,128,512]{3,2,1,0:T(8,128)(2,1)S(1)} %point_queries.1.query_any.query_ref, s32[32,128]{1,0:T(8,128)S(1)} %copy-done.8, ...), custom_call_target="tpu_custom_call" | custom-call | flops 3500000000 | bytes 7000000 | tf_op jit(solution)/shard_map/attend_points/pallas_call | solution.py:535
  60.0 24.7 %all_to_all.15.rows_ref = bf16[16,2,128,128]{3,2,1,0:T(8,128)(2,1)S(1)} all-to-all(bf16[16,2,128,128]{3,2,1,0:T(8,128)(2,1)S(1)} %attend_points.1), channel_id=1, replica_groups=mesh['tx'=8,'zh'=2,'zl'=2] {'tx','zl'}, dimensions={0} | all-to-all | bytes 2097152 | tf_op jit(solution)/shard_map/all_to_all | solution.py:613
  84.7 0.0 copy-done.10
  84.7 5.2 %scatter_rows.1 = bf16[4096,128]{1,0:T(8,128)(2,1)} custom-call(bf16[16,2,128,128]{3,2,1,0:T(8,128)(2,1)S(1)} %all_to_all.15.rows_ref, s32[32,128]{1,0:T(8,128)S(1)} %copy-done.10), custom_call_target="tpu_custom_call" | custom-call | flops 2500000000 | bytes 5000000 | tf_op jit(solution)/shard_map/scatter_rows/pallas_call | solution.py:535
Async XLA Ops:
  0.0 13.8 %copy-start.2 = (bf16[4096,128]{1,0:T(8,128)(2,1)S(1)}, bf16[4096,128]{1,0:T(8,128)(2,1)}, u32[]{:S(2)}) copy-start(bf16[4096,128]{1,0:T(8,128)(2,1)} %points_ref.1) | copy-start | bytes 3145732
  0.0 13.8 %copy-start.3 = (bf16[1,512,512]{2,1,0:T(8,128)(2,1)S(1)}, bf16[1,512,512]{2,1,0:T(8,128)(2,1)}, u32[]{:S(2)}) copy-start(bf16[1,512,512]{2,1,0:T(8,128)(2,1)} %w2_ref.1) | copy-start | bytes 1572868
  0.0 13.8 %copy-start.5 = (bf16[128,512]{1,0:T(8,128)(2,1)S(1)}, bf16[128,512]{1,0:T(8,128)(2,1)}, u32[]{:S(2)}) copy-start(bf16[128,512]{1,0:T(8,128)(2,1)} %w1_ref.1) | copy-start | bytes 393220
  0.0 13.9 %copy-start.6 = (bf16[512,128]{1,0:T(8,128)(2,1)S(1)}, bf16[512,128]{1,0:T(8,128)(2,1)}, u32[]{:S(2)}) copy-start(bf16[512,128]{1,0:T(8,128)(2,1)} %w3_ref.1) | copy-start | bytes 393220
  7.5 15.0 %all-to-all-start = ((bf16[16,128,128]{2,1,0:T(8,128)(2,1)}), bf16[16,128,128]{2,1,0:T(8,128)(2,1)S(1)}, u32[]{:S(2)}, u32[]{:S(2)}) async-start(bf16[16,128,128]{2,1,0:T(8,128)(2,1)} %get-tuple-element.20), calls=%async_computation | async-start | bytes 1048576 | tf_op jit(solution)/shard_map/all_to_all | solution.py:613
  13.9 0.7 copy-start.9
  14.6 11.8 %copy-start = (bf16[4,128,128]{2,1,0:T(8,128)(2,1)S(1)}, bf16[4,128,128]{2,1,0:T(8,128)(2,1)}, u32[]{:S(2)}) copy-start(bf16[4,128,128]{2,1,0:T(8,128)(2,1)} %proj_ref.5) | copy-start | bytes 393220
  14.6 11.8 %copy-start.1 = (bf16[128,128]{1,0:T(8,128)(2,1)S(1)}, bf16[128,128]{1,0:T(8,128)(2,1)}, u32[]{:S(2)}) copy-start(bf16[128,128]{1,0:T(8,128)(2,1)} %inducing_ref.1) | copy-start | bytes 98308
  14.6 11.8 %copy-start.8 = (s32[32,128]{1,0:T(8,128)S(1)}, s32[32,128]{1,0:T(8,128)}, u32[]{:S(2)}) copy-start(s32[32,128]{1,0:T(8,128)} %counts_ref.7) | copy-start | bytes 49156
  22.6 12.5 %all-to-all-start.1 = ((bf16[16,128,128]{2,1,0:T(8,128)(2,1)}), bf16[16,128,128]{2,1,0:T(8,128)(2,1)S(1)}, u32[]{:S(2)}, u32[]{:S(2)}) async-start(bf16[16,128,128]{2,1,0:T(8,128)(2,1)} %encode_second.1), calls=%async_computation.1 | async-start | bytes 1048576 | tf_op jit(solution)/shard_map/all_to_all | solution.py:613
  26.4 17.9 %copy-start.7 = (bf16[4,128,128]{2,1,0:T(8,128)(2,1)S(1)}, bf16[4,128,128]{2,1,0:T(8,128)(2,1)}, u32[]{:S(2)}) copy-start(bf16[4,128,128]{2,1,0:T(8,128)(2,1)} %proj_ref.7) | copy-start | bytes 393220
  29.5 9.6 %collective-permute-start.1 = (bf16[272,128]{1,0:T(8,128)(2,1)S(1)}, bf16[272,128]{1,0:T(8,128)(2,1)S(1)}, u32[]{:S(2)}, u32[]{:S(2)}) collective-permute-start(bf16[272,128]{1,0:T(8,128)(2,1)S(1)} %get-tuple-element.25), channel_id=1, source_target_pairs={{0,3},{1,2},{2,1},{3,0},{4,7},{5,6},{6,5},{7,4},{8,11},{9,10},{10,... | collective-permute-start | bytes 208904 | tf_op jit(solution)/shard_map/ppermute | solution.py:640
  33.5 7.4 %collective-permute-start = (bf16[272,128]{1,0:T(8,128)(2,1)S(1)}, bf16[272,128]{1,0:T(8,128)(2,1)S(1)}, u32[]{:S(2)}, u32[]{:S(2)}) collective-permute-start(bf16[272,128]{1,0:T(8,128)(2,1)S(1)} %get-tuple-element.25), channel_id=1, source_target_pairs={{0,1},{1,0},{2,3},{3,2},{4,5},{5,4},{6,7},{7,6},{8,9},{9,8},{10,11... | collective-permute-start | bytes 208904 | tf_op jit(solution)/shard_map/ppermute | solution.py:640
  33.5 14.1 %collective-permute-start.2 = (bf16[528,128]{1,0:T(8,128)(2,1)S(1)}, bf16[528,128]{1,0:T(8,128)(2,1)S(1)}, u32[]{:S(2)}, u32[]{:S(2)}) collective-permute-start(bf16[528,128]{1,0:T(8,128)(2,1)S(1)} %get-tuple-element.27), channel_id=1, source_target_pairs={{0,2},{1,3},{2,0},{3,1},{4,6},{5,7},{6,4},{7,5},{8,10},{9,11},{10,... | collective-permute-start | bytes 405512 | tf_op jit(solution)/shard_map/ppermute | solution.py:640
  44.0 8.6 %copy-start.4 = (bf16[8,128,128]{2,1,0:T(8,128)(2,1)S(1)}, bf16[8,128,128]{2,1,0:T(8,128)(2,1)}, u32[]{:S(2)}) copy-start(bf16[8,128,128]{2,1,0:T(8,128)(2,1)} %mixing_ref.1) | copy-start | bytes 786436
  44.0 6.7 %collective-permute-start.3 = (bf16[528,128]{1,0:T(8,128)(2,1)S(1)}, bf16[528,128]{1,0:T(8,128)(2,1)S(1)}, u32[]{:S(2)}, u32[]{:S(2)}) collective-permute-start(bf16[528,128]{1,0:T(8,128)(2,1)S(1)} %get-tuple-element.28), channel_id=1, source_target_pairs={{0,2},{1,3},{2,0},{3,1},{4,6},{5,7},{6,4},{7,5},{8,10},{9,11},{10,... | collective-permute-start | bytes 405512 | tf_op jit(solution)/shard_map/ppermute | solution.py:640
  51.1 1.5 %collective-permute-start.4 = (bf16[5,128,128]{2,1,0:T(8,128)(2,1)S(1)}, bf16[5,128,128]{2,1,0:T(8,128)(2,1)S(1)}, u32[]{:S(2)}, u32[]{:S(2)}) collective-permute-start(bf16[5,128,128]{2,1,0:T(8,128)(2,1)S(1)} %get-tuple-element.31), channel_id=1, source_target_pairs={{0,4},{4,0},{8,12},{12,8},{16,20},{20,16},{24,28},{28,24},{1,5},{5... | collective-permute-start | bytes 491528 | tf_op jit(solution)/shard_map/ppermute | solution.py:678
  51.2 1.4 %collective-permute-start.5 = (bf16[5,128,128]{2,1,0:T(8,128)(2,1)S(1)}, bf16[5,128,128]{2,1,0:T(8,128)(2,1)S(1)}, u32[]{:S(2)}, u32[]{:S(2)}) collective-permute-start(bf16[5,128,128]{2,1,0:T(8,128)(2,1)S(1)} %get-tuple-element.32), channel_id=1, source_target_pairs={{4,8},{8,4},{12,16},{16,12},{20,24},{24,20},{5,9},{9,5},{13,17},{1... | collective-permute-start | bytes 491528 | tf_op jit(solution)/shard_map/ppermute | solution.py:679
  53.5 31.2 %copy-start.10 = (s32[32,128]{1,0:T(8,128)S(1)}, s32[32,128]{1,0:T(8,128)}, u32[]{:S(2)}) copy-start(s32[32,128]{1,0:T(8,128)} %get-tuple-element.21.index_any.index_ref) | copy-start | bytes 49156

commit v6 on v5

--- a/solution.py
+++ b/solution.py
@@ -31,24 +31,24 @@
 
 
 def head_ones():
-    row = lax.broadcasted_iota(jnp.int32, (2 * LANES, LANES), 0)
-    col = lax.broadcasted_iota(jnp.int32, (2 * LANES, LANES), 1)
+    row = lax.broadcasted_iota(jnp.int32, (LANES, LANES), 0)
+    col = lax.broadcasted_iota(jnp.int32, (LANES, LANES), 1)
     half = LANES // HEADS
-    same = ((row % LANES) // half) == (col // half)
-    return jnp.where(same, 1.0, 0.0).astype(BF)
+    return jnp.where((row // half) == (col // half), 1.0, 0.0).astype(BF)
 
 
 def unit(v, ones):
-    square = v * v
-    high = square.astype(BF)
-    low = (square - high.astype(F32)).astype(BF)
-    total = dot(jnp.concatenate([high, low], axis=1), ones)
-    return v * lax.rsqrt(total + epsilon)
+    return v * lax.rsqrt(dot((v * v).astype(BF), ones) + epsilon)
 
 
 def silu(v):
-    half = 0.5 * v
+    half = (0.5 * v).astype(BF)
     return half + half * jnp.tanh(half)
+
+
+def quotient(a, b):
+    guess = pl.reciprocal(b, approx=True)
+    return a * (guess * (2.0 - b * guess))
 
 
 def place():
@@ -59,10 +59,11 @@
     return low if half_id else 1 - low
 
 
-def encode_rows(half_id, quota, chunk, points, weights_ready, w1_ref, w2_ref, w3_ref, index_s, feat_ref, wide_ref, xs):
+def encode_rows(half_id, quota, chunk, points, index_ready, weights_ready, w1_ref, w2_ref, w3_ref, index_s, feat_ref, wide_ref, xs):
     rows_total = points.shape[0] // 2
     group = chunk // quota
     wide_ref[...] = points[...].astype(F32)
+    index_ready()
 
     def gather(c, buffer, first, last):
         for r in range(first, last):
@@ -76,7 +77,7 @@
         step = w.shape[1] // 2
         for k in range(2):
             ahead(cuts[k], cuts[k + 1])
-            parts.append(silu(dot(x, w[:, k * step : (k + 1) * step])).astype(BF))
+            parts.append(silu(dot(x, w[:, k * step : (k + 1) * step])))
         return jnp.concatenate(parts, axis=1)
 
     def apply(c, buffer, ahead):
@@ -89,11 +90,8 @@
             feat_ref[c * group + k] = out[k * quota : (k + 1) * quota]
 
     chunks = rows_total // chunk
-    if half_id:
-        weights_ready()
     gather(0, xs[0], 0, chunk)
-    if not half_id:
-        weights_ready()
+    weights_ready()
 
     def step(k, carry):
         c = 2 * k
@@ -178,14 +176,13 @@
     copy = pltpu.make_async_copy(index_ref, index_s, sems.at[6])
     copy.start()
     copies[2].wait()
-    copy.wait()
 
     def weights_ready():
         for k in (3, 4, 5):
             copies[k].wait()
 
     encode_rows(
-        0, quota, xa_ref.shape[0], points_ref, weights_ready, w1_ref, w2_ref, w3_ref, index_s,
+        0, quota, xa_ref.shape[0], points_ref, copy.wait, weights_ready, w1_ref, w2_ref, w3_ref, index_s,
         feat_ref, wide_ref, (xa_ref, xb_ref),
     )
 
@@ -196,7 +193,7 @@
     copy = pltpu.make_async_copy(index_any, index_s, sem)
     copy.start()
     encode_rows(
-        1, quota, xa_ref.shape[0], points_ref, copy.wait, w1_ref, w2_ref, w3_ref, index_s,
+        1, quota, xa_ref.shape[0], points_ref, copy.wait, lambda: None, w1_ref, w2_ref, w3_ref, index_s,
         feat_ref, wide_ref, (xa_ref, xb_ref),
     )
 
@@ -230,9 +227,9 @@
 def partial_kernel(half_id, along_y, rows_ref, counts_ref, *rest):
     num_ref = rest[-1]
     if half_id:
-        query_ref, wv_ref, proj_ref, near_any, far_any, own_ref, send_ref = rest[:-1]
+        query_ref, wv_ref, proj_ref, before_any, own_ref, send_ref = rest[:-1]
     else:
-        inducing_ref, proj_ref, own_ref, send_ref, edge_ref, query_ref, wv_ref = rest[:-1]
+        inducing_ref, proj_ref, own_ref, send_ref, query_ref, wv_ref = rest[:-1]
     members, quota, width = rows_ref.shape
     grid_y = along_y * TLY
     half = LANES // HEADS
@@ -290,15 +287,6 @@
     )
     own_ref[last:, :] = totals
     send_ref[last:, :] = totals.astype(BF)
-    if half_id == 0:
-        zl = lax.axis_index("zl")
-        for x in range(TLX):
-            rows = slice(x * LANES, (x + 1) * LANES)
-            high = send_ref[(2 * x + 1) * LANES : (2 * x + 2) * LANES, :]
-            low = send_ref[2 * x * LANES : (2 * x + 1) * LANES, :]
-            edge_ref[rows, :] = jnp.where(zl == 0, high, low)
-        edge_ref[TLX * LANES :, :] = send_ref[last:, :]
-
 
 def row_bounds(piece, counts_ref, grid_y):
     s, base = piece
@@ -307,7 +295,7 @@
     return n0, n1, n1 + counts_ref[s, base + grid_y]
 
 
-def queries_kernel(along_y, rows0_ref, rows1_ref, counts_ref, proj_ref, out_ref):
+def queries_kernel(along_y, rows0_ref, rows1_ref, counts_ref, proj_ref, column_any, out_ref):
     ones = head_ones()
     for half_id, rows_ref in enumerate((rows0_ref, rows1_ref)):
         members, quota, width = rows_ref.shape
@@ -327,50 +315,53 @@
                 )
 
 
-def combine_kernel(
-    own0_ref,
-    own1_ref,
-    other0_ref,
-    other1_ref,
-    near_ref,
-    far_ref,
+def summarize(half_id, own_ref, other_ref, inducing_ref, proj_ref, store):
+    half = LANES // HEADS
+    last = 4 * LANES
+    totals = own_ref[last:, :] + other_ref[last:, :].astype(F32)
+    for t in range(4):
+        rows = slice(t * LANES, (t + 1) * LANES)
+        value = own_ref[rows, :] + other_ref[rows, :].astype(F32)
+        attended = jnp.concatenate(
+            [value[:half] / totals[t : t + 1], value[half:] / totals[t + 4 : t + 5]], axis=0
+        )
+        out = inducing_ref[...].astype(F32) + dot(attended.T.astype(BF), proj_ref[3])
+        store(t // TLY, t % TLY, out.astype(BF))
+
+
+def combine_first_kernel(own_ref, other_ref, inducing_ref, proj_ref, out_ref, column_ref):
+    def store(x, y, value):
+        out_ref[x, y] = value
+
+    summarize(0, own_ref, other_ref, inducing_ref, proj_ref, store)
+    for x in range(TLX):
+        column_ref[x] = jnp.where(lax.axis_index("zl") == 0, out_ref[x, TLY - 1], out_ref[x, 0])
+
+
+def combine_second_kernel(
+    own_ref,
+    other_ref,
     inducing_ref,
     proj_ref,
+    first_ref,
+    column_ref,
     query_any,
     out0_ref,
     out1_ref,
     near_pair_ref,
     far_pair_ref,
 ):
-    half = LANES // HEADS
-    last = 4 * LANES
     outs = (out0_ref, out1_ref)
     zl = lax.axis_index("zl")
 
-    def summarize(value, total0, total1):
-        attended = jnp.concatenate([value[:half] / total0, value[half:] / total1], axis=0)
-        attended = attended.T.astype(BF)
-        out = inducing_ref[...].astype(F32) + dot(attended, proj_ref[3])
-        return out.astype(BF)
-
-    for half_id, (own_ref, other_ref) in enumerate(((own0_ref, other0_ref), (own1_ref, other1_ref))):
-        b = block_of(half_id, zl)
-        totals = own_ref[last:, :] + other_ref[last:, :].astype(F32)
-        for t in range(4):
-            rows = slice(t * LANES, (t + 1) * LANES)
-            value = own_ref[rows, :] + other_ref[rows, :].astype(F32)
-            outs[t // 2][b * TLY + t % 2] = summarize(
-                value, totals[t : t + 1], totals[t + 4 : t + 5]
-            )
-    totals = near_ref[TLX * LANES :, :].astype(F32) + far_ref[TLX * LANES :, :].astype(F32)
+    def store(x, y, value):
+        outs[x][block_of(1, zl) * TLY + y] = value
+
     for x in range(TLX):
-        rows = slice(x * LANES, (x + 1) * LANES)
-        value = near_ref[rows, :].astype(F32) + far_ref[rows, :].astype(F32)
-        lines = [
-            jnp.where(zl == 1, totals[k + 1 : k + 2], totals[k : k + 1])
-            for k in (2 * x, 2 * x + 4)
-        ]
-        outs[x][2 * TLY] = summarize(value, *lines)
+        for y in range(TLY):
+            outs[x][block_of(0, zl) * TLY + y] = first_ref[x, y]
+        outs[x][2 * TLY] = column_ref[x]
+    summarize(1, own_ref, other_ref, inducing_ref, proj_ref, store)
     even = lax.axis_index("tx") % 2 == 0
     for j in range(out0_ref.shape[0]):
         near_pair_ref[j] = jnp.where(even, out1_ref[j], out0_ref[j])
@@ -501,7 +492,7 @@
                 for t, bound in enumerate(bounds):
                     tile = part[:, (t + 1) * LANES : (t + 2) * LANES]
                     picked = jnp.where(row >= bound, tile, picked)
-                attended.append((picked / part[:, 4 * LANES :]).astype(BF))
+                attended.append(quotient(picked, part[:, 4 * LANES :]).astype(BF))
             x = jnp.concatenate([rows_ref[c * group + k] for k in range(group)], axis=0)
             added = dot(jnp.concatenate(attended, axis=0), proj_ref[3])
             result = (x.astype(F32) + added).astype(BF)
@@ -616,14 +607,13 @@
     rows1 = exchange(second)
 
     part_rows = 4 * LANES + 16
-    edge_rows = TLX * LANES + 16
     parts = (shape((part_rows, LANES), F32), shape((part_rows, LANES)))
     sums = [VMEM((part_rows, HEADS * LANES), F32)]
-    own0, send0, edge, first_queries, value_weight = call(
+    own0, send0, first_queries, value_weight = call(
         functools.partial(partial_kernel, 0, along_y),
         "partial_first",
         parts
-        + (shape((edge_rows, LANES)), shape((HEADS * LANES, width)), shape((LANES, width))),
+        + (shape((HEADS * LANES, width)), shape((LANES, width))),
         "vsvv",
         sums,
         3,
@@ -639,39 +629,45 @@
             steps.append((h * lows + l, other_h * lows + other_l))
         return lax.ppermute(value, ("zh", "zl"), steps)
 
-    far = swap(edge, True, True)
-    near = swap(edge, False, True)
     other0 = swap(send0, True, False)
+    first_half, border = call(
+        combine_first_kernel,
+        "combine_first",
+        (shape((TLX, TLY, LANES, width)), shape((TLX, LANES, width))),
+        "vvvv",
+        [],
+        0.3,
+        (own0, other0, inducing, first_proj),
+    )
+    column = swap(border, False, True)
     own1, send1 = call(
         functools.partial(partial_kernel, 1, along_y),
         "partial_second",
         parts,
-        "vsvvvaa",
+        "vsvvva",
         sums,
         3,
-        (rows1, counts, first_queries, value_weight, first_proj, near, far),
+        (rows1, counts, first_queries, value_weight, first_proj, border),
     )
     other1 = swap(send1, True, False)
-
     queries = call(
         functools.partial(queries_kernel, along_y),
         "point_queries",
         shape((2, members, quota, 4 * width)),
-        "vvsv",
+        "vvsva",
         [],
         3,
-        (rows0, rows1, counts, second_proj),
-    )
-
+        (rows0, rows1, counts, second_proj, column),
+    )
     line = shape((tall + 1, LANES, width))
     summary0, summary1, near_line, far_line = call(
-        combine_kernel,
-        "combine_partials",
+        combine_second_kernel,
+        "combine_second",
         (line,) * 4,
-        "v" * 8 + "a",
+        "vvvvvva",
         [],
-        1,
-        (own0, own1, other0, other1, near, far, inducing, first_proj, queries),
+        0.3,
+        (own1, other1, inducing, first_proj, first_half, column, queries),
     )
     near_pairs = [(i, i ^ 1) for i in range(along_x)]
     far_pairs = [(i, ((i + 1) ^ 1) - 1) for i in range(1, along_x - 1)]

time: 90.2 us -> 92.1 us (1.021)
  starting transfers between devices: 16 us -> 20.7 us
  waiting for transfers between devices: 12.7 us -> 10.8 us
  Pallas kernels: 35.5 us -> 34.5 us
    ppermute x4 -> x3, starting transfers between devices: 4.94 us -> 9.71 us  [swap(): return lax.ppermute(value, ('zh', 'zl'), steps)]
    ppermute x4 -> x3, waiting for transfers between devices: 8.91 us -> 7.57 us  [swap(): return lax.ppermute(value, ('zh', 'zl'), steps)]
    pallas_call x9 -> x10, Pallas kernels: 35.5 us -> 34.5 us  [call(): pl.pallas_call(kernel, out_shape=out_shape, in_specs=[pl.BlockSpec(memory...]
  transfers between devices with their start and end apart: 8 -> 7, of which waited for: 6 -> 4; matrix products, arithmetic and copies ran while one was open for 0% -> 0% of each run, Pallas kernels for 17% -> 16%
where the time goes in v6:
time: 92.1 us; the launch traced here: 91.6 us
  Pallas kernels  34.5 us (37%)
  blocking collectives  24.7 us (27%)
  starting transfers between devices  20.7 us (22%)
  waiting for transfers between devices  10.8 us (12%)
    pallas_call x10, Pallas kernels, call(): pl.pallas_call(kernel, out_shape=out_shape, in_specs=[pl.BlockSpec(memory...  34.5 us
    all_to_all x1, blocking collectives, exchange(): lax.all_to_all(rows, ('tx', 'zl'), split_axis=0, concat_axis=0, tiled=True)  24.7 us
    all_to_all x2, starting transfers between devices, exchange(): lax.all_to_all(rows, ('tx', 'zl'), split_axis=0, concat_axis=0, tiled=True)  10.1 us
    ppermute x3, starting transfers between devices, swap(): return lax.ppermute(value, ('zh', 'zl'), steps)  9.71 us
    ppermute x3, waiting for transfers between devices, swap(): return lax.ppermute(value, ('zh', 'zl'), steps)  7.57 us
    all_to_all x2, waiting for transfers between devices, exchange(): lax.all_to_all(rows, ('tx', 'zl'), split_axis=0, concat_axis=0, tiled=True)  2.7 us
  transfers between devices with their start and end apart: 7, of which 4 were waited for; matrix products, arithmetic and copies ran while one was open for 0% of the time, Pallas kernels for 16%

profile of v6, /device:TPU:0, one launch (start us, length us, event | category | flops | bytes accessed | tf_op | source)
XLA Modules:
  0.0 91.6 jit_solution(15418298427759271658)
XLA Ops:
  0.0 0.0 copy-start.2
  0.0 0.0 copy-start.3
  0.0 0.0 copy-start.5
  0.0 0.0 copy-start.6
  0.0 7.1 %encode_first.1 = (bf16[16,128,128]{2,1,0:T(8,128)(2,1)}, s32[32,128]{1,0:T(8,128)}) custom-call(bf16[4096,128]{1,0:T(8,128)(2,1)} %points_ref.1, bf16[128,512]{1,0:T(8,128)(2,1)} %w1_ref.1, bf16[1,512,512]{2,1,0:T(8,128)(2,1)} %w2_ref.1, bf16[512,128]{1,0:T(8,128)(2,1)} %w3_ref.1, s32[32,128]{1,0:T(8,128)} %counts_ref.7, s32[32,128]{1,0:T(8,128)} %bitcast.1), custom_call_target="tpu_custom_call" | custom-call | flops 4000000000 | bytes 8000000 | tf_op jit(solution)/shard_map/encode_first/pallas_call | solution.py:526
  7.1 6.3 %all-to-all-start = ((bf16[16,128,128]{2,1,0:T(8,128)(2,1)}), bf16[16,128,128]{2,1,0:T(8,128)(2,1)S(1)}, u32[]{:S(2)}, u32[]{:S(2)}) async-start(bf16[16,128,128]{2,1,0:T(8,128)(2,1)} %get-tuple-element.21), calls=%async_computation | async-start | bytes 1048576 | tf_op jit(solution)/shard_map/all_to_all | solution.py:604
  13.5 0.0 copy-done.2
  13.5 0.0 copy-done.3
  13.5 0.0 copy-done.5
  13.5 0.0 copy-done.6
  13.5 0.0 copy-start.9
  13.5 0.7 copy-done.9
  14.2 0.0 copy-start
  14.2 0.0 copy-start.1
  14.2 0.0 copy-start.8
  14.2 5.3 %encode_second.1 = bf16[16,128,128]{2,1,0:T(8,128)(2,1)} custom-call(bf16[4096,128]{1,0:T(8,128)(2,1)S(1)} %copy-done.2, bf16[128,512]{1,0:T(8,128)(2,1)S(1)} %copy-done.5, bf16[1,512,512]{2,1,0:T(8,128)(2,1)S(1)} %copy-done.3, bf16[512,128]{1,0:T(8,128)(2,1)S(1)} %copy-done.6, s32[32,128]{1,0:T(8,128)S(1)} %copy-done.9), custom_call_target="tpu_custom_call" | custom-call | flops 3000000000 | bytes 6000000 | tf_op jit(solution)/shard_map/encode_second/pallas_call | solution.py:526
  19.5 2.7 %all-to-all-done.rows_ref.rows0_ref = bf16[16,128,128]{2,1,0:T(8,128)(2,1)S(1)} async-done(((bf16[16,128,128]{2,1,0:T(8,128)(2,1)}), bf16[16,128,128]{2,1,0:T(8,128)(2,1)S(1)}, u32[]{:S(2)}, u32[]{:S(2)}) %all-to-all-start) | async-done | bytes 524320 | tf_op jit(solution)/shard_map/all_to_all | solution.py:604
  22.2 3.8 %all-to-all-start.1 = ((bf16[16,128,128]{2,1,0:T(8,128)(2,1)}), bf16[16,128,128]{2,1,0:T(8,128)(2,1)S(1)}, u32[]{:S(2)}, u32[]{:S(2)}) async-start(bf16[16,128,128]{2,1,0:T(8,128)(2,1)} %encode_second.1), calls=%async_computation.1 | async-start | bytes 1048576 | tf_op jit(solution)/shard_map/all_to_all | solution.py:604
  26.0 0.0 copy-done
  26.0 0.0 copy-done.1
  26.0 0.0 copy-done.8
  26.0 3.2 %partial_first.1 = (f32[528,128]{1,0:T(8,128)S(1)}, bf16[528,128]{1,0:T(8,128)(2,1)S(1)}, bf16[256,128]{1,0:T(8,128)(2,1)S(1)}, bf16[128,128]{1,0:T(8,128)(2,1)S(1)}) custom-call(bf16[16,128,128]{2,1,0:T(8,128)(2,1)S(1)} %all-to-all-done.rows_ref.rows0_ref, s32[32,128]{1,0:T(8,128)S(1)} %copy-done.8, bf16[128,128]{1,0:T(8,128)(2,1)S(1)} %copy-done.1, ...), custom_call_target="tpu_custom_call" | custom-call | flops 1500000000 | bytes 3000000 | tf_op jit(solution)/shard_map/partial_first/pallas_call | solution.py:526
  29.2 0.0 copy-start.7
  29.2 2.6 %collective-permute-start = (bf16[528,128]{1,0:T(8,128)(2,1)S(1)}, bf16[528,128]{1,0:T(8,128)(2,1)S(1)}, u32[]{:S(2)}, u32[]{:S(2)}) collective-permute-start(bf16[528,128]{1,0:T(8,128)(2,1)S(1)} %get-tuple-element.24), channel_id=1, source_target_pairs={{0,2},{1,3},{2,0},{3,1},{4,6},{5,7},{6,4},{7,5},{8,10},{9,11},{10,... | collective-permute-start | bytes 405512 | tf_op jit(solution)/shard_map/ppermute | solution.py:630
  31.8 4.3 %collective-permute-done.other_ref = bf16[528,128]{1,0:T(8,128)(2,1)S(1)} collective-permute-done((bf16[528,128]{1,0:T(8,128)(2,1)S(1)}, bf16[528,128]{1,0:T(8,128)(2,1)S(1)}, u32[]{:S(2)}, u32[]{:S(2)}) %collective-permute-start) | collective-permute-done | bytes 135200 | tf_op jit(solution)/shard_map/ppermute | solution.py:630
  36.2 0.3 combine_first.1
  36.4 4.1 %collective-permute-start.1 = (bf16[2,128,128]{2,1,0:T(8,128)(2,1)S(1)}, bf16[2,128,128]{2,1,0:T(8,128)(2,1)S(1)}, u32[]{:S(2)}, u32[]{:S(2)}) collective-permute-start(bf16[2,128,128]{2,1,0:T(8,128)(2,1)S(1)} %get-tuple-element.25.rest_3_), channel_id=1, source_target_pairs={{0,1},{1,0},{2,3},{3,2},{4,5},{5,4},{6,7},{7,6},{8,9},{9,8},{10,11... | collective-permute-start | bytes 196616 | tf_op jit(solution)/shard_map/ppermute | solution.py:630
  40.5 0.0 all-to-all-done.1.rows1_ref.rows_ref
  40.5 3.1 %partial_second.1 = (f32[528,128]{1,0:T(8,128)S(1)}, bf16[528,128]{1,0:T(8,128)(2,1)S(1)}) custom-call(bf16[16,128,128]{2,1,0:T(8,128)(2,1)S(1)} %all-to-all-done.1.rows1_ref.rows_ref, s32[32,128]{1,0:T(8,128)S(1)} %copy-done.8, bf16[256,128]{1,0:T(8,128)(2,1)S(1)} %get-tuple-element.26.rest_0_, bf16[128,128]{1,0:T(8,128)(2,1)S(1)} %get-tuple-element.27.rest_1_, ...), custom_call_target="tpu_custom_call" | custom-call | flops 1500000000 | bytes 3000000 | tf_op jit(solution)/shard_map/partial_second/pallas_call | solution.py:526
  43.7 0.0 copy-start.4
  43.7 3.0 %collective-permute-start.2 = (bf16[528,128]{1,0:T(8,128)(2,1)S(1)}, bf16[528,128]{1,0:T(8,128)(2,1)S(1)}, u32[]{:S(2)}, u32[]{:S(2)}) collective-permute-start(bf16[528,128]{1,0:T(8,128)(2,1)S(1)} %get-tuple-element.29), channel_id=1, source_target_pairs={{0,2},{1,3},{2,0},{3,1},{4,6},{5,7},{6,4},{7,5},{8,10},{9,11},{10,... | collective-permute-start | bytes 405512 | tf_op jit(solution)/shard_map/ppermute | solution.py:630
  46.7 0.0 collective-permute-done.1.column_any.column_ref
  46.7 0.0 copy-done.7
  46.7 2.7 %point_queries.1.query_any.query_ref = bf16[2,16,128,512]{3,2,1,0:T(8,128)(2,1)S(1)} custom-call(bf16[16,128,128]{2,1,0:T(8,128)(2,1)S(1)} %all-to-all-done.rows_ref.rows0_ref, bf16[16,128,128]{2,1,0:T(8,128)(2,1)S(1)} %all-to-all-done.1.rows1_ref.rows_ref, s32[32,128]{1,0:T(8,128)S(1)} %copy-done.8, bf16[4,128,128]{2,1,0:T(8,128)(2,1)S(1)} %copy-done.7, ...), custom_call_target="tpu_custom_call" | custom-call | flops 1500000000 | bytes 3000000 | tf_op jit(solution)/shard_map/point_queries/pallas_call | solution.py:526
  49.4 3.2 %collective-permute-done.2.other_ref = bf16[528,128]{1,0:T(8,128)(2,1)S(1)} collective-permute-done((bf16[528,128]{1,0:T(8,128)(2,1)S(1)}, bf16[528,128]{1,0:T(8,128)(2,1)S(1)}, u32[]{:S(2)}, u32[]{:S(2)}) %collective-permute-start.2) | collective-permute-done | bytes 135200 | tf_op jit(solution)/shard_map/ppermute | solution.py:630
  52.7 0.3 combine_second.1
  53.0 0.1 collective-permute-start.3
  53.1 0.8 collective-permute-start.4
  53.9 0.5 collective-permute-done.3.near_pair_ref
  54.4 0.0 collective-permute-done.4.far_pair_ref
  54.4 0.0 copy-done.4
  54.4 0.9 mix_tiles.1
  55.3 0.0 copy-start.10
  55.3 6.5 %attend_points.1 = bf16[16,2,128,128]{3,2,1,0:T(8,128)(2,1)S(1)} custom-call(bf16[16,128,128]{2,1,0:T(8,128)(2,1)S(1)} %all-to-all-done.rows_ref.rows0_ref, bf16[16,128,128]{2,1,0:T(8,128)(2,1)S(1)} %all-to-all-done.1.rows1_ref.rows_ref, bf16[2,16,128,512]{3,2,1,0:T(8,128)(2,1)S(1)} %point_queries.1.query_any.query_ref, s32[32,128]{1,0:T(8,128)S(1)} %copy-done.8, ...), custom_call_target="tpu_custom_call" | custom-call | flops 3500000000 | bytes 7000000 | tf_op jit(solution)/shard_map/attend_points/pallas_call | solution.py:526
  61.8 24.7 %all_to_all.15.rows_ref = bf16[16,2,128,128]{3,2,1,0:T(8,128)(2,1)S(1)} all-to-all(bf16[16,2,128,128]{3,2,1,0:T(8,128)(2,1)S(1)} %attend_points.1), channel_id=1, replica_groups=mesh['tx'=8,'zh'=2,'zl'=2] {'tx','zl'}, dimensions={0} | all-to-all | bytes 2097152 | tf_op jit(solution)/shard_map/all_to_all | solution.py:604
  86.5 0.0 copy-done.10
  86.5 5.2 %scatter_rows.1 = bf16[4096,128]{1,0:T(8,128)(2,1)} custom-call(bf16[16,2,128,128]{3,2,1,0:T(8,128)(2,1)S(1)} %all_to_all.15.rows_ref, s32[32,128]{1,0:T(8,128)S(1)} %copy-done.10), custom_call_target="tpu_custom_call" | custom-call | flops 2500000000 | bytes 5000000 | tf_op jit(solution)/shard_map/scatter_rows/pallas_call | solution.py:526
Async XLA Ops:
  0.0 13.5 %copy-start.2 = (bf16[4096,128]{1,0:T(8,128)(2,1)S(1)}, bf16[4096,128]{1,0:T(8,128)(2,1)}, u32[]{:S(2)}) copy-start(bf16[4096,128]{1,0:T(8,128)(2,1)} %points_ref.1) | copy-start | bytes 3145732
  0.0 13.5 %copy-start.3 = (bf16[1,512,512]{2,1,0:T(8,128)(2,1)S(1)}, bf16[1,512,512]{2,1,0:T(8,128)(2,1)}, u32[]{:S(2)}) copy-start(bf16[1,512,512]{2,1,0:T(8,128)(2,1)} %w2_ref.1) | copy-start | bytes 1572868
  0.0 13.5 %copy-start.5 = (bf16[128,512]{1,0:T(8,128)(2,1)S(1)}, bf16[128,512]{1,0:T(8,128)(2,1)}, u32[]{:S(2)}) copy-start(bf16[128,512]{1,0:T(8,128)(2,1)} %w1_ref.1) | copy-start | bytes 393220
  0.0 13.5 %copy-start.6 = (bf16[512,128]{1,0:T(8,128)(2,1)S(1)}, bf16[512,128]{1,0:T(8,128)(2,1)}, u32[]{:S(2)}) copy-start(bf16[512,128]{1,0:T(8,128)(2,1)} %w3_ref.1) | copy-start | bytes 393220
  7.1 15.1 %all-to-all-start = ((bf16[16,128,128]{2,1,0:T(8,128)(2,1)}), bf16[16,128,128]{2,1,0:T(8,128)(2,1)S(1)}, u32[]{:S(2)}, u32[]{:S(2)}) async-start(bf16[16,128,128]{2,1,0:T(8,128)(2,1)} %get-tuple-element.21), calls=%async_computation | async-start | bytes 1048576 | tf_op jit(solution)/shard_map/all_to_all | solution.py:604
  13.5 0.7 copy-start.9
  14.2 11.8 %copy-start = (bf16[4,128,128]{2,1,0:T(8,128)(2,1)S(1)}, bf16[4,128,128]{2,1,0:T(8,128)(2,1)}, u32[]{:S(2)}) copy-start(bf16[4,128,128]{2,1,0:T(8,128)(2,1)} %proj_ref.7) | copy-start | bytes 393220
  14.2 11.8 %copy-start.1 = (bf16[128,128]{1,0:T(8,128)(2,1)S(1)}, bf16[128,128]{1,0:T(8,128)(2,1)}, u32[]{:S(2)}) copy-start(bf16[128,128]{1,0:T(8,128)(2,1)} %inducing_ref.3) | copy-start | bytes 98308
  14.2 11.8 %copy-start.8 = (s32[32,128]{1,0:T(8,128)S(1)}, s32[32,128]{1,0:T(8,128)}, u32[]{:S(2)}) copy-start(s32[32,128]{1,0:T(8,128)} %counts_ref.7) | copy-start | bytes 49156
  22.2 18.3 %all-to-all-start.1 = ((bf16[16,128,128]{2,1,0:T(8,128)(2,1)}), bf16[16,128,128]{2,1,0:T(8,128)(2,1)S(1)}, u32[]{:S(2)}, u32[]{:S(2)}) async-start(bf16[16,128,128]{2,1,0:T(8,128)(2,1)} %encode_second.1), calls=%async_computation.1 | async-start | bytes 1048576 | tf_op jit(solution)/shard_map/all_to_all | solution.py:604
  29.2 17.5 %copy-start.7 = (bf16[4,128,128]{2,1,0:T(8,128)(2,1)S(1)}, bf16[4,128,128]{2,1,0:T(8,128)(2,1)}, u32[]{:S(2)}) copy-start(bf16[4,128,128]{2,1,0:T(8,128)(2,1)} %proj_ref.9) | copy-start | bytes 393220
  29.2 7.0 %collective-permute-start = (bf16[528,128]{1,0:T(8,128)(2,1)S(1)}, bf16[528,128]{1,0:T(8,128)(2,1)S(1)}, u32[]{:S(2)}, u32[]{:S(2)}) collective-permute-start(bf16[528,128]{1,0:T(8,128)(2,1)S(1)} %get-tuple-element.24), channel_id=1, source_target_pairs={{0,2},{1,3},{2,0},{3,1},{4,6},{5,7},{6,4},{7,5},{8,10},{9,11},{10,... | collective-permute-start | bytes 405512 | tf_op jit(solution)/shard_map/ppermute | solution.py:630
  36.4 10.2 %collective-permute-start.1 = (bf16[2,128,128]{2,1,0:T(8,128)(2,1)S(1)}, bf16[2,128,128]{2,1,0:T(8,128)(2,1)S(1)}, u32[]{:S(2)}, u32[]{:S(2)}) collective-permute-start(bf16[2,128,128]{2,1,0:T(8,128)(2,1)S(1)} %get-tuple-element.25.rest_3_), channel_id=1, source_target_pairs={{0,1},{1,0},{2,3},{3,2},{4,5},{5,4},{6,7},{7,6},{8,9},{9,8},{10,11... | collective-permute-start | bytes 196616 | tf_op jit(solution)/shard_map/ppermute | solution.py:630
  43.7 10.8 %copy-start.4 = (bf16[8,128,128]{2,1,0:T(8,128)(2,1)S(1)}, bf16[8,128,128]{2,1,0:T(8,128)(2,1)}, u32[]{:S(2)}) copy-start(bf16[8,128,128]{2,1,0:T(8,128)(2,1)} %mixing_ref.1) | copy-start | bytes 786436
  43.7 9.0 %collective-permute-start.2 = (bf16[528,128]{1,0:T(8,128)(2,1)S(1)}, bf16[528,128]{1,0:T(8,128)(2,1)S(1)}, u32[]{:S(2)}, u32[]{:S(2)}) collective-permute-start(bf16[528,128]{1,0:T(8,128)(2,1)S(1)} %get-tuple-element.29), channel_id=1, source_target_pairs={{0,2},{1,3},{2,0},{3,1},{4,6},{5,7},{6,4},{7,5},{8,10},{9,11},{10,... | collective-permute-start | bytes 405512 | tf_op jit(solution)/shard_map/ppermute | solution.py:630
  53.0 1.5 %collective-permute-start.3 = (bf16[5,128,128]{2,1,0:T(8,128)(2,1)S(1)}, bf16[5,128,128]{2,1,0:T(8,128)(2,1)S(1)}, u32[]{:S(2)}, u32[]{:S(2)}) collective-permute-start(bf16[5,128,128]{2,1,0:T(8,128)(2,1)S(1)} %get-tuple-element.33), channel_id=1, source_target_pairs={{0,4},{4,0},{8,12},{12,8},{16,20},{20,16},{24,28},{28,24},{1,5},{5... | collective-permute-start | bytes 491528 | tf_op jit(solution)/shard_map/ppermute | solution.py:674
  53.1 1.4 %collective-permute-start.4 = (bf16[5,128,128]{2,1,0:T(8,128)(2,1)S(1)}, bf16[5,128,128]{2,1,0:T(8,128)(2,1)S(1)}, u32[]{:S(2)}, u32[]{:S(2)}) collective-permute-start(bf16[5,128,128]{2,1,0:T(8,128)(2,1)S(1)} %get-tuple-element.34), channel_id=1, source_target_pairs={{4,8},{8,4},{12,16},{16,12},{20,24},{24,20},{5,9},{9,5},{13,17},{1... | collective-permute-start | bytes 491528 | tf_op jit(solution)/shard_map/ppermute | solution.py:675
  55.3 31.1 %copy-start.10 = (s32[32,128]{1,0:T(8,128)S(1)}, s32[32,128]{1,0:T(8,128)}, u32[]{:S(2)}) copy-start(s32[32,128]{1,0:T(8,128)} %get-tuple-element.22.index_any.index_ref) | copy-start | bytes 49156

commit v7 on v6

--- a/solution.py
+++ b/solution.py
@@ -12,6 +12,7 @@
 TLX = 2
 TLY = 2
 LANES = 128
+GROUP_ROWS = 2048
 BF = jnp.bfloat16
 F32 = jnp.float32
 
@@ -42,8 +43,8 @@
 
 
 def silu(v):
-    half = (0.5 * v).astype(BF)
-    return half + half * jnp.tanh(half)
+    half = 0.5 * v
+    return (half + half * jnp.tanh(half)).astype(BF)
 
 
 def quotient(a, b):
@@ -92,14 +93,13 @@
     chunks = rows_total // chunk
     gather(0, xs[0], 0, chunk)
     weights_ready()
-
-    def step(k, carry):
-        c = 2 * k
-        apply(c, xs[0], lambda a, b: gather(c + 1, xs[1], a, b))
-        apply(c + 1, xs[1], lambda a, b: gather(jnp.minimum(c + 2, chunks - 1), xs[0], a, b))
-        return carry
-
-    lax.fori_loop(0, chunks // 2, step, 0)
+    for c in range(chunks):
+
+        def ahead(a, b):
+            if c + 1 < chunks:
+                gather(c + 1, xs[(c + 1) % 2], a, b)
+
+        apply(c, xs[c % 2], ahead)
 
 
 def encode_first_kernel(
@@ -227,13 +227,13 @@
 def partial_kernel(half_id, along_y, rows_ref, counts_ref, *rest):
     num_ref = rest[-1]
     if half_id:
-        query_ref, wv_ref, proj_ref, before_any, own_ref, send_ref = rest[:-1]
+        query_ref, wv_ref, proj_ref, own_ref, send_ref = rest[:-1]
     else:
         inducing_ref, proj_ref, own_ref, send_ref, query_ref, wv_ref = rest[:-1]
     members, quota, width = rows_ref.shape
     grid_y = along_y * TLY
     half = LANES // HEADS
-    group = min(512 // quota, members)
+    group = min(GROUP_ROWS // quota, members)
     chunk = group * quota
     ones = head_ones()
     lane = lax.broadcasted_iota(jnp.int32, (1, LANES), 1)
@@ -299,7 +299,7 @@
     ones = head_ones()
     for half_id, rows_ref in enumerate((rows0_ref, rows1_ref)):
         members, quota, width = rows_ref.shape
-        group = min(512 // quota, members)
+        group = min(GROUP_ROWS // quota, members)
         row = lax.broadcasted_iota(jnp.int32, (quota, LANES), 0)
         for c in range(members // group):
             x = jnp.concatenate([rows_ref[c * group + k] for k in range(group)], axis=0)
@@ -329,7 +329,9 @@
         store(t // TLY, t % TLY, out.astype(BF))
 
 
-def combine_first_kernel(own_ref, other_ref, inducing_ref, proj_ref, out_ref, column_ref):
+def combine_first_kernel(
+    own_ref, other_ref, inducing_ref, proj_ref, after_any, out_ref, column_ref
+):
     def store(x, y, value):
         out_ref[x, y] = value
 
@@ -338,45 +340,41 @@
         column_ref[x] = jnp.where(lax.axis_index("zl") == 0, out_ref[x, TLY - 1], out_ref[x, 0])
 
 
+def pair_lines(rows, near_ref, far_ref):
+    even = lax.axis_index("tx") % 2 == 0
+    for y, (low, high) in enumerate(zip(*rows)):
+        near_ref[y] = jnp.where(even, high, low)
+        far_ref[y] = jnp.where(even, low, high)
+
+
+def early_lines_kernel(first_ref, column_ref, query_any, near_ref, far_ref):
+    rows = [[first_ref[x, y] for y in range(TLY)] + [column_ref[x]] for x in range(TLX)]
+    pair_lines(rows, near_ref, far_ref)
+
+
 def combine_second_kernel(
-    own_ref,
-    other_ref,
-    inducing_ref,
-    proj_ref,
+    own_ref, other_ref, inducing_ref, proj_ref, query_any, out_ref, near_ref, far_ref
+):
+    def store(x, y, value):
+        out_ref[x, y] = value
+
+    summarize(1, own_ref, other_ref, inducing_ref, proj_ref, store)
+    pair_lines([[out_ref[x, y] for y in range(TLY)] for x in range(TLX)], near_ref, far_ref)
+
+
+def mixture_kernel(
     first_ref,
     column_ref,
-    query_any,
-    out0_ref,
-    out1_ref,
-    near_pair_ref,
-    far_pair_ref,
-):
-    outs = (out0_ref, out1_ref)
-    zl = lax.axis_index("zl")
-
-    def store(x, y, value):
-        outs[x][block_of(1, zl) * TLY + y] = value
-
-    for x in range(TLX):
-        for y in range(TLY):
-            outs[x][block_of(0, zl) * TLY + y] = first_ref[x, y]
-        outs[x][2 * TLY] = column_ref[x]
-    summarize(1, own_ref, other_ref, inducing_ref, proj_ref, store)
-    even = lax.axis_index("tx") % 2 == 0
-    for j in range(out0_ref.shape[0]):
-        near_pair_ref[j] = jnp.where(even, out1_ref[j], out0_ref[j])
-        far_pair_ref[j] = jnp.where(even, out0_ref[j], out1_ref[j])
-
-
-def mixture_kernel(
-    own0_ref,
-    own1_ref,
-    near_pair_ref,
-    far_pair_ref,
+    second_ref,
+    near0_ref,
+    far0_ref,
+    near1_ref,
+    far1_ref,
     proj_ref,
     mixing_ref,
     key_ref,
     value_ref,
+    grid_ref,
     mid_ref,
     side_ref,
 ):
@@ -415,20 +413,26 @@
     ones = head_ones()
     lane = lax.broadcasted_iota(jnp.int32, (1, LANES), 1)
     left = lane < half
-    even = lax.axis_index("tx") % 2 == 0
-
-    def held(i, j):
-        if i in (1, 2):
-            return (own0_ref, own1_ref)[i - 1][j]
-        near, far = near_pair_ref[j], far_pair_ref[j]
-        return jnp.where(even, far, near) if i == 0 else jnp.where(even, near, far)
-
-    grid = [[held(i, j) for j in range(tall + 1)] for i in range(4)]
+    even = lax.axis_index("tx") % 2
+    near_row = (1 - even) * (TLX + 1)
+    far_row = even * (TLX + 1)
+    border = (1 - low) * (tall + 1)
+    outside = low * (tall + 1)
+    for x in range(TLX):
+        for y in range(TLY):
+            grid_ref[1 + x, 1 + block_of(0, low) * TLY + y] = first_ref[x, y]
+            grid_ref[1 + x, 1 + block_of(1, low) * TLY + y] = second_ref[x, y]
+        grid_ref[1 + x, border] = column_ref[x]
+    for line, early_ref, late_ref in ((near_row, near0_ref, near1_ref), (far_row, far0_ref, far1_ref)):
+        for y in range(TLY):
+            grid_ref[line, 1 + block_of(0, low) * TLY + y] = early_ref[y]
+            grid_ref[line, 1 + block_of(1, low) * TLY + y] = late_ref[y]
+        grid_ref[line, border] = early_ref[TLY]
+    for x in range(TLX + 2):
+        grid_ref[x, outside] = blank
 
     def tile(i, j):
-        if 0 <= j < tall:
-            return grid[i][j]
-        return jnp.where(low == (1 if j < 0 else 0), grid[i][tall], blank)
+        return grid_ref[i, j + 1]
 
     mids, lefts, rights = [], [], []
     for i in range(2):
@@ -472,7 +476,7 @@
     along_y, rows0_ref, rows1_ref, query_ref, counts_ref, key_ref, value_ref, proj_ref, out_ref
 ):
     members, quota, width = rows0_ref.shape
-    group = min(512 // quota, members)
+    group = min(GROUP_ROWS // quota, members)
     row = lax.broadcasted_iota(jnp.int32, (quota, LANES), 0)
     for half_id, rows_ref in enumerate((rows0_ref, rows1_ref)):
         block = block_of(half_id, lax.axis_index("zl"))
@@ -561,7 +565,7 @@
     members = along_x * lows
     tall = blocks * TLY
     lines = point_count // LANES
-    chunk = 512
+    chunk = 1024
     half_rows = (members, quota, width)
 
     def shape(sizes, dtype=BF):
@@ -630,58 +634,78 @@
         return lax.ppermute(value, ("zh", "zl"), steps)
 
     other0 = swap(send0, True, False)
+    own1, send1 = call(
+        functools.partial(partial_kernel, 1, along_y),
+        "partial_second",
+        parts,
+        "vsvvv",
+        sums,
+        3,
+        (rows1, counts, first_queries, value_weight, first_proj),
+    )
+    other1 = swap(send1, True, False)
     first_half, border = call(
         combine_first_kernel,
         "combine_first",
         (shape((TLX, TLY, LANES, width)), shape((TLX, LANES, width))),
-        "vvvv",
+        "vvvva",
         [],
-        0.3,
-        (own0, other0, inducing, first_proj),
+        0.01,
+        (own0, other0, inducing, first_proj, send1),
     )
     column = swap(border, False, True)
-    own1, send1 = call(
-        functools.partial(partial_kernel, 1, along_y),
-        "partial_second",
-        parts,
-        "vsvvva",
-        sums,
-        3,
-        (rows1, counts, first_queries, value_weight, first_proj, border),
-    )
-    other1 = swap(send1, True, False)
     queries = call(
         functools.partial(queries_kernel, along_y),
         "point_queries",
         shape((2, members, quota, 4 * width)),
         "vvsva",
         [],
-        3,
-        (rows0, rows1, counts, second_proj, column),
-    )
-    line = shape((tall + 1, LANES, width))
-    summary0, summary1, near_line, far_line = call(
+        0.01,
+        (rows0, rows1, counts, second_proj, border),
+    )
+    near_pairs = [(i, i ^ 1) for i in range(along_x)]
+    far_pairs = [(i, ((i + 1) ^ 1) - 1) for i in range(1, along_x - 1)]
+
+    def halo(near, far):
+        far = lax.ppermute(far, "tx", far_pairs)
+        return lax.ppermute(near, "tx", near_pairs), far
+
+    early = shape((TLY + 1, LANES, width))
+    near0, far0 = halo(
+        *call(
+            early_lines_kernel,
+            "early_lines",
+            (early,) * 2,
+            "vva",
+            [],
+            0.01,
+            (first_half, column, queries),
+        )
+    )
+    late = shape((TLY, LANES, width))
+    second_half, near1, far1 = call(
         combine_second_kernel,
         "combine_second",
-        (line,) * 4,
-        "vvvvvva",
+        (shape((TLX, TLY, LANES, width)), late, late),
+        "vvvva",
         [],
-        0.3,
-        (own1, other1, inducing, first_proj, first_half, column, queries),
-    )
-    near_pairs = [(i, i ^ 1) for i in range(along_x)]
-    far_pairs = [(i, ((i + 1) ^ 1) - 1) for i in range(1, along_x - 1)]
-    near_line = lax.ppermute(near_line, "tx", near_pairs)
-    far_line = lax.ppermute(far_line, "tx", far_pairs)
+        0.01,
+        (own1, other1, inducing, first_proj, queries),
+    )
+    near1, far1 = halo(near1, far1)
 
     keys, values = call(
         mixture_kernel,
         "mix_tiles",
         (shape((blocks, HEADS * LANES, 4 * LANES)), shape((blocks, HEADS * LANES, 5 * LANES))),
-        "v" * 6,
-        [VMEM((6 * LANES, 2 * LANES), BF), VMEM((2, 4 * LANES, 2 * LANES), BF)],
-        4,
-        (summary0, summary1, near_line, far_line, second_proj, mixing),
+        "v" * 9,
+        [
+            VMEM((TLX + 2, tall + 2, LANES, width), BF),
+            VMEM((6 * LANES, 2 * LANES), BF),
+            VMEM((2, 4 * LANES, 2 * LANES), BF),
+        ],
+        1,
+        (first_half, column, second_half, near0, far0, near1, far1, second_proj, mixing),
     )
 
     result = call(
@@ -698,7 +722,7 @@
         "scatter_rows",
         shape((point_count, width)),
         "vs",
-        [VMEM((point_count, width), F32), VMEM((chunk, width), F32)],
+        [VMEM((point_count, width), F32), VMEM((512, width), F32)],
         5,
         (exchange(result), index),
     )

time: 92.1 us -> 87 us (0.945)
  starting transfers between devices: 20.7 us -> 16.6 us
  Pallas kernels: 34.5 us -> 32.7 us
  waiting for transfers between devices: 10.8 us -> 11.8 us
    all_to_all x2, waiting for transfers between devices: 2.7 us -> 8.91 us  [exchange(): lax.all_to_all(rows, ('tx', 'zl'), split_axis=0, concat_axis=0, tiled=True)]
    ppermute x3, starting transfers between devices: 9.71 us -> 4.38 us  [swap(): return lax.ppermute(value, ('zh', 'zl'), steps)]
    ppermute x3, waiting for transfers between devices: 7.57 us -> 2.65 us  [swap(): return lax.ppermute(value, ('zh', 'zl'), steps)]
    pallas_call x10 -> x11, Pallas kernels: 34.5 us -> 32.7 us  [call(): pl.pallas_call(kernel, out_shape=out_shape, in_specs=[pl.BlockSpec(memory...]
    ppermute x2 -> x4, starting transfers between devices: 0.93 us -> 2.08 us  [the longest x2 1.32 us: halo(): far = lax.ppermute(far, 'tx', far_pairs)]
  transfers between devices with their start and end apart: 7 -> 9, of which waited for: 4 -> 5; matrix products, arithmetic and copies ran while one was open for 0% -> 0% of each run, Pallas kernels for 16% -> 16%
where the time goes in v7:
time: 87 us; the launch traced here: 86.5 us
  Pallas kernels  32.7 us (38%)
  blocking collectives  24.5 us (28%)
  starting transfers between devices  16.6 us (19%)
  waiting for transfers between devices  11.8 us (14%)
    pallas_call x11, Pallas kernels, call(): pl.pallas_call(kernel, out_shape=out_shape, in_specs=[pl.BlockSpec(memory...  32.7 us
    all_to_all x1, blocking collectives, exchange(): lax.all_to_all(rows, ('tx', 'zl'), split_axis=0, concat_axis=0, tiled=True)  24.5 us
    all_to_all x2, starting transfers between devices, exchange(): lax.all_to_all(rows, ('tx', 'zl'), split_axis=0, concat_axis=0, tiled=True)  10.1 us
    all_to_all x2, waiting for transfers between devices, exchange(): lax.all_to_all(rows, ('tx', 'zl'), split_axis=0, concat_axis=0, tiled=True)  8.91 us
    ppermute x3, starting transfers between devices, swap(): return lax.ppermute(value, ('zh', 'zl'), steps)  4.38 us
    ppermute x3, waiting for transfers between devices, swap(): return lax.ppermute(value, ('zh', 'zl'), steps)  2.65 us
  transfers between devices with their start and end apart: 9, of which 5 were waited for; matrix products, arithmetic and copies ran while one was open for 0% of the time, Pallas kernels for 16%

profile of v7, /device:TPU:0, one launch (start us, length us, event | category | flops | bytes accessed | tf_op | source)
XLA Modules:
  0.0 86.5 jit_solution(7526774774209291854)
XLA Ops:
  0.0 0.0 copy-start.4
  0.0 0.0 copy-start.5
  0.0 0.0 copy-start.7
  0.0 7.1 %encode_first.1 = (bf16[16,128,128]{2,1,0:T(8,128)(2,1)}, s32[32,128]{1,0:T(8,128)}) custom-call(bf16[4096,128]{1,0:T(8,128)(2,1)} %points_ref.1, bf16[128,512]{1,0:T(8,128)(2,1)} %w1_ref.1, bf16[1,512,512]{2,1,0:T(8,128)(2,1)} %w2_ref.1, bf16[512,128]{1,0:T(8,128)(2,1)} %w3_ref.1, s32[32,128]{1,0:T(8,128)} %counts_ref.7, s32[32,128]{1,0:T(8,128)} %bitcast.1), custom_call_target="tpu_custom_call" | custom-call | flops 4000000000 | bytes 8000000 | tf_op jit(solution)/shard_map/encode_first/pallas_call | solution.py:530
  7.1 6.3 %all-to-all-start = ((bf16[16,128,128]{2,1,0:T(8,128)(2,1)}), bf16[16,128,128]{2,1,0:T(8,128)(2,1)S(1)}, u32[]{:S(2)}, u32[]{:S(2)}) async-start(bf16[16,128,128]{2,1,0:T(8,128)(2,1)} %get-tuple-element.22), calls=%async_computation | async-start | bytes 1048576 | tf_op jit(solution)/shard_map/all_to_all | solution.py:608
  13.5 0.0 copy-done.4
  13.5 0.0 copy-done.5
  13.5 0.0 copy-done.7
  13.5 0.0 copy-done.8
  13.5 0.0 copy-start.9
  13.5 0.7 copy-done.9
  14.2 0.0 copy-start
  14.2 0.0 copy-start.1
  14.2 5.2 %encode_second.1 = bf16[16,128,128]{2,1,0:T(8,128)(2,1)} custom-call(bf16[4096,128]{1,0:T(8,128)(2,1)S(1)} %copy-done.4, bf16[128,512]{1,0:T(8,128)(2,1)S(1)} %copy-done.7, bf16[1,512,512]{2,1,0:T(8,128)(2,1)S(1)} %copy-done.5, bf16[512,128]{1,0:T(8,128)(2,1)S(1)} %copy-done.8, s32[32,128]{1,0:T(8,128)S(1)} %copy-done.9), custom_call_target="tpu_custom_call" | custom-call | flops 3000000000 | bytes 6000000 | tf_op jit(solution)/shard_map/encode_second/pallas_call | solution.py:530
  19.5 2.7 %all-to-all-done.rows_ref.rows0_ref = bf16[16,128,128]{2,1,0:T(8,128)(2,1)S(1)} async-done(((bf16[16,128,128]{2,1,0:T(8,128)(2,1)}), bf16[16,128,128]{2,1,0:T(8,128)(2,1)S(1)}, u32[]{:S(2)}, u32[]{:S(2)}) %all-to-all-start) | async-done | bytes 524320 | tf_op jit(solution)/shard_map/all_to_all | solution.py:608
  22.2 3.8 %all-to-all-start.1 = ((bf16[16,128,128]{2,1,0:T(8,128)(2,1)}), bf16[16,128,128]{2,1,0:T(8,128)(2,1)S(1)}, u32[]{:S(2)}, u32[]{:S(2)}) async-start(bf16[16,128,128]{2,1,0:T(8,128)(2,1)} %encode_second.1), calls=%async_computation.1 | async-start | bytes 1048576 | tf_op jit(solution)/shard_map/all_to_all | solution.py:608
  26.0 0.0 copy-done
  26.0 0.0 copy-done.1
  26.0 0.0 copy-done.3
  26.0 2.7 %partial_first.1 = (f32[528,128]{1,0:T(8,128)S(1)}, bf16[528,128]{1,0:T(8,128)(2,1)S(1)}, bf16[256,128]{1,0:T(8,128)(2,1)S(1)}, bf16[128,128]{1,0:T(8,128)(2,1)S(1)}) custom-call(bf16[16,128,128]{2,1,0:T(8,128)(2,1)S(1)} %all-to-all-done.rows_ref.rows0_ref, s32[32,128]{1,0:T(8,128)S(1)} %copy-done.3, bf16[128,128]{1,0:T(8,128)(2,1)S(1)} %copy-done.1, ...), custom_call_target="tpu_custom_call" | custom-call | flops 1500000000 | bytes 3000000 | tf_op jit(solution)/shard_map/partial_first/pallas_call | solution.py:530
  28.8 0.0 copy-start.2
  28.8 2.7 %collective-permute-start = (bf16[528,128]{1,0:T(8,128)(2,1)S(1)}, bf16[528,128]{1,0:T(8,128)(2,1)S(1)}, u32[]{:S(2)}, u32[]{:S(2)}) collective-permute-start(bf16[528,128]{1,0:T(8,128)(2,1)S(1)} %get-tuple-element.25), channel_id=1, source_target_pairs={{0,2},{1,3},{2,0},{3,1},{4,6},{5,7},{6,4},{7,5},{8,10},{9,11},{10,... | collective-permute-start | bytes 405512 | tf_op jit(solution)/shard_map/ppermute | solution.py:634
  31.5 6.2 %all-to-all-done.1.rows_ref.rows1_ref = bf16[16,128,128]{2,1,0:T(8,128)(2,1)S(1)} async-done(((bf16[16,128,128]{2,1,0:T(8,128)(2,1)}), bf16[16,128,128]{2,1,0:T(8,128)(2,1)S(1)}, u32[]{:S(2)}, u32[]{:S(2)}) %all-to-all-start.1) | async-done | bytes 524320 | tf_op jit(solution)/shard_map/all_to_all | solution.py:608
  37.6 2.7 %partial_second.1 = (f32[528,128]{1,0:T(8,128)S(1)}, bf16[528,128]{1,0:T(8,128)(2,1)S(1)}) custom-call(bf16[16,128,128]{2,1,0:T(8,128)(2,1)S(1)} %all-to-all-done.1.rows_ref.rows1_ref, s32[32,128]{1,0:T(8,128)S(1)} %copy-done.3, bf16[256,128]{1,0:T(8,128)(2,1)S(1)} %get-tuple-element.26.rest_0_, bf16[128,128]{1,0:T(8,128)(2,1)S(1)} %get-tuple-element.27.rest_1_, ...), custom_call_target="tpu_custom_call" | custom-call | flops 1500000000 | bytes 3000000 | tf_op jit(solution)/shard_map/partial_second/pallas_call | solution.py:530
  40.3 0.2 collective-permute-start.2
  40.6 0.0 collective-permute-done.other_ref
  40.6 0.3 combine_first.1
  40.8 1.5 %collective-permute-start.1 = (bf16[2,128,128]{2,1,0:T(8,128)(2,1)S(1)}, bf16[2,128,128]{2,1,0:T(8,128)(2,1)S(1)}, u32[]{:S(2)}, u32[]{:S(2)}) collective-permute-start(bf16[2,128,128]{2,1,0:T(8,128)(2,1)S(1)} %get-tuple-element.29.column_any), channel_id=1, source_target_pairs={{0,1},{1,0},{2,3},{3,2},{4,5},{5,4},{6,7},{7,6},{8,9},{9,8},{10,11... | collective-permute-start | bytes 196616 | tf_op jit(solution)/shard_map/ppermute | solution.py:634
  42.3 0.0 copy-done.2
  42.3 2.7 %point_queries.1.query_any.query_ref = bf16[2,16,128,512]{3,2,1,0:T(8,128)(2,1)S(1)} custom-call(bf16[16,128,128]{2,1,0:T(8,128)(2,1)S(1)} %all-to-all-done.rows_ref.rows0_ref, bf16[16,128,128]{2,1,0:T(8,128)(2,1)S(1)} %all-to-all-done.1.rows_ref.rows1_ref, s32[32,128]{1,0:T(8,128)S(1)} %copy-done.3, bf16[4,128,128]{2,1,0:T(8,128)(2,1)S(1)} %copy-done.2, ...), custom_call_target="tpu_custom_call" | custom-call | flops 5000000 | bytes 10000 | tf_op jit(solution)/shard_map/point_queries/pallas_call | solution.py:530
  45.1 0.4 collective-permute-done.1.column_ref
  45.6 0.1 collective-permute-start.3
  45.6 0.7 collective-permute-start.4
  46.3 2.2 %collective-permute-done.2.other_ref = bf16[528,128]{1,0:T(8,128)(2,1)S(1)} collective-permute-done((bf16[528,128]{1,0:T(8,128)(2,1)S(1)}, bf16[528,128]{1,0:T(8,128)(2,1)S(1)}, u32[]{:S(2)}, u32[]{:S(2)}) %collective-permute-start.2) | collective-permute-done | bytes 135200 | tf_op jit(solution)/shard_map/ppermute | solution.py:634
  48.5 0.3 combine_second.1
  48.8 0.7 collective-permute-start.5
  49.5 0.7 collective-permute-start.6
  50.2 0.2 collective-permute-done.5.near1_ref
  50.4 0.0 collective-permute-done.6.far1_ref
  50.4 0.0 collective-permute-done.3.near0_ref
  50.4 0.0 collective-permute-done.4.far0_ref
  50.4 0.0 copy-done.6
  50.4 0.9 %mix_tiles.1 = (bf16[2,256,512]{2,1,0:T(8,128)(2,1)S(1)}, bf16[2,256,640]{2,1,0:T(8,128)(2,1)S(1)}) custom-call(bf16[2,2,128,128]{3,2,1,0:T(8,128)(2,1)S(1)} %get-tuple-element.30.first_ref, bf16[2,128,128]{2,1,0:T(8,128)(2,1)S(1)} %collective-permute-done.1.column_ref, bf16[2,2,128,128]{3,2,1,0:T(8,128)(2,1)S(1)} %get-tuple-element.32.second_ref, ...), custom_call_target="tpu_custom_call" | custom-call | flops 500000000 | bytes 1000000 | tf_op jit(solution)/shard_map/mix_tiles/pallas_call | solution.py:530
  51.4 0.0 copy-start.10
  51.4 5.5 %attend_points.1 = bf16[16,2,128,128]{3,2,1,0:T(8,128)(2,1)S(1)} custom-call(bf16[16,128,128]{2,1,0:T(8,128)(2,1)S(1)} %all-to-all-done.rows_ref.rows0_ref, bf16[16,128,128]{2,1,0:T(8,128)(2,1)S(1)} %all-to-all-done.1.rows_ref.rows1_ref, bf16[2,16,128,512]{3,2,1,0:T(8,128)(2,1)S(1)} %point_queries.1.query_any.query_ref, s32[32,128]{1,0:T(8,128)S(1)} %copy-done.3, ...), custom_call_target="tpu_custom_call" | custom-call | flops 3500000000 | bytes 7000000 | tf_op jit(solution)/shard_map/attend_points/pallas_call | solution.py:530
  56.9 24.5 %all_to_all.15.rows_ref = bf16[16,2,128,128]{3,2,1,0:T(8,128)(2,1)S(1)} all-to-all(bf16[16,2,128,128]{3,2,1,0:T(8,128)(2,1)S(1)} %attend_points.1), channel_id=1, replica_groups=mesh['tx'=8,'zh'=2,'zl'=2] {'tx','zl'}, dimensions={0} | all-to-all | bytes 2097152 | tf_op jit(solution)/shard_map/all_to_all | solution.py:608
  81.4 0.0 copy-done.10
  81.4 5.2 %scatter_rows.1 = bf16[4096,128]{1,0:T(8,128)(2,1)} custom-call(bf16[16,2,128,128]{3,2,1,0:T(8,128)(2,1)S(1)} %all_to_all.15.rows_ref, s32[32,128]{1,0:T(8,128)S(1)} %copy-done.10), custom_call_target="tpu_custom_call" | custom-call | flops 2500000000 | bytes 5000000 | tf_op jit(solution)/shard_map/scatter_rows/pallas_call | solution.py:530
  (4 shorter events, 0.0 us)
Async XLA Ops:
  0.0 13.5 %copy-start.4 = (bf16[4096,128]{1,0:T(8,128)(2,1)S(1)}, bf16[4096,128]{1,0:T(8,128)(2,1)}, u32[]{:S(2)}) copy-start(bf16[4096,128]{1,0:T(8,128)(2,1)} %points_ref.1) | copy-start | bytes 3145732
  0.0 13.5 %copy-start.5 = (bf16[1,512,512]{2,1,0:T(8,128)(2,1)S(1)}, bf16[1,512,512]{2,1,0:T(8,128)(2,1)}, u32[]{:S(2)}) copy-start(bf16[1,512,512]{2,1,0:T(8,128)(2,1)} %w2_ref.1) | copy-start | bytes 1572868
  0.0 13.5 %copy-start.7 = (bf16[128,512]{1,0:T(8,128)(2,1)S(1)}, bf16[128,512]{1,0:T(8,128)(2,1)}, u32[]{:S(2)}) copy-start(bf16[128,512]{1,0:T(8,128)(2,1)} %w1_ref.1) | copy-start | bytes 393220
  0.0 13.5 %copy-start.8 = (bf16[512,128]{1,0:T(8,128)(2,1)S(1)}, bf16[512,128]{1,0:T(8,128)(2,1)}, u32[]{:S(2)}) copy-start(bf16[512,128]{1,0:T(8,128)(2,1)} %w3_ref.1) | copy-start | bytes 393220
  7.1 15.1 %all-to-all-start = ((bf16[16,128,128]{2,1,0:T(8,128)(2,1)}), bf16[16,128,128]{2,1,0:T(8,128)(2,1)S(1)}, u32[]{:S(2)}, u32[]{:S(2)}) async-start(bf16[16,128,128]{2,1,0:T(8,128)(2,1)} %get-tuple-element.22), calls=%async_computation | async-start | bytes 1048576 | tf_op jit(solution)/shard_map/all_to_all | solution.py:608
  13.5 0.7 copy-start.9
  14.2 11.8 %copy-start = (bf16[4,128,128]{2,1,0:T(8,128)(2,1)S(1)}, bf16[4,128,128]{2,1,0:T(8,128)(2,1)}, u32[]{:S(2)}) copy-start(bf16[4,128,128]{2,1,0:T(8,128)(2,1)} %proj_ref.7) | copy-start | bytes 393220
  14.2 11.8 %copy-start.1 = (bf16[128,128]{1,0:T(8,128)(2,1)S(1)}, bf16[128,128]{1,0:T(8,128)(2,1)}, u32[]{:S(2)}) copy-start(bf16[128,128]{1,0:T(8,128)(2,1)} %inducing_ref.3) | copy-start | bytes 98308
  14.2 11.8 %copy-start.3 = (s32[32,128]{1,0:T(8,128)S(1)}, s32[32,128]{1,0:T(8,128)}, u32[]{:S(2)}) copy-start(s32[32,128]{1,0:T(8,128)} %counts_ref.7) | copy-start | bytes 49156
  22.2 15.4 %all-to-all-start.1 = ((bf16[16,128,128]{2,1,0:T(8,128)(2,1)}), bf16[16,128,128]{2,1,0:T(8,128)(2,1)S(1)}, u32[]{:S(2)}, u32[]{:S(2)}) async-start(bf16[16,128,128]{2,1,0:T(8,128)(2,1)} %encode_second.1), calls=%async_computation.1 | async-start | bytes 1048576 | tf_op jit(solution)/shard_map/all_to_all | solution.py:608
  28.8 13.6 %copy-start.2 = (bf16[4,128,128]{2,1,0:T(8,128)(2,1)S(1)}, bf16[4,128,128]{2,1,0:T(8,128)(2,1)}, u32[]{:S(2)}) copy-start(bf16[4,128,128]{2,1,0:T(8,128)(2,1)} %proj_ref.9) | copy-start | bytes 393220
  28.8 11.8 %collective-permute-start = (bf16[528,128]{1,0:T(8,128)(2,1)S(1)}, bf16[528,128]{1,0:T(8,128)(2,1)S(1)}, u32[]{:S(2)}, u32[]{:S(2)}) collective-permute-start(bf16[528,128]{1,0:T(8,128)(2,1)S(1)} %get-tuple-element.25), channel_id=1, source_target_pairs={{0,2},{1,3},{2,0},{3,1},{4,6},{5,7},{6,4},{7,5},{8,10},{9,11},{10,... | collective-permute-start | bytes 405512 | tf_op jit(solution)/shard_map/ppermute | solution.py:634
  40.3 8.2 %collective-permute-start.2 = (bf16[528,128]{1,0:T(8,128)(2,1)S(1)}, bf16[528,128]{1,0:T(8,128)(2,1)S(1)}, u32[]{:S(2)}, u32[]{:S(2)}) collective-permute-start(bf16[528,128]{1,0:T(8,128)(2,1)S(1)} %get-tuple-element.28.after_any), channel_id=1, source_target_pairs={{0,2},{1,3},{2,0},{3,1},{4,6},{5,7},{6,4},{7,5},{8,10},{9,11},{10,... | collective-permute-start | bytes 405512 | tf_op jit(solution)/shard_map/ppermute | solution.py:634
  40.8 4.7 %collective-permute-start.1 = (bf16[2,128,128]{2,1,0:T(8,128)(2,1)S(1)}, bf16[2,128,128]{2,1,0:T(8,128)(2,1)S(1)}, u32[]{:S(2)}, u32[]{:S(2)}) collective-permute-start(bf16[2,128,128]{2,1,0:T(8,128)(2,1)S(1)} %get-tuple-element.29.column_any), channel_id=1, source_target_pairs={{0,1},{1,0},{2,3},{3,2},{4,5},{5,4},{6,7},{7,6},{8,9},{9,8},{10,11... | collective-permute-start | bytes 196616 | tf_op jit(solution)/shard_map/ppermute | solution.py:634
  45.5 4.9 %copy-start.6 = (bf16[8,128,128]{2,1,0:T(8,128)(2,1)S(1)}, bf16[8,128,128]{2,1,0:T(8,128)(2,1)}, u32[]{:S(2)}) copy-start(bf16[8,128,128]{2,1,0:T(8,128)(2,1)} %mixing_ref.1) | copy-start | bytes 786436
  45.6 4.9 %collective-permute-start.3 = (bf16[3,128,128]{2,1,0:T(8,128)(2,1)S(1)}, bf16[3,128,128]{2,1,0:T(8,128)(2,1)S(1)}, u32[]{:S(2)}, u32[]{:S(2)}) collective-permute-start(bf16[3,128,128]{2,1,0:T(8,128)(2,1)S(1)} %get-tuple-element.33), channel_id=1, source_target_pairs={{0,4},{4,0},{8,12},{12,8},{16,20},{20,16},{24,28},{28,24},{1,5},{5... | collective-permute-start | bytes 294920 | tf_op jit(solution)/shard_map/ppermute | solution.py:671
  45.6 4.8 %collective-permute-start.4 = (bf16[3,128,128]{2,1,0:T(8,128)(2,1)S(1)}, bf16[3,128,128]{2,1,0:T(8,128)(2,1)S(1)}, u32[]{:S(2)}, u32[]{:S(2)}) collective-permute-start(bf16[3,128,128]{2,1,0:T(8,128)(2,1)S(1)} %get-tuple-element.34), channel_id=1, source_target_pairs={{4,8},{8,4},{12,16},{16,12},{20,24},{24,20},{5,9},{9,5},{13,17},{1... | collective-permute-start | bytes 294920 | tf_op jit(solution)/shard_map/ppermute | solution.py:670
  48.8 1.6 %collective-permute-start.5 = (bf16[2,128,128]{2,1,0:T(8,128)(2,1)S(1)}, bf16[2,128,128]{2,1,0:T(8,128)(2,1)S(1)}, u32[]{:S(2)}, u32[]{:S(2)}) collective-permute-start(bf16[2,128,128]{2,1,0:T(8,128)(2,1)S(1)} %get-tuple-element.35), channel_id=1, source_target_pairs={{0,4},{4,0},{8,12},{12,8},{16,20},{20,16},{24,28},{28,24},{1,5},{5... | collective-permute-start | bytes 196616 | tf_op jit(solution)/shard_map/ppermute | solution.py:671
  49.5 0.9 %collective-permute-start.6 = (bf16[2,128,128]{2,1,0:T(8,128)(2,1)S(1)}, bf16[2,128,128]{2,1,0:T(8,128)(2,1)S(1)}, u32[]{:S(2)}, u32[]{:S(2)}) collective-permute-start(bf16[2,128,128]{2,1,0:T(8,128)(2,1)S(1)} %get-tuple-element.36), channel_id=1, source_target_pairs={{4,8},{8,4},{12,16},{16,12},{20,24},{24,20},{5,9},{9,5},{13,17},{1... | collective-permute-start | bytes 196616 | tf_op jit(solution)/shard_map/ppermute | solution.py:670
  51.4 30.0 %copy-start.10 = (s32[32,128]{1,0:T(8,128)S(1)}, s32[32,128]{1,0:T(8,128)}, u32[]{:S(2)}) copy-start(s32[32,128]{1,0:T(8,128)} %get-tuple-element.23.index_any.index_ref) | copy-start | bytes 49156

commit v8 on v7

--- a/solution.py
+++ b/solution.py
@@ -38,8 +38,28 @@
     return jnp.where((row // half) == (col // half), 1.0, 0.0).astype(BF)
 
 
+def doubled(w):
+    blank = jnp.zeros_like(w)
+    return jnp.concatenate(
+        [jnp.concatenate([w, blank], axis=1), jnp.concatenate([blank, w], axis=1)], axis=0
+    )
+
+
+def beside(x):
+    half = x.shape[0] // 2
+    return jnp.concatenate([x[:half], x[half:]], axis=1)
+
+
+def stacked_back(x):
+    return jnp.concatenate([x[:, :LANES], x[:, LANES:]], axis=0)
+
+
 def unit(v, ones):
     return v * lax.rsqrt(dot((v * v).astype(BF), ones) + epsilon)
+
+
+def unit_pair(x, w, ones):
+    return stacked_back(unit(dot(beside(x), doubled(w)), doubled(ones)))
 
 
 def silu(v):
@@ -60,18 +80,24 @@
     return low if half_id else 1 - low
 
 
-def encode_rows(half_id, quota, chunk, points, index_ready, weights_ready, w1_ref, w2_ref, w3_ref, index_s, feat_ref, wide_ref, xs):
-    rows_total = points.shape[0] // 2
-    group = chunk // quota
+def encode_rows(
+    quota, points, index_ready, weights_ready, w1_ref, w2_ref, w3_ref, index_s, feat_ref, wide_ref, xs
+):
+    rows_total = points.shape[0]
     wide_ref[...] = points[...].astype(F32)
     index_ready()
-
-    def gather(c, buffer, first, last):
+    longest = xs[0].shape[0]
+    sizes = [longest // 4, 3 * longest // 4] + [longest] * (rows_total // longest - 1)
+    starts = [sum(sizes[:k]) for k in range(len(sizes))]
+
+    def gather(c, first, last):
         for r in range(first, last):
-            member = r // quota
-            spot = (member * 2 + block_of(half_id, member % 2)) * quota + r % quota
-            i = index_s[c * (2 * chunk // LANES) + spot // LANES, spot % LANES]
-            buffer[pl.ds(r, 1), :] = wide_ref[pl.ds(i, 1), :]
+            row = starts[c] + r
+            member, rest = row // (2 * quota), row % (2 * quota)
+            half_id, spot = rest // quota, rest % quota
+            spot += (member * 2 + block_of(half_id, member % 2)) * quota
+            i = index_s[spot // LANES, spot % LANES]
+            xs[c % 2][pl.ds(r, 1), :] = wide_ref[pl.ds(i, 1), :]
 
     def layer(x, w, ahead, cuts):
         parts = []
@@ -81,28 +107,25 @@
             parts.append(silu(dot(x, w[:, k * step : (k + 1) * step])))
         return jnp.concatenate(parts, axis=1)
 
-    def apply(c, buffer, ahead):
-        cuts = [chunk * k // 5 for k in range(6)]
-        hidden = layer(buffer[...].astype(BF), w1_ref, ahead, cuts[:3])
+    gather(0, 0, sizes[0])
+    weights_ready()
+    for c, size in enumerate(sizes):
+        coming = sizes[c + 1] if c + 1 < len(sizes) else 0
+
+        def ahead(a, b):
+            gather(c + 1, a, b)
+
+        cuts = [coming * k // 5 for k in range(6)]
+        hidden = layer(xs[c % 2][:size].astype(BF), w1_ref, ahead, cuts[:3])
         hidden = layer(hidden, w2_ref.at[0], ahead, cuts[2:5])
         ahead(cuts[4], cuts[5])
         out = dot(hidden, w3_ref[...]).astype(BF)
-        for k in range(group):
-            feat_ref[c * group + k] = out[k * quota : (k + 1) * quota]
-
-    chunks = rows_total // chunk
-    gather(0, xs[0], 0, chunk)
-    weights_ready()
-    for c in range(chunks):
-
-        def ahead(a, b):
-            if c + 1 < chunks:
-                gather(c + 1, xs[(c + 1) % 2], a, b)
-
-        apply(c, xs[c % 2], ahead)
-
-
-def encode_first_kernel(
+        for k in range(size // quota):
+            row = starts[c] + k * quota
+            feat_ref[row // (2 * quota), (row // quota) % 2] = out[k * quota : (k + 1) * quota]
+
+
+def encode_kernel(
     grid_y,
     along_y,
     quota,
@@ -182,19 +205,8 @@
             copies[k].wait()
 
     encode_rows(
-        0, quota, xa_ref.shape[0], points_ref, copy.wait, weights_ready, w1_ref, w2_ref, w3_ref, index_s,
-        feat_ref, wide_ref, (xa_ref, xb_ref),
-    )
-
-
-def encode_second_kernel(
-    quota, points_ref, w1_ref, w2_ref, w3_ref, index_any, feat_ref, index_s, wide_ref, xa_ref, xb_ref, sem
-):
-    copy = pltpu.make_async_copy(index_any, index_s, sem)
-    copy.start()
-    encode_rows(
-        1, quota, xa_ref.shape[0], points_ref, copy.wait, lambda: None, w1_ref, w2_ref, w3_ref, index_s,
-        feat_ref, wide_ref, (xa_ref, xb_ref),
+        quota, points_ref, copy.wait, weights_ready, w1_ref, w2_ref, w3_ref, index_s, feat_ref,
+        wide_ref, (xa_ref, xb_ref),
     )
 
 
@@ -230,7 +242,7 @@
         query_ref, wv_ref, proj_ref, own_ref, send_ref = rest[:-1]
     else:
         inducing_ref, proj_ref, own_ref, send_ref, query_ref, wv_ref = rest[:-1]
-    members, quota, width = rows_ref.shape
+    members, halves, quota, width = rows_ref.shape
     grid_y = along_y * TLY
     half = LANES // HEADS
     group = min(GROUP_ROWS // quota, members)
@@ -252,8 +264,8 @@
     spot = lax.broadcasted_iota(jnp.int32, (16, chunk), 1)
     tile_row = lax.broadcasted_iota(jnp.int32, (16, chunk), 0)
     for c in range(members // group):
-        x = jnp.concatenate([rows_ref[c * group + k] for k in range(group)], axis=0)
-        keys = unit(dot(x, proj_ref[1]), ones).astype(BF)
+        x = jnp.concatenate([rows_ref[c * group + k, half_id] for k in range(group)], axis=0)
+        keys = unit_pair(x, proj_ref[1], ones).astype(BF)
         weights = jnp.exp2(dot_t(keys, queries) * (sharpness * math.log2(math.e))).astype(BF)
         values = dot_t(wv_t, x).astype(BF)
         pieces = pieces_of(c * group, group, half_id, along_y)
@@ -295,15 +307,15 @@
     return n0, n1, n1 + counts_ref[s, base + grid_y]
 
 
-def queries_kernel(along_y, rows0_ref, rows1_ref, counts_ref, proj_ref, column_any, out_ref):
+def queries_kernel(along_y, rows_ref, counts_ref, proj_ref, border_any, out_ref):
     ones = head_ones()
-    for half_id, rows_ref in enumerate((rows0_ref, rows1_ref)):
-        members, quota, width = rows_ref.shape
-        group = min(GROUP_ROWS // quota, members)
-        row = lax.broadcasted_iota(jnp.int32, (quota, LANES), 0)
+    members, halves, quota, width = rows_ref.shape
+    group = min(GROUP_ROWS // quota, members)
+    row = lax.broadcasted_iota(jnp.int32, (quota, LANES), 0)
+    for half_id in range(halves):
         for c in range(members // group):
-            x = jnp.concatenate([rows_ref[c * group + k] for k in range(group)], axis=0)
-            query = unit(dot(x, proj_ref[0]), ones)
+            x = jnp.concatenate([rows_ref[c * group + k, half_id] for k in range(group)], axis=0)
+            query = unit_pair(x, proj_ref[0], ones)
             pieces = pieces_of(c * group, group, half_id, along_y)
             for k in range(group):
                 bounds = row_bounds(pieces[k], counts_ref, along_y * TLY)
@@ -473,12 +485,13 @@
 
 
 def attend_kernel(
-    along_y, rows0_ref, rows1_ref, query_ref, counts_ref, key_ref, value_ref, proj_ref, out_ref
+    along_y, rows_ref, query_ref, counts_ref, key_ref, value_ref, proj_ref, out_ref
 ):
-    members, quota, width = rows0_ref.shape
+    members, halves, quota, width = rows_ref.shape
     group = min(GROUP_ROWS // quota, members)
     row = lax.broadcasted_iota(jnp.int32, (quota, LANES), 0)
-    for half_id, rows_ref in enumerate((rows0_ref, rows1_ref)):
+    output_weight = doubled(proj_ref[3])
+    for half_id in range(halves):
         block = block_of(half_id, lax.axis_index("zl"))
         for c in range(members // group):
             expanded = jnp.concatenate(
@@ -497,8 +510,8 @@
                     tile = part[:, (t + 1) * LANES : (t + 2) * LANES]
                     picked = jnp.where(row >= bound, tile, picked)
                 attended.append(quotient(picked, part[:, 4 * LANES :]).astype(BF))
-            x = jnp.concatenate([rows_ref[c * group + k] for k in range(group)], axis=0)
-            added = dot(jnp.concatenate(attended, axis=0), proj_ref[3])
+            x = jnp.concatenate([rows_ref[c * group + k, half_id] for k in range(group)], axis=0)
+            added = stacked_back(dot(beside(jnp.concatenate(attended, axis=0)), output_weight))
             result = (x.astype(F32) + added).astype(BF)
             for k in range(group):
                 out_ref[c * group + k, half_id] = result[k * quota : (k + 1) * quota]
@@ -566,7 +579,6 @@
     tall = blocks * TLY
     lines = point_count // LANES
     chunk = 1024
-    half_rows = (members, quota, width)
 
     def shape(sizes, dtype=BF):
         return jax.ShapeDtypeStruct(sizes, dtype)
@@ -577,10 +589,11 @@
         VMEM((chunk, width), F32),
         VMEM((chunk, width), F32),
     ]
-    first, index = call(
-        functools.partial(encode_first_kernel, grid_y, along_y, quota),
-        "encode_first",
-        (shape(half_rows), shape((lines, LANES), jnp.int32)),
+    both_halves = (members, 2, quota, width)
+    features, index = call(
+        functools.partial(encode_kernel, grid_y, along_y, quota),
+        "encode_points",
+        (shape(both_halves), shape((lines, LANES), jnp.int32)),
         "aaaaaa",
         [
             SMEM((counts.shape[1],), jnp.int32),
@@ -590,25 +603,15 @@
         + buffers
         + [VMEM(a.shape, BF) for a in (points, *weights)]
         + [VMEM((lines, LANES), jnp.int32), pltpu.SemaphoreType.DMA((7,))],
-        8,
+        12,
         (points, *weights, counts, point_order.reshape(lines, LANES)),
         megabytes=56,
     )
-    second = call(
-        functools.partial(encode_second_kernel, quota),
-        "encode_second",
-        shape(half_rows),
-        "vvvva",
-        [SMEM((lines, LANES), jnp.int32)] + buffers + [pltpu.SemaphoreType.DMA],
-        6,
-        (points, *weights, index),
-    )
 
     def exchange(rows):
         return lax.all_to_all(rows, ("tx", "zl"), split_axis=0, concat_axis=0, tiled=True)
 
-    rows0 = exchange(first)
-    rows1 = exchange(second)
+    rows = exchange(features)
 
     part_rows = 4 * LANES + 16
     parts = (shape((part_rows, LANES), F32), shape((part_rows, LANES)))
@@ -621,7 +624,7 @@
         "vsvv",
         sums,
         3,
-        (rows0, counts, inducing, first_proj),
+        (rows, counts, inducing, first_proj),
     )
     pairs = [(h, l) for h in range(highs) for l in range(lows)]
 
@@ -641,7 +644,7 @@
         "vsvvv",
         sums,
         3,
-        (rows1, counts, first_queries, value_weight, first_proj),
+        (rows, counts, first_queries, value_weight, first_proj),
     )
     other1 = swap(send1, True, False)
     first_half, border = call(
@@ -658,10 +661,10 @@
         functools.partial(queries_kernel, along_y),
         "point_queries",
         shape((2, members, quota, 4 * width)),
-        "vvsva",
+        "vsva",
         [],
         0.01,
-        (rows0, rows1, counts, second_proj, border),
+        (rows, counts, second_proj, border),
     )
     near_pairs = [(i, i ^ 1) for i in range(along_x)]
     far_pairs = [(i, ((i + 1) ^ 1) - 1) for i in range(1, along_x - 1)]
@@ -711,11 +714,11 @@
     result = call(
         functools.partial(attend_kernel, along_y),
         "attend_points",
-        shape((members, 2, quota, width)),
-        "vvvsvvv",
+        shape(both_halves),
+        "vvsvvv",
         [],
         7,
-        (rows0, rows1, queries, counts, keys, values, second_proj),
+        (rows, queries, counts, keys, values, second_proj),
     )
     return call(
         scatter_kernel,

time: 87 us -> 91.3 us (1.049)
  blocking collectives: 24.5 us -> 43.3 us
  starting transfers between devices: 16.6 us -> 7.8 us
  waiting for transfers between devices: 11.8 us -> 8.8 us
  Pallas kernels: 32.7 us -> 31 us
    all_to_all x1 -> x2, blocking collectives: 24.5 us -> 43.3 us  [exchange(): lax.all_to_all(rows, ('tx', 'zl'), split_axis=0, concat_axis=0, tiled=True)]
    all_to_all x2 -> x0, starting transfers between devices: 10.1 us -> none  [exchange(): lax.all_to_all(rows, ('tx', 'zl'), split_axis=0, concat_axis=0, tiled=True)]
    all_to_all x2 -> x0, waiting for transfers between devices: 8.91 us -> none  [exchange(): lax.all_to_all(rows, ('tx', 'zl'), split_axis=0, concat_axis=0, tiled=True)]
    ppermute x3, waiting for transfers between devices: 2.65 us -> 8.55 us  [swap(): return lax.ppermute(value, ('zh', 'zl'), steps)]
    ppermute x2, starting transfers between devices: 0.76 us -> 3.1 us  [halo(): return (lax.ppermute(near, 'tx', near_pairs), far)]
    pallas_call x11 -> x10, Pallas kernels: 32.7 us -> 31 us  [call(): pl.pallas_call(kernel, out_shape=out_shape, in_specs=[pl.BlockSpec(memory...]
    ppermute x3, starting transfers between devices: 4.38 us -> 3.39 us  [swap(): return lax.ppermute(value, ('zh', 'zl'), steps)]
  transfers between devices with their start and end apart: 9 -> 7, of which waited for: 5 -> 3; matrix products, arithmetic and copies ran while one was open for 0% -> 0% of each run, Pallas kernels for 16% -> 7%
where the time goes in v8:
time: 91.3 us; the launch traced here: 91 us
  blocking collectives  43.3 us (47%)
  Pallas kernels  31 us (34%)
  waiting for transfers between devices  8.8 us (10%)
  starting transfers between devices  7.8 us (9%)
    all_to_all x2, blocking collectives, exchange(): lax.all_to_all(rows, ('tx', 'zl'), split_axis=0, concat_axis=0, tiled=True)  43.3 us
    pallas_call x10, Pallas kernels, call(): pl.pallas_call(kernel, out_shape=out_shape, in_specs=[pl.BlockSpec(memory...  31 us
    ppermute x3, waiting for transfers between devices, swap(): return lax.ppermute(value, ('zh', 'zl'), steps)  8.55 us
    ppermute x3, starting transfers between devices, swap(): return lax.ppermute(value, ('zh', 'zl'), steps)  3.39 us
    ppermute x2, starting transfers between devices, halo(): return (lax.ppermute(near, 'tx', near_pairs), far)  3.1 us
  transfers between devices with their start and end apart: 7, of which 3 were waited for; matrix products, arithmetic and copies ran while one was open for 0% of the time, Pallas kernels for 7%

profile of v8, /device:TPU:0, one launch (start us, length us, event | category | flops | bytes accessed | tf_op | source)
XLA Modules:
  0.0 91.0 jit_solution(7365854096419200390)
XLA Ops:
  0.0 0.0 copy-start
  0.0 0.0 copy-start.1
  0.0 0.0 copy-start.3
  0.0 10.6 %encode_points.1 = (bf16[16,2,128,128]{3,2,1,0:T(8,128)(2,1)}, s32[32,128]{1,0:T(8,128)}) custom-call(bf16[4096,128]{1,0:T(8,128)(2,1)} %points_hbm.1, bf16[128,512]{1,0:T(8,128)(2,1)} %w1_hbm.1, bf16[1,512,512]{2,1,0:T(8,128)(2,1)} %w2_hbm.1, bf16[512,128]{1,0:T(8,128)(2,1)} %w3_hbm.1, s32[32,128]{1,0:T(8,128)} %counts_ref.7, s32[32,128]{1,0:T(8,128)} %bitcast.1), custom_call_target="tpu_custom_call" | custom-call | flops 6000000000 | bytes 12000000 | tf_op jit(solution)/shard_map/encode_points/pallas_call | solution.py:543
  10.6 20.7 %all_to_all.10.rows_ref = bf16[16,2,128,128]{3,2,1,0:T(8,128)(2,1)S(1)} all-to-all(bf16[16,2,128,128]{3,2,1,0:T(8,128)(2,1)} %get-tuple-element.22), channel_id=1, replica_groups=mesh['tx'=8,'zh'=2,'zl'=2] {'tx','zl'}, dimensions={0} | all-to-all | bytes 2097152 | tf_op jit(solution)/shard_map/all_to_all | solution.py:612
  31.3 0.0 copy-done
  31.3 0.0 copy-done.1
  31.3 0.0 copy-done.3
  31.3 2.8 %partial_first.1 = (f32[528,128]{1,0:T(8,128)S(1)}, bf16[528,128]{1,0:T(8,128)(2,1)S(1)}, bf16[256,128]{1,0:T(8,128)(2,1)S(1)}, bf16[128,128]{1,0:T(8,128)(2,1)S(1)}) custom-call(bf16[16,2,128,128]{3,2,1,0:T(8,128)(2,1)S(1)} %all_to_all.10.rows_ref, s32[32,128]{1,0:T(8,128)S(1)} %copy-done.3, bf16[128,128]{1,0:T(8,128)(2,1)S(1)} %copy-done.1, ...), custom_call_target="tpu_custom_call" | custom-call | flops 1500000000 | bytes 3000000 | tf_op jit(solution)/shard_map/partial_first/pallas_call | solution.py:543
  34.1 0.0 copy-start.2
  34.1 2.7 %collective-permute-start = (bf16[528,128]{1,0:T(8,128)(2,1)S(1)}, bf16[528,128]{1,0:T(8,128)(2,1)S(1)}, u32[]{:S(2)}, u32[]{:S(2)}) collective-permute-start(bf16[528,128]{1,0:T(8,128)(2,1)S(1)} %get-tuple-element.24), channel_id=1, source_target_pairs={{0,2},{1,3},{2,0},{3,1},{4,6},{5,7},{6,4},{7,5},{8,10},{9,11},{10,... | collective-permute-start | bytes 405512 | tf_op jit(solution)/shard_map/ppermute | solution.py:637
  36.7 2.7 %partial_second.1 = (f32[528,128]{1,0:T(8,128)S(1)}, bf16[528,128]{1,0:T(8,128)(2,1)S(1)}) custom-call(bf16[16,2,128,128]{3,2,1,0:T(8,128)(2,1)S(1)} %all_to_all.10.rows_ref, s32[32,128]{1,0:T(8,128)S(1)} %copy-done.3, bf16[256,128]{1,0:T(8,128)(2,1)S(1)} %get-tuple-element.25.rest_0_, bf16[128,128]{1,0:T(8,128)(2,1)S(1)} %get-tuple-element.26.rest_1_, ...), custom_call_target="tpu_custom_call" | custom-call | flops 1500000000 | bytes 3000000 | tf_op jit(solution)/shard_map/partial_second/pallas_call | solution.py:543
  39.5 0.4 collective-permute-start.2
  39.9 7.3 %collective-permute-done.other_ref = bf16[528,128]{1,0:T(8,128)(2,1)S(1)} collective-permute-done((bf16[528,128]{1,0:T(8,128)(2,1)S(1)}, bf16[528,128]{1,0:T(8,128)(2,1)S(1)}, u32[]{:S(2)}, u32[]{:S(2)}) %collective-permute-start) | collective-permute-done | bytes 135200 | tf_op jit(solution)/shard_map/ppermute | solution.py:637
  47.2 0.3 combine_first.1
  47.5 0.3 collective-permute-start.1
  47.8 0.0 copy-done.2
  47.8 2.8 %point_queries.1.query_any.query_ref = bf16[2,16,128,512]{3,2,1,0:T(8,128)(2,1)S(1)} custom-call(bf16[16,2,128,128]{3,2,1,0:T(8,128)(2,1)S(1)} %all_to_all.10.rows_ref, s32[32,128]{1,0:T(8,128)S(1)} %copy-done.3, bf16[4,128,128]{2,1,0:T(8,128)(2,1)S(1)} %copy-done.2, bf16[2,128,128]{2,1,0:T(8,128)(2,1)S(1)} %get-tuple-element.28.border_any), custom_call_target="tpu_custom_call" | custom-call | flops 5000000 | bytes 10000 | tf_op jit(solution)/shard_map/point_queries/pallas_call | solution.py:543
  50.6 1.2 %collective-permute-done.1.column_ref = bf16[2,128,128]{2,1,0:T(8,128)(2,1)S(1)} collective-permute-done((bf16[2,128,128]{2,1,0:T(8,128)(2,1)S(1)}, bf16[2,128,128]{2,1,0:T(8,128)(2,1)S(1)}, u32[]{:S(2)}, u32[]{:S(2)}) %collective-permute-start.1) | collective-permute-done | bytes 65568 | tf_op jit(solution)/shard_map/ppermute | solution.py:637
  51.8 0.0 copy-start.4
  51.8 0.1 collective-permute-start.3
  51.9 0.7 collective-permute-start.4
  52.6 0.0 collective-permute-done.2.other_ref
  52.6 0.3 combine_second.1
  52.9 3.0 %collective-permute-start.5 = (bf16[2,128,128]{2,1,0:T(8,128)(2,1)S(1)}, bf16[2,128,128]{2,1,0:T(8,128)(2,1)S(1)}, u32[]{:S(2)}, u32[]{:S(2)}) collective-permute-start(bf16[2,128,128]{2,1,0:T(8,128)(2,1)S(1)} %get-tuple-element.34), channel_id=1, source_target_pairs={{0,4},{4,0},{8,12},{12,8},{16,20},{20,16},{24,28},{28,24},{1,5},{5... | collective-permute-start | bytes 196616 | tf_op jit(solution)/shard_map/ppermute | solution.py:674
  55.9 0.7 collective-permute-start.6
  56.6 0.2 collective-permute-done.5.near1_ref
  56.8 0.0 collective-permute-done.6.far1_ref
  56.8 0.0 collective-permute-done.3.near0_ref
  56.8 0.0 collective-permute-done.4.far0_ref
  56.8 0.0 copy-done.4
  56.9 0.9 %mix_tiles.1 = (bf16[2,256,512]{2,1,0:T(8,128)(2,1)S(1)}, bf16[2,256,640]{2,1,0:T(8,128)(2,1)S(1)}) custom-call(bf16[2,2,128,128]{3,2,1,0:T(8,128)(2,1)S(1)} %get-tuple-element.29.first_ref, bf16[2,128,128]{2,1,0:T(8,128)(2,1)S(1)} %collective-permute-done.1.column_ref, bf16[2,2,128,128]{3,2,1,0:T(8,128)(2,1)S(1)} %get-tuple-element.31.second_ref, ...), custom_call_target="tpu_custom_call" | custom-call | flops 500000000 | bytes 1000000 | tf_op jit(solution)/shard_map/mix_tiles/pallas_call | solution.py:543
  57.8 0.0 copy-start.5
  57.8 5.5 %attend_points.1 = bf16[16,2,128,128]{3,2,1,0:T(8,128)(2,1)S(1)} custom-call(bf16[16,2,128,128]{3,2,1,0:T(8,128)(2,1)S(1)} %all_to_all.10.rows_ref, bf16[2,16,128,512]{3,2,1,0:T(8,128)(2,1)S(1)} %point_queries.1.query_any.query_ref, s32[32,128]{1,0:T(8,128)S(1)} %copy-done.3, bf16[2,256,512]{2,1,0:T(8,128)(2,1)S(1)} %get-tuple-element.36.key_ref, ...), custom_call_target="tpu_custom_call" | custom-call | flops 3500000000 | bytes 7000000 | tf_op jit(solution)/shard_map/attend_points/pallas_call | solution.py:543
  63.3 22.6 %all_to_all.11.rows_ref = bf16[16,2,128,128]{3,2,1,0:T(8,128)(2,1)S(1)} all-to-all(bf16[16,2,128,128]{3,2,1,0:T(8,128)(2,1)S(1)} %attend_points.1), channel_id=1, replica_groups=mesh['tx'=8,'zh'=2,'zl'=2] {'tx','zl'}, dimensions={0} | all-to-all | bytes 2097152 | tf_op jit(solution)/shard_map/all_to_all | solution.py:612
  85.9 0.0 copy-done.5
  85.9 5.2 %scatter_rows.1 = bf16[4096,128]{1,0:T(8,128)(2,1)} custom-call(bf16[16,2,128,128]{3,2,1,0:T(8,128)(2,1)S(1)} %all_to_all.11.rows_ref, s32[32,128]{1,0:T(8,128)S(1)} %copy-done.5), custom_call_target="tpu_custom_call" | custom-call | flops 2500000000 | bytes 5000000 | tf_op jit(solution)/shard_map/scatter_rows/pallas_call | solution.py:543
  (1 shorter events, 0.0 us)
Async XLA Ops:
  0.0 31.3 %copy-start = (bf16[4,128,128]{2,1,0:T(8,128)(2,1)S(1)}, bf16[4,128,128]{2,1,0:T(8,128)(2,1)}, u32[]{:S(2)}) copy-start(bf16[4,128,128]{2,1,0:T(8,128)(2,1)} %proj_ref.7) | copy-start | bytes 393220
  0.0 31.3 %copy-start.1 = (bf16[128,128]{1,0:T(8,128)(2,1)S(1)}, bf16[128,128]{1,0:T(8,128)(2,1)}, u32[]{:S(2)}) copy-start(bf16[128,128]{1,0:T(8,128)(2,1)} %inducing_ref.3) | copy-start | bytes 98308
  0.0 31.3 %copy-start.3 = (s32[32,128]{1,0:T(8,128)S(1)}, s32[32,128]{1,0:T(8,128)}, u32[]{:S(2)}) copy-start(s32[32,128]{1,0:T(8,128)} %counts_ref.7) | copy-start | bytes 49156
  34.1 13.7 %copy-start.2 = (bf16[4,128,128]{2,1,0:T(8,128)(2,1)S(1)}, bf16[4,128,128]{2,1,0:T(8,128)(2,1)}, u32[]{:S(2)}) copy-start(bf16[4,128,128]{2,1,0:T(8,128)(2,1)} %proj_ref.9) | copy-start | bytes 393220
  34.1 13.1 %collective-permute-start = (bf16[528,128]{1,0:T(8,128)(2,1)S(1)}, bf16[528,128]{1,0:T(8,128)(2,1)S(1)}, u32[]{:S(2)}, u32[]{:S(2)}) collective-permute-start(bf16[528,128]{1,0:T(8,128)(2,1)S(1)} %get-tuple-element.24), channel_id=1, source_target_pairs={{0,2},{1,3},{2,0},{3,1},{4,6},{5,7},{6,4},{7,5},{8,10},{9,11},{10,... | collective-permute-start | bytes 405512 | tf_op jit(solution)/shard_map/ppermute | solution.py:637
  39.5 13.1 %collective-permute-start.2 = (bf16[528,128]{1,0:T(8,128)(2,1)S(1)}, bf16[528,128]{1,0:T(8,128)(2,1)S(1)}, u32[]{:S(2)}, u32[]{:S(2)}) collective-permute-start(bf16[528,128]{1,0:T(8,128)(2,1)S(1)} %get-tuple-element.27.after_any), channel_id=1, source_target_pairs={{0,2},{1,3},{2,0},{3,1},{4,6},{5,7},{6,4},{7,5},{8,10},{9,11},{10,... | collective-permute-start | bytes 405512 | tf_op jit(solution)/shard_map/ppermute | solution.py:637
  47.5 4.3 %collective-permute-start.1 = (bf16[2,128,128]{2,1,0:T(8,128)(2,1)S(1)}, bf16[2,128,128]{2,1,0:T(8,128)(2,1)S(1)}, u32[]{:S(2)}, u32[]{:S(2)}) collective-permute-start(bf16[2,128,128]{2,1,0:T(8,128)(2,1)S(1)} %get-tuple-element.28.border_any), channel_id=1, source_target_pairs={{0,1},{1,0},{2,3},{3,2},{4,5},{5,4},{6,7},{7,6},{8,9},{9,8},{10,11... | collective-permute-start | bytes 196616 | tf_op jit(solution)/shard_map/ppermute | solution.py:637
  51.8 5.0 %copy-start.4 = (bf16[8,128,128]{2,1,0:T(8,128)(2,1)S(1)}, bf16[8,128,128]{2,1,0:T(8,128)(2,1)}, u32[]{:S(2)}) copy-start(bf16[8,128,128]{2,1,0:T(8,128)(2,1)} %mixing_ref.1) | copy-start | bytes 786436
  51.8 5.0 %collective-permute-start.3 = (bf16[3,128,128]{2,1,0:T(8,128)(2,1)S(1)}, bf16[3,128,128]{2,1,0:T(8,128)(2,1)S(1)}, u32[]{:S(2)}, u32[]{:S(2)}) collective-permute-start(bf16[3,128,128]{2,1,0:T(8,128)(2,1)S(1)} %get-tuple-element.32), channel_id=1, source_target_pairs={{0,4},{4,0},{8,12},{12,8},{16,20},{20,16},{24,28},{28,24},{1,5},{5... | collective-permute-start | bytes 294920 | tf_op jit(solution)/shard_map/ppermute | solution.py:674
  51.9 4.9 %collective-permute-start.4 = (bf16[3,128,128]{2,1,0:T(8,128)(2,1)S(1)}, bf16[3,128,128]{2,1,0:T(8,128)(2,1)S(1)}, u32[]{:S(2)}, u32[]{:S(2)}) collective-permute-start(bf16[3,128,128]{2,1,0:T(8,128)(2,1)S(1)} %get-tuple-element.33), channel_id=1, source_target_pairs={{4,8},{8,4},{12,16},{16,12},{20,24},{24,20},{5,9},{9,5},{13,17},{1... | collective-permute-start | bytes 294920 | tf_op jit(solution)/shard_map/ppermute | solution.py:673
  52.9 3.9 %collective-permute-start.5 = (bf16[2,128,128]{2,1,0:T(8,128)(2,1)S(1)}, bf16[2,128,128]{2,1,0:T(8,128)(2,1)S(1)}, u32[]{:S(2)}, u32[]{:S(2)}) collective-permute-start(bf16[2,128,128]{2,1,0:T(8,128)(2,1)S(1)} %get-tuple-element.34), channel_id=1, source_target_pairs={{0,4},{4,0},{8,12},{12,8},{16,20},{20,16},{24,28},{28,24},{1,5},{5... | collective-permute-start | bytes 196616 | tf_op jit(solution)/shard_map/ppermute | solution.py:674
  55.9 0.9 collective-permute-start.6
  57.8 28.1 %copy-start.5 = (s32[32,128]{1,0:T(8,128)S(1)}, s32[32,128]{1,0:T(8,128)}, u32[]{:S(2)}) copy-start(s32[32,128]{1,0:T(8,128)} %get-tuple-element.38.index_ref) | copy-start | bytes 49156

commit v9 on v7

--- a/solution.py
+++ b/solution.py
@@ -60,18 +60,31 @@
     return low if half_id else 1 - low
 
 
-def encode_rows(half_id, quota, chunk, points, index_ready, weights_ready, w1_ref, w2_ref, w3_ref, index_s, feat_ref, wide_ref, xs):
+def move_rows(pairs, source_ref, target_ref):
+    for k in range(0, len(pairs), 16):
+        batch = [(t, source_ref[pl.ds(f, 1), :]) for f, t in pairs[k : k + 16]]
+        for target, row in batch:
+            target_ref[pl.ds(target, 1), :] = row
+
+
+def encode_rows(
+    half_id, quota, points, index_ready, weights_ready, w1_ref, w2_ref, w3_ref, index_s, feat_ref,
+    wide_ref, xs,
+):
     rows_total = points.shape[0] // 2
-    group = chunk // quota
     wide_ref[...] = points[...].astype(F32)
     index_ready()
-
-    def gather(c, buffer, first, last):
+    longest = xs[0].shape[0]
+    sizes = [longest // 4, 3 * longest // 4] + [longest] * (rows_total // longest - 1)
+    starts = [sum(sizes[:k]) for k in range(len(sizes))]
+
+    def gather(c, first, last):
+        pairs = []
         for r in range(first, last):
-            member = r // quota
-            spot = (member * 2 + block_of(half_id, member % 2)) * quota + r % quota
-            i = index_s[c * (2 * chunk // LANES) + spot // LANES, spot % LANES]
-            buffer[pl.ds(r, 1), :] = wide_ref[pl.ds(i, 1), :]
+            member, rest = divmod(starts[c] + r, quota)
+            spot = (member * 2 + block_of(half_id, member % 2)) * quota + rest
+            pairs.append((index_s[spot // LANES, spot % LANES], r))
+        move_rows(pairs, wide_ref, xs[c % 2])
 
     def layer(x, w, ahead, cuts):
         parts = []
@@ -81,25 +94,22 @@
             parts.append(silu(dot(x, w[:, k * step : (k + 1) * step])))
         return jnp.concatenate(parts, axis=1)
 
-    def apply(c, buffer, ahead):
-        cuts = [chunk * k // 5 for k in range(6)]
-        hidden = layer(buffer[...].astype(BF), w1_ref, ahead, cuts[:3])
+    gather(0, 0, sizes[0])
+    weights_ready()
+    for c, size in enumerate(sizes):
+        coming = sizes[c + 1] if c + 1 < len(sizes) else 0
+
+        def ahead(a, b):
+            gather(c + 1, a, b)
+
+        cuts = [coming * k // 80 * 16 for k in range(6)]
+        cuts[5] = coming
+        hidden = layer(xs[c % 2][:size].astype(BF), w1_ref, ahead, cuts[:3])
         hidden = layer(hidden, w2_ref.at[0], ahead, cuts[2:5])
         ahead(cuts[4], cuts[5])
         out = dot(hidden, w3_ref[...]).astype(BF)
-        for k in range(group):
-            feat_ref[c * group + k] = out[k * quota : (k + 1) * quota]
-
-    chunks = rows_total // chunk
-    gather(0, xs[0], 0, chunk)
-    weights_ready()
-    for c in range(chunks):
-
-        def ahead(a, b):
-            if c + 1 < chunks:
-                gather(c + 1, xs[(c + 1) % 2], a, b)
-
-        apply(c, xs[c % 2], ahead)
+        for k in range(size // quota):
+            feat_ref[starts[c] // quota + k] = out[k * quota : (k + 1) * quota]
 
 
 def encode_first_kernel(
@@ -182,7 +192,7 @@
             copies[k].wait()
 
     encode_rows(
-        0, quota, xa_ref.shape[0], points_ref, copy.wait, weights_ready, w1_ref, w2_ref, w3_ref, index_s,
+        0, quota, points_ref, copy.wait, weights_ready, w1_ref, w2_ref, w3_ref, index_s,
         feat_ref, wide_ref, (xa_ref, xb_ref),
     )
 
@@ -193,7 +203,7 @@
     copy = pltpu.make_async_copy(index_any, index_s, sem)
     copy.start()
     encode_rows(
-        1, quota, xa_ref.shape[0], points_ref, copy.wait, lambda: None, w1_ref, w2_ref, w3_ref, index_s,
+        1, quota, points_ref, copy.wait, lambda: None, w1_ref, w2_ref, w3_ref, index_s,
         feat_ref, wide_ref, (xa_ref, xb_ref),
     )
 
@@ -340,35 +350,37 @@
         column_ref[x] = jnp.where(lax.axis_index("zl") == 0, out_ref[x, TLY - 1], out_ref[x, 0])
 
 
-def pair_lines(rows, near_ref, far_ref):
-    even = lax.axis_index("tx") % 2 == 0
+def line_to(near, rows, out_ref):
+    upper = lax.axis_index("tx") % 2 == (0 if near else 1)
     for y, (low, high) in enumerate(zip(*rows)):
-        near_ref[y] = jnp.where(even, high, low)
-        far_ref[y] = jnp.where(even, low, high)
-
-
-def early_lines_kernel(first_ref, column_ref, query_any, near_ref, far_ref):
+        out_ref[y] = jnp.where(upper, high, low)
+
+
+def early_line_kernel(first_ref, column_ref, query_any, far_ref):
     rows = [[first_ref[x, y] for y in range(TLY)] + [column_ref[x]] for x in range(TLX)]
-    pair_lines(rows, near_ref, far_ref)
+    line_to(False, rows, far_ref)
 
 
 def combine_second_kernel(
-    own_ref, other_ref, inducing_ref, proj_ref, query_any, out_ref, near_ref, far_ref
+    own_ref, other_ref, inducing_ref, proj_ref, first_ref, column_ref, query_any, out_ref, near_ref, far_ref
 ):
     def store(x, y, value):
         out_ref[x, y] = value
 
     summarize(1, own_ref, other_ref, inducing_ref, proj_ref, store)
-    pair_lines([[out_ref[x, y] for y in range(TLY)] for x in range(TLX)], near_ref, far_ref)
+    rows = [[out_ref[x, y] for y in range(TLY)] for x in range(TLX)]
+    line_to(False, rows, far_ref)
+    for x in range(TLX):
+        rows[x] += [first_ref[x, y] for y in range(TLY)] + [column_ref[x]]
+    line_to(True, rows, near_ref)
 
 
 def mixture_kernel(
     first_ref,
     column_ref,
     second_ref,
-    near0_ref,
+    near_ref,
     far0_ref,
-    near1_ref,
     far1_ref,
     proj_ref,
     mixing_ref,
@@ -423,11 +435,13 @@
             grid_ref[1 + x, 1 + block_of(0, low) * TLY + y] = first_ref[x, y]
             grid_ref[1 + x, 1 + block_of(1, low) * TLY + y] = second_ref[x, y]
         grid_ref[1 + x, border] = column_ref[x]
-    for line, early_ref, late_ref in ((near_row, near0_ref, near1_ref), (far_row, far0_ref, far1_ref)):
-        for y in range(TLY):
-            grid_ref[line, 1 + block_of(0, low) * TLY + y] = early_ref[y]
-            grid_ref[line, 1 + block_of(1, low) * TLY + y] = late_ref[y]
-        grid_ref[line, border] = early_ref[TLY]
+    for y in range(TLY):
+        grid_ref[near_row, 1 + block_of(1, low) * TLY + y] = near_ref[y]
+        grid_ref[near_row, 1 + block_of(0, low) * TLY + y] = near_ref[TLY + y]
+        grid_ref[far_row, 1 + block_of(1, low) * TLY + y] = far1_ref[y]
+        grid_ref[far_row, 1 + block_of(0, low) * TLY + y] = far0_ref[y]
+    grid_ref[near_row, border] = near_ref[2 * TLY]
+    grid_ref[far_row, border] = far0_ref[TLY]
     for x in range(TLX + 2):
         grid_ref[x, outside] = blank
 
@@ -514,9 +528,10 @@
             for half_id in range(halves):
                 row = (k * halves + block_of(half_id, k % 2)) * quota
                 part_ref[row : row + quota, :] = rows_ref[c * group + k, half_id].astype(F32)
+        pairs = []
         for r in range(chunk):
-            i = index_ref[c * (chunk // LANES) + r // LANES, r % LANES]
-            wide_ref[pl.ds(i, 1), :] = part_ref[pl.ds(r, 1), :]
+            pairs.append((r, index_ref[c * (chunk // LANES) + r // LANES, r % LANES]))
+        move_rows(pairs, part_ref, wide_ref)
         return carry
 
     lax.fori_loop(0, members // group, step, 0)
@@ -666,46 +681,43 @@
     near_pairs = [(i, i ^ 1) for i in range(along_x)]
     far_pairs = [(i, ((i + 1) ^ 1) - 1) for i in range(1, along_x - 1)]
 
-    def halo(near, far):
-        far = lax.ppermute(far, "tx", far_pairs)
-        return lax.ppermute(near, "tx", near_pairs), far
-
-    early = shape((TLY + 1, LANES, width))
-    near0, far0 = halo(
-        *call(
-            early_lines_kernel,
-            "early_lines",
-            (early,) * 2,
-            "vva",
-            [],
-            0.01,
-            (first_half, column, queries),
-        )
-    )
-    late = shape((TLY, LANES, width))
-    second_half, near1, far1 = call(
+    def tiles(count):
+        return shape((count, LANES, width))
+
+    early = call(
+        early_line_kernel,
+        "early_line",
+        tiles(TLY + 1),
+        "vva",
+        [],
+        0.01,
+        (first_half, column, queries),
+    )
+    far0 = lax.ppermute(early, "tx", far_pairs)
+    second_half, near, far1 = call(
         combine_second_kernel,
         "combine_second",
-        (shape((TLX, TLY, LANES, width)), late, late),
-        "vvvva",
+        (shape((TLX, TLY, LANES, width)), tiles(2 * TLY + 1), tiles(TLY)),
+        "vvvvvva",
         [],
         0.01,
-        (own1, other1, inducing, first_proj, queries),
-    )
-    near1, far1 = halo(near1, far1)
+        (own1, other1, inducing, first_proj, first_half, column, early),
+    )
+    near = lax.ppermute(near, "tx", near_pairs)
+    far1 = lax.ppermute(far1, "tx", far_pairs)
 
     keys, values = call(
         mixture_kernel,
         "mix_tiles",
         (shape((blocks, HEADS * LANES, 4 * LANES)), shape((blocks, HEADS * LANES, 5 * LANES))),
-        "v" * 9,
+        "v" * 8,
         [
             VMEM((TLX + 2, tall + 2, LANES, width), BF),
             VMEM((6 * LANES, 2 * LANES), BF),
             VMEM((2, 4 * LANES, 2 * LANES), BF),
         ],
         1,
-        (first_half, column, second_half, near0, far0, near1, far1, second_proj, mixing),
+        (first_half, column, second_half, near, far0, far1, second_proj, mixing),
     )
 
     result = call(

time: 87 us -> 90.1 us (1.036)
  Pallas kernels: 32.7 us -> 35.1 us
  blocking collectives: 24.5 us -> 25.5 us
    pallas_call x11, Pallas kernels: 32.7 us -> 35.1 us  [call(): pl.pallas_call(kernel, out_shape=out_shape, in_specs=[pl.BlockSpec(memory...]
    all_to_all x1, blocking collectives: 24.5 us -> 25.5 us  [exchange(): lax.all_to_all(rows, ('tx', 'zl'), split_axis=0, concat_axis=0, tiled=True)]
    ppermute x4 -> x3, starting transfers between devices: 2.08 us -> 1.44 us  [the longest x1 0.66 us: body(): far1 = lax.ppermute(far1, 'tx', far_pairs)]
  transfers between devices with their start and end apart: 9 -> 8, of which waited for: 5 -> 4; matrix products, arithmetic and copies ran while one was open for 0% -> 0% of each run, Pallas kernels for 16% -> 15%
where the time goes in v9:
time: 90.1 us; the launch traced here: 89.7 us
  Pallas kernels  35.1 us (39%)
  blocking collectives  25.5 us (28%)
  starting transfers between devices  15.9 us (18%)
  waiting for transfers between devices  12.2 us (14%)
    pallas_call x11, Pallas kernels, call(): pl.pallas_call(kernel, out_shape=out_shape, in_specs=[pl.BlockSpec(memory...  35.1 us
    all_to_all x1, blocking collectives, exchange(): lax.all_to_all(rows, ('tx', 'zl'), split_axis=0, concat_axis=0, tiled=True)  25.5 us
    all_to_all x2, starting transfers between devices, exchange(): lax.all_to_all(rows, ('tx', 'zl'), split_axis=0, concat_axis=0, tiled=True)  10.1 us
    all_to_all x2, waiting for transfers between devices, exchange(): lax.all_to_all(rows, ('tx', 'zl'), split_axis=0, concat_axis=0, tiled=True)  8.81 us
    ppermute x3, starting transfers between devices, swap(): return lax.ppermute(value, ('zh', 'zl'), steps)  4.39 us
    ppermute x3, waiting for transfers between devices, swap(): return lax.ppermute(value, ('zh', 'zl'), steps)  3.41 us
  transfers between devices with their start and end apart: 8, of which 4 were waited for; matrix products, arithmetic and copies ran while one was open for 0% of the time, Pallas kernels for 15%

profile of v9, /device:TPU:0, one launch (start us, length us, event | category | flops | bytes accessed | tf_op | source)
XLA Modules:
  0.0 89.7 jit_solution(13347264066009971235)
XLA Ops:
  0.0 0.0 copy-start.4
  0.0 0.0 copy-start.5
  0.0 0.0 copy-start.7
  0.0 0.0 copy-start.8
  0.0 7.1 %encode_first.1 = (bf16[16,128,128]{2,1,0:T(8,128)(2,1)}, s32[32,128]{1,0:T(8,128)}) custom-call(bf16[4096,128]{1,0:T(8,128)(2,1)} %points_ref.1, bf16[128,512]{1,0:T(8,128)(2,1)} %w1_ref.1, bf16[1,512,512]{2,1,0:T(8,128)(2,1)} %w2_ref.1, bf16[512,128]{1,0:T(8,128)(2,1)} %w3_ref.1, s32[32,128]{1,0:T(8,128)} %counts_ref.7, s32[32,128]{1,0:T(8,128)} %bitcast.1), custom_call_target="tpu_custom_call" | custom-call | flops 4000000000 | bytes 8000000 | tf_op jit(solution)/shard_map/encode_first/pallas_call | solution.py:545
  7.1 6.3 %all-to-all-start = ((bf16[16,128,128]{2,1,0:T(8,128)(2,1)}), bf16[16,128,128]{2,1,0:T(8,128)(2,1)S(1)}, u32[]{:S(2)}, u32[]{:S(2)}) async-start(bf16[16,128,128]{2,1,0:T(8,128)(2,1)} %get-tuple-element.20), calls=%async_computation | async-start | bytes 1048576 | tf_op jit(solution)/shard_map/all_to_all | solution.py:623
  13.4 0.0 copy-done.4
  13.4 0.0 copy-done.5
  13.4 0.0 copy-done.7
  13.4 0.0 copy-done.8
  13.4 0.0 copy-start.9
  13.5 0.7 copy-done.9
  14.2 0.0 copy-start
  14.2 0.0 copy-start.2
  14.2 5.3 %encode_second.1 = bf16[16,128,128]{2,1,0:T(8,128)(2,1)} custom-call(bf16[4096,128]{1,0:T(8,128)(2,1)S(1)} %copy-done.4, bf16[128,512]{1,0:T(8,128)(2,1)S(1)} %copy-done.7, bf16[1,512,512]{2,1,0:T(8,128)(2,1)S(1)} %copy-done.5, bf16[512,128]{1,0:T(8,128)(2,1)S(1)} %copy-done.8, s32[32,128]{1,0:T(8,128)S(1)} %copy-done.9), custom_call_target="tpu_custom_call" | custom-call | flops 3000000000 | bytes 6000000 | tf_op jit(solution)/shard_map/encode_second/pallas_call | solution.py:545
  19.5 2.6 %all-to-all-done.rows_ref.rows0_ref = bf16[16,128,128]{2,1,0:T(8,128)(2,1)S(1)} async-done(((bf16[16,128,128]{2,1,0:T(8,128)(2,1)}), bf16[16,128,128]{2,1,0:T(8,128)(2,1)S(1)}, u32[]{:S(2)}, u32[]{:S(2)}) %all-to-all-start) | async-done | bytes 524320 | tf_op jit(solution)/shard_map/all_to_all | solution.py:623
  22.2 3.8 %all-to-all-start.1 = ((bf16[16,128,128]{2,1,0:T(8,128)(2,1)}), bf16[16,128,128]{2,1,0:T(8,128)(2,1)S(1)}, u32[]{:S(2)}, u32[]{:S(2)}) async-start(bf16[16,128,128]{2,1,0:T(8,128)(2,1)} %encode_second.1), calls=%async_computation.1 | async-start | bytes 1048576 | tf_op jit(solution)/shard_map/all_to_all | solution.py:623
  26.0 0.0 copy-done
  26.0 0.0 copy-done.2
  26.0 0.0 copy-done.3
  26.0 2.7 %partial_first.1 = (f32[528,128]{1,0:T(8,128)S(1)}, bf16[528,128]{1,0:T(8,128)(2,1)S(1)}, bf16[256,128]{1,0:T(8,128)(2,1)S(1)}, bf16[128,128]{1,0:T(8,128)(2,1)S(1)}) custom-call(bf16[16,128,128]{2,1,0:T(8,128)(2,1)S(1)} %all-to-all-done.rows_ref.rows0_ref, s32[32,128]{1,0:T(8,128)S(1)} %copy-done.3, bf16[128,128]{1,0:T(8,128)(2,1)S(1)} %copy-done.2, ...), custom_call_target="tpu_custom_call" | custom-call | flops 1500000000 | bytes 3000000 | tf_op jit(solution)/shard_map/partial_first/pallas_call | solution.py:545
  28.7 0.0 copy-start.1
  28.7 2.7 %collective-permute-start = (bf16[528,128]{1,0:T(8,128)(2,1)S(1)}, bf16[528,128]{1,0:T(8,128)(2,1)S(1)}, u32[]{:S(2)}, u32[]{:S(2)}) collective-permute-start(bf16[528,128]{1,0:T(8,128)(2,1)S(1)} %get-tuple-element.23), channel_id=1, source_target_pairs={{0,2},{1,3},{2,0},{3,1},{4,6},{5,7},{6,4},{7,5},{8,10},{9,11},{10,... | collective-permute-start | bytes 405512 | tf_op jit(solution)/shard_map/ppermute | solution.py:649
  31.4 6.2 %all-to-all-done.1.rows_ref.rows1_ref = bf16[16,128,128]{2,1,0:T(8,128)(2,1)S(1)} async-done(((bf16[16,128,128]{2,1,0:T(8,128)(2,1)}), bf16[16,128,128]{2,1,0:T(8,128)(2,1)S(1)}, u32[]{:S(2)}, u32[]{:S(2)}) %all-to-all-start.1) | async-done | bytes 524320 | tf_op jit(solution)/shard_map/all_to_all | solution.py:623
  37.6 2.7 %partial_second.1 = (f32[528,128]{1,0:T(8,128)S(1)}, bf16[528,128]{1,0:T(8,128)(2,1)S(1)}) custom-call(bf16[16,128,128]{2,1,0:T(8,128)(2,1)S(1)} %all-to-all-done.1.rows_ref.rows1_ref, s32[32,128]{1,0:T(8,128)S(1)} %copy-done.3, bf16[256,128]{1,0:T(8,128)(2,1)S(1)} %get-tuple-element.24.rest_0_, bf16[128,128]{1,0:T(8,128)(2,1)S(1)} %get-tuple-element.25.rest_1_, ...), custom_call_target="tpu_custom_call" | custom-call | flops 1500000000 | bytes 3000000 | tf_op jit(solution)/shard_map/partial_second/pallas_call | solution.py:545
  40.3 0.2 collective-permute-start.2
  40.5 0.0 collective-permute-done.other_ref
  40.5 0.3 combine_first.1
  40.8 0.0 copy-start.6
  40.8 1.5 %collective-permute-start.1 = (bf16[2,128,128]{2,1,0:T(8,128)(2,1)S(1)}, bf16[2,128,128]{2,1,0:T(8,128)(2,1)S(1)}, u32[]{:S(2)}, u32[]{:S(2)}) collective-permute-start(bf16[2,128,128]{2,1,0:T(8,128)(2,1)S(1)} %get-tuple-element.27.column_any), channel_id=1, source_target_pairs={{0,1},{1,0},{2,3},{3,2},{4,5},{5,4},{6,7},{7,6},{8,9},{9,8},{10,11... | collective-permute-start | bytes 196616 | tf_op jit(solution)/shard_map/ppermute | solution.py:649
  42.3 0.0 copy-done.1
  42.3 2.7 %point_queries.1.query_any.query_ref = bf16[2,16,128,512]{3,2,1,0:T(8,128)(2,1)S(1)} custom-call(bf16[16,128,128]{2,1,0:T(8,128)(2,1)S(1)} %all-to-all-done.rows_ref.rows0_ref, bf16[16,128,128]{2,1,0:T(8,128)(2,1)S(1)} %all-to-all-done.1.rows_ref.rows1_ref, s32[32,128]{1,0:T(8,128)S(1)} %copy-done.3, bf16[4,128,128]{2,1,0:T(8,128)(2,1)S(1)} %copy-done.1, ...), custom_call_target="tpu_custom_call" | custom-call | flops 5000000 | bytes 10000 | tf_op jit(solution)/shard_map/point_queries/pallas_call | solution.py:545
  45.0 0.4 collective-permute-done.1.column_ref
  45.5 3.0 %collective-permute-done.2.other_ref = bf16[528,128]{1,0:T(8,128)(2,1)S(1)} collective-permute-done((bf16[528,128]{1,0:T(8,128)(2,1)S(1)}, bf16[528,128]{1,0:T(8,128)(2,1)S(1)}, u32[]{:S(2)}, u32[]{:S(2)}) %collective-permute-start.2) | collective-permute-done | bytes 135200 | tf_op jit(solution)/shard_map/ppermute | solution.py:649
  48.5 0.3 combine_second.1
  48.8 0.1 collective-permute-start.3
  48.9 0.7 collective-permute-start.4
  49.6 0.7 collective-permute-start.5
  50.2 0.0 collective-permute-done.5.far1_ref
  50.2 0.0 collective-permute-done.4.far0_ref
  50.2 0.0 collective-permute-done.3.near_ref
  50.3 0.0 copy-done.6
  50.3 0.9 %mix_tiles.1 = (bf16[2,256,512]{2,1,0:T(8,128)(2,1)S(1)}, bf16[2,256,640]{2,1,0:T(8,128)(2,1)S(1)}) custom-call(bf16[2,2,128,128]{3,2,1,0:T(8,128)(2,1)S(1)} %get-tuple-element.28.first_ref, bf16[2,128,128]{2,1,0:T(8,128)(2,1)S(1)} %collective-permute-done.1.column_ref, bf16[2,2,128,128]{3,2,1,0:T(8,128)(2,1)S(1)} %get-tuple-element.30.second_ref, ...), custom_call_target="tpu_custom_call" | custom-call | flops 500000000 | bytes 1000000 | tf_op jit(solution)/shard_map/mix_tiles/pallas_call | solution.py:545
  51.2 0.0 copy-start.10
  51.2 5.5 %attend_points.1 = bf16[16,2,128,128]{3,2,1,0:T(8,128)(2,1)S(1)} custom-call(bf16[16,128,128]{2,1,0:T(8,128)(2,1)S(1)} %all-to-all-done.rows_ref.rows0_ref, bf16[16,128,128]{2,1,0:T(8,128)(2,1)S(1)} %all-to-all-done.1.rows_ref.rows1_ref, bf16[2,16,128,512]{3,2,1,0:T(8,128)(2,1)S(1)} %point_queries.1.query_any.query_ref, s32[32,128]{1,0:T(8,128)S(1)} %copy-done.3, ...), custom_call_target="tpu_custom_call" | custom-call | flops 3500000000 | bytes 7000000 | tf_op jit(solution)/shard_map/attend_points/pallas_call | solution.py:545
  56.7 25.5 %all_to_all.15.rows_ref = bf16[16,2,128,128]{3,2,1,0:T(8,128)(2,1)S(1)} all-to-all(bf16[16,2,128,128]{3,2,1,0:T(8,128)(2,1)S(1)} %attend_points.1), channel_id=1, replica_groups=mesh['tx'=8,'zh'=2,'zl'=2] {'tx','zl'}, dimensions={0} | all-to-all | bytes 2097152 | tf_op jit(solution)/shard_map/all_to_all | solution.py:623
  82.2 0.0 copy-done.10
  82.2 7.5 %scatter_rows.1 = bf16[4096,128]{1,0:T(8,128)(2,1)} custom-call(bf16[16,2,128,128]{3,2,1,0:T(8,128)(2,1)S(1)} %all_to_all.15.rows_ref, s32[32,128]{1,0:T(8,128)S(1)} %copy-done.10), custom_call_target="tpu_custom_call" | custom-call | flops 2500000000 | bytes 5000000 | tf_op jit(solution)/shard_map/scatter_rows/pallas_call | solution.py:545
  (2 shorter events, 0.0 us)
Async XLA Ops:
  0.0 13.4 %copy-start.4 = (bf16[4096,128]{1,0:T(8,128)(2,1)S(1)}, bf16[4096,128]{1,0:T(8,128)(2,1)}, u32[]{:S(2)}) copy-start(bf16[4096,128]{1,0:T(8,128)(2,1)} %points_ref.1) | copy-start | bytes 3145732
  0.0 13.4 %copy-start.5 = (bf16[1,512,512]{2,1,0:T(8,128)(2,1)S(1)}, bf16[1,512,512]{2,1,0:T(8,128)(2,1)}, u32[]{:S(2)}) copy-start(bf16[1,512,512]{2,1,0:T(8,128)(2,1)} %w2_ref.1) | copy-start | bytes 1572868
  0.0 13.4 %copy-start.7 = (bf16[128,512]{1,0:T(8,128)(2,1)S(1)}, bf16[128,512]{1,0:T(8,128)(2,1)}, u32[]{:S(2)}) copy-start(bf16[128,512]{1,0:T(8,128)(2,1)} %w1_ref.1) | copy-start | bytes 393220
  0.0 13.4 %copy-start.8 = (bf16[512,128]{1,0:T(8,128)(2,1)S(1)}, bf16[512,128]{1,0:T(8,128)(2,1)}, u32[]{:S(2)}) copy-start(bf16[512,128]{1,0:T(8,128)(2,1)} %w3_ref.1) | copy-start | bytes 393220
  7.1 15.1 %all-to-all-start = ((bf16[16,128,128]{2,1,0:T(8,128)(2,1)}), bf16[16,128,128]{2,1,0:T(8,128)(2,1)S(1)}, u32[]{:S(2)}, u32[]{:S(2)}) async-start(bf16[16,128,128]{2,1,0:T(8,128)(2,1)} %get-tuple-element.20), calls=%async_computation | async-start | bytes 1048576 | tf_op jit(solution)/shard_map/all_to_all | solution.py:623
  13.4 0.7 copy-start.9
  14.2 11.8 %copy-start = (bf16[4,128,128]{2,1,0:T(8,128)(2,1)S(1)}, bf16[4,128,128]{2,1,0:T(8,128)(2,1)}, u32[]{:S(2)}) copy-start(bf16[4,128,128]{2,1,0:T(8,128)(2,1)} %proj_ref.7) | copy-start | bytes 393220
  14.2 11.8 %copy-start.2 = (bf16[128,128]{1,0:T(8,128)(2,1)S(1)}, bf16[128,128]{1,0:T(8,128)(2,1)}, u32[]{:S(2)}) copy-start(bf16[128,128]{1,0:T(8,128)(2,1)} %inducing_ref.3) | copy-start | bytes 98308
  14.2 11.8 %copy-start.3 = (s32[32,128]{1,0:T(8,128)S(1)}, s32[32,128]{1,0:T(8,128)}, u32[]{:S(2)}) copy-start(s32[32,128]{1,0:T(8,128)} %counts_ref.7) | copy-start | bytes 49156
  22.2 15.4 %all-to-all-start.1 = ((bf16[16,128,128]{2,1,0:T(8,128)(2,1)}), bf16[16,128,128]{2,1,0:T(8,128)(2,1)S(1)}, u32[]{:S(2)}, u32[]{:S(2)}) async-start(bf16[16,128,128]{2,1,0:T(8,128)(2,1)} %encode_second.1), calls=%async_computation.1 | async-start | bytes 1048576 | tf_op jit(solution)/shard_map/all_to_all | solution.py:623
  28.7 13.6 %copy-start.1 = (bf16[4,128,128]{2,1,0:T(8,128)(2,1)S(1)}, bf16[4,128,128]{2,1,0:T(8,128)(2,1)}, u32[]{:S(2)}) copy-start(bf16[4,128,128]{2,1,0:T(8,128)(2,1)} %proj_ref.9) | copy-start | bytes 393220
  28.7 11.8 %collective-permute-start = (bf16[528,128]{1,0:T(8,128)(2,1)S(1)}, bf16[528,128]{1,0:T(8,128)(2,1)S(1)}, u32[]{:S(2)}, u32[]{:S(2)}) collective-permute-start(bf16[528,128]{1,0:T(8,128)(2,1)S(1)} %get-tuple-element.23), channel_id=1, source_target_pairs={{0,2},{1,3},{2,0},{3,1},{4,6},{5,7},{6,4},{7,5},{8,10},{9,11},{10,... | collective-permute-start | bytes 405512 | tf_op jit(solution)/shard_map/ppermute | solution.py:649
  40.3 8.2 %collective-permute-start.2 = (bf16[528,128]{1,0:T(8,128)(2,1)S(1)}, bf16[528,128]{1,0:T(8,128)(2,1)S(1)}, u32[]{:S(2)}, u32[]{:S(2)}) collective-permute-start(bf16[528,128]{1,0:T(8,128)(2,1)S(1)} %get-tuple-element.26.after_any), channel_id=1, source_target_pairs={{0,2},{1,3},{2,0},{3,1},{4,6},{5,7},{6,4},{7,5},{8,10},{9,11},{10,... | collective-permute-start | bytes 405512 | tf_op jit(solution)/shard_map/ppermute | solution.py:649
  40.8 9.5 %copy-start.6 = (bf16[8,128,128]{2,1,0:T(8,128)(2,1)S(1)}, bf16[8,128,128]{2,1,0:T(8,128)(2,1)}, u32[]{:S(2)}) copy-start(bf16[8,128,128]{2,1,0:T(8,128)(2,1)} %mixing_ref.1) | copy-start | bytes 786436
  40.8 4.7 %collective-permute-start.1 = (bf16[2,128,128]{2,1,0:T(8,128)(2,1)S(1)}, bf16[2,128,128]{2,1,0:T(8,128)(2,1)S(1)}, u32[]{:S(2)}, u32[]{:S(2)}) collective-permute-start(bf16[2,128,128]{2,1,0:T(8,128)(2,1)S(1)} %get-tuple-element.27.column_any), channel_id=1, source_target_pairs={{0,1},{1,0},{2,3},{3,2},{4,5},{5,4},{6,7},{7,6},{8,9},{9,8},{10,11... | collective-permute-start | bytes 196616 | tf_op jit(solution)/shard_map/ppermute | solution.py:649
  48.8 1.5 %collective-permute-start.3 = (bf16[5,128,128]{2,1,0:T(8,128)(2,1)S(1)}, bf16[5,128,128]{2,1,0:T(8,128)(2,1)S(1)}, u32[]{:S(2)}, u32[]{:S(2)}) collective-permute-start(bf16[5,128,128]{2,1,0:T(8,128)(2,1)S(1)} %get-tuple-element.31), channel_id=1, source_target_pairs={{0,4},{4,0},{8,12},{12,8},{16,20},{20,16},{24,28},{28,24},{1,5},{5... | collective-permute-start | bytes 491528 | tf_op jit(solution)/shard_map/ppermute | solution.py:706
  48.9 1.3 %collective-permute-start.4 = (bf16[3,128,128]{2,1,0:T(8,128)(2,1)S(1)}, bf16[3,128,128]{2,1,0:T(8,128)(2,1)S(1)}, u32[]{:S(2)}, u32[]{:S(2)}) collective-permute-start(bf16[3,128,128]{2,1,0:T(8,128)(2,1)S(1)} %early_line.1.query_any), channel_id=1, source_target_pairs={{4,8},{8,4},{12,16},{16,12},{20,24},{24,20},{5,9},{9,5},{13,17},{1... | collective-permute-start | bytes 294920 | tf_op jit(solution)/shard_map/ppermute | solution.py:696
  49.6 0.7 collective-permute-start.5
  51.2 31.0 %copy-start.10 = (s32[32,128]{1,0:T(8,128)S(1)}, s32[32,128]{1,0:T(8,128)}, u32[]{:S(2)}) copy-start(s32[32,128]{1,0:T(8,128)} %get-tuple-element.21.index_any.index_ref) | copy-start | bytes 49156

commit v10 on v7

--- a/solution.py
+++ b/solution.py
@@ -227,7 +227,7 @@
 def partial_kernel(half_id, along_y, rows_ref, counts_ref, *rest):
     num_ref = rest[-1]
     if half_id:
-        query_ref, wv_ref, proj_ref, own_ref, send_ref = rest[:-1]
+        query_ref, wv_ref, proj_ref, before_any, own_ref, send_ref = rest[:-1]
     else:
         inducing_ref, proj_ref, own_ref, send_ref, query_ref, wv_ref = rest[:-1]
     members, quota, width = rows_ref.shape
@@ -295,24 +295,24 @@
     return n0, n1, n1 + counts_ref[s, base + grid_y]
 
 
-def queries_kernel(along_y, rows0_ref, rows1_ref, counts_ref, proj_ref, column_any, out_ref):
+def queries_kernel(half_id, along_y, rows_ref, counts_ref, proj_ref, *rest):
+    out_ref = rest[-1]
     ones = head_ones()
-    for half_id, rows_ref in enumerate((rows0_ref, rows1_ref)):
-        members, quota, width = rows_ref.shape
-        group = min(GROUP_ROWS // quota, members)
-        row = lax.broadcasted_iota(jnp.int32, (quota, LANES), 0)
-        for c in range(members // group):
-            x = jnp.concatenate([rows_ref[c * group + k] for k in range(group)], axis=0)
-            query = unit(dot(x, proj_ref[0]), ones)
-            pieces = pieces_of(c * group, group, half_id, along_y)
-            for k in range(group):
-                bounds = row_bounds(pieces[k], counts_ref, along_y * TLY)
-                past = [row >= b for b in bounds]
-                mine = query[k * quota : (k + 1) * quota]
-                masks = (~past[0], past[0] & ~past[1], past[1] & ~past[2], past[2])
-                out_ref[half_id, c * group + k] = jnp.concatenate(
-                    [jnp.where(m, mine, 0.0).astype(BF) for m in masks], axis=1
-                )
+    members, quota, width = rows_ref.shape
+    group = min(GROUP_ROWS // quota, members)
+    row = lax.broadcasted_iota(jnp.int32, (quota, LANES), 0)
+    for c in range(members // group):
+        x = jnp.concatenate([rows_ref[c * group + k] for k in range(group)], axis=0)
+        query = unit(dot(x, proj_ref[0]), ones)
+        pieces = pieces_of(c * group, group, half_id, along_y)
+        for k in range(group):
+            bounds = row_bounds(pieces[k], counts_ref, along_y * TLY)
+            past = [row >= b for b in bounds]
+            mine = query[k * quota : (k + 1) * quota]
+            masks = (~past[0], past[0] & ~past[1], past[1] & ~past[2], past[2])
+            out_ref[c * group + k] = jnp.concatenate(
+                [jnp.where(m, mine, 0.0).astype(BF) for m in masks], axis=1
+            )
 
 
 def summarize(half_id, own_ref, other_ref, inducing_ref, proj_ref, store):
@@ -466,37 +466,52 @@
             key_ref[b, h * LANES : (h + 1) * LANES, :] = jnp.concatenate(
                 [jnp.where(mine, keys[s], 0.0) for s in spans], axis=1
             ).astype(BF)
-            flags = jnp.broadcast_to(jnp.where(mine, 1.0, 0.0), (LANES, LANES))
             value_ref[b, h * LANES : (h + 1) * LANES, :] = jnp.concatenate(
-                [jnp.where(mine, values[s], 0.0) for s in spans] + [flags], axis=1
+                [jnp.where(mine, values[s], 0.0) for s in spans], axis=1
             ).astype(BF)
 
 
 def attend_kernel(
-    along_y, rows0_ref, rows1_ref, query_ref, counts_ref, key_ref, value_ref, proj_ref, out_ref
+    along_y,
+    rows0_ref,
+    rows1_ref,
+    query0_ref,
+    query1_ref,
+    counts_ref,
+    key_ref,
+    value_ref,
+    proj_ref,
+    out_ref,
 ):
     members, quota, width = rows0_ref.shape
     group = min(GROUP_ROWS // quota, members)
     row = lax.broadcasted_iota(jnp.int32, (quota, LANES), 0)
-    for half_id, rows_ref in enumerate((rows0_ref, rows1_ref)):
+    left = lax.broadcasted_iota(jnp.int32, (1, LANES), 1) < LANES // HEADS
+    for half_id, (rows_ref, query_ref) in enumerate(
+        ((rows0_ref, query0_ref), (rows1_ref, query1_ref))
+    ):
         block = block_of(half_id, lax.axis_index("zl"))
         for c in range(members // group):
-            expanded = jnp.concatenate(
-                [query_ref[half_id, c * group + k] for k in range(group)], axis=0
-            )
+            expanded = jnp.concatenate([query_ref[c * group + k] for k in range(group)], axis=0)
             scores = dot_t(expanded, key_ref[block])
-            weights = jnp.exp2(scores * (sharpness * math.log2(math.e))).astype(BF)
-            every = dot(weights, value_ref[block])
+            weights = jnp.exp2(scores * (sharpness * math.log2(math.e)))
+            totals = [
+                jnp.sum(weights[:, h * LANES : (h + 1) * LANES], axis=1, keepdims=True)
+                for h in range(HEADS)
+            ]
+            every = dot(weights.astype(BF), value_ref[block])
             pieces = pieces_of(c * group, group, half_id, along_y)
             attended = []
             for k in range(group):
                 bounds = row_bounds(pieces[k], counts_ref, along_y * TLY)
-                part = every[k * quota : (k + 1) * quota]
+                span = slice(k * quota, (k + 1) * quota)
+                part = every[span]
                 picked = part[:, :LANES]
                 for t, bound in enumerate(bounds):
                     tile = part[:, (t + 1) * LANES : (t + 2) * LANES]
                     picked = jnp.where(row >= bound, tile, picked)
-                attended.append(quotient(picked, part[:, 4 * LANES :]).astype(BF))
+                total = jnp.where(left, totals[0][span], totals[1][span])
+                attended.append(quotient(picked, total).astype(BF))
             x = jnp.concatenate([rows_ref[c * group + k] for k in range(group)], axis=0)
             added = dot(jnp.concatenate(attended, axis=0), proj_ref[3])
             result = (x.astype(F32) + added).astype(BF)
@@ -504,7 +519,7 @@
                 out_ref[c * group + k, half_id] = result[k * quota : (k + 1) * quota]
 
 
-def scatter_kernel(rows_ref, index_ref, out_ref, wide_ref, part_ref):
+def scatter_kernel(rows_ref, index_ref, out_hbm, wide_ref, part_ref, out_ref, sems):
     chunk = part_ref.shape[0]
     members, halves, quota, width = rows_ref.shape
     group = chunk // (halves * quota)
@@ -520,13 +535,22 @@
         return carry
 
     lax.fori_loop(0, members // group, step, 0)
-    out_ref[...] = wide_ref[...].astype(BF)
-
-
-def call(kernel, name, out_shape, in_specs, scratch, micros, operands, megabytes=20, **more):
+    count = sems.shape[0]
+    size = wide_ref.shape[0] // count
+    copies = []
+    for k in range(count):
+        span = pl.ds(k * size, size)
+        out_ref[span, :] = wide_ref[span, :].astype(BF)
+        copies.append(pltpu.make_async_copy(out_ref.at[span], out_hbm.at[span], sems.at[k]))
+        copies[k].start()
+    for copy in copies:
+        copy.wait()
+
+
+def call(kernel, name, out_shape, in_specs, scratch, micros, operands, megabytes=20, out_space=pltpu.VMEM):
     spaces = {"v": pltpu.VMEM, "s": pltpu.SMEM, "a": pl.ANY}
     many = isinstance(out_shape, tuple)
-    whole = pl.BlockSpec(memory_space=pltpu.VMEM)
+    whole = pl.BlockSpec(memory_space=out_space)
     return pl.pallas_call(
         kernel,
         out_shape=out_shape,
@@ -538,7 +562,6 @@
             flops=int(micros * 5e8), bytes_accessed=int(micros * 1e6), transcendentals=0
         ),
         name=name,
-        **more,
     )(*operands)
 
 
@@ -634,14 +657,23 @@
         return lax.ppermute(value, ("zh", "zl"), steps)
 
     other0 = swap(send0, True, False)
+    query0 = call(
+        functools.partial(queries_kernel, 0, along_y),
+        "queries_first",
+        shape((members, quota, 4 * width)),
+        "vsva",
+        [],
+        1,
+        (rows0, counts, second_proj, send0),
+    )
     own1, send1 = call(
         functools.partial(partial_kernel, 1, along_y),
         "partial_second",
         parts,
-        "vsvvv",
+        "vsvvva",
         sums,
         3,
-        (rows1, counts, first_queries, value_weight, first_proj),
+        (rows1, counts, first_queries, value_weight, first_proj, query0),
     )
     other1 = swap(send1, True, False)
     first_half, border = call(
@@ -654,14 +686,14 @@
         (own0, other0, inducing, first_proj, send1),
     )
     column = swap(border, False, True)
-    queries = call(
-        functools.partial(queries_kernel, along_y),
-        "point_queries",
-        shape((2, members, quota, 4 * width)),
-        "vvsva",
+    query1 = call(
+        functools.partial(queries_kernel, 1, along_y),
+        "queries_second",
+        shape((members, quota, 4 * width)),
+        "vsva",
         [],
         0.01,
-        (rows0, rows1, counts, second_proj, border),
+        (rows1, counts, second_proj, border),
     )
     near_pairs = [(i, i ^ 1) for i in range(along_x)]
     far_pairs = [(i, ((i + 1) ^ 1) - 1) for i in range(1, along_x - 1)]
@@ -679,7 +711,7 @@
             "vva",
             [],
             0.01,
-            (first_half, column, queries),
+            (first_half, column, query1),
         )
     )
     late = shape((TLY, LANES, width))
@@ -690,14 +722,14 @@
         "vvvva",
         [],
         0.01,
-        (own1, other1, inducing, first_proj, queries),
+        (own1, other1, inducing, first_proj, query1),
     )
     near1, far1 = halo(near1, far1)
 
     keys, values = call(
         mixture_kernel,
         "mix_tiles",
-        (shape((blocks, HEADS * LANES, 4 * LANES)), shape((blocks, HEADS * LANES, 5 * LANES))),
+        (shape((blocks, HEADS * LANES, 4 * LANES)), shape((blocks, HEADS * LANES, 4 * LANES))),
         "v" * 9,
         [
             VMEM((TLX + 2, tall + 2, LANES, width), BF),
@@ -712,19 +744,25 @@
         functools.partial(attend_kernel, along_y),
         "attend_points",
         shape((members, 2, quota, width)),
-        "vvvsvvv",
+        "vvvvsvvv",
         [],
         7,
-        (rows0, rows1, queries, counts, keys, values, second_proj),
+        (rows0, rows1, query0, query1, counts, keys, values, second_proj),
     )
     return call(
         scatter_kernel,
         "scatter_rows",
         shape((point_count, width)),
         "vs",
-        [VMEM((point_count, width), F32), VMEM((512, width), F32)],
+        [
+            VMEM((point_count, width), F32),
+            VMEM((512, width), F32),
+            VMEM((point_count, width), BF),
+            pltpu.SemaphoreType.DMA((4,)),
+        ],
         5,
         (exchange(result), index),
+        out_space=pl.ANY,
     )
 
 

time: 87 us -> 88.1 us (1.013)
  local copies, waits for them, and re-layouts: 0.75 us -> 4.99 us
  waiting for transfers between devices: 11.8 us -> 7.58 us
  blocking collectives: 24.5 us -> 22.8 us
  starting transfers between devices: 16.6 us -> 18.2 us
    all_to_all x2, waiting for transfers between devices: 8.91 us -> 3.97 us  [exchange(): lax.all_to_all(rows, ('tx', 'zl'), split_axis=0, concat_axis=0, tiled=True)]
    unnamed x22 -> x42, local copies, waits for them, and re-layouts: 0.75 us -> 4.99 us
    all_to_all x1, blocking collectives: 24.5 us -> 22.8 us  [exchange(): lax.all_to_all(rows, ('tx', 'zl'), split_axis=0, concat_axis=0, tiled=True)]
    ppermute x2, starting transfers between devices: 0.76 us -> 1.87 us  [halo(): return (lax.ppermute(near, 'tx', near_pairs), far)]
    pallas_call x11 -> x12, Pallas kernels: 32.7 us -> 33.4 us  [call(): pl.pallas_call(kernel, out_shape=out_shape, in_specs=[pl.BlockSpec(memory...]
  transfers between devices with their start and end apart: 9 -> 9, of which waited for: 5 -> 4; matrix products, arithmetic and copies ran while one was open for 0% -> 0% of each run, Pallas kernels for 16% -> 18%
where the time goes in v10:
time: 88.1 us; the launch traced here: 87.4 us
  Pallas kernels  33.4 us (38%)
  blocking collectives  22.8 us (26%)
  starting transfers between devices  18.2 us (21%)
  waiting for transfers between devices  7.58 us (9%)
  local copies, waits for them, and re-layouts  4.99 us (6%)
    pallas_call x12, Pallas kernels, call(): pl.pallas_call(kernel, out_shape=out_shape, in_specs=[pl.BlockSpec(memory...  33.4 us
    all_to_all x1, blocking collectives, exchange(): lax.all_to_all(rows, ('tx', 'zl'), split_axis=0, concat_axis=0, tiled=True)  22.8 us
    all_to_all x2, starting transfers between devices, exchange(): lax.all_to_all(rows, ('tx', 'zl'), split_axis=0, concat_axis=0, tiled=True)  10.1 us
    unnamed x42, local copies, waits for them, and re-layouts  4.99 us
    ppermute x3, starting transfers between devices, swap(): return lax.ppermute(value, ('zh', 'zl'), steps)  4.86 us
    all_to_all x2, waiting for transfers between devices, exchange(): lax.all_to_all(rows, ('tx', 'zl'), split_axis=0, concat_axis=0, tiled=True)  3.97 us
    ppermute x3, waiting for transfers between devices, swap(): return lax.ppermute(value, ('zh', 'zl'), steps)  3.36 us
    ppermute x2, starting transfers between devices, halo(): return (lax.ppermute(near, 'tx', near_pairs), far)  1.87 us
  transfers between devices with their start and end apart: 9, of which 4 were waited for; matrix products, arithmetic and copies ran while one was open for 0% of the time, Pallas kernels for 18%

profile of v10, /device:TPU:0, one launch (start us, length us, event | category | flops | bytes accessed | tf_op | source)
XLA Modules:
  0.0 87.4 jit_solution(6887781097783788940)
XLA Ops:
  0.0 7.1 %encode_first.1 = (bf16[16,128,128]{2,1,0:T(8,128)(2,1)}, s32[32,128]{1,0:T(8,128)}) custom-call(bf16[4096,128]{1,0:T(8,128)(2,1)} %points_ref.1, bf16[128,512]{1,0:T(8,128)(2,1)} %w1_ref.1, bf16[1,512,512]{2,1,0:T(8,128)(2,1)} %w2_ref.1, bf16[512,128]{1,0:T(8,128)(2,1)} %w3_ref.1, s32[32,128]{1,0:T(8,128)} %counts_ref.9, s32[32,128]{1,0:T(8,128)} %bitcast.1), custom_call_target="tpu_custom_call" | custom-call | flops 4000000000 | bytes 8000000 | tf_op jit(solution)/shard_map/encode_first/pallas_call | solution.py:554
  7.1 6.3 %all-to-all-start = ((bf16[16,128,128]{2,1,0:T(8,128)(2,1)}), bf16[16,128,128]{2,1,0:T(8,128)(2,1)S(1)}, u32[]{:S(2)}, u32[]{:S(2)}) async-start(bf16[16,128,128]{2,1,0:T(8,128)(2,1)} %get-tuple-element.22), calls=%async_computation | async-start | bytes 1048576 | tf_op jit(solution)/shard_map/all_to_all | solution.py:631
  13.5 0.0 copy-done.10
  13.5 0.0 copy-done.11
  13.5 0.7 copy-done.19
  14.2 5.2 %encode_second.1 = bf16[16,128,128]{2,1,0:T(8,128)(2,1)} custom-call(bf16[4096,128]{1,0:T(8,128)(2,1)S(1)} %copy-done.10, bf16[128,512]{1,0:T(8,128)(2,1)S(1)} %copy-done.13, bf16[1,512,512]{2,1,0:T(8,128)(2,1)S(1)} %copy-done.11, bf16[512,128]{1,0:T(8,128)(2,1)S(1)} %copy-done.14, s32[32,128]{1,0:T(8,128)S(1)} %copy-done.19), custom_call_target="tpu_custom_call" | custom-call | flops 3000000000 | bytes 6000000 | tf_op jit(solution)/shard_map/encode_second/pallas_call | solution.py:554
  19.5 2.7 %all-to-all-done.rows_ref.rows0_ref = bf16[16,128,128]{2,1,0:T(8,128)(2,1)S(1)} async-done(((bf16[16,128,128]{2,1,0:T(8,128)(2,1)}), bf16[16,128,128]{2,1,0:T(8,128)(2,1)S(1)}, u32[]{:S(2)}, u32[]{:S(2)}) %all-to-all-start) | async-done | bytes 524320 | tf_op jit(solution)/shard_map/all_to_all | solution.py:631
  22.2 3.8 %all-to-all-start.1 = ((bf16[16,128,128]{2,1,0:T(8,128)(2,1)}), bf16[16,128,128]{2,1,0:T(8,128)(2,1)S(1)}, u32[]{:S(2)}, u32[]{:S(2)}) async-start(bf16[16,128,128]{2,1,0:T(8,128)(2,1)} %encode_second.1), calls=%async_computation.1 | async-start | bytes 1048576 | tf_op jit(solution)/shard_map/all_to_all | solution.py:631
  26.0 0.0 copy-done.1
  26.0 0.0 copy-done.4
  26.0 0.0 copy-done.6
  26.0 0.0 copy-start
  26.1 0.0 copy-start.7
  26.1 2.7 %partial_first.1 = (f32[528,128]{1,0:T(8,128)S(1)}, bf16[528,128]{1,0:T(8,128)(2,1)S(1)}, bf16[256,128]{1,0:T(8,128)(2,1)S(1)}, bf16[128,128]{1,0:T(8,128)(2,1)S(1)}) custom-call(bf16[16,128,128]{2,1,0:T(8,128)(2,1)S(1)} %all-to-all-done.rows_ref.rows0_ref, s32[32,128]{1,0:T(8,128)S(1)} %copy-done.6, bf16[128,128]{1,0:T(8,128)(2,1)S(1)} %copy-done.4, ...), custom_call_target="tpu_custom_call" | custom-call | flops 1500000000 | bytes 3000000 | tf_op jit(solution)/shard_map/partial_first/pallas_call | solution.py:554
  28.8 0.0 copy-start.2
  28.8 0.7 copy-done.2
  29.5 0.6 copy-done.15
  30.1 0.6 copy-done.17
  30.7 2.6 %collective-permute-start = (bf16[528,128]{1,0:T(8,128)(2,1)S(1)}, bf16[528,128]{1,0:T(8,128)(2,1)}, u32[]{:S(2)}, u32[]{:S(2)}) collective-permute-start(bf16[528,128]{1,0:T(8,128)(2,1)S(1)} %get-tuple-element.24.rest_0_), channel_id=1, source_target_pairs={{0,2},{1,3},{2,0},{3,1},{4,6},{5,7},{6,4},{7,5},{8,10},{9,11},{10,... | collective-permute-start | bytes 405512 | tf_op jit(solution)/shard_map/ppermute | solution.py:657
  33.3 0.0 copy-done
  33.3 1.9 %queries_first.1.rest_3_.query0_ref = bf16[16,128,512]{2,1,0:T(8,128)(2,1)S(1)} custom-call(bf16[16,128,128]{2,1,0:T(8,128)(2,1)S(1)} %all-to-all-done.rows_ref.rows0_ref, s32[32,128]{1,0:T(8,128)S(1)} %copy-done.7, bf16[4,128,128]{2,1,0:T(8,128)(2,1)S(1)} %copy-done, bf16[528,128]{1,0:T(8,128)(2,1)S(1)} %get-tuple-element.24.rest_0_), custom_call_target="tpu_custom_call" | custom-call | flops 500000000 | bytes 1000000 | tf_op jit(solution)/shard_map/queries_first/pallas_call | solution.py:554
  35.2 1.2 %all-to-all-done.1.rows_ref.rows1_ref = bf16[16,128,128]{2,1,0:T(8,128)(2,1)S(1)} async-done(((bf16[16,128,128]{2,1,0:T(8,128)(2,1)}), bf16[16,128,128]{2,1,0:T(8,128)(2,1)S(1)}, u32[]{:S(2)}, u32[]{:S(2)}) %all-to-all-start.1) | async-done | bytes 524320 | tf_op jit(solution)/shard_map/all_to_all | solution.py:631
  36.5 0.7 copy-done.8
  37.2 0.8 copy-done.16
  38.0 0.8 copy-done.18
  38.8 2.7 %partial_second.1 = (f32[528,128]{1,0:T(8,128)S(1)}, bf16[528,128]{1,0:T(8,128)(2,1)S(1)}) custom-call(bf16[16,128,128]{2,1,0:T(8,128)(2,1)S(1)} %all-to-all-done.1.rows_ref.rows1_ref, s32[32,128]{1,0:T(8,128)S(1)} %copy-done.8, bf16[256,128]{1,0:T(8,128)(2,1)S(1)} %copy-done.16, bf16[128,128]{1,0:T(8,128)(2,1)S(1)} %copy-done.18, ...), custom_call_target="tpu_custom_call" | custom-call | flops 1500000000 | bytes 3000000 | tf_op jit(solution)/shard_map/partial_second/pallas_call | solution.py:554
  41.5 1.4 %collective-permute-start.2 = (bf16[528,128]{1,0:T(8,128)(2,1)S(1)}, bf16[528,128]{1,0:T(8,128)(2,1)S(1)}, u32[]{:S(2)}, u32[]{:S(2)}) collective-permute-start(bf16[528,128]{1,0:T(8,128)(2,1)S(1)} %get-tuple-element.28.after_any), channel_id=1, source_target_pairs={{0,2},{1,3},{2,0},{3,1},{4,6},{5,7},{6,4},{7,5},{8,10},{9,11},{10,... | collective-permute-start | bytes 405512 | tf_op jit(solution)/shard_map/ppermute | solution.py:657
  42.9 0.0 collective-permute-done.other_ref
  42.9 1.2 %combine_first.1 = (bf16[2,2,128,128]{3,2,1,0:T(8,128)(2,1)S(1)}, bf16[2,128,128]{2,1,0:T(8,128)(2,1)S(1)}) custom-call(f32[528,128]{1,0:T(8,128)S(1)} %copy-done.3, bf16[528,128]{1,0:T(8,128)(2,1)} %collective-permute-done.other_ref, bf16[128,128]{1,0:T(8,128)(2,1)S(1)} %copy-done.5, bf16[4,128,128]{2,1,0:T(8,128)(2,1)S(1)} %copy-done.1, ...), custom_call_target="tpu_custom_call" | custom-call | flops 5000000 | bytes 10000 | tf_op jit(solution)/shard_map/combine_first/pallas_call | solution.py:554
  44.1 0.9 collective-permute-start.1
  44.9 0.0 copy-done.9
  44.9 1.9 %queries_second.1.query_any.query1_ref = bf16[16,128,512]{2,1,0:T(8,128)(2,1)S(1)} custom-call(bf16[16,128,128]{2,1,0:T(8,128)(2,1)S(1)} %all-to-all-done.1.rows_ref.rows1_ref, s32[32,128]{1,0:T(8,128)S(1)} %copy-done.9, bf16[4,128,128]{2,1,0:T(8,128)(2,1)S(1)} %copy-done, bf16[2,128,128]{2,1,0:T(8,128)(2,1)S(1)} %get-tuple-element.29.rest_0_), custom_call_target="tpu_custom_call" | custom-call | flops 5000000 | bytes 10000 | tf_op jit(solution)/shard_map/queries_second/pallas_call | solution.py:554
  46.9 3.4 %collective-permute-done.1.column_ref = bf16[2,128,128]{2,1,0:T(8,128)(2,1)S(1)} collective-permute-done((bf16[2,128,128]{2,1,0:T(8,128)(2,1)S(1)}, bf16[2,128,128]{2,1,0:T(8,128)(2,1)S(1)}, u32[]{:S(2)}, u32[]{:S(2)}) %collective-permute-start.1) | collective-permute-done | bytes 65568 | tf_op jit(solution)/shard_map/ppermute | solution.py:657
  50.3 0.1 collective-permute-start.3
  50.3 0.7 collective-permute-start.4
  51.0 0.0 collective-permute-done.2.other_ref
  51.0 0.3 combine_second.1
  51.3 1.8 %collective-permute-start.5 = (bf16[2,128,128]{2,1,0:T(8,128)(2,1)S(1)}, bf16[2,128,128]{2,1,0:T(8,128)(2,1)S(1)}, u32[]{:S(2)}, u32[]{:S(2)}) collective-permute-start(bf16[2,128,128]{2,1,0:T(8,128)(2,1)S(1)} %get-tuple-element.35), channel_id=1, source_target_pairs={{0,4},{4,0},{8,12},{12,8},{16,20},{20,16},{24,28},{28,24},{1,5},{5... | collective-permute-start | bytes 196616 | tf_op jit(solution)/shard_map/ppermute | solution.py:703
  53.1 0.7 collective-permute-start.6
  53.8 0.2 collective-permute-done.5.near1_ref
  54.0 0.0 collective-permute-done.6.far1_ref
  54.0 0.0 collective-permute-done.3.near0_ref
  54.0 0.0 collective-permute-done.4.far0_ref
  54.0 0.0 copy-done.12
  54.0 0.9 %mix_tiles.1 = (bf16[2,256,512]{2,1,0:T(8,128)(2,1)S(1)}, bf16[2,256,512]{2,1,0:T(8,128)(2,1)S(1)}) custom-call(bf16[2,2,128,128]{3,2,1,0:T(8,128)(2,1)S(1)} %get-tuple-element.30.first_ref, bf16[2,128,128]{2,1,0:T(8,128)(2,1)S(1)} %collective-permute-done.1.column_ref, bf16[2,2,128,128]{3,2,1,0:T(8,128)(2,1)S(1)} %get-tuple-element.32.second_ref, ...), custom_call_target="tpu_custom_call" | custom-call | flops 500000000 | bytes 1000000 | tf_op jit(solution)/shard_map/mix_tiles/pallas_call | solution.py:554
  55.0 4.3 %attend_points.1 = bf16[16,2,128,128]{3,2,1,0:T(8,128)(2,1)S(1)} custom-call(bf16[16,128,128]{2,1,0:T(8,128)(2,1)S(1)} %all-to-all-done.rows_ref.rows0_ref, bf16[16,128,128]{2,1,0:T(8,128)(2,1)S(1)} %all-to-all-done.1.rows_ref.rows1_ref, bf16[16,128,512]{2,1,0:T(8,128)(2,1)S(1)} %queries_first.1.rest_3_.query0_ref, ...), custom_call_target="tpu_custom_call" | custom-call | flops 3500000000 | bytes 7000000 | tf_op jit(solution)/shard_map/attend_points/pallas_call | solution.py:554
  59.3 22.8 %all_to_all.15.rows_ref = bf16[16,2,128,128]{3,2,1,0:T(8,128)(2,1)S(1)} all-to-all(bf16[16,2,128,128]{3,2,1,0:T(8,128)(2,1)S(1)} %attend_points.1), channel_id=1, replica_groups=mesh['tx'=8,'zh'=2,'zl'=2] {'tx','zl'}, dimensions={0} | all-to-all | bytes 2097152 | tf_op jit(solution)/shard_map/all_to_all | solution.py:631
  82.1 5.1 %scatter_rows.1 = bf16[4096,128]{1,0:T(8,128)(2,1)} custom-call(bf16[16,2,128,128]{3,2,1,0:T(8,128)(2,1)S(1)} %all_to_all.15.rows_ref, s32[32,128]{1,0:T(8,128)S(1)} %copy-done.20), custom_call_target="tpu_custom_call" | custom-call | flops 2500000000 | bytes 5000000 | tf_op jit(solution)/shard_map/scatter_rows/pallas_call | solution.py:554
  (25 shorter events, 0.1 us)
Async XLA Ops:
  0.0 13.5 %copy-start.10 = (bf16[4096,128]{1,0:T(8,128)(2,1)S(1)}, bf16[4096,128]{1,0:T(8,128)(2,1)}, u32[]{:S(2)}) copy-start(bf16[4096,128]{1,0:T(8,128)(2,1)} %points_ref.1) | copy-start | bytes 3145732
  0.0 13.5 %copy-start.11 = (bf16[1,512,512]{2,1,0:T(8,128)(2,1)S(1)}, bf16[1,512,512]{2,1,0:T(8,128)(2,1)}, u32[]{:S(2)}) copy-start(bf16[1,512,512]{2,1,0:T(8,128)(2,1)} %w2_ref.1) | copy-start | bytes 1572868
  0.0 13.5 %copy-start.13 = (bf16[128,512]{1,0:T(8,128)(2,1)S(1)}, bf16[128,512]{1,0:T(8,128)(2,1)}, u32[]{:S(2)}) copy-start(bf16[128,512]{1,0:T(8,128)(2,1)} %w1_ref.1) | copy-start | bytes 393220
  0.0 13.5 %copy-start.14 = (bf16[512,128]{1,0:T(8,128)(2,1)S(1)}, bf16[512,128]{1,0:T(8,128)(2,1)}, u32[]{:S(2)}) copy-start(bf16[512,128]{1,0:T(8,128)(2,1)} %w3_ref.1) | copy-start | bytes 393220
  7.1 15.1 %all-to-all-start = ((bf16[16,128,128]{2,1,0:T(8,128)(2,1)}), bf16[16,128,128]{2,1,0:T(8,128)(2,1)S(1)}, u32[]{:S(2)}, u32[]{:S(2)}) async-start(bf16[16,128,128]{2,1,0:T(8,128)(2,1)} %get-tuple-element.22), calls=%async_computation | async-start | bytes 1048576 | tf_op jit(solution)/shard_map/all_to_all | solution.py:631
  13.5 0.7 copy-start.19
  14.2 11.8 %copy-start.1 = (bf16[4,128,128]{2,1,0:T(8,128)(2,1)S(1)}, bf16[4,128,128]{2,1,0:T(8,128)(2,1)}, u32[]{:S(2)}) copy-start(bf16[4,128,128]{2,1,0:T(8,128)(2,1)} %proj_ref.9) | copy-start | bytes 393220
  14.2 11.8 %copy-start.4 = (bf16[128,128]{1,0:T(8,128)(2,1)S(1)}, bf16[128,128]{1,0:T(8,128)(2,1)}, u32[]{:S(2)}) copy-start(bf16[128,128]{1,0:T(8,128)(2,1)} %inducing_ref.3) | copy-start | bytes 98308
  14.2 11.8 %copy-start.6 = (s32[32,128]{1,0:T(8,128)S(1)}, s32[32,128]{1,0:T(8,128)}, u32[]{:S(2)}) copy-start(s32[32,128]{1,0:T(8,128)} %counts_ref.9) | copy-start | bytes 49156
  22.2 14.3 %all-to-all-start.1 = ((bf16[16,128,128]{2,1,0:T(8,128)(2,1)}), bf16[16,128,128]{2,1,0:T(8,128)(2,1)S(1)}, u32[]{:S(2)}, u32[]{:S(2)}) async-start(bf16[16,128,128]{2,1,0:T(8,128)(2,1)} %encode_second.1), calls=%async_computation.1 | async-start | bytes 1048576 | tf_op jit(solution)/shard_map/all_to_all | solution.py:631
  26.0 7.3 %copy-start = (bf16[4,128,128]{2,1,0:T(8,128)(2,1)S(1)}, bf16[4,128,128]{2,1,0:T(8,128)(2,1)}, u32[]{:S(2)}) copy-start(bf16[4,128,128]{2,1,0:T(8,128)(2,1)} %proj_ref.11) | copy-start | bytes 393220
  26.1 7.3 %copy-start.7 = (s32[32,128]{1,0:T(8,128)S(1)}, s32[32,128]{1,0:T(8,128)}, u32[]{:S(2)}) copy-start(s32[32,128]{1,0:T(8,128)} %counts_ref.9) | copy-start | bytes 49156
  28.8 0.7 copy-start.2
  29.5 0.6 copy-start.15
  30.1 0.6 copy-start.17
  30.7 12.2 %collective-permute-start = (bf16[528,128]{1,0:T(8,128)(2,1)S(1)}, bf16[528,128]{1,0:T(8,128)(2,1)}, u32[]{:S(2)}, u32[]{:S(2)}) collective-permute-start(bf16[528,128]{1,0:T(8,128)(2,1)S(1)} %get-tuple-element.24.rest_0_), channel_id=1, source_target_pairs={{0,2},{1,3},{2,0},{3,1},{4,6},{5,7},{6,4},{7,5},{8,10},{9,11},{10,... | collective-permute-start | bytes 405512 | tf_op jit(solution)/shard_map/ppermute | solution.py:657
  36.5 0.7 copy-start.8
  37.2 0.8 copy-start.16
  38.0 0.8 copy-start.18
  38.8 4.1 %copy-start.3 = (f32[528,128]{1,0:T(8,128)S(1)}, f32[528,128]{1,0:T(8,128)}, u32[]{:S(2)}) copy-start(f32[528,128]{1,0:T(8,128)} %copy-done.2) | copy-start | bytes 811012
  38.8 4.1 %copy-start.5 = (bf16[128,128]{1,0:T(8,128)(2,1)S(1)}, bf16[128,128]{1,0:T(8,128)(2,1)}, u32[]{:S(2)}) copy-start(bf16[128,128]{1,0:T(8,128)(2,1)} %inducing_ref.3) | copy-start | bytes 98308
  38.8 6.2 %copy-start.9 = (s32[32,128]{1,0:T(8,128)S(1)}, s32[32,128]{1,0:T(8,128)}, u32[]{:S(2)}) copy-start(s32[32,128]{1,0:T(8,128)} %counts_ref.9) | copy-start | bytes 49156
  41.5 9.5 %collective-permute-start.2 = (bf16[528,128]{1,0:T(8,128)(2,1)S(1)}, bf16[528,128]{1,0:T(8,128)(2,1)S(1)}, u32[]{:S(2)}, u32[]{:S(2)}) collective-permute-start(bf16[528,128]{1,0:T(8,128)(2,1)S(1)} %get-tuple-element.28.after_any), channel_id=1, source_target_pairs={{0,2},{1,3},{2,0},{3,1},{4,6},{5,7},{6,4},{7,5},{8,10},{9,11},{10,... | collective-permute-start | bytes 405512 | tf_op jit(solution)/shard_map/ppermute | solution.py:657
  44.1 6.1 %collective-permute-start.1 = (bf16[2,128,128]{2,1,0:T(8,128)(2,1)S(1)}, bf16[2,128,128]{2,1,0:T(8,128)(2,1)S(1)}, u32[]{:S(2)}, u32[]{:S(2)}) collective-permute-start(bf16[2,128,128]{2,1,0:T(8,128)(2,1)S(1)} %get-tuple-element.29.rest_0_), channel_id=1, source_target_pairs={{0,1},{1,0},{2,3},{3,2},{4,5},{5,4},{6,7},{7,6},{8,9},{9,8},{10,11... | collective-permute-start | bytes 196616 | tf_op jit(solution)/shard_map/ppermute | solution.py:657
  50.2 3.8 %copy-start.12 = (bf16[8,128,128]{2,1,0:T(8,128)(2,1)S(1)}, bf16[8,128,128]{2,1,0:T(8,128)(2,1)}, u32[]{:S(2)}) copy-start(bf16[8,128,128]{2,1,0:T(8,128)(2,1)} %mixing_ref.1) | copy-start | bytes 786436
  50.3 3.8 %collective-permute-start.3 = (bf16[3,128,128]{2,1,0:T(8,128)(2,1)S(1)}, bf16[3,128,128]{2,1,0:T(8,128)(2,1)S(1)}, u32[]{:S(2)}, u32[]{:S(2)}) collective-permute-start(bf16[3,128,128]{2,1,0:T(8,128)(2,1)S(1)} %get-tuple-element.33), channel_id=1, source_target_pairs={{0,4},{4,0},{8,12},{12,8},{16,20},{20,16},{24,28},{28,24},{1,5},{5... | collective-permute-start | bytes 294920 | tf_op jit(solution)/shard_map/ppermute | solution.py:703
  50.3 3.7 %collective-permute-start.4 = (bf16[3,128,128]{2,1,0:T(8,128)(2,1)S(1)}, bf16[3,128,128]{2,1,0:T(8,128)(2,1)S(1)}, u32[]{:S(2)}, u32[]{:S(2)}) collective-permute-start(bf16[3,128,128]{2,1,0:T(8,128)(2,1)S(1)} %get-tuple-element.34), channel_id=1, source_target_pairs={{4,8},{8,4},{12,16},{16,12},{20,24},{24,20},{5,9},{9,5},{13,17},{1... | collective-permute-start | bytes 294920 | tf_op jit(solution)/shard_map/ppermute | solution.py:702
  51.3 2.7 %collective-permute-start.5 = (bf16[2,128,128]{2,1,0:T(8,128)(2,1)S(1)}, bf16[2,128,128]{2,1,0:T(8,128)(2,1)S(1)}, u32[]{:S(2)}, u32[]{:S(2)}) collective-permute-start(bf16[2,128,128]{2,1,0:T(8,128)(2,1)S(1)} %get-tuple-element.35), channel_id=1, source_target_pairs={{0,4},{4,0},{8,12},{12,8},{16,20},{20,16},{24,28},{28,24},{1,5},{5... | collective-permute-start | bytes 196616 | tf_op jit(solution)/shard_map/ppermute | solution.py:703
  53.1 0.9 %collective-permute-start.6 = (bf16[2,128,128]{2,1,0:T(8,128)(2,1)S(1)}, bf16[2,128,128]{2,1,0:T(8,128)(2,1)S(1)}, u32[]{:S(2)}, u32[]{:S(2)}) collective-permute-start(bf16[2,128,128]{2,1,0:T(8,128)(2,1)S(1)} %get-tuple-element.36), channel_id=1, source_target_pairs={{4,8},{8,4},{12,16},{16,12},{20,24},{24,20},{5,9},{9,5},{13,17},{1... | collective-permute-start | bytes 196616 | tf_op jit(solution)/shard_map/ppermute | solution.py:702
  59.3 22.9 %copy-start.20 = (s32[32,128]{1,0:T(8,128)S(1)}, s32[32,128]{1,0:T(8,128)}, u32[]{:S(2)}) copy-start(s32[32,128]{1,0:T(8,128)} %get-tuple-element.23.index_any.index_ref) | copy-start | bytes 49156

commit v11 on v10

--- a/solution.py
+++ b/solution.py
@@ -224,12 +224,39 @@
     return found
 
 
+def row_bounds(piece, counts_ref, grid_y):
+    s, base = piece
+    n0 = counts_ref[s, base]
+    n1 = n0 + counts_ref[s, base + 1]
+    return n0, n1, n1 + counts_ref[s, base + grid_y]
+
+
+def expand_queries(half_id, along_y, rows_ref, counts_ref, proj_ref, out_ref):
+    ones = head_ones()
+    members, quota, width = rows_ref.shape
+    group = min(GROUP_ROWS // quota, members)
+    row = lax.broadcasted_iota(jnp.int32, (quota, LANES), 0)
+    for c in range(members // group):
+        x = jnp.concatenate([rows_ref[c * group + k] for k in range(group)], axis=0)
+        query = unit(dot(x, proj_ref[0]), ones)
+        pieces = pieces_of(c * group, group, half_id, along_y)
+        for k in range(group):
+            bounds = row_bounds(pieces[k], counts_ref, along_y * TLY)
+            past = [row >= b for b in bounds]
+            mine = query[k * quota : (k + 1) * quota]
+            masks = (~past[0], past[0] & ~past[1], past[1] & ~past[2], past[2])
+            out_ref[c * group + k] = jnp.concatenate(
+                [jnp.where(m, mine, 0.0).astype(BF) for m in masks], axis=1
+            )
+
+
 def partial_kernel(half_id, along_y, rows_ref, counts_ref, *rest):
     num_ref = rest[-1]
     if half_id:
-        query_ref, wv_ref, proj_ref, before_any, own_ref, send_ref = rest[:-1]
+        query_ref, wv_ref, proj_ref, own_ref, send_ref = rest[:-1]
     else:
-        inducing_ref, proj_ref, own_ref, send_ref, query_ref, wv_ref = rest[:-1]
+        inducing_ref, proj_ref, second_ref, own_ref, send_ref, query_ref, wv_ref, point_ref = rest[:-1]
+        expand_queries(0, along_y, rows_ref, counts_ref, second_ref, point_ref)
     members, quota, width = rows_ref.shape
     grid_y = along_y * TLY
     half = LANES // HEADS
@@ -288,31 +315,8 @@
     own_ref[last:, :] = totals
     send_ref[last:, :] = totals.astype(BF)
 
-def row_bounds(piece, counts_ref, grid_y):
-    s, base = piece
-    n0 = counts_ref[s, base]
-    n1 = n0 + counts_ref[s, base + 1]
-    return n0, n1, n1 + counts_ref[s, base + grid_y]
-
-
-def queries_kernel(half_id, along_y, rows_ref, counts_ref, proj_ref, *rest):
-    out_ref = rest[-1]
-    ones = head_ones()
-    members, quota, width = rows_ref.shape
-    group = min(GROUP_ROWS // quota, members)
-    row = lax.broadcasted_iota(jnp.int32, (quota, LANES), 0)
-    for c in range(members // group):
-        x = jnp.concatenate([rows_ref[c * group + k] for k in range(group)], axis=0)
-        query = unit(dot(x, proj_ref[0]), ones)
-        pieces = pieces_of(c * group, group, half_id, along_y)
-        for k in range(group):
-            bounds = row_bounds(pieces[k], counts_ref, along_y * TLY)
-            past = [row >= b for b in bounds]
-            mine = query[k * quota : (k + 1) * quota]
-            masks = (~past[0], past[0] & ~past[1], past[1] & ~past[2], past[2])
-            out_ref[c * group + k] = jnp.concatenate(
-                [jnp.where(m, mine, 0.0).astype(BF) for m in masks], axis=1
-            )
+def queries_kernel(along_y, rows_ref, counts_ref, proj_ref, before_any, out_ref):
+    expand_queries(1, along_y, rows_ref, counts_ref, proj_ref, out_ref)
 
 
 def summarize(half_id, own_ref, other_ref, inducing_ref, proj_ref, store):
@@ -466,8 +470,15 @@
             key_ref[b, h * LANES : (h + 1) * LANES, :] = jnp.concatenate(
                 [jnp.where(mine, keys[s], 0.0) for s in spans], axis=1
             ).astype(BF)
-            value_ref[b, h * LANES : (h + 1) * LANES, :] = jnp.concatenate(
-                [jnp.where(mine, values[s], 0.0) for s in spans], axis=1
+            turned = [pltpu.roll(values[s], LANES // HEADS, 1) for s in spans]
+            value_ref[b, h] = jnp.concatenate(
+                [
+                    jnp.where(left, values[spans[p]], turned[p + 1])
+                    if h == 0
+                    else jnp.where(left, turned[p + 1], values[spans[p]])
+                    for p in (0, 2)
+                ],
+                axis=1,
             ).astype(BF)
 
 
@@ -499,18 +510,22 @@
                 jnp.sum(weights[:, h * LANES : (h + 1) * LANES], axis=1, keepdims=True)
                 for h in range(HEADS)
             ]
-            every = dot(weights.astype(BF), value_ref[block])
+            every = [
+                dot(weights[:, h * LANES : (h + 1) * LANES].astype(BF), value_ref[block, h])
+                for h in range(HEADS)
+            ]
             pieces = pieces_of(c * group, group, half_id, along_y)
             attended = []
             for k in range(group):
-                bounds = row_bounds(pieces[k], counts_ref, along_y * TLY)
+                first, second, third = row_bounds(pieces[k], counts_ref, along_y * TLY)
                 span = slice(k * quota, (k + 1) * quota)
-                part = every[span]
-                picked = part[:, :LANES]
-                for t, bound in enumerate(bounds):
-                    tile = part[:, (t + 1) * LANES : (t + 2) * LANES]
-                    picked = jnp.where(row >= bound, tile, picked)
+                upper = row >= second
+                odd = ((row >= first) & (row < second)) | (row >= third)
+                part = [jnp.where(upper, e[span, LANES:], e[span, :LANES]) for e in every]
+                even_tile = jnp.where(left, part[0], part[1])
+                odd_tile = pltpu.roll(jnp.where(left, part[1], part[0]), LANES // HEADS, 1)
                 total = jnp.where(left, totals[0][span], totals[1][span])
+                picked = jnp.where(odd, odd_tile, even_tile)
                 attended.append(quotient(picked, total).astype(BF))
             x = jnp.concatenate([rows_ref[c * group + k] for k in range(group)], axis=0)
             added = dot(jnp.concatenate(attended, axis=0), proj_ref[3])
@@ -636,15 +651,16 @@
     part_rows = 4 * LANES + 16
     parts = (shape((part_rows, LANES), F32), shape((part_rows, LANES)))
     sums = [VMEM((part_rows, HEADS * LANES), F32)]
-    own0, send0, first_queries, value_weight = call(
+    expanded = shape((members, quota, 4 * width))
+    own0, send0, first_queries, value_weight, query0 = call(
         functools.partial(partial_kernel, 0, along_y),
         "partial_first",
         parts
-        + (shape((HEADS * LANES, width)), shape((LANES, width))),
-        "vsvv",
+        + (shape((HEADS * LANES, width)), shape((LANES, width)), expanded),
+        "vsvvv",
         sums,
         3,
-        (rows0, counts, inducing, first_proj),
+        (rows0, counts, inducing, first_proj, second_proj),
     )
     pairs = [(h, l) for h in range(highs) for l in range(lows)]
 
@@ -657,23 +673,14 @@
         return lax.ppermute(value, ("zh", "zl"), steps)
 
     other0 = swap(send0, True, False)
-    query0 = call(
-        functools.partial(queries_kernel, 0, along_y),
-        "queries_first",
-        shape((members, quota, 4 * width)),
-        "vsva",
-        [],
-        1,
-        (rows0, counts, second_proj, send0),
-    )
     own1, send1 = call(
         functools.partial(partial_kernel, 1, along_y),
         "partial_second",
         parts,
-        "vsvvva",
+        "vsvvv",
         sums,
         3,
-        (rows1, counts, first_queries, value_weight, first_proj, query0),
+        (rows1, counts, first_queries, value_weight, first_proj),
     )
     other1 = swap(send1, True, False)
     first_half, border = call(
@@ -687,9 +694,9 @@
     )
     column = swap(border, False, True)
     query1 = call(
-        functools.partial(queries_kernel, 1, along_y),
+        functools.partial(queries_kernel, along_y),
         "queries_second",
-        shape((members, quota, 4 * width)),
+        expanded,
         "vsva",
         [],
         0.01,
@@ -729,7 +736,7 @@
     keys, values = call(
         mixture_kernel,
         "mix_tiles",
-        (shape((blocks, HEADS * LANES, 4 * LANES)), shape((blocks, HEADS * LANES, 4 * LANES))),
+        (shape((blocks, HEADS * LANES, 4 * LANES)), shape((blocks, HEADS, LANES, 2 * LANES))),
         "v" * 9,
         [
             VMEM((TLX + 2, tall + 2, LANES, width), BF),

time: 88.1 us -> 92.7 us (1.052)
  Pallas kernels: 33.4 us -> 36.8 us
  local copies, waits for them, and re-layouts: 4.99 us -> 2.1 us
  starting transfers between devices: 18.2 us -> 21 us
  blocking collectives: 22.8 us -> 23.8 us
    pallas_call x12 -> x11, Pallas kernels: 33.4 us -> 36.8 us  [call(): pl.pallas_call(kernel, out_shape=out_shape, in_specs=[pl.BlockSpec(memory...]
    unnamed x42 -> x26, local copies, waits for them, and re-layouts: 4.99 us -> 2.1 us
    ppermute x3, starting transfers between devices: 4.86 us -> 6.48 us  [swap(): return lax.ppermute(value, ('zh', 'zl'), steps)]
    ppermute x3, waiting for transfers between devices: 3.36 us -> 4.43 us  [swap(): return lax.ppermute(value, ('zh', 'zl'), steps)]
    ppermute x2, starting transfers between devices: 1.87 us -> 2.91 us  [halo(): return (lax.ppermute(near, 'tx', near_pairs), far)]
    all_to_all x1, blocking collectives: 22.8 us -> 23.8 us  [exchange(): lax.all_to_all(rows, ('tx', 'zl'), split_axis=0, concat_axis=0, tiled=True)]
  transfers between devices with their start and end apart: 9 -> 9, of which waited for: 4 -> 4; matrix products, arithmetic and copies ran while one was open for 0% -> 0% of each run, Pallas kernels for 18% -> 16%
where the time goes in v11:
time: 92.7 us; the launch traced here: 92.2 us
  Pallas kernels  36.8 us (40%)
  blocking collectives  23.8 us (26%)
  starting transfers between devices  21 us (23%)
  waiting for transfers between devices  8.04 us (9%)
  local copies, waits for them, and re-layouts  2.1 us (2%)
    pallas_call x11, Pallas kernels, call(): pl.pallas_call(kernel, out_shape=out_shape, in_specs=[pl.BlockSpec(memory...  36.8 us
    all_to_all x1, blocking collectives, exchange(): lax.all_to_all(rows, ('tx', 'zl'), split_axis=0, concat_axis=0, tiled=True)  23.8 us
    all_to_all x2, starting transfers between devices, exchange(): lax.all_to_all(rows, ('tx', 'zl'), split_axis=0, concat_axis=0, tiled=True)  10.1 us
    ppermute x3, starting transfers between devices, swap(): return lax.ppermute(value, ('zh', 'zl'), steps)  6.48 us
    ppermute x3, waiting for transfers between devices, swap(): return lax.ppermute(value, ('zh', 'zl'), steps)  4.43 us
    all_to_all x2, waiting for transfers between devices, exchange(): lax.all_to_all(rows, ('tx', 'zl'), split_axis=0, concat_axis=0, tiled=True)  3.59 us
    ppermute x2, starting transfers between devices, halo(): return (lax.ppermute(near, 'tx', near_pairs), far)  2.91 us
    unnamed x26, local copies, waits for them, and re-layouts  2.1 us
  transfers between devices with their start and end apart: 9, of which 4 were waited for; matrix products, arithmetic and copies ran while one was open for 0% of the time, Pallas kernels for 16%

profile of v11, /device:TPU:0, one launch (start us, length us, event | category | flops | bytes accessed | tf_op | source)
XLA Modules:
  0.0 92.2 jit_solution(15756302469865928697)
XLA Ops:
  0.0 0.0 copy-start.4
  0.0 0.0 copy-start.5
  0.0 7.1 %encode_first.1 = (bf16[16,128,128]{2,1,0:T(8,128)(2,1)}, s32[32,128]{1,0:T(8,128)}) custom-call(bf16[4096,128]{1,0:T(8,128)(2,1)} %points_ref.1, bf16[128,512]{1,0:T(8,128)(2,1)} %w1_ref.1, bf16[1,512,512]{2,1,0:T(8,128)(2,1)} %w2_ref.1, bf16[512,128]{1,0:T(8,128)(2,1)} %w3_ref.1, s32[32,128]{1,0:T(8,128)} %counts_ref.7, s32[32,128]{1,0:T(8,128)} %bitcast.1), custom_call_target="tpu_custom_call" | custom-call | flops 4000000000 | bytes 8000000 | tf_op jit(solution)/shard_map/encode_first/pallas_call | solution.py:569
  7.1 6.3 %all-to-all-start = ((bf16[16,128,128]{2,1,0:T(8,128)(2,1)}), bf16[16,128,128]{2,1,0:T(8,128)(2,1)S(1)}, u32[]{:S(2)}, u32[]{:S(2)}) async-start(bf16[16,128,128]{2,1,0:T(8,128)(2,1)} %get-tuple-element.23), calls=%async_computation | async-start | bytes 1048576 | tf_op jit(solution)/shard_map/all_to_all | solution.py:646
  13.5 0.0 copy-done.4
  13.5 0.0 copy-done.5
  13.5 0.0 copy-done.7
  13.5 0.0 copy-done.8
  13.5 0.0 copy-start.11
  13.5 0.7 copy-done.11
  14.2 5.2 %encode_second.1 = bf16[16,128,128]{2,1,0:T(8,128)(2,1)} custom-call(bf16[4096,128]{1,0:T(8,128)(2,1)S(1)} %copy-done.4, bf16[128,512]{1,0:T(8,128)(2,1)S(1)} %copy-done.7, bf16[1,512,512]{2,1,0:T(8,128)(2,1)S(1)} %copy-done.5, bf16[512,128]{1,0:T(8,128)(2,1)S(1)} %copy-done.8, s32[32,128]{1,0:T(8,128)S(1)} %copy-done.11), custom_call_target="tpu_custom_call" | custom-call | flops 3000000000 | bytes 6000000 | tf_op jit(solution)/shard_map/encode_second/pallas_call | solution.py:569
  19.5 2.7 %all-to-all-done.rows_ref.rows0_ref = bf16[16,128,128]{2,1,0:T(8,128)(2,1)S(1)} async-done(((bf16[16,128,128]{2,1,0:T(8,128)(2,1)}), bf16[16,128,128]{2,1,0:T(8,128)(2,1)S(1)}, u32[]{:S(2)}, u32[]{:S(2)}) %all-to-all-start) | async-done | bytes 524320 | tf_op jit(solution)/shard_map/all_to_all | solution.py:646
  22.2 3.8 %all-to-all-start.1 = ((bf16[16,128,128]{2,1,0:T(8,128)(2,1)}), bf16[16,128,128]{2,1,0:T(8,128)(2,1)S(1)}, u32[]{:S(2)}, u32[]{:S(2)}) async-start(bf16[16,128,128]{2,1,0:T(8,128)(2,1)} %encode_second.1), calls=%async_computation.1 | async-start | bytes 1048576 | tf_op jit(solution)/shard_map/all_to_all | solution.py:646
  26.0 0.0 copy-done
  26.0 0.0 copy-done.1
  26.0 0.0 copy-done.2
  26.0 0.0 copy-done.3
  26.0 3.8 %partial_first.1 = (f32[528,128]{1,0:T(8,128)S(1)}, bf16[528,128]{1,0:T(8,128)(2,1)S(1)}, bf16[256,128]{1,0:T(8,128)(2,1)S(1)}, bf16[128,128]{1,0:T(8,128)(2,1)S(1)}, bf16[16,128,512]{2,1,0:T(8,128)(2,1)S(1)}) custom-call(bf16[16,128,128]{2,1,0:T(8,128)(2,1)S(1)} %all-to-all-done.rows_ref.rows0_ref, s32[32,128]{1,0:T(8,128)S(1)} %copy-done.3, ...), custom_call_target="tpu_custom_call" | custom-call | flops 1500000000 | bytes 3000000 | tf_op jit(solution)/shard_map/partial_first/pallas_call | solution.py:569
  29.9 0.0 copy-start.9
  29.9 1.3 %copy-done.9 = bf16[16,128,512]{2,1,0:T(8,128)(2,1)} copy-done((bf16[16,128,512]{2,1,0:T(8,128)(2,1)}, bf16[16,128,512]{2,1,0:T(8,128)(2,1)S(1)}, u32[]{:S(2)}) %copy-start.9) | copy-done | bytes 2097176
  31.3 2.6 %collective-permute-start = (bf16[528,128]{1,0:T(8,128)(2,1)S(1)}, bf16[528,128]{1,0:T(8,128)(2,1)S(1)}, u32[]{:S(2)}, u32[]{:S(2)}) collective-permute-start(bf16[528,128]{1,0:T(8,128)(2,1)S(1)} %get-tuple-element.27), channel_id=1, source_target_pairs={{0,2},{1,3},{2,0},{3,1},{4,6},{5,7},{6,4},{7,5},{8,10},{9,11},{10,... | collective-permute-start | bytes 405512 | tf_op jit(solution)/shard_map/ppermute | solution.py:673
  33.9 0.9 all-to-all-done.1.rows_ref.rows1_ref
  34.7 2.7 %partial_second.1 = (f32[528,128]{1,0:T(8,128)S(1)}, bf16[528,128]{1,0:T(8,128)(2,1)S(1)}) custom-call(bf16[16,128,128]{2,1,0:T(8,128)(2,1)S(1)} %all-to-all-done.1.rows_ref.rows1_ref, s32[32,128]{1,0:T(8,128)S(1)} %copy-done.3, bf16[256,128]{1,0:T(8,128)(2,1)S(1)} %get-tuple-element.28.rest_0_, bf16[128,128]{1,0:T(8,128)(2,1)S(1)} %get-tuple-element.29.rest_1_, ...), custom_call_target="tpu_custom_call" | custom-call | flops 1500000000 | bytes 3000000 | tf_op jit(solution)/shard_map/partial_second/pallas_call | solution.py:569
  37.4 3.1 %collective-permute-start.2 = (bf16[528,128]{1,0:T(8,128)(2,1)S(1)}, bf16[528,128]{1,0:T(8,128)(2,1)S(1)}, u32[]{:S(2)}, u32[]{:S(2)}) collective-permute-start(bf16[528,128]{1,0:T(8,128)(2,1)S(1)} %get-tuple-element.30.after_any), channel_id=1, source_target_pairs={{0,2},{1,3},{2,0},{3,1},{4,6},{5,7},{6,4},{7,5},{8,10},{9,11},{10,... | collective-permute-start | bytes 405512 | tf_op jit(solution)/shard_map/ppermute | solution.py:673
  40.6 0.4 collective-permute-done.other_ref
  40.9 0.3 combine_first.1
  41.2 0.8 collective-permute-start.1
  41.9 1.9 %queries_second.1.query_any.query1_ref = bf16[16,128,512]{2,1,0:T(8,128)(2,1)S(1)} custom-call(bf16[16,128,128]{2,1,0:T(8,128)(2,1)S(1)} %all-to-all-done.1.rows_ref.rows1_ref, s32[32,128]{1,0:T(8,128)S(1)} %copy-done.3, bf16[4,128,128]{2,1,0:T(8,128)(2,1)S(1)} %copy-done.1, bf16[2,128,128]{2,1,0:T(8,128)(2,1)S(1)} %get-tuple-element.31.before_any), custom_call_target="tpu_custom_call" | custom-call | flops 5000000 | bytes 10000 | tf_op jit(solution)/shard_map/queries_second/pallas_call | solution.py:569
  43.9 4.1 %collective-permute-done.1.column_ref = bf16[2,128,128]{2,1,0:T(8,128)(2,1)S(1)} collective-permute-done((bf16[2,128,128]{2,1,0:T(8,128)(2,1)S(1)}, bf16[2,128,128]{2,1,0:T(8,128)(2,1)S(1)}, u32[]{:S(2)}, u32[]{:S(2)}) %collective-permute-start.1) | collective-permute-done | bytes 65568 | tf_op jit(solution)/shard_map/ppermute | solution.py:673
  48.0 0.1 collective-permute-start.3
  48.1 0.7 collective-permute-start.4
  48.7 0.0 collective-permute-done.2.other_ref
  48.7 0.0 copy-start.10
  48.8 0.3 combine_second.1
  49.0 2.8 %collective-permute-start.5 = (bf16[2,128,128]{2,1,0:T(8,128)(2,1)S(1)}, bf16[2,128,128]{2,1,0:T(8,128)(2,1)S(1)}, u32[]{:S(2)}, u32[]{:S(2)}) collective-permute-start(bf16[2,128,128]{2,1,0:T(8,128)(2,1)S(1)} %get-tuple-element.37), channel_id=1, source_target_pairs={{0,4},{4,0},{8,12},{12,8},{16,20},{20,16},{24,28},{28,24},{1,5},{5... | collective-permute-start | bytes 196616 | tf_op jit(solution)/shard_map/ppermute | solution.py:710
  51.9 0.9 collective-permute-start.6
  52.8 0.0 collective-permute-done.5.near1_ref
  52.8 0.0 collective-permute-done.6.far1_ref
  52.8 0.0 collective-permute-done.3.near0_ref
  52.8 0.0 collective-permute-done.4.far0_ref
  52.8 0.0 copy-done.6
  52.8 1.0 %mix_tiles.1 = (bf16[2,256,512]{2,1,0:T(8,128)(2,1)S(1)}, bf16[2,2,128,256]{3,2,1,0:T(8,128)(2,1)S(1)}) custom-call(bf16[2,2,128,128]{3,2,1,0:T(8,128)(2,1)S(1)} %get-tuple-element.32.first_ref, bf16[2,128,128]{2,1,0:T(8,128)(2,1)S(1)} %collective-permute-done.1.column_ref, bf16[2,2,128,128]{3,2,1,0:T(8,128)(2,1)S(1)} %get-tuple-element.34.second_ref, ...), custom_call_target="tpu_custom_call" | custom-call | flops 500000000 | bytes 1000000 | tf_op jit(solution)/shard_map/mix_tiles/pallas_call | solution.py:569
  53.8 0.0 copy-done.10
  53.8 9.2 %attend_points.1 = bf16[16,2,128,128]{3,2,1,0:T(8,128)(2,1)S(1)} custom-call(bf16[16,128,128]{2,1,0:T(8,128)(2,1)S(1)} %all-to-all-done.rows_ref.rows0_ref, bf16[16,128,128]{2,1,0:T(8,128)(2,1)S(1)} %all-to-all-done.1.rows_ref.rows1_ref, bf16[16,128,512]{2,1,0:T(8,128)(2,1)S(1)} %copy-done.10, bf16[16,128,512]{2,1,0:T(8,128)(2,1)S(1)} %queries_second.1.query_any.query1_ref, ...), custom_call_target="tpu_custom_call" | custom-call | flops 3500000000 | bytes 7000000 | tf_op jit(solution)/shard_map/attend_points/pallas_call | solution.py:569
  63.1 0.0 copy-start.12
  63.1 23.8 %all_to_all.15.rows_ref = bf16[16,2,128,128]{3,2,1,0:T(8,128)(2,1)S(1)} all-to-all(bf16[16,2,128,128]{3,2,1,0:T(8,128)(2,1)S(1)} %attend_points.1), channel_id=1, replica_groups=mesh['tx'=8,'zh'=2,'zl'=2] {'tx','zl'}, dimensions={0} | all-to-all | bytes 2097152 | tf_op jit(solution)/shard_map/all_to_all | solution.py:646
  86.9 0.0 copy-done.12
  86.9 5.1 %scatter_rows.1 = bf16[4096,128]{1,0:T(8,128)(2,1)} custom-call(bf16[16,2,128,128]{3,2,1,0:T(8,128)(2,1)S(1)} %all_to_all.15.rows_ref, s32[32,128]{1,0:T(8,128)S(1)} %copy-done.12), custom_call_target="tpu_custom_call" | custom-call | flops 2500000000 | bytes 5000000 | tf_op jit(solution)/shard_map/scatter_rows/pallas_call | solution.py:569
  (8 shorter events, 0.1 us)
Async XLA Ops:
  0.0 13.5 %copy-start.4 = (bf16[4096,128]{1,0:T(8,128)(2,1)S(1)}, bf16[4096,128]{1,0:T(8,128)(2,1)}, u32[]{:S(2)}) copy-start(bf16[4096,128]{1,0:T(8,128)(2,1)} %points_ref.1) | copy-start | bytes 3145732
  0.0 13.5 %copy-start.5 = (bf16[1,512,512]{2,1,0:T(8,128)(2,1)S(1)}, bf16[1,512,512]{2,1,0:T(8,128)(2,1)}, u32[]{:S(2)}) copy-start(bf16[1,512,512]{2,1,0:T(8,128)(2,1)} %w2_ref.1) | copy-start | bytes 1572868
  0.0 13.5 %copy-start.7 = (bf16[128,512]{1,0:T(8,128)(2,1)S(1)}, bf16[128,512]{1,0:T(8,128)(2,1)}, u32[]{:S(2)}) copy-start(bf16[128,512]{1,0:T(8,128)(2,1)} %w1_ref.1) | copy-start | bytes 393220
  0.0 13.5 %copy-start.8 = (bf16[512,128]{1,0:T(8,128)(2,1)S(1)}, bf16[512,128]{1,0:T(8,128)(2,1)}, u32[]{:S(2)}) copy-start(bf16[512,128]{1,0:T(8,128)(2,1)} %w3_ref.1) | copy-start | bytes 393220
  7.1 15.1 %all-to-all-start = ((bf16[16,128,128]{2,1,0:T(8,128)(2,1)}), bf16[16,128,128]{2,1,0:T(8,128)(2,1)S(1)}, u32[]{:S(2)}, u32[]{:S(2)}) async-start(bf16[16,128,128]{2,1,0:T(8,128)(2,1)} %get-tuple-element.23), calls=%async_computation | async-start | bytes 1048576 | tf_op jit(solution)/shard_map/all_to_all | solution.py:646
  13.5 0.7 copy-start.11
  14.2 11.8 %copy-start = (bf16[4,128,128]{2,1,0:T(8,128)(2,1)S(1)}, bf16[4,128,128]{2,1,0:T(8,128)(2,1)}, u32[]{:S(2)}) copy-start(bf16[4,128,128]{2,1,0:T(8,128)(2,1)} %proj_ref.7) | copy-start | bytes 393220
  14.2 11.8 %copy-start.1 = (bf16[4,128,128]{2,1,0:T(8,128)(2,1)S(1)}, bf16[4,128,128]{2,1,0:T(8,128)(2,1)}, u32[]{:S(2)}) copy-start(bf16[4,128,128]{2,1,0:T(8,128)(2,1)} %proj_ref.9) | copy-start | bytes 393220
  14.2 11.8 %copy-start.2 = (bf16[128,128]{1,0:T(8,128)(2,1)S(1)}, bf16[128,128]{1,0:T(8,128)(2,1)}, u32[]{:S(2)}) copy-start(bf16[128,128]{1,0:T(8,128)(2,1)} %inducing_ref.3) | copy-start | bytes 98308
  14.2 11.8 %copy-start.3 = (s32[32,128]{1,0:T(8,128)S(1)}, s32[32,128]{1,0:T(8,128)}, u32[]{:S(2)}) copy-start(s32[32,128]{1,0:T(8,128)} %counts_ref.7) | copy-start | bytes 49156
  22.2 12.5 %all-to-all-start.1 = ((bf16[16,128,128]{2,1,0:T(8,128)(2,1)}), bf16[16,128,128]{2,1,0:T(8,128)(2,1)S(1)}, u32[]{:S(2)}, u32[]{:S(2)}) async-start(bf16[16,128,128]{2,1,0:T(8,128)(2,1)} %encode_second.1), calls=%async_computation.1 | async-start | bytes 1048576 | tf_op jit(solution)/shard_map/all_to_all | solution.py:646
  29.9 1.4 %copy-start.9 = (bf16[16,128,512]{2,1,0:T(8,128)(2,1)}, bf16[16,128,512]{2,1,0:T(8,128)(2,1)S(1)}, u32[]{:S(2)}) copy-start(bf16[16,128,512]{2,1,0:T(8,128)(2,1)S(1)} %get-tuple-element.25.query0_ref) | copy-start | bytes 6291460
  31.3 9.7 %collective-permute-start = (bf16[528,128]{1,0:T(8,128)(2,1)S(1)}, bf16[528,128]{1,0:T(8,128)(2,1)S(1)}, u32[]{:S(2)}, u32[]{:S(2)}) collective-permute-start(bf16[528,128]{1,0:T(8,128)(2,1)S(1)} %get-tuple-element.27), channel_id=1, source_target_pairs={{0,2},{1,3},{2,0},{3,1},{4,6},{5,7},{6,4},{7,5},{8,10},{9,11},{10,... | collective-permute-start | bytes 405512 | tf_op jit(solution)/shard_map/ppermute | solution.py:673
  37.4 11.3 %collective-permute-start.2 = (bf16[528,128]{1,0:T(8,128)(2,1)S(1)}, bf16[528,128]{1,0:T(8,128)(2,1)S(1)}, u32[]{:S(2)}, u32[]{:S(2)}) collective-permute-start(bf16[528,128]{1,0:T(8,128)(2,1)S(1)} %get-tuple-element.30.after_any), channel_id=1, source_target_pairs={{0,2},{1,3},{2,0},{3,1},{4,6},{5,7},{6,4},{7,5},{8,10},{9,11},{10,... | collective-permute-start | bytes 405512 | tf_op jit(solution)/shard_map/ppermute | solution.py:673
  41.2 6.7 %collective-permute-start.1 = (bf16[2,128,128]{2,1,0:T(8,128)(2,1)S(1)}, bf16[2,128,128]{2,1,0:T(8,128)(2,1)S(1)}, u32[]{:S(2)}, u32[]{:S(2)}) collective-permute-start(bf16[2,128,128]{2,1,0:T(8,128)(2,1)S(1)} %get-tuple-element.31.before_any), channel_id=1, source_target_pairs={{0,1},{1,0},{2,3},{3,2},{4,5},{5,4},{6,7},{7,6},{8,9},{9,8},{10,11... | collective-permute-start | bytes 196616 | tf_op jit(solution)/shard_map/ppermute | solution.py:673
  47.9 4.9 %copy-start.6 = (bf16[8,128,128]{2,1,0:T(8,128)(2,1)S(1)}, bf16[8,128,128]{2,1,0:T(8,128)(2,1)}, u32[]{:S(2)}) copy-start(bf16[8,128,128]{2,1,0:T(8,128)(2,1)} %mixing_ref.1) | copy-start | bytes 786436
  48.0 4.8 %collective-permute-start.3 = (bf16[3,128,128]{2,1,0:T(8,128)(2,1)S(1)}, bf16[3,128,128]{2,1,0:T(8,128)(2,1)S(1)}, u32[]{:S(2)}, u32[]{:S(2)}) collective-permute-start(bf16[3,128,128]{2,1,0:T(8,128)(2,1)S(1)} %get-tuple-element.35), channel_id=1, source_target_pairs={{0,4},{4,0},{8,12},{12,8},{16,20},{20,16},{24,28},{28,24},{1,5},{5... | collective-permute-start | bytes 294920 | tf_op jit(solution)/shard_map/ppermute | solution.py:710
  48.1 4.7 %collective-permute-start.4 = (bf16[3,128,128]{2,1,0:T(8,128)(2,1)S(1)}, bf16[3,128,128]{2,1,0:T(8,128)(2,1)S(1)}, u32[]{:S(2)}, u32[]{:S(2)}) collective-permute-start(bf16[3,128,128]{2,1,0:T(8,128)(2,1)S(1)} %get-tuple-element.36), channel_id=1, source_target_pairs={{4,8},{8,4},{12,16},{16,12},{20,24},{24,20},{5,9},{9,5},{13,17},{1... | collective-permute-start | bytes 294920 | tf_op jit(solution)/shard_map/ppermute | solution.py:709
  48.7 5.1 %copy-start.10 = (bf16[16,128,512]{2,1,0:T(8,128)(2,1)S(1)}, bf16[16,128,512]{2,1,0:T(8,128)(2,1)}, u32[]{:S(2)}) copy-start(bf16[16,128,512]{2,1,0:T(8,128)(2,1)} %copy-done.9) | copy-start | bytes 6291460
  49.0 3.7 %collective-permute-start.5 = (bf16[2,128,128]{2,1,0:T(8,128)(2,1)S(1)}, bf16[2,128,128]{2,1,0:T(8,128)(2,1)S(1)}, u32[]{:S(2)}, u32[]{:S(2)}) collective-permute-start(bf16[2,128,128]{2,1,0:T(8,128)(2,1)S(1)} %get-tuple-element.37), channel_id=1, source_target_pairs={{0,4},{4,0},{8,12},{12,8},{16,20},{20,16},{24,28},{28,24},{1,5},{5... | collective-permute-start | bytes 196616 | tf_op jit(solution)/shard_map/ppermute | solution.py:710
  51.9 0.9 collective-permute-start.6
  63.1 23.9 %copy-start.12 = (s32[32,128]{1,0:T(8,128)S(1)}, s32[32,128]{1,0:T(8,128)}, u32[]{:S(2)}) copy-start(s32[32,128]{1,0:T(8,128)} %get-tuple-element.24.index_any.index_ref) | copy-start | bytes 49156

commit v12 on v11

--- a/solution.py
+++ b/solution.py
@@ -351,29 +351,26 @@
         far_ref[y] = jnp.where(even, low, high)
 
 
-def early_lines_kernel(first_ref, column_ref, query_any, near_ref, far_ref):
-    rows = [[first_ref[x, y] for y in range(TLY)] + [column_ref[x]] for x in range(TLX)]
-    pair_lines(rows, near_ref, far_ref)
-
-
 def combine_second_kernel(
-    own_ref, other_ref, inducing_ref, proj_ref, query_any, out_ref, near_ref, far_ref
+    own_ref, other_ref, inducing_ref, proj_ref, first_ref, column_ref, query_any, out_ref, near_ref, far_ref
 ):
     def store(x, y, value):
         out_ref[x, y] = value
 
     summarize(1, own_ref, other_ref, inducing_ref, proj_ref, store)
-    pair_lines([[out_ref[x, y] for y in range(TLY)] for x in range(TLX)], near_ref, far_ref)
+    rows = [
+        [out_ref[x, y] for y in range(TLY)] + [first_ref[x, y] for y in range(TLY)] + [column_ref[x]]
+        for x in range(TLX)
+    ]
+    pair_lines(rows, near_ref, far_ref)
 
 
 def mixture_kernel(
     first_ref,
     column_ref,
     second_ref,
-    near0_ref,
-    far0_ref,
-    near1_ref,
-    far1_ref,
+    near_ref,
+    far_ref,
     proj_ref,
     mixing_ref,
     key_ref,
@@ -427,11 +424,11 @@
             grid_ref[1 + x, 1 + block_of(0, low) * TLY + y] = first_ref[x, y]
             grid_ref[1 + x, 1 + block_of(1, low) * TLY + y] = second_ref[x, y]
         grid_ref[1 + x, border] = column_ref[x]
-    for line, early_ref, late_ref in ((near_row, near0_ref, near1_ref), (far_row, far0_ref, far1_ref)):
+    for line, line_ref in ((near_row, near_ref), (far_row, far_ref)):
         for y in range(TLY):
-            grid_ref[line, 1 + block_of(0, low) * TLY + y] = early_ref[y]
-            grid_ref[line, 1 + block_of(1, low) * TLY + y] = late_ref[y]
-        grid_ref[line, border] = early_ref[TLY]
+            grid_ref[line, 1 + block_of(1, low) * TLY + y] = line_ref[y]
+            grid_ref[line, 1 + block_of(0, low) * TLY + y] = line_ref[TLY + y]
+        grid_ref[line, border] = line_ref[2 * TLY]
     for x in range(TLX + 2):
         grid_ref[x, outside] = blank
 
@@ -470,15 +467,8 @@
             key_ref[b, h * LANES : (h + 1) * LANES, :] = jnp.concatenate(
                 [jnp.where(mine, keys[s], 0.0) for s in spans], axis=1
             ).astype(BF)
-            turned = [pltpu.roll(values[s], LANES // HEADS, 1) for s in spans]
-            value_ref[b, h] = jnp.concatenate(
-                [
-                    jnp.where(left, values[spans[p]], turned[p + 1])
-                    if h == 0
-                    else jnp.where(left, turned[p + 1], values[spans[p]])
-                    for p in (0, 2)
-                ],
-                axis=1,
+            value_ref[b, h * LANES : (h + 1) * LANES, :] = jnp.concatenate(
+                [jnp.where(mine, values[s], 0.0) for s in spans], axis=1
             ).astype(BF)
 
 
@@ -510,22 +500,18 @@
                 jnp.sum(weights[:, h * LANES : (h + 1) * LANES], axis=1, keepdims=True)
                 for h in range(HEADS)
             ]
-            every = [
-                dot(weights[:, h * LANES : (h + 1) * LANES].astype(BF), value_ref[block, h])
-                for h in range(HEADS)
-            ]
+            every = dot(weights.astype(BF), value_ref[block])
             pieces = pieces_of(c * group, group, half_id, along_y)
             attended = []
             for k in range(group):
-                first, second, third = row_bounds(pieces[k], counts_ref, along_y * TLY)
+                bounds = row_bounds(pieces[k], counts_ref, along_y * TLY)
                 span = slice(k * quota, (k + 1) * quota)
-                upper = row >= second
-                odd = ((row >= first) & (row < second)) | (row >= third)
-                part = [jnp.where(upper, e[span, LANES:], e[span, :LANES]) for e in every]
-                even_tile = jnp.where(left, part[0], part[1])
-                odd_tile = pltpu.roll(jnp.where(left, part[1], part[0]), LANES // HEADS, 1)
+                part = every[span]
+                picked = part[:, :LANES]
+                for t, bound in enumerate(bounds):
+                    tile = part[:, (t + 1) * LANES : (t + 2) * LANES]
+                    picked = jnp.where(row >= bound, tile, picked)
                 total = jnp.where(left, totals[0][span], totals[1][span])
-                picked = jnp.where(odd, odd_tile, even_tile)
                 attended.append(quotient(picked, total).astype(BF))
             x = jnp.concatenate([rows_ref[c * group + k] for k in range(group)], axis=0)
             added = dot(jnp.concatenate(attended, axis=0), proj_ref[3])
@@ -705,46 +691,31 @@
     near_pairs = [(i, i ^ 1) for i in range(along_x)]
     far_pairs = [(i, ((i + 1) ^ 1) - 1) for i in range(1, along_x - 1)]
 
-    def halo(near, far):
-        far = lax.ppermute(far, "tx", far_pairs)
-        return lax.ppermute(near, "tx", near_pairs), far
-
-    early = shape((TLY + 1, LANES, width))
-    near0, far0 = halo(
-        *call(
-            early_lines_kernel,
-            "early_lines",
-            (early,) * 2,
-            "vva",
-            [],
-            0.01,
-            (first_half, column, query1),
-        )
-    )
-    late = shape((TLY, LANES, width))
-    second_half, near1, far1 = call(
+    line = shape((2 * TLY + 1, LANES, width))
+    second_half, near, far = call(
         combine_second_kernel,
         "combine_second",
-        (shape((TLX, TLY, LANES, width)), late, late),
-        "vvvva",
+        (shape((TLX, TLY, LANES, width)), line, line),
+        "vvvvvva",
         [],
         0.01,
-        (own1, other1, inducing, first_proj, query1),
-    )
-    near1, far1 = halo(near1, far1)
+        (own1, other1, inducing, first_proj, first_half, column, query1),
+    )
+    near = lax.ppermute(near, "tx", near_pairs)
+    far = lax.ppermute(far, "tx", far_pairs)
 
     keys, values = call(
         mixture_kernel,
         "mix_tiles",
-        (shape((blocks, HEADS * LANES, 4 * LANES)), shape((blocks, HEADS, LANES, 2 * LANES))),
-        "v" * 9,
+        (shape((blocks, HEADS * LANES, 4 * LANES)), shape((blocks, HEADS * LANES, 4 * LANES))),
+        "v" * 7,
         [
             VMEM((TLX + 2, tall + 2, LANES, width), BF),
             VMEM((6 * LANES, 2 * LANES), BF),
             VMEM((2, 4 * LANES, 2 * LANES), BF),
         ],
         1,
-        (first_half, column, second_half, near0, far0, near1, far1, second_proj, mixing),
+        (first_half, column, second_half, near, far, second_proj, mixing),
     )
 
     result = call(

time: 92.7 us -> 86.2 us (0.930)
  Pallas kernels: 36.8 us -> 31.7 us
  starting transfers between devices: 21 us -> 17.5 us
  blocking collectives: 23.8 us -> 25.5 us
    pallas_call x11 -> x10, Pallas kernels: 36.8 us -> 31.7 us  [call(): pl.pallas_call(kernel, out_shape=out_shape, in_specs=[pl.BlockSpec(memory...]
    ppermute x4 -> x2, starting transfers between devices: 4.45 us -> 0.87 us  [the longest x1 0.8 us: body(): far = lax.ppermute(far, 'tx', far_pairs)]
    all_to_all x1, blocking collectives: 23.8 us -> 25.5 us  [exchange(): lax.all_to_all(rows, ('tx', 'zl'), split_axis=0, concat_axis=0, tiled=True)]
  transfers between devices with their start and end apart: 9 -> 7, of which waited for: 4 -> 6; matrix products, arithmetic and copies ran while one was open for 0% -> 0% of each run, Pallas kernels for 16% -> 16%
where the time goes in v12:
time: 86.2 us; the launch traced here: 85.7 us
  Pallas kernels  31.7 us (37%)
  blocking collectives  25.5 us (30%)
  starting transfers between devices  17.5 us (20%)
  waiting for transfers between devices  8.61 us (10%)
  local copies, waits for them, and re-layouts  2.08 us (2%)
    pallas_call x10, Pallas kernels, call(): pl.pallas_call(kernel, out_shape=out_shape, in_specs=[pl.BlockSpec(memory...  31.7 us
    all_to_all x1, blocking collectives, exchange(): lax.all_to_all(rows, ('tx', 'zl'), split_axis=0, concat_axis=0, tiled=True)  25.5 us
    all_to_all x2, starting transfers between devices, exchange(): lax.all_to_all(rows, ('tx', 'zl'), split_axis=0, concat_axis=0, tiled=True)  10.1 us
    ppermute x3, starting transfers between devices, swap(): return lax.ppermute(value, ('zh', 'zl'), steps)  6.48 us
    ppermute x3, waiting for transfers between devices, swap(): return lax.ppermute(value, ('zh', 'zl'), steps)  4.41 us
    all_to_all x2, waiting for transfers between devices, exchange(): lax.all_to_all(rows, ('tx', 'zl'), split_axis=0, concat_axis=0, tiled=True)  3.63 us
    unnamed x26, local copies, waits for them, and re-layouts  2.08 us
  transfers between devices with their start and end apart: 7, of which 6 were waited for; matrix products, arithmetic and copies ran while one was open for 0% of the time, Pallas kernels for 16%

profile of v12, /device:TPU:0, one launch (start us, length us, event | category | flops | bytes accessed | tf_op | source)
XLA Modules:
  0.0 85.7 jit_solution(11071021124767171488)
XLA Ops:
  0.0 0.0 copy-start.4
  0.0 0.0 copy-start.5
  0.0 0.0 copy-start.7
  0.0 0.0 copy-start.8
  0.0 7.1 %encode_first.1 = (bf16[16,128,128]{2,1,0:T(8,128)(2,1)}, s32[32,128]{1,0:T(8,128)}) custom-call(bf16[4096,128]{1,0:T(8,128)(2,1)} %points_ref.1, bf16[128,512]{1,0:T(8,128)(2,1)} %w1_ref.1, bf16[1,512,512]{2,1,0:T(8,128)(2,1)} %w2_ref.1, bf16[512,128]{1,0:T(8,128)(2,1)} %w3_ref.1, s32[32,128]{1,0:T(8,128)} %counts_ref.7, s32[32,128]{1,0:T(8,128)} %bitcast.1), custom_call_target="tpu_custom_call" | custom-call | flops 4000000000 | bytes 8000000 | tf_op jit(solution)/shard_map/encode_first/pallas_call | solution.py:555
  7.1 6.3 %all-to-all-start = ((bf16[16,128,128]{2,1,0:T(8,128)(2,1)}), bf16[16,128,128]{2,1,0:T(8,128)(2,1)S(1)}, u32[]{:S(2)}, u32[]{:S(2)}) async-start(bf16[16,128,128]{2,1,0:T(8,128)(2,1)} %get-tuple-element.21), calls=%async_computation | async-start | bytes 1048576 | tf_op jit(solution)/shard_map/all_to_all | solution.py:632
  13.5 0.0 copy-done.4
  13.5 0.0 copy-done.5
  13.5 0.0 copy-done.7
  13.5 0.0 copy-done.8
  13.5 0.0 copy-start.11
  13.5 0.7 copy-done.11
  14.2 0.0 copy-start
  14.2 0.0 copy-start.1
  14.2 5.2 %encode_second.1 = bf16[16,128,128]{2,1,0:T(8,128)(2,1)} custom-call(bf16[4096,128]{1,0:T(8,128)(2,1)S(1)} %copy-done.4, bf16[128,512]{1,0:T(8,128)(2,1)S(1)} %copy-done.7, bf16[1,512,512]{2,1,0:T(8,128)(2,1)S(1)} %copy-done.5, bf16[512,128]{1,0:T(8,128)(2,1)S(1)} %copy-done.8, s32[32,128]{1,0:T(8,128)S(1)} %copy-done.11), custom_call_target="tpu_custom_call" | custom-call | flops 3000000000 | bytes 6000000 | tf_op jit(solution)/shard_map/encode_second/pallas_call | solution.py:555
  19.5 2.7 %all-to-all-done.rows_ref.rows0_ref = bf16[16,128,128]{2,1,0:T(8,128)(2,1)S(1)} async-done(((bf16[16,128,128]{2,1,0:T(8,128)(2,1)}), bf16[16,128,128]{2,1,0:T(8,128)(2,1)S(1)}, u32[]{:S(2)}, u32[]{:S(2)}) %all-to-all-start) | async-done | bytes 524320 | tf_op jit(solution)/shard_map/all_to_all | solution.py:632
  22.2 3.8 %all-to-all-start.1 = ((bf16[16,128,128]{2,1,0:T(8,128)(2,1)}), bf16[16,128,128]{2,1,0:T(8,128)(2,1)S(1)}, u32[]{:S(2)}, u32[]{:S(2)}) async-start(bf16[16,128,128]{2,1,0:T(8,128)(2,1)} %encode_second.1), calls=%async_computation.1 | async-start | bytes 1048576 | tf_op jit(solution)/shard_map/all_to_all | solution.py:632
  26.0 0.0 copy-done
  26.0 0.0 copy-done.1
  26.0 0.0 copy-done.2
  26.0 0.0 copy-done.3
  26.0 3.8 %partial_first.1 = (f32[528,128]{1,0:T(8,128)S(1)}, bf16[528,128]{1,0:T(8,128)(2,1)S(1)}, bf16[256,128]{1,0:T(8,128)(2,1)S(1)}, bf16[128,128]{1,0:T(8,128)(2,1)S(1)}, bf16[16,128,512]{2,1,0:T(8,128)(2,1)S(1)}) custom-call(bf16[16,128,128]{2,1,0:T(8,128)(2,1)S(1)} %all-to-all-done.rows_ref.rows0_ref, s32[32,128]{1,0:T(8,128)S(1)} %copy-done.3, ...), custom_call_target="tpu_custom_call" | custom-call | flops 1500000000 | bytes 3000000 | tf_op jit(solution)/shard_map/partial_first/pallas_call | solution.py:555
  29.9 0.0 copy-start.9
  29.9 1.3 %copy-done.9 = bf16[16,128,512]{2,1,0:T(8,128)(2,1)} copy-done((bf16[16,128,512]{2,1,0:T(8,128)(2,1)}, bf16[16,128,512]{2,1,0:T(8,128)(2,1)S(1)}, u32[]{:S(2)}) %copy-start.9) | copy-done | bytes 2097176
  31.2 2.6 %collective-permute-start = (bf16[528,128]{1,0:T(8,128)(2,1)S(1)}, bf16[528,128]{1,0:T(8,128)(2,1)S(1)}, u32[]{:S(2)}, u32[]{:S(2)}) collective-permute-start(bf16[528,128]{1,0:T(8,128)(2,1)S(1)} %get-tuple-element.25), channel_id=1, source_target_pairs={{0,2},{1,3},{2,0},{3,1},{4,6},{5,7},{6,4},{7,5},{8,10},{9,11},{10,... | collective-permute-start | bytes 405512 | tf_op jit(solution)/shard_map/ppermute | solution.py:659
  33.8 0.9 %all-to-all-done.1.rows_ref.rows1_ref = bf16[16,128,128]{2,1,0:T(8,128)(2,1)S(1)} async-done(((bf16[16,128,128]{2,1,0:T(8,128)(2,1)}), bf16[16,128,128]{2,1,0:T(8,128)(2,1)S(1)}, u32[]{:S(2)}, u32[]{:S(2)}) %all-to-all-start.1) | async-done | bytes 524320 | tf_op jit(solution)/shard_map/all_to_all | solution.py:632
  34.7 2.7 %partial_second.1 = (f32[528,128]{1,0:T(8,128)S(1)}, bf16[528,128]{1,0:T(8,128)(2,1)S(1)}) custom-call(bf16[16,128,128]{2,1,0:T(8,128)(2,1)S(1)} %all-to-all-done.1.rows_ref.rows1_ref, s32[32,128]{1,0:T(8,128)S(1)} %copy-done.3, bf16[256,128]{1,0:T(8,128)(2,1)S(1)} %get-tuple-element.26.rest_0_, bf16[128,128]{1,0:T(8,128)(2,1)S(1)} %get-tuple-element.27.rest_1_, ...), custom_call_target="tpu_custom_call" | custom-call | flops 1500000000 | bytes 3000000 | tf_op jit(solution)/shard_map/partial_second/pallas_call | solution.py:555
  37.4 3.1 %collective-permute-start.2 = (bf16[528,128]{1,0:T(8,128)(2,1)S(1)}, bf16[528,128]{1,0:T(8,128)(2,1)S(1)}, u32[]{:S(2)}, u32[]{:S(2)}) collective-permute-start(bf16[528,128]{1,0:T(8,128)(2,1)S(1)} %get-tuple-element.28.after_any), channel_id=1, source_target_pairs={{0,2},{1,3},{2,0},{3,1},{4,6},{5,7},{6,4},{7,5},{8,10},{9,11},{10,... | collective-permute-start | bytes 405512 | tf_op jit(solution)/shard_map/ppermute | solution.py:659
  40.6 0.3 collective-permute-done.other_ref
  40.9 0.3 combine_first.1
  41.2 0.8 collective-permute-start.1
  41.9 1.9 %queries_second.1.query_any.query1_ref = bf16[16,128,512]{2,1,0:T(8,128)(2,1)S(1)} custom-call(bf16[16,128,128]{2,1,0:T(8,128)(2,1)S(1)} %all-to-all-done.1.rows_ref.rows1_ref, s32[32,128]{1,0:T(8,128)S(1)} %copy-done.3, bf16[4,128,128]{2,1,0:T(8,128)(2,1)S(1)} %copy-done.2, bf16[2,128,128]{2,1,0:T(8,128)(2,1)S(1)} %get-tuple-element.29.before_any), custom_call_target="tpu_custom_call" | custom-call | flops 5000000 | bytes 10000 | tf_op jit(solution)/shard_map/queries_second/pallas_call | solution.py:555
  43.8 0.0 copy-start.6
  43.9 3.5 %collective-permute-done.2.other_ref = bf16[528,128]{1,0:T(8,128)(2,1)S(1)} collective-permute-done((bf16[528,128]{1,0:T(8,128)(2,1)S(1)}, bf16[528,128]{1,0:T(8,128)(2,1)S(1)}, u32[]{:S(2)}, u32[]{:S(2)}) %collective-permute-start.2) | collective-permute-done | bytes 135200 | tf_op jit(solution)/shard_map/ppermute | solution.py:659
  47.3 0.6 collective-permute-done.1.column_ref
  47.9 0.3 combine_second.1
  48.2 0.1 collective-permute-start.3
  48.3 0.8 collective-permute-start.4
  49.1 0.6 collective-permute-done.3.near_ref
  49.7 0.0 collective-permute-done.4.far_ref
  49.7 0.0 copy-done.6
  49.7 0.9 %mix_tiles.1 = (bf16[2,256,512]{2,1,0:T(8,128)(2,1)S(1)}, bf16[2,256,512]{2,1,0:T(8,128)(2,1)S(1)}) custom-call(bf16[2,2,128,128]{3,2,1,0:T(8,128)(2,1)S(1)} %get-tuple-element.30.first_ref, bf16[2,128,128]{2,1,0:T(8,128)(2,1)S(1)} %collective-permute-done.1.column_ref, bf16[2,2,128,128]{3,2,1,0:T(8,128)(2,1)S(1)} %get-tuple-element.32.second_ref, ...), custom_call_target="tpu_custom_call" | custom-call | flops 500000000 | bytes 1000000 | tf_op jit(solution)/shard_map/mix_tiles/pallas_call | solution.py:555
  50.6 0.0 copy-done.10
  50.6 4.3 %attend_points.1 = bf16[16,2,128,128]{3,2,1,0:T(8,128)(2,1)S(1)} custom-call(bf16[16,128,128]{2,1,0:T(8,128)(2,1)S(1)} %all-to-all-done.rows_ref.rows0_ref, bf16[16,128,128]{2,1,0:T(8,128)(2,1)S(1)} %all-to-all-done.1.rows_ref.rows1_ref, bf16[16,128,512]{2,1,0:T(8,128)(2,1)S(1)} %copy-done.10, bf16[16,128,512]{2,1,0:T(8,128)(2,1)S(1)} %queries_second.1.query_any.query1_ref, ...), custom_call_target="tpu_custom_call" | custom-call | flops 3500000000 | bytes 7000000 | tf_op jit(solution)/shard_map/attend_points/pallas_call | solution.py:555
  54.9 0.0 copy-start.12
  54.9 25.5 %all_to_all.15.rows_ref = bf16[16,2,128,128]{3,2,1,0:T(8,128)(2,1)S(1)} all-to-all(bf16[16,2,128,128]{3,2,1,0:T(8,128)(2,1)S(1)} %attend_points.1), channel_id=1, replica_groups=mesh['tx'=8,'zh'=2,'zl'=2] {'tx','zl'}, dimensions={0} | all-to-all | bytes 2097152 | tf_op jit(solution)/shard_map/all_to_all | solution.py:632
  80.5 0.0 copy-done.12
  80.5 5.1 %scatter_rows.1 = bf16[4096,128]{1,0:T(8,128)(2,1)} custom-call(bf16[16,2,128,128]{3,2,1,0:T(8,128)(2,1)S(1)} %all_to_all.15.rows_ref, s32[32,128]{1,0:T(8,128)S(1)} %copy-done.12), custom_call_target="tpu_custom_call" | custom-call | flops 2500000000 | bytes 5000000 | tf_op jit(solution)/shard_map/scatter_rows/pallas_call | solution.py:555
  (3 shorter events, 0.0 us)
Async XLA Ops:
  0.0 13.5 %copy-start.4 = (bf16[4096,128]{1,0:T(8,128)(2,1)S(1)}, bf16[4096,128]{1,0:T(8,128)(2,1)}, u32[]{:S(2)}) copy-start(bf16[4096,128]{1,0:T(8,128)(2,1)} %points_ref.1) | copy-start | bytes 3145732
  0.0 13.5 %copy-start.5 = (bf16[1,512,512]{2,1,0:T(8,128)(2,1)S(1)}, bf16[1,512,512]{2,1,0:T(8,128)(2,1)}, u32[]{:S(2)}) copy-start(bf16[1,512,512]{2,1,0:T(8,128)(2,1)} %w2_ref.1) | copy-start | bytes 1572868
  0.0 13.5 %copy-start.7 = (bf16[128,512]{1,0:T(8,128)(2,1)S(1)}, bf16[128,512]{1,0:T(8,128)(2,1)}, u32[]{:S(2)}) copy-start(bf16[128,512]{1,0:T(8,128)(2,1)} %w1_ref.1) | copy-start | bytes 393220
  0.0 13.5 %copy-start.8 = (bf16[512,128]{1,0:T(8,128)(2,1)S(1)}, bf16[512,128]{1,0:T(8,128)(2,1)}, u32[]{:S(2)}) copy-start(bf16[512,128]{1,0:T(8,128)(2,1)} %w3_ref.1) | copy-start | bytes 393220
  7.1 15.1 %all-to-all-start = ((bf16[16,128,128]{2,1,0:T(8,128)(2,1)}), bf16[16,128,128]{2,1,0:T(8,128)(2,1)S(1)}, u32[]{:S(2)}, u32[]{:S(2)}) async-start(bf16[16,128,128]{2,1,0:T(8,128)(2,1)} %get-tuple-element.21), calls=%async_computation | async-start | bytes 1048576 | tf_op jit(solution)/shard_map/all_to_all | solution.py:632
  13.5 0.7 copy-start.11
  14.2 11.8 %copy-start = (bf16[4,128,128]{2,1,0:T(8,128)(2,1)S(1)}, bf16[4,128,128]{2,1,0:T(8,128)(2,1)}, u32[]{:S(2)}) copy-start(bf16[4,128,128]{2,1,0:T(8,128)(2,1)} %proj_ref.7) | copy-start | bytes 393220
  14.2 11.8 %copy-start.1 = (bf16[128,128]{1,0:T(8,128)(2,1)S(1)}, bf16[128,128]{1,0:T(8,128)(2,1)}, u32[]{:S(2)}) copy-start(bf16[128,128]{1,0:T(8,128)(2,1)} %inducing_ref.3) | copy-start | bytes 98308
  14.2 11.8 %copy-start.2 = (bf16[4,128,128]{2,1,0:T(8,128)(2,1)S(1)}, bf16[4,128,128]{2,1,0:T(8,128)(2,1)}, u32[]{:S(2)}) copy-start(bf16[4,128,128]{2,1,0:T(8,128)(2,1)} %proj_ref.9) | copy-start | bytes 393220
  14.2 11.8 %copy-start.3 = (s32[32,128]{1,0:T(8,128)S(1)}, s32[32,128]{1,0:T(8,128)}, u32[]{:S(2)}) copy-start(s32[32,128]{1,0:T(8,128)} %counts_ref.7) | copy-start | bytes 49156
  22.2 12.5 %all-to-all-start.1 = ((bf16[16,128,128]{2,1,0:T(8,128)(2,1)}), bf16[16,128,128]{2,1,0:T(8,128)(2,1)S(1)}, u32[]{:S(2)}, u32[]{:S(2)}) async-start(bf16[16,128,128]{2,1,0:T(8,128)(2,1)} %encode_second.1), calls=%async_computation.1 | async-start | bytes 1048576 | tf_op jit(solution)/shard_map/all_to_all | solution.py:632
  29.9 1.3 %copy-start.9 = (bf16[16,128,512]{2,1,0:T(8,128)(2,1)}, bf16[16,128,512]{2,1,0:T(8,128)(2,1)S(1)}, u32[]{:S(2)}) copy-start(bf16[16,128,512]{2,1,0:T(8,128)(2,1)S(1)} %get-tuple-element.23.query0_ref) | copy-start | bytes 6291460
  31.2 9.7 %collective-permute-start = (bf16[528,128]{1,0:T(8,128)(2,1)S(1)}, bf16[528,128]{1,0:T(8,128)(2,1)S(1)}, u32[]{:S(2)}, u32[]{:S(2)}) collective-permute-start(bf16[528,128]{1,0:T(8,128)(2,1)S(1)} %get-tuple-element.25), channel_id=1, source_target_pairs={{0,2},{1,3},{2,0},{3,1},{4,6},{5,7},{6,4},{7,5},{8,10},{9,11},{10,... | collective-permute-start | bytes 405512 | tf_op jit(solution)/shard_map/ppermute | solution.py:659
  37.4 9.9 %collective-permute-start.2 = (bf16[528,128]{1,0:T(8,128)(2,1)S(1)}, bf16[528,128]{1,0:T(8,128)(2,1)S(1)}, u32[]{:S(2)}, u32[]{:S(2)}) collective-permute-start(bf16[528,128]{1,0:T(8,128)(2,1)S(1)} %get-tuple-element.28.after_any), channel_id=1, source_target_pairs={{0,2},{1,3},{2,0},{3,1},{4,6},{5,7},{6,4},{7,5},{8,10},{9,11},{10,... | collective-permute-start | bytes 405512 | tf_op jit(solution)/shard_map/ppermute | solution.py:659
  41.2 6.7 %collective-permute-start.1 = (bf16[2,128,128]{2,1,0:T(8,128)(2,1)S(1)}, bf16[2,128,128]{2,1,0:T(8,128)(2,1)S(1)}, u32[]{:S(2)}, u32[]{:S(2)}) collective-permute-start(bf16[2,128,128]{2,1,0:T(8,128)(2,1)S(1)} %get-tuple-element.29.before_any), channel_id=1, source_target_pairs={{0,1},{1,0},{2,3},{3,2},{4,5},{5,4},{6,7},{7,6},{8,9},{9,8},{10,11... | collective-permute-start | bytes 196616 | tf_op jit(solution)/shard_map/ppermute | solution.py:659
  43.8 5.8 %copy-start.6 = (bf16[8,128,128]{2,1,0:T(8,128)(2,1)S(1)}, bf16[8,128,128]{2,1,0:T(8,128)(2,1)}, u32[]{:S(2)}) copy-start(bf16[8,128,128]{2,1,0:T(8,128)(2,1)} %mixing_ref.1) | copy-start | bytes 786436
  47.9 2.7 %copy-start.10 = (bf16[16,128,512]{2,1,0:T(8,128)(2,1)S(1)}, bf16[16,128,512]{2,1,0:T(8,128)(2,1)}, u32[]{:S(2)}) copy-start(bf16[16,128,512]{2,1,0:T(8,128)(2,1)} %copy-done.9) | copy-start | bytes 6291460
  48.2 1.5 %collective-permute-start.3 = (bf16[5,128,128]{2,1,0:T(8,128)(2,1)S(1)}, bf16[5,128,128]{2,1,0:T(8,128)(2,1)S(1)}, u32[]{:S(2)}, u32[]{:S(2)}) collective-permute-start(bf16[5,128,128]{2,1,0:T(8,128)(2,1)S(1)} %get-tuple-element.33), channel_id=1, source_target_pairs={{0,4},{4,0},{8,12},{12,8},{16,20},{20,16},{24,28},{28,24},{1,5},{5... | collective-permute-start | bytes 491528 | tf_op jit(solution)/shard_map/ppermute | solution.py:704
  48.3 1.4 %collective-permute-start.4 = (bf16[5,128,128]{2,1,0:T(8,128)(2,1)S(1)}, bf16[5,128,128]{2,1,0:T(8,128)(2,1)S(1)}, u32[]{:S(2)}, u32[]{:S(2)}) collective-permute-start(bf16[5,128,128]{2,1,0:T(8,128)(2,1)S(1)} %get-tuple-element.34), channel_id=1, source_target_pairs={{4,8},{8,4},{12,16},{16,12},{20,24},{24,20},{5,9},{9,5},{13,17},{1... | collective-permute-start | bytes 491528 | tf_op jit(solution)/shard_map/ppermute | solution.py:705
  54.9 25.5 %copy-start.12 = (s32[32,128]{1,0:T(8,128)S(1)}, s32[32,128]{1,0:T(8,128)}, u32[]{:S(2)}) copy-start(s32[32,128]{1,0:T(8,128)} %get-tuple-element.22.index_any.index_ref) | copy-start | bytes 49156

commit v13 on v12

--- a/solution.py
+++ b/solution.py
@@ -344,32 +344,42 @@
         column_ref[x] = jnp.where(lax.axis_index("zl") == 0, out_ref[x, TLY - 1], out_ref[x, 0])
 
 
-def pair_lines(rows, near_ref, far_ref):
-    even = lax.axis_index("tx") % 2 == 0
+def send_line(near, rows, out_ref):
+    upper = lax.axis_index("tx") % 2 == (0 if near else 1)
     for y, (low, high) in enumerate(zip(*rows)):
-        near_ref[y] = jnp.where(even, high, low)
-        far_ref[y] = jnp.where(even, low, high)
+        out_ref[y] = jnp.where(upper, high, low)
 
 
 def combine_second_kernel(
-    own_ref, other_ref, inducing_ref, proj_ref, first_ref, column_ref, query_any, out_ref, near_ref, far_ref
+    own_ref,
+    other_ref,
+    inducing_ref,
+    proj_ref,
+    first_ref,
+    column_ref,
+    query_any,
+    out_ref,
+    near0_ref,
+    near1_ref,
+    far_ref,
 ):
     def store(x, y, value):
         out_ref[x, y] = value
 
     summarize(1, own_ref, other_ref, inducing_ref, proj_ref, store)
-    rows = [
-        [out_ref[x, y] for y in range(TLY)] + [first_ref[x, y] for y in range(TLY)] + [column_ref[x]]
-        for x in range(TLX)
-    ]
-    pair_lines(rows, near_ref, far_ref)
+    late = [[out_ref[x, y] for y in range(TLY)] for x in range(TLX)]
+    early = [[first_ref[x, y] for y in range(TLY)] + [column_ref[x]] for x in range(TLX)]
+    send_line(False, [a + b for a, b in zip(late, early)], far_ref)
+    send_line(True, early, near0_ref)
+    send_line(True, late, near1_ref)
 
 
 def mixture_kernel(
     first_ref,
     column_ref,
     second_ref,
-    near_ref,
+    near0_ref,
+    near1_ref,
     far_ref,
     proj_ref,
     mixing_ref,
@@ -424,11 +434,13 @@
             grid_ref[1 + x, 1 + block_of(0, low) * TLY + y] = first_ref[x, y]
             grid_ref[1 + x, 1 + block_of(1, low) * TLY + y] = second_ref[x, y]
         grid_ref[1 + x, border] = column_ref[x]
-    for line, line_ref in ((near_row, near_ref), (far_row, far_ref)):
-        for y in range(TLY):
-            grid_ref[line, 1 + block_of(1, low) * TLY + y] = line_ref[y]
-            grid_ref[line, 1 + block_of(0, low) * TLY + y] = line_ref[TLY + y]
-        grid_ref[line, border] = line_ref[2 * TLY]
+    for y in range(TLY):
+        grid_ref[near_row, 1 + block_of(1, low) * TLY + y] = near1_ref[y]
+        grid_ref[near_row, 1 + block_of(0, low) * TLY + y] = near0_ref[y]
+        grid_ref[far_row, 1 + block_of(1, low) * TLY + y] = far_ref[y]
+        grid_ref[far_row, 1 + block_of(0, low) * TLY + y] = far_ref[TLY + y]
+    grid_ref[near_row, border] = near0_ref[TLY]
+    grid_ref[far_row, border] = far_ref[2 * TLY]
     for x in range(TLX + 2):
         grid_ref[x, outside] = blank
 
@@ -691,31 +703,34 @@
     near_pairs = [(i, i ^ 1) for i in range(along_x)]
     far_pairs = [(i, ((i + 1) ^ 1) - 1) for i in range(1, along_x - 1)]
 
-    line = shape((2 * TLY + 1, LANES, width))
-    second_half, near, far = call(
+    def tiles(count):
+        return shape((count, LANES, width))
+
+    second_half, near0, near1, far = call(
         combine_second_kernel,
         "combine_second",
-        (shape((TLX, TLY, LANES, width)), line, line),
+        (shape((TLX, TLY, LANES, width)), tiles(TLY + 1), tiles(TLY), tiles(2 * TLY + 1)),
         "vvvvvva",
         [],
         0.01,
         (own1, other1, inducing, first_proj, first_half, column, query1),
     )
-    near = lax.ppermute(near, "tx", near_pairs)
     far = lax.ppermute(far, "tx", far_pairs)
+    near0 = lax.ppermute(near0, "tx", near_pairs)
+    near1 = lax.ppermute(near1, "tx", near_pairs)
 
     keys, values = call(
         mixture_kernel,
         "mix_tiles",
         (shape((blocks, HEADS * LANES, 4 * LANES)), shape((blocks, HEADS * LANES, 4 * LANES))),
-        "v" * 7,
+        "v" * 8,
         [
             VMEM((TLX + 2, tall + 2, LANES, width), BF),
             VMEM((6 * LANES, 2 * LANES), BF),
             VMEM((2, 4 * LANES, 2 * LANES), BF),
         ],
         1,
-        (first_half, column, second_half, near, far, second_proj, mixing),
+        (first_half, column, second_half, near0, near1, far, second_proj, mixing),
     )
 
     result = call(

time: 86.2 us -> 85.2 us (0.988)
  blocking collectives: 25.5 us -> 21 us
  starting transfers between devices: 17.5 us -> 20.3 us
    all_to_all x1, blocking collectives: 25.5 us -> 21 us  [exchange(): lax.all_to_all(rows, ('tx', 'zl'), split_axis=0, concat_axis=0, tiled=True)]
    ppermute x1 -> x2, starting transfers between devices: 0.07 us -> 2.91 us  [the longest x1 2.83 us: body(): near0 = lax.ppermute(near0, 'tx', near_pairs)]
  transfers between devices with their start and end apart: 7 -> 8, of which waited for: 6 -> 6; matrix products, arithmetic and copies ran while one was open for 0% -> 0% of each run, Pallas kernels for 16% -> 16%
where the time goes in v13:
time: 85.2 us; the launch traced here: 84.7 us
  Pallas kernels  31.7 us (37%)
  blocking collectives  21 us (25%)
  starting transfers between devices  20.3 us (24%)
  waiting for transfers between devices  9.21 us (11%)
  local copies, waits for them, and re-layouts  2.09 us (2%)
    pallas_call x10, Pallas kernels, call(): pl.pallas_call(kernel, out_shape=out_shape, in_specs=[pl.BlockSpec(memory...  31.7 us
    all_to_all x1, blocking collectives, exchange(): lax.all_to_all(rows, ('tx', 'zl'), split_axis=0, concat_axis=0, tiled=True)  21 us
    all_to_all x2, starting transfers between devices, exchange(): lax.all_to_all(rows, ('tx', 'zl'), split_axis=0, concat_axis=0, tiled=True)  10.1 us
    ppermute x3, starting transfers between devices, swap(): return lax.ppermute(value, ('zh', 'zl'), steps)  6.47 us
    ppermute x3, waiting for transfers between devices, swap(): return lax.ppermute(value, ('zh', 'zl'), steps)  4.42 us
    all_to_all x2, waiting for transfers between devices, exchange(): lax.all_to_all(rows, ('tx', 'zl'), split_axis=0, concat_axis=0, tiled=True)  3.61 us
    ppermute x1, starting transfers between devices, body(): near0 = lax.ppermute(near0, 'tx', near_pairs)  2.83 us
    unnamed x26, local copies, waits for them, and re-layouts  2.09 us
  transfers between devices with their start and end apart: 8, of which 6 were waited for; matrix products, arithmetic and copies ran while one was open for 0% of the time, Pallas kernels for 16%

profile of v13, /device:TPU:0, one launch (start us, length us, event | category | flops | bytes accessed | tf_op | source)
XLA Modules:
  0.0 84.7 jit_solution(2481665826595508701)
XLA Ops:
  0.0 0.0 copy-start.4
  0.0 0.0 copy-start.5
  0.0 0.0 copy-start.7
  0.0 0.0 copy-start.8
  0.0 7.1 %encode_first.1 = (bf16[16,128,128]{2,1,0:T(8,128)(2,1)}, s32[32,128]{1,0:T(8,128)}) custom-call(bf16[4096,128]{1,0:T(8,128)(2,1)} %points_ref.1, bf16[128,512]{1,0:T(8,128)(2,1)} %w1_ref.1, bf16[1,512,512]{2,1,0:T(8,128)(2,1)} %w2_ref.1, bf16[512,128]{1,0:T(8,128)(2,1)} %w3_ref.1, s32[32,128]{1,0:T(8,128)} %counts_ref.7, s32[32,128]{1,0:T(8,128)} %bitcast.1), custom_call_target="tpu_custom_call" | custom-call | flops 4000000000 | bytes 8000000 | tf_op jit(solution)/shard_map/encode_first/pallas_call | solution.py:567
  7.1 6.3 %all-to-all-start = ((bf16[16,128,128]{2,1,0:T(8,128)(2,1)}), bf16[16,128,128]{2,1,0:T(8,128)(2,1)S(1)}, u32[]{:S(2)}, u32[]{:S(2)}) async-start(bf16[16,128,128]{2,1,0:T(8,128)(2,1)} %get-tuple-element.22), calls=%async_computation | async-start | bytes 1048576 | tf_op jit(solution)/shard_map/all_to_all | solution.py:644
  13.5 0.0 copy-done.4
  13.5 0.0 copy-done.5
  13.5 0.0 copy-done.7
  13.5 0.0 copy-done.8
  13.5 0.0 copy-start.11
  13.5 0.7 copy-done.11
  14.2 5.2 %encode_second.1 = bf16[16,128,128]{2,1,0:T(8,128)(2,1)} custom-call(bf16[4096,128]{1,0:T(8,128)(2,1)S(1)} %copy-done.4, bf16[128,512]{1,0:T(8,128)(2,1)S(1)} %copy-done.7, bf16[1,512,512]{2,1,0:T(8,128)(2,1)S(1)} %copy-done.5, bf16[512,128]{1,0:T(8,128)(2,1)S(1)} %copy-done.8, s32[32,128]{1,0:T(8,128)S(1)} %copy-done.11), custom_call_target="tpu_custom_call" | custom-call | flops 3000000000 | bytes 6000000 | tf_op jit(solution)/shard_map/encode_second/pallas_call | solution.py:567
  19.5 2.7 %all-to-all-done.rows_ref.rows0_ref = bf16[16,128,128]{2,1,0:T(8,128)(2,1)S(1)} async-done(((bf16[16,128,128]{2,1,0:T(8,128)(2,1)}), bf16[16,128,128]{2,1,0:T(8,128)(2,1)S(1)}, u32[]{:S(2)}, u32[]{:S(2)}) %all-to-all-start) | async-done | bytes 524320 | tf_op jit(solution)/shard_map/all_to_all | solution.py:644
  22.2 3.8 %all-to-all-start.1 = ((bf16[16,128,128]{2,1,0:T(8,128)(2,1)}), bf16[16,128,128]{2,1,0:T(8,128)(2,1)S(1)}, u32[]{:S(2)}, u32[]{:S(2)}) async-start(bf16[16,128,128]{2,1,0:T(8,128)(2,1)} %encode_second.1), calls=%async_computation.1 | async-start | bytes 1048576 | tf_op jit(solution)/shard_map/all_to_all | solution.py:644
  26.0 0.0 copy-done
  26.0 0.0 copy-done.1
  26.0 0.0 copy-done.2
  26.0 0.0 copy-done.3
  26.1 3.8 %partial_first.1 = (f32[528,128]{1,0:T(8,128)S(1)}, bf16[528,128]{1,0:T(8,128)(2,1)S(1)}, bf16[256,128]{1,0:T(8,128)(2,1)S(1)}, bf16[128,128]{1,0:T(8,128)(2,1)S(1)}, bf16[16,128,512]{2,1,0:T(8,128)(2,1)S(1)}) custom-call(bf16[16,128,128]{2,1,0:T(8,128)(2,1)S(1)} %all-to-all-done.rows_ref.rows0_ref, s32[32,128]{1,0:T(8,128)S(1)} %copy-done.3, ...), custom_call_target="tpu_custom_call" | custom-call | flops 1500000000 | bytes 3000000 | tf_op jit(solution)/shard_map/partial_first/pallas_call | solution.py:567
  29.9 0.0 copy-start.9
  29.9 1.3 %copy-done.9 = bf16[16,128,512]{2,1,0:T(8,128)(2,1)} copy-done((bf16[16,128,512]{2,1,0:T(8,128)(2,1)}, bf16[16,128,512]{2,1,0:T(8,128)(2,1)S(1)}, u32[]{:S(2)}) %copy-start.9) | copy-done | bytes 2097176
  31.3 2.6 %collective-permute-start = (bf16[528,128]{1,0:T(8,128)(2,1)S(1)}, bf16[528,128]{1,0:T(8,128)(2,1)S(1)}, u32[]{:S(2)}, u32[]{:S(2)}) collective-permute-start(bf16[528,128]{1,0:T(8,128)(2,1)S(1)} %get-tuple-element.26), channel_id=1, source_target_pairs={{0,2},{1,3},{2,0},{3,1},{4,6},{5,7},{6,4},{7,5},{8,10},{9,11},{10,... | collective-permute-start | bytes 405512 | tf_op jit(solution)/shard_map/ppermute | solution.py:671
  33.9 0.9 %all-to-all-done.1.rows_ref.rows1_ref = bf16[16,128,128]{2,1,0:T(8,128)(2,1)S(1)} async-done(((bf16[16,128,128]{2,1,0:T(8,128)(2,1)}), bf16[16,128,128]{2,1,0:T(8,128)(2,1)S(1)}, u32[]{:S(2)}, u32[]{:S(2)}) %all-to-all-start.1) | async-done | bytes 524320 | tf_op jit(solution)/shard_map/all_to_all | solution.py:644
  34.7 2.7 %partial_second.1 = (f32[528,128]{1,0:T(8,128)S(1)}, bf16[528,128]{1,0:T(8,128)(2,1)S(1)}) custom-call(bf16[16,128,128]{2,1,0:T(8,128)(2,1)S(1)} %all-to-all-done.1.rows_ref.rows1_ref, s32[32,128]{1,0:T(8,128)S(1)} %copy-done.3, bf16[256,128]{1,0:T(8,128)(2,1)S(1)} %get-tuple-element.27.rest_0_, bf16[128,128]{1,0:T(8,128)(2,1)S(1)} %get-tuple-element.28.rest_1_, ...), custom_call_target="tpu_custom_call" | custom-call | flops 1500000000 | bytes 3000000 | tf_op jit(solution)/shard_map/partial_second/pallas_call | solution.py:567
  37.4 3.1 %collective-permute-start.2 = (bf16[528,128]{1,0:T(8,128)(2,1)S(1)}, bf16[528,128]{1,0:T(8,128)(2,1)S(1)}, u32[]{:S(2)}, u32[]{:S(2)}) collective-permute-start(bf16[528,128]{1,0:T(8,128)(2,1)S(1)} %get-tuple-element.29.after_any), channel_id=1, source_target_pairs={{0,2},{1,3},{2,0},{3,1},{4,6},{5,7},{6,4},{7,5},{8,10},{9,11},{10,... | collective-permute-start | bytes 405512 | tf_op jit(solution)/shard_map/ppermute | solution.py:671
  40.6 0.4 collective-permute-done.other_ref
  40.9 0.3 combine_first.1
  41.2 0.7 collective-permute-start.1
  41.9 1.9 %queries_second.1.query_any.query1_ref = bf16[16,128,512]{2,1,0:T(8,128)(2,1)S(1)} custom-call(bf16[16,128,128]{2,1,0:T(8,128)(2,1)S(1)} %all-to-all-done.1.rows_ref.rows1_ref, s32[32,128]{1,0:T(8,128)S(1)} %copy-done.3, bf16[4,128,128]{2,1,0:T(8,128)(2,1)S(1)} %copy-done.2, bf16[2,128,128]{2,1,0:T(8,128)(2,1)S(1)} %get-tuple-element.30.before_any), custom_call_target="tpu_custom_call" | custom-call | flops 5000000 | bytes 10000 | tf_op jit(solution)/shard_map/queries_second/pallas_call | solution.py:567
  43.9 0.0 copy-start.6
  43.9 3.5 %collective-permute-done.2.other_ref = bf16[528,128]{1,0:T(8,128)(2,1)S(1)} collective-permute-done((bf16[528,128]{1,0:T(8,128)(2,1)S(1)}, bf16[528,128]{1,0:T(8,128)(2,1)S(1)}, u32[]{:S(2)}, u32[]{:S(2)}) %collective-permute-start.2) | collective-permute-done | bytes 135200 | tf_op jit(solution)/shard_map/ppermute | solution.py:671
  47.3 0.6 collective-permute-done.1.column_ref
  47.9 0.3 combine_second.1
  48.2 0.8 collective-permute-start.5
  49.0 2.8 %collective-permute-start.3 = (bf16[3,128,128]{2,1,0:T(8,128)(2,1)S(1)}, bf16[3,128,128]{2,1,0:T(8,128)(2,1)S(1)}, u32[]{:S(2)}, u32[]{:S(2)}) collective-permute-start(bf16[3,128,128]{2,1,0:T(8,128)(2,1)S(1)} %get-tuple-element.34), channel_id=1, source_target_pairs={{0,4},{4,0},{8,12},{12,8},{16,20},{20,16},{24,28},{28,24},{1,5},{5... | collective-permute-start | bytes 294920 | tf_op jit(solution)/shard_map/ppermute | solution.py:719
  51.9 0.1 collective-permute-start.4
  51.9 1.2 %collective-permute-done.4.near1_ref = bf16[2,128,128]{2,1,0:T(8,128)(2,1)S(1)} collective-permute-done((bf16[2,128,128]{2,1,0:T(8,128)(2,1)S(1)}, bf16[2,128,128]{2,1,0:T(8,128)(2,1)S(1)}, u32[]{:S(2)}, u32[]{:S(2)}) %collective-permute-start.4) | collective-permute-done | bytes 65568 | tf_op jit(solution)/shard_map/ppermute | solution.py:720
  53.1 0.0 collective-permute-done.3.near0_ref
  53.1 0.0 collective-permute-done.5.far_ref
  53.1 0.0 copy-done.6
  53.1 0.9 %mix_tiles.1 = (bf16[2,256,512]{2,1,0:T(8,128)(2,1)S(1)}, bf16[2,256,512]{2,1,0:T(8,128)(2,1)S(1)}) custom-call(bf16[2,2,128,128]{3,2,1,0:T(8,128)(2,1)S(1)} %get-tuple-element.31.first_ref, bf16[2,128,128]{2,1,0:T(8,128)(2,1)S(1)} %collective-permute-done.1.column_ref, bf16[2,2,128,128]{3,2,1,0:T(8,128)(2,1)S(1)} %get-tuple-element.33.second_ref, ...), custom_call_target="tpu_custom_call" | custom-call | flops 500000000 | bytes 1000000 | tf_op jit(solution)/shard_map/mix_tiles/pallas_call | solution.py:567
  54.1 0.0 copy-done.10
  54.1 4.3 %attend_points.1 = bf16[16,2,128,128]{3,2,1,0:T(8,128)(2,1)S(1)} custom-call(bf16[16,128,128]{2,1,0:T(8,128)(2,1)S(1)} %all-to-all-done.rows_ref.rows0_ref, bf16[16,128,128]{2,1,0:T(8,128)(2,1)S(1)} %all-to-all-done.1.rows_ref.rows1_ref, bf16[16,128,512]{2,1,0:T(8,128)(2,1)S(1)} %copy-done.10, bf16[16,128,512]{2,1,0:T(8,128)(2,1)S(1)} %queries_second.1.query_any.query1_ref, ...), custom_call_target="tpu_custom_call" | custom-call | flops 3500000000 | bytes 7000000 | tf_op jit(solution)/shard_map/attend_points/pallas_call | solution.py:567
  58.4 0.0 copy-start.12
  58.4 21.0 %all_to_all.15.rows_ref = bf16[16,2,128,128]{3,2,1,0:T(8,128)(2,1)S(1)} all-to-all(bf16[16,2,128,128]{3,2,1,0:T(8,128)(2,1)S(1)} %attend_points.1), channel_id=1, replica_groups=mesh['tx'=8,'zh'=2,'zl'=2] {'tx','zl'}, dimensions={0} | all-to-all | bytes 2097152 | tf_op jit(solution)/shard_map/all_to_all | solution.py:644
  79.4 0.0 copy-done.12
  79.4 5.1 %scatter_rows.1 = bf16[4096,128]{1,0:T(8,128)(2,1)} custom-call(bf16[16,2,128,128]{3,2,1,0:T(8,128)(2,1)S(1)} %all_to_all.15.rows_ref, s32[32,128]{1,0:T(8,128)S(1)} %copy-done.12), custom_call_target="tpu_custom_call" | custom-call | flops 2500000000 | bytes 5000000 | tf_op jit(solution)/shard_map/scatter_rows/pallas_call | solution.py:567
  (5 shorter events, 0.0 us)
Async XLA Ops:
  0.0 13.5 %copy-start.4 = (bf16[4096,128]{1,0:T(8,128)(2,1)S(1)}, bf16[4096,128]{1,0:T(8,128)(2,1)}, u32[]{:S(2)}) copy-start(bf16[4096,128]{1,0:T(8,128)(2,1)} %points_ref.1) | copy-start | bytes 3145732
  0.0 13.5 %copy-start.5 = (bf16[1,512,512]{2,1,0:T(8,128)(2,1)S(1)}, bf16[1,512,512]{2,1,0:T(8,128)(2,1)}, u32[]{:S(2)}) copy-start(bf16[1,512,512]{2,1,0:T(8,128)(2,1)} %w2_ref.1) | copy-start | bytes 1572868
  0.0 13.5 %copy-start.7 = (bf16[128,512]{1,0:T(8,128)(2,1)S(1)}, bf16[128,512]{1,0:T(8,128)(2,1)}, u32[]{:S(2)}) copy-start(bf16[128,512]{1,0:T(8,128)(2,1)} %w1_ref.1) | copy-start | bytes 393220
  0.0 13.5 %copy-start.8 = (bf16[512,128]{1,0:T(8,128)(2,1)S(1)}, bf16[512,128]{1,0:T(8,128)(2,1)}, u32[]{:S(2)}) copy-start(bf16[512,128]{1,0:T(8,128)(2,1)} %w3_ref.1) | copy-start | bytes 393220
  7.1 15.1 %all-to-all-start = ((bf16[16,128,128]{2,1,0:T(8,128)(2,1)}), bf16[16,128,128]{2,1,0:T(8,128)(2,1)S(1)}, u32[]{:S(2)}, u32[]{:S(2)}) async-start(bf16[16,128,128]{2,1,0:T(8,128)(2,1)} %get-tuple-element.22), calls=%async_computation | async-start | bytes 1048576 | tf_op jit(solution)/shard_map/all_to_all | solution.py:644
  13.5 0.7 copy-start.11
  14.2 11.8 %copy-start = (bf16[4,128,128]{2,1,0:T(8,128)(2,1)S(1)}, bf16[4,128,128]{2,1,0:T(8,128)(2,1)}, u32[]{:S(2)}) copy-start(bf16[4,128,128]{2,1,0:T(8,128)(2,1)} %proj_ref.7) | copy-start | bytes 393220
  14.2 11.8 %copy-start.1 = (bf16[128,128]{1,0:T(8,128)(2,1)S(1)}, bf16[128,128]{1,0:T(8,128)(2,1)}, u32[]{:S(2)}) copy-start(bf16[128,128]{1,0:T(8,128)(2,1)} %inducing_ref.3) | copy-start | bytes 98308
  14.2 11.8 %copy-start.2 = (bf16[4,128,128]{2,1,0:T(8,128)(2,1)S(1)}, bf16[4,128,128]{2,1,0:T(8,128)(2,1)}, u32[]{:S(2)}) copy-start(bf16[4,128,128]{2,1,0:T(8,128)(2,1)} %proj_ref.9) | copy-start | bytes 393220
  14.2 11.8 %copy-start.3 = (s32[32,128]{1,0:T(8,128)S(1)}, s32[32,128]{1,0:T(8,128)}, u32[]{:S(2)}) copy-start(s32[32,128]{1,0:T(8,128)} %counts_ref.7) | copy-start | bytes 49156
  22.2 12.5 %all-to-all-start.1 = ((bf16[16,128,128]{2,1,0:T(8,128)(2,1)}), bf16[16,128,128]{2,1,0:T(8,128)(2,1)S(1)}, u32[]{:S(2)}, u32[]{:S(2)}) async-start(bf16[16,128,128]{2,1,0:T(8,128)(2,1)} %encode_second.1), calls=%async_computation.1 | async-start | bytes 1048576 | tf_op jit(solution)/shard_map/all_to_all | solution.py:644
  29.9 1.3 %copy-start.9 = (bf16[16,128,512]{2,1,0:T(8,128)(2,1)}, bf16[16,128,512]{2,1,0:T(8,128)(2,1)S(1)}, u32[]{:S(2)}) copy-start(bf16[16,128,512]{2,1,0:T(8,128)(2,1)S(1)} %get-tuple-element.24.query0_ref) | copy-start | bytes 6291460
  31.3 9.7 %collective-permute-start = (bf16[528,128]{1,0:T(8,128)(2,1)S(1)}, bf16[528,128]{1,0:T(8,128)(2,1)S(1)}, u32[]{:S(2)}, u32[]{:S(2)}) collective-permute-start(bf16[528,128]{1,0:T(8,128)(2,1)S(1)} %get-tuple-element.26), channel_id=1, source_target_pairs={{0,2},{1,3},{2,0},{3,1},{4,6},{5,7},{6,4},{7,5},{8,10},{9,11},{10,... | collective-permute-start | bytes 405512 | tf_op jit(solution)/shard_map/ppermute | solution.py:671
  37.4 9.9 %collective-permute-start.2 = (bf16[528,128]{1,0:T(8,128)(2,1)S(1)}, bf16[528,128]{1,0:T(8,128)(2,1)S(1)}, u32[]{:S(2)}, u32[]{:S(2)}) collective-permute-start(bf16[528,128]{1,0:T(8,128)(2,1)S(1)} %get-tuple-element.29.after_any), channel_id=1, source_target_pairs={{0,2},{1,3},{2,0},{3,1},{4,6},{5,7},{6,4},{7,5},{8,10},{9,11},{10,... | collective-permute-start | bytes 405512 | tf_op jit(solution)/shard_map/ppermute | solution.py:671
  41.2 6.7 %collective-permute-start.1 = (bf16[2,128,128]{2,1,0:T(8,128)(2,1)S(1)}, bf16[2,128,128]{2,1,0:T(8,128)(2,1)S(1)}, u32[]{:S(2)}, u32[]{:S(2)}) collective-permute-start(bf16[2,128,128]{2,1,0:T(8,128)(2,1)S(1)} %get-tuple-element.30.before_any), channel_id=1, source_target_pairs={{0,1},{1,0},{2,3},{3,2},{4,5},{5,4},{6,7},{7,6},{8,9},{9,8},{10,11... | collective-permute-start | bytes 196616 | tf_op jit(solution)/shard_map/ppermute | solution.py:671
  43.9 9.3 %copy-start.6 = (bf16[8,128,128]{2,1,0:T(8,128)(2,1)S(1)}, bf16[8,128,128]{2,1,0:T(8,128)(2,1)}, u32[]{:S(2)}) copy-start(bf16[8,128,128]{2,1,0:T(8,128)(2,1)} %mixing_ref.1) | copy-start | bytes 786436
  47.9 6.1 %copy-start.10 = (bf16[16,128,512]{2,1,0:T(8,128)(2,1)S(1)}, bf16[16,128,512]{2,1,0:T(8,128)(2,1)}, u32[]{:S(2)}) copy-start(bf16[16,128,512]{2,1,0:T(8,128)(2,1)} %copy-done.9) | copy-start | bytes 6291460
  48.2 4.9 %collective-permute-start.5 = (bf16[5,128,128]{2,1,0:T(8,128)(2,1)S(1)}, bf16[5,128,128]{2,1,0:T(8,128)(2,1)S(1)}, u32[]{:S(2)}, u32[]{:S(2)}) collective-permute-start(bf16[5,128,128]{2,1,0:T(8,128)(2,1)S(1)} %get-tuple-element.36), channel_id=1, source_target_pairs={{4,8},{8,4},{12,16},{16,12},{20,24},{24,20},{5,9},{9,5},{13,17},{1... | collective-permute-start | bytes 491528 | tf_op jit(solution)/shard_map/ppermute | solution.py:718
  49.0 4.1 %collective-permute-start.3 = (bf16[3,128,128]{2,1,0:T(8,128)(2,1)S(1)}, bf16[3,128,128]{2,1,0:T(8,128)(2,1)S(1)}, u32[]{:S(2)}, u32[]{:S(2)}) collective-permute-start(bf16[3,128,128]{2,1,0:T(8,128)(2,1)S(1)} %get-tuple-element.34), channel_id=1, source_target_pairs={{0,4},{4,0},{8,12},{12,8},{16,20},{20,16},{24,28},{28,24},{1,5},{5... | collective-permute-start | bytes 294920 | tf_op jit(solution)/shard_map/ppermute | solution.py:719
  51.9 1.3 %collective-permute-start.4 = (bf16[2,128,128]{2,1,0:T(8,128)(2,1)S(1)}, bf16[2,128,128]{2,1,0:T(8,128)(2,1)S(1)}, u32[]{:S(2)}, u32[]{:S(2)}) collective-permute-start(bf16[2,128,128]{2,1,0:T(8,128)(2,1)S(1)} %get-tuple-element.35), channel_id=1, source_target_pairs={{0,4},{4,0},{8,12},{12,8},{16,20},{20,16},{24,28},{28,24},{1,5},{5... | collective-permute-start | bytes 196616 | tf_op jit(solution)/shard_map/ppermute | solution.py:720
  58.4 21.0 %copy-start.12 = (s32[32,128]{1,0:T(8,128)S(1)}, s32[32,128]{1,0:T(8,128)}, u32[]{:S(2)}) copy-start(s32[32,128]{1,0:T(8,128)} %get-tuple-element.23.index_any.index_ref) | copy-start | bytes 49156

commit v14 on v13

--- a/solution.py
+++ b/solution.py
@@ -374,138 +374,100 @@
     send_line(True, late, near1_ref)
 
 
-def mixture_kernel(
-    first_ref,
-    column_ref,
-    second_ref,
-    near0_ref,
-    near1_ref,
-    far_ref,
-    proj_ref,
-    mixing_ref,
-    key_ref,
-    value_ref,
-    grid_ref,
-    mid_ref,
-    side_ref,
-):
+def row_of(near):
+    odd = lax.axis_index("tx") % 2
+    return 1 - odd if near else odd
+
+
+def mixture_kernel(near, first_ref, column_ref, second_ref, *rest):
+    if near:
+        early_ref, late_ref = rest[:2]
+        rest = rest[2:]
+        line = [late_ref[y] for y in range(TLY)] + [early_ref[y] for y in range(TLY + 1)]
+    else:
+        line_ref = rest[0]
+        rest = rest[1:]
+        line = [line_ref[y] for y in range(2 * TLY + 1)]
+    proj_ref, mixing_ref, key_ref, value_ref, grid_ref, mid_ref = rest
     half = LANES // HEADS
     blocks = key_ref.shape[0]
     tall = blocks * TLY
     low = lax.axis_index("zl")
-
+    above = row_of(near)
     row = lax.broadcasted_iota(jnp.int32, (LANES, LANES), 0)
     col = lax.broadcasted_iota(jnp.int32, (LANES, LANES), 1)
     eye = jnp.where(row == col, 1.0, 0.0).astype(BF)
     blank = jnp.zeros((LANES, LANES), BF)
 
     def mix(a, b):
+        if abs(b) > 1:
+            return blank
         return eye if (a, b) == (0, 0) else mixing_ref[neighbour_steps.index((a, b))]
 
-    for k, a in enumerate((-1, 0, 1)):
-        rows = slice(k * 2 * LANES, (k + 1) * 2 * LANES)
-        mid_ref[rows, :] = jnp.concatenate(
-            [
-                jnp.concatenate([mix(a, 0), mix(a, -1)], axis=1),
-                jnp.concatenate([mix(a, 1), mix(a, 0)], axis=1),
-            ],
-            axis=0,
+    for k, (a, c) in enumerate((a, c) for a in (-1, 0, 1) for c in range(4)):
+        mid_ref[k * LANES : (k + 1) * LANES, :] = jnp.concatenate(
+            [mix(a, c - 1), mix(a, c - 2)], axis=1
         )
-    for k, b in enumerate((-1, 1)):
-        side_ref[k] = jnp.concatenate(
-            [
-                jnp.concatenate([mix(0, b), mix(-1, b)], axis=1),
-                jnp.concatenate([mix(1, b), mix(0, b)], axis=1),
-                jnp.concatenate([mix(-1, b), blank], axis=1),
-                jnp.concatenate([blank, mix(1, b)], axis=1),
-            ],
-            axis=0,
-        )
-    ones = head_ones()
-    lane = lax.broadcasted_iota(jnp.int32, (1, LANES), 1)
-    left = lane < half
-    even = lax.axis_index("tx") % 2
-    near_row = (1 - even) * (TLX + 1)
-    far_row = even * (TLX + 1)
     border = (1 - low) * (tall + 1)
     outside = low * (tall + 1)
+    nb = 2 * above
+    for y in range(TLY):
+        for x in range(TLX):
+            grid_ref[1 - above + x, 1 + block_of(0, low) * TLY + y] = first_ref[x, y]
+            grid_ref[1 - above + x, 1 + block_of(1, low) * TLY + y] = second_ref[x, y]
+        grid_ref[nb, 1 + block_of(1, low) * TLY + y] = line[y]
+        grid_ref[nb, 1 + block_of(0, low) * TLY + y] = line[TLY + y]
     for x in range(TLX):
-        for y in range(TLY):
-            grid_ref[1 + x, 1 + block_of(0, low) * TLY + y] = first_ref[x, y]
-            grid_ref[1 + x, 1 + block_of(1, low) * TLY + y] = second_ref[x, y]
-        grid_ref[1 + x, border] = column_ref[x]
-    for y in range(TLY):
-        grid_ref[near_row, 1 + block_of(1, low) * TLY + y] = near1_ref[y]
-        grid_ref[near_row, 1 + block_of(0, low) * TLY + y] = near0_ref[y]
-        grid_ref[far_row, 1 + block_of(1, low) * TLY + y] = far_ref[y]
-        grid_ref[far_row, 1 + block_of(0, low) * TLY + y] = far_ref[TLY + y]
-    grid_ref[near_row, border] = near0_ref[TLY]
-    grid_ref[far_row, border] = far_ref[2 * TLY]
-    for x in range(TLX + 2):
+        grid_ref[1 - above + x, border] = column_ref[x]
+    grid_ref[nb, border] = line[2 * TLY]
+    for x in range(TLX + 1):
         grid_ref[x, outside] = blank
-
-    def tile(i, j):
-        return grid_ref[i, j + 1]
-
-    mids, lefts, rights = [], [], []
-    for i in range(2):
-        for b in range(blocks):
-            mids.append(
-                jnp.concatenate(
-                    [tile(i + r, 2 * b + s) for r in range(3) for s in range(2)], axis=1
-                )
-            )
+    around = [
+        jnp.concatenate([grid_ref[r, 2 * b + c] for r in range(3) for c in range(4)], axis=1)
+        for b in range(blocks)
+    ]
+    mixed = dot(jnp.concatenate(around, axis=0), mid_ref[...]).astype(BF)
+    mixtures = jnp.concatenate(
+        [
+            mixed[b * LANES : (b + 1) * LANES, y * LANES : (y + 1) * LANES]
+            for b in range(blocks)
+            for y in range(TLY)
+        ],
+        axis=0,
+    )
+    keys = unit(dot(mixtures, proj_ref[1]), head_ones())
+    values = dot(mixtures, proj_ref[2])
+    left = lax.broadcasted_iota(jnp.int32, (1, LANES), 1) < half
     for b in range(blocks):
-        lefts.append(jnp.concatenate([tile(i, 2 * b - 1) for i in (1, 2, 0, 3)], axis=1))
-        rights.append(jnp.concatenate([tile(i, 2 * b + 2) for i in (1, 2, 0, 3)], axis=1))
-    middle = dot(jnp.concatenate(mids, axis=0), mid_ref[...])
-    from_left = dot(jnp.concatenate(lefts, axis=0), side_ref[0])
-    from_right = dot(jnp.concatenate(rights, axis=0), side_ref[1])
-    mixtures = []
-    for b in range(blocks):
-        span = slice(b * LANES, (b + 1) * LANES)
-        for i in range(2):
-            m = middle[(i * blocks + b) * LANES : (i * blocks + b + 1) * LANES]
-            cols = slice(i * LANES, (i + 1) * LANES)
-            mixtures.append((m[:, :LANES] + from_left[span, cols]).astype(BF))
-            mixtures.append((m[:, LANES:] + from_right[span, cols]).astype(BF))
-    mixtures = jnp.concatenate(mixtures, axis=0)
-    keys = unit(dot(mixtures, proj_ref[1]), ones)
-    values = dot(mixtures, proj_ref[2])
-    for b in range(blocks):
-        spans = [slice((b * 4 + t) * LANES, (b * 4 + t + 1) * LANES) for t in range(4)]
+        spans = [slice((b * TLY + y) * LANES, (b * TLY + y + 1) * LANES) for y in range(TLY)]
         for h in range(HEADS):
             mine = left if h == 0 else ~left
-            key_ref[b, h * LANES : (h + 1) * LANES, :] = jnp.concatenate(
+            rows = slice(h * LANES, (h + 1) * LANES)
+            key_ref[b, rows, :] = jnp.concatenate(
                 [jnp.where(mine, keys[s], 0.0) for s in spans], axis=1
             ).astype(BF)
-            value_ref[b, h * LANES : (h + 1) * LANES, :] = jnp.concatenate(
+            value_ref[b, rows, :] = jnp.concatenate(
                 [jnp.where(mine, values[s], 0.0) for s in spans], axis=1
             ).astype(BF)
 
 
 def attend_kernel(
-    along_y,
-    rows0_ref,
-    rows1_ref,
-    query0_ref,
-    query1_ref,
-    counts_ref,
-    key_ref,
-    value_ref,
-    proj_ref,
-    out_ref,
+    near, along_y, query0_ref, query1_ref, counts_ref, key_ref, value_ref, *rest
 ):
-    members, quota, width = rows0_ref.shape
+    if near:
+        (out_ref,) = rest
+    else:
+        rows0_ref, rows1_ref, before_ref, proj_ref, out_ref = rest
+    members, quota, wide = query0_ref.shape
     group = min(GROUP_ROWS // quota, members)
     row = lax.broadcasted_iota(jnp.int32, (quota, LANES), 0)
     left = lax.broadcasted_iota(jnp.int32, (1, LANES), 1) < LANES // HEADS
-    for half_id, (rows_ref, query_ref) in enumerate(
-        ((rows0_ref, query0_ref), (rows1_ref, query1_ref))
-    ):
+    side = row_of(near)
+    for half_id, query_ref in enumerate((query0_ref, query1_ref)):
         block = block_of(half_id, lax.axis_index("zl"))
         for c in range(members // group):
             expanded = jnp.concatenate([query_ref[c * group + k] for k in range(group)], axis=0)
+            expanded = jnp.where(side == 1, expanded[:, 2 * LANES :], expanded[:, : 2 * LANES])
             scores = dot_t(expanded, key_ref[block])
             weights = jnp.exp2(scores * (sharpness * math.log2(math.e)))
             totals = [
@@ -516,15 +478,22 @@
             pieces = pieces_of(c * group, group, half_id, along_y)
             attended = []
             for k in range(group):
-                bounds = row_bounds(pieces[k], counts_ref, along_y * TLY)
+                first, second, third = row_bounds(pieces[k], counts_ref, along_y * TLY)
                 span = slice(k * quota, (k + 1) * quota)
-                part = every[span]
-                picked = part[:, :LANES]
-                for t, bound in enumerate(bounds):
-                    tile = part[:, (t + 1) * LANES : (t + 2) * LANES]
-                    picked = jnp.where(row >= bound, tile, picked)
+                bound = jnp.where(side == 1, third, first)
+                picked = jnp.where(row >= bound, every[span, LANES:], every[span, :LANES])
                 total = jnp.where(left, totals[0][span], totals[1][span])
-                attended.append(quotient(picked, total).astype(BF))
+                value = quotient(picked, total)
+                if not near:
+                    inside = (row >= second).astype(jnp.int32) == side
+                    other = before_ref[c * group + k, half_id].astype(F32)
+                    value = jnp.where(inside, value, other)
+                attended.append(value.astype(BF))
+            if near:
+                for k in range(group):
+                    out_ref[c * group + k, half_id] = attended[k]
+                continue
+            rows_ref = (rows0_ref, rows1_ref)[half_id]
             x = jnp.concatenate([rows_ref[c * group + k] for k in range(group)], axis=0)
             added = dot(jnp.concatenate(attended, axis=0), proj_ref[3])
             result = (x.astype(F32) + added).astype(BF)
@@ -719,28 +688,37 @@
     near0 = lax.ppermute(near0, "tx", near_pairs)
     near1 = lax.ppermute(near1, "tx", near_pairs)
 
-    keys, values = call(
-        mixture_kernel,
-        "mix_tiles",
-        (shape((blocks, HEADS * LANES, 4 * LANES)), shape((blocks, HEADS * LANES, 4 * LANES))),
-        "v" * 8,
-        [
-            VMEM((TLX + 2, tall + 2, LANES, width), BF),
-            VMEM((6 * LANES, 2 * LANES), BF),
-            VMEM((2, 4 * LANES, 2 * LANES), BF),
-        ],
-        1,
-        (first_half, column, second_half, near0, near1, far, second_proj, mixing),
-    )
-
-    result = call(
-        functools.partial(attend_kernel, along_y),
-        "attend_points",
-        shape((members, 2, quota, width)),
-        "vvvvsvvv",
-        [],
-        7,
-        (rows0, rows1, query0, query1, counts, keys, values, second_proj),
+    both_halves = shape((members, 2, quota, width))
+    kv = shape((blocks, HEADS * LANES, TLY * LANES))
+
+    def mix(is_near, name, lines):
+        return call(
+            functools.partial(mixture_kernel, is_near),
+            name,
+            (kv, kv),
+            "v" * (5 + len(lines)),
+            [
+                VMEM((TLX + 1, tall + 2, LANES, width), BF),
+                VMEM((12 * LANES, TLY * LANES), BF),
+            ],
+            0.01 if is_near else 1,
+            (first_half, column, second_half, *lines, second_proj, mixing),
+        )
+
+    def attend(is_near, name, pair, more):
+        return call(
+            functools.partial(attend_kernel, is_near, along_y),
+            name,
+            both_halves,
+            "vvsvv" + "v" * len(more),
+            [],
+            0.01 if is_near else 2,
+            (query0, query1, counts, *pair, *more),
+        )
+
+    before = attend(True, "attend_near", mix(True, "mix_near", (near0, near1)), ())
+    result = attend(
+        False, "attend_far", mix(False, "mix_far", (far,)), (rows0, rows1, before, second_proj)
     )
     return call(
         scatter_kernel,

time: 85.2 us -> 85.5 us (level)
  Pallas kernels: 31.7 us -> 35 us
  blocking collectives: 21 us -> 19.6 us
    pallas_call x10 -> x12, Pallas kernels: 31.7 us -> 35 us  [call(): pl.pallas_call(kernel, out_shape=out_shape, in_specs=[pl.BlockSpec(memory...]
    all_to_all x1, blocking collectives: 21 us -> 19.6 us  [exchange(): lax.all_to_all(rows, ('tx', 'zl'), split_axis=0, concat_axis=0, tiled=True)]
  transfers between devices with their start and end apart: 8 -> 8, of which waited for: 6 -> 6; matrix products, arithmetic and copies ran while one was open for 0% -> 0% of each run, Pallas kernels for 16% -> 22%
where the time goes in v14:
time: 85.5 us; the launch traced here: 85 us
  Pallas kernels  35 us (41%)
  starting transfers between devices  19.7 us (23%)
  blocking collectives  19.6 us (23%)
  waiting for transfers between devices  8.91 us (10%)
  local copies, waits for them, and re-layouts  1.46 us (2%)
    pallas_call x12, Pallas kernels, call(): pl.pallas_call(kernel, out_shape=out_shape, in_specs=[pl.BlockSpec(memory...  35 us
    all_to_all x1, blocking collectives, exchange(): lax.all_to_all(rows, ('tx', 'zl'), split_axis=0, concat_axis=0, tiled=True)  19.6 us
    all_to_all x2, starting transfers between devices, exchange(): lax.all_to_all(rows, ('tx', 'zl'), split_axis=0, concat_axis=0, tiled=True)  10.1 us
    ppermute x3, starting transfers between devices, swap(): return lax.ppermute(value, ('zh', 'zl'), steps)  6.29 us
    ppermute x3, waiting for transfers between devices, swap(): return lax.ppermute(value, ('zh', 'zl'), steps)  4.15 us
    all_to_all x2, waiting for transfers between devices, exchange(): lax.all_to_all(rows, ('tx', 'zl'), split_axis=0, concat_axis=0, tiled=True)  3.58 us
    ppermute x1, starting transfers between devices, body(): near0 = lax.ppermute(near0, 'tx', near_pairs)  2.57 us
  transfers between devices with their start and end apart: 8, of which 6 were waited for; matrix products, arithmetic and copies ran while one was open for 0% of the time, Pallas kernels for 22%

profile of v14, /device:TPU:0, one launch (start us, length us, event | category | flops | bytes accessed | tf_op | source)
XLA Modules:
  0.0 85.0 jit_solution(10810156535023599780)
XLA Ops:
  0.0 0.0 copy-start.7
  0.0 0.0 copy-start.8
  0.0 0.0 copy-start.9
  0.0 7.1 %encode_first.1 = (bf16[16,128,128]{2,1,0:T(8,128)(2,1)}, s32[32,128]{1,0:T(8,128)}) custom-call(bf16[4096,128]{1,0:T(8,128)(2,1)} %points_ref.1, bf16[128,512]{1,0:T(8,128)(2,1)} %w1_ref.1, bf16[1,512,512]{2,1,0:T(8,128)(2,1)} %w2_ref.1, bf16[512,128]{1,0:T(8,128)(2,1)} %w3_ref.1, s32[32,128]{1,0:T(8,128)} %counts_ref.9, s32[32,128]{1,0:T(8,128)} %bitcast.1), custom_call_target="tpu_custom_call" | custom-call | flops 4000000000 | bytes 8000000 | tf_op jit(solution)/shard_map/encode_first/pallas_call | solution.py:536
  7.1 6.3 %all-to-all-start = ((bf16[16,128,128]{2,1,0:T(8,128)(2,1)}), bf16[16,128,128]{2,1,0:T(8,128)(2,1)S(1)}, u32[]{:S(2)}, u32[]{:S(2)}) async-start(bf16[16,128,128]{2,1,0:T(8,128)(2,1)} %get-tuple-element.24), calls=%async_computation | async-start | bytes 1048576 | tf_op jit(solution)/shard_map/all_to_all | solution.py:613
  13.5 0.0 copy-done.7
  13.5 0.0 copy-done.8
  13.5 0.0 copy-done.9
  13.5 0.0 copy-done.10
  13.5 0.0 copy-start.11
  13.5 0.7 copy-done.11
  14.2 5.3 %encode_second.1 = bf16[16,128,128]{2,1,0:T(8,128)(2,1)} custom-call(bf16[4096,128]{1,0:T(8,128)(2,1)S(1)} %copy-done.7, bf16[128,512]{1,0:T(8,128)(2,1)S(1)} %copy-done.9, bf16[1,512,512]{2,1,0:T(8,128)(2,1)S(1)} %copy-done.8, bf16[512,128]{1,0:T(8,128)(2,1)S(1)} %copy-done.10, s32[32,128]{1,0:T(8,128)S(1)} %copy-done.11), custom_call_target="tpu_custom_call" | custom-call | flops 3000000000 | bytes 6000000 | tf_op jit(solution)/shard_map/encode_second/pallas_call | solution.py:536
  19.5 2.7 %all-to-all-done.rows_ref.rest_0_ = bf16[16,128,128]{2,1,0:T(8,128)(2,1)S(1)} async-done(((bf16[16,128,128]{2,1,0:T(8,128)(2,1)}), bf16[16,128,128]{2,1,0:T(8,128)(2,1)S(1)}, u32[]{:S(2)}, u32[]{:S(2)}) %all-to-all-start) | async-done | bytes 524320 | tf_op jit(solution)/shard_map/all_to_all | solution.py:613
  22.2 3.8 %all-to-all-start.1 = ((bf16[16,128,128]{2,1,0:T(8,128)(2,1)}), bf16[16,128,128]{2,1,0:T(8,128)(2,1)S(1)}, u32[]{:S(2)}, u32[]{:S(2)}) async-start(bf16[16,128,128]{2,1,0:T(8,128)(2,1)} %encode_second.1), calls=%async_computation.1 | async-start | bytes 1048576 | tf_op jit(solution)/shard_map/all_to_all | solution.py:613
  26.0 0.0 copy-done
  26.0 0.0 copy-done.1
  26.0 0.0 copy-done.5
  26.0 0.0 copy-done.6
  26.1 4.5 %partial_first.1 = (f32[528,128]{1,0:T(8,128)S(1)}, bf16[528,128]{1,0:T(8,128)(2,1)}, bf16[256,128]{1,0:T(8,128)(2,1)S(1)}, bf16[128,128]{1,0:T(8,128)(2,1)S(1)}, bf16[16,128,512]{2,1,0:T(8,128)(2,1)S(1)}) custom-call(bf16[16,128,128]{2,1,0:T(8,128)(2,1)S(1)} %all-to-all-done.rows_ref.rest_0_, s32[32,128]{1,0:T(8,128)S(1)} %copy-done.5, ...), custom_call_target="tpu_custom_call" | custom-call | flops 1500000000 | bytes 3000000 | tf_op jit(solution)/shard_map/partial_first/pallas_call | solution.py:536
  30.6 0.7 copy-done.2
  31.3 2.6 %collective-permute-start = (bf16[528,128]{1,0:T(8,128)(2,1)}, bf16[528,128]{1,0:T(8,128)(2,1)}, u32[]{:S(2)}, u32[]{:S(2)}) collective-permute-start(bf16[528,128]{1,0:T(8,128)(2,1)} %get-tuple-element.28), channel_id=1, source_target_pairs={{0,2},{1,3},{2,0},{3,1},{4,6},{5,7},{6,4},{7,5},{8,10},{9,11},{10,... | collective-permute-start | bytes 405512 | tf_op jit(solution)/shard_map/ppermute | solution.py:640
  33.9 0.9 %all-to-all-done.1.rows_ref.rest_1_ = bf16[16,128,128]{2,1,0:T(8,128)(2,1)S(1)} async-done(((bf16[16,128,128]{2,1,0:T(8,128)(2,1)}), bf16[16,128,128]{2,1,0:T(8,128)(2,1)S(1)}, u32[]{:S(2)}, u32[]{:S(2)}) %all-to-all-start.1) | async-done | bytes 524320 | tf_op jit(solution)/shard_map/all_to_all | solution.py:613
  34.7 2.7 %partial_second.1 = (f32[528,128]{1,0:T(8,128)S(1)}, bf16[528,128]{1,0:T(8,128)(2,1)S(1)}) custom-call(bf16[16,128,128]{2,1,0:T(8,128)(2,1)S(1)} %all-to-all-done.1.rows_ref.rest_1_, s32[32,128]{1,0:T(8,128)S(1)} %copy-done.5, bf16[256,128]{1,0:T(8,128)(2,1)S(1)} %get-tuple-element.29.rest_0_, bf16[128,128]{1,0:T(8,128)(2,1)S(1)} %get-tuple-element.30.rest_1_, ...), custom_call_target="tpu_custom_call" | custom-call | flops 1500000000 | bytes 3000000 | tf_op jit(solution)/shard_map/partial_second/pallas_call | solution.py:536
  37.4 2.9 %collective-permute-start.2 = (bf16[528,128]{1,0:T(8,128)(2,1)S(1)}, bf16[528,128]{1,0:T(8,128)(2,1)S(1)}, u32[]{:S(2)}, u32[]{:S(2)}) collective-permute-start(bf16[528,128]{1,0:T(8,128)(2,1)S(1)} %get-tuple-element.31.after_any), channel_id=1, source_target_pairs={{0,2},{1,3},{2,0},{3,1},{4,6},{5,7},{6,4},{7,5},{8,10},{9,11},{10,... | collective-permute-start | bytes 405512 | tf_op jit(solution)/shard_map/ppermute | solution.py:640
  40.3 0.9 %collective-permute-done.other_ref = bf16[528,128]{1,0:T(8,128)(2,1)} collective-permute-done((bf16[528,128]{1,0:T(8,128)(2,1)}, bf16[528,128]{1,0:T(8,128)(2,1)}, u32[]{:S(2)}, u32[]{:S(2)}) %collective-permute-start) | collective-permute-done | bytes 135200 | tf_op jit(solution)/shard_map/ppermute | solution.py:640
  41.2 0.0 copy-done.3
  41.2 1.2 %combine_first.1 = (bf16[2,2,128,128]{3,2,1,0:T(8,128)(2,1)S(1)}, bf16[2,128,128]{2,1,0:T(8,128)(2,1)S(1)}) custom-call(f32[528,128]{1,0:T(8,128)S(1)} %copy-done.3, bf16[528,128]{1,0:T(8,128)(2,1)} %collective-permute-done.other_ref, bf16[128,128]{1,0:T(8,128)(2,1)S(1)} %copy-done.6, bf16[4,128,128]{2,1,0:T(8,128)(2,1)S(1)} %copy-done.1, ...), custom_call_target="tpu_custom_call" | custom-call | flops 5000000 | bytes 10000 | tf_op jit(solution)/shard_map/combine_first/pallas_call | solution.py:536
  42.4 0.8 collective-permute-start.1
  43.2 1.9 %queries_second.1.query_any.query1_ref = bf16[16,128,512]{2,1,0:T(8,128)(2,1)S(1)} custom-call(bf16[16,128,128]{2,1,0:T(8,128)(2,1)S(1)} %all-to-all-done.1.rows_ref.rest_1_, s32[32,128]{1,0:T(8,128)S(1)} %copy-done.5, bf16[4,128,128]{2,1,0:T(8,128)(2,1)S(1)} %copy-done, bf16[2,128,128]{2,1,0:T(8,128)(2,1)S(1)} %get-tuple-element.32.before_any), custom_call_target="tpu_custom_call" | custom-call | flops 5000000 | bytes 10000 | tf_op jit(solution)/shard_map/queries_second/pallas_call | solution.py:536
  45.1 0.0 copy-start.4
  45.1 2.1 %collective-permute-done.2.other_ref = bf16[528,128]{1,0:T(8,128)(2,1)S(1)} collective-permute-done((bf16[528,128]{1,0:T(8,128)(2,1)S(1)}, bf16[528,128]{1,0:T(8,128)(2,1)S(1)}, u32[]{:S(2)}, u32[]{:S(2)}) %collective-permute-start.2) | collective-permute-done | bytes 135200 | tf_op jit(solution)/shard_map/ppermute | solution.py:640
  47.3 1.1 %collective-permute-done.1.column_ref = bf16[2,128,128]{2,1,0:T(8,128)(2,1)S(1)} collective-permute-done((bf16[2,128,128]{2,1,0:T(8,128)(2,1)S(1)}, bf16[2,128,128]{2,1,0:T(8,128)(2,1)S(1)}, u32[]{:S(2)}, u32[]{:S(2)}) %collective-permute-start.1) | collective-permute-done | bytes 65568 | tf_op jit(solution)/shard_map/ppermute | solution.py:640
  48.4 0.3 combine_second.1
  48.7 0.7 collective-permute-start.3
  49.4 2.6 %collective-permute-start.4 = (bf16[3,128,128]{2,1,0:T(8,128)(2,1)S(1)}, bf16[3,128,128]{2,1,0:T(8,128)(2,1)S(1)}, u32[]{:S(2)}, u32[]{:S(2)}) collective-permute-start(bf16[3,128,128]{2,1,0:T(8,128)(2,1)S(1)} %get-tuple-element.39), channel_id=1, source_target_pairs={{0,4},{4,0},{8,12},{12,8},{16,20},{20,16},{24,28},{28,24},{1,5},{5... | collective-permute-start | bytes 294920 | tf_op jit(solution)/shard_map/ppermute | solution.py:688
  51.9 0.1 collective-permute-start.5
  52.0 1.2 %collective-permute-done.5.rest_1_ = bf16[2,128,128]{2,1,0:T(8,128)(2,1)S(1)} collective-permute-done((bf16[2,128,128]{2,1,0:T(8,128)(2,1)S(1)}, bf16[2,128,128]{2,1,0:T(8,128)(2,1)S(1)}, u32[]{:S(2)}, u32[]{:S(2)}) %collective-permute-start.5) | collective-permute-done | bytes 65568 | tf_op jit(solution)/shard_map/ppermute | solution.py:689
  53.2 0.0 collective-permute-done.4.rest_0_
  53.2 0.0 copy-done.4
  53.2 0.8 mix_near.1
  54.0 2.4 %attend_near.1.rest_2_ = bf16[16,2,128,128]{3,2,1,0:T(8,128)(2,1)S(1)} custom-call(bf16[16,128,512]{2,1,0:T(8,128)(2,1)S(1)} %get-tuple-element.25.query0_ref, bf16[16,128,512]{2,1,0:T(8,128)(2,1)S(1)} %queries_second.1.query_any.query1_ref, s32[32,128]{1,0:T(8,128)S(1)} %copy-done.5, bf16[2,256,256]{2,1,0:T(8,128)(2,1)S(1)} %get-tuple-element.41.key_ref, ...), custom_call_target="tpu_custom_call" | custom-call | flops 5000000 | bytes 10000 | tf_op jit(solution)/shard_map/attend_near/pallas_call | solution.py:536
  56.4 0.0 collective-permute-done.3.rest_0_
  56.4 0.8 mix_far.1
  57.3 2.9 %attend_far.1 = bf16[16,2,128,128]{3,2,1,0:T(8,128)(2,1)S(1)} custom-call(bf16[16,128,512]{2,1,0:T(8,128)(2,1)S(1)} %get-tuple-element.25.query0_ref, bf16[16,128,512]{2,1,0:T(8,128)(2,1)S(1)} %queries_second.1.query_any.query1_ref, s32[32,128]{1,0:T(8,128)S(1)} %copy-done.5, bf16[2,256,256]{2,1,0:T(8,128)(2,1)S(1)} %get-tuple-element.37.key_ref, ...), custom_call_target="tpu_custom_call" | custom-call | flops 1000000000 | bytes 2000000 | tf_op jit(solution)/shard_map/attend_far/pallas_call | solution.py:536
  60.2 0.0 copy-start.12
  60.2 19.6 %all_to_all.15.rows_ref = bf16[16,2,128,128]{3,2,1,0:T(8,128)(2,1)S(1)} all-to-all(bf16[16,2,128,128]{3,2,1,0:T(8,128)(2,1)S(1)} %attend_far.1), channel_id=1, replica_groups=mesh['tx'=8,'zh'=2,'zl'=2] {'tx','zl'}, dimensions={0} | all-to-all | bytes 2097152 | tf_op jit(solution)/shard_map/all_to_all | solution.py:613
  79.7 0.0 copy-done.12
  79.7 5.1 %scatter_rows.1 = bf16[4096,128]{1,0:T(8,128)(2,1)} custom-call(bf16[16,2,128,128]{3,2,1,0:T(8,128)(2,1)S(1)} %all_to_all.15.rows_ref, s32[32,128]{1,0:T(8,128)S(1)} %copy-done.12), custom_call_target="tpu_custom_call" | custom-call | flops 2500000000 | bytes 5000000 | tf_op jit(solution)/shard_map/scatter_rows/pallas_call | solution.py:536
  (7 shorter events, 0.0 us)
Async XLA Ops:
  0.0 13.5 %copy-start.7 = (bf16[4096,128]{1,0:T(8,128)(2,1)S(1)}, bf16[4096,128]{1,0:T(8,128)(2,1)}, u32[]{:S(2)}) copy-start(bf16[4096,128]{1,0:T(8,128)(2,1)} %points_ref.1) | copy-start | bytes 3145732
  0.0 13.5 %copy-start.8 = (bf16[1,512,512]{2,1,0:T(8,128)(2,1)S(1)}, bf16[1,512,512]{2,1,0:T(8,128)(2,1)}, u32[]{:S(2)}) copy-start(bf16[1,512,512]{2,1,0:T(8,128)(2,1)} %w2_ref.1) | copy-start | bytes 1572868
  0.0 13.5 %copy-start.9 = (bf16[128,512]{1,0:T(8,128)(2,1)S(1)}, bf16[128,512]{1,0:T(8,128)(2,1)}, u32[]{:S(2)}) copy-start(bf16[128,512]{1,0:T(8,128)(2,1)} %w1_ref.1) | copy-start | bytes 393220
  0.0 13.5 %copy-start.10 = (bf16[512,128]{1,0:T(8,128)(2,1)S(1)}, bf16[512,128]{1,0:T(8,128)(2,1)}, u32[]{:S(2)}) copy-start(bf16[512,128]{1,0:T(8,128)(2,1)} %w3_ref.1) | copy-start | bytes 393220
  7.1 15.1 %all-to-all-start = ((bf16[16,128,128]{2,1,0:T(8,128)(2,1)}), bf16[16,128,128]{2,1,0:T(8,128)(2,1)S(1)}, u32[]{:S(2)}, u32[]{:S(2)}) async-start(bf16[16,128,128]{2,1,0:T(8,128)(2,1)} %get-tuple-element.24), calls=%async_computation | async-start | bytes 1048576 | tf_op jit(solution)/shard_map/all_to_all | solution.py:613
  13.5 0.7 copy-start.11
  14.2 11.8 %copy-start = (bf16[4,128,128]{2,1,0:T(8,128)(2,1)S(1)}, bf16[4,128,128]{2,1,0:T(8,128)(2,1)}, u32[]{:S(2)}) copy-start(bf16[4,128,128]{2,1,0:T(8,128)(2,1)} %rest_3_.3) | copy-start | bytes 393220
  14.2 11.8 %copy-start.1 = (bf16[4,128,128]{2,1,0:T(8,128)(2,1)S(1)}, bf16[4,128,128]{2,1,0:T(8,128)(2,1)}, u32[]{:S(2)}) copy-start(bf16[4,128,128]{2,1,0:T(8,128)(2,1)} %proj_ref.5) | copy-start | bytes 393220
  14.2 11.8 %copy-start.5 = (s32[32,128]{1,0:T(8,128)S(1)}, s32[32,128]{1,0:T(8,128)}, u32[]{:S(2)}) copy-start(s32[32,128]{1,0:T(8,128)} %counts_ref.9) | copy-start | bytes 49156
  14.2 11.8 %copy-start.6 = (bf16[128,128]{1,0:T(8,128)(2,1)S(1)}, bf16[128,128]{1,0:T(8,128)(2,1)}, u32[]{:S(2)}) copy-start(bf16[128,128]{1,0:T(8,128)(2,1)} %inducing_ref.3) | copy-start | bytes 98308
  22.2 12.5 %all-to-all-start.1 = ((bf16[16,128,128]{2,1,0:T(8,128)(2,1)}), bf16[16,128,128]{2,1,0:T(8,128)(2,1)S(1)}, u32[]{:S(2)}, u32[]{:S(2)}) async-start(bf16[16,128,128]{2,1,0:T(8,128)(2,1)} %encode_second.1), calls=%async_computation.1 | async-start | bytes 1048576 | tf_op jit(solution)/shard_map/all_to_all | solution.py:613
  30.6 0.7 copy-start.2
  31.3 10.0 %collective-permute-start = (bf16[528,128]{1,0:T(8,128)(2,1)}, bf16[528,128]{1,0:T(8,128)(2,1)}, u32[]{:S(2)}, u32[]{:S(2)}) collective-permute-start(bf16[528,128]{1,0:T(8,128)(2,1)} %get-tuple-element.28), channel_id=1, source_target_pairs={{0,2},{1,3},{2,0},{3,1},{4,6},{5,7},{6,4},{7,5},{8,10},{9,11},{10,... | collective-permute-start | bytes 405512 | tf_op jit(solution)/shard_map/ppermute | solution.py:640
  34.7 6.5 %copy-start.3 = (f32[528,128]{1,0:T(8,128)S(1)}, f32[528,128]{1,0:T(8,128)}, u32[]{:S(2)}) copy-start(f32[528,128]{1,0:T(8,128)} %copy-done.2) | copy-start | bytes 811012
  37.4 9.8 %collective-permute-start.2 = (bf16[528,128]{1,0:T(8,128)(2,1)S(1)}, bf16[528,128]{1,0:T(8,128)(2,1)S(1)}, u32[]{:S(2)}, u32[]{:S(2)}) collective-permute-start(bf16[528,128]{1,0:T(8,128)(2,1)S(1)} %get-tuple-element.31.after_any), channel_id=1, source_target_pairs={{0,2},{1,3},{2,0},{3,1},{4,6},{5,7},{6,4},{7,5},{8,10},{9,11},{10,... | collective-permute-start | bytes 405512 | tf_op jit(solution)/shard_map/ppermute | solution.py:640
  42.4 6.0 %collective-permute-start.1 = (bf16[2,128,128]{2,1,0:T(8,128)(2,1)S(1)}, bf16[2,128,128]{2,1,0:T(8,128)(2,1)S(1)}, u32[]{:S(2)}, u32[]{:S(2)}) collective-permute-start(bf16[2,128,128]{2,1,0:T(8,128)(2,1)S(1)} %get-tuple-element.32.before_any), channel_id=1, source_target_pairs={{0,1},{1,0},{2,3},{3,2},{4,5},{5,4},{6,7},{7,6},{8,9},{9,8},{10,11... | collective-permute-start | bytes 196616 | tf_op jit(solution)/shard_map/ppermute | solution.py:640
  45.1 8.1 %copy-start.4 = (bf16[8,128,128]{2,1,0:T(8,128)(2,1)S(1)}, bf16[8,128,128]{2,1,0:T(8,128)(2,1)}, u32[]{:S(2)}) copy-start(bf16[8,128,128]{2,1,0:T(8,128)(2,1)} %rest_3_.2) | copy-start | bytes 786436
  48.7 7.8 %collective-permute-start.3 = (bf16[5,128,128]{2,1,0:T(8,128)(2,1)S(1)}, bf16[5,128,128]{2,1,0:T(8,128)(2,1)S(1)}, u32[]{:S(2)}, u32[]{:S(2)}) collective-permute-start(bf16[5,128,128]{2,1,0:T(8,128)(2,1)S(1)} %get-tuple-element.36), channel_id=1, source_target_pairs={{4,8},{8,4},{12,16},{16,12},{20,24},{24,20},{5,9},{9,5},{13,17},{1... | collective-permute-start | bytes 491528 | tf_op jit(solution)/shard_map/ppermute | solution.py:687
  49.4 3.8 %collective-permute-start.4 = (bf16[3,128,128]{2,1,0:T(8,128)(2,1)S(1)}, bf16[3,128,128]{2,1,0:T(8,128)(2,1)S(1)}, u32[]{:S(2)}, u32[]{:S(2)}) collective-permute-start(bf16[3,128,128]{2,1,0:T(8,128)(2,1)S(1)} %get-tuple-element.39), channel_id=1, source_target_pairs={{0,4},{4,0},{8,12},{12,8},{16,20},{20,16},{24,28},{28,24},{1,5},{5... | collective-permute-start | bytes 294920 | tf_op jit(solution)/shard_map/ppermute | solution.py:688
  51.9 1.3 %collective-permute-start.5 = (bf16[2,128,128]{2,1,0:T(8,128)(2,1)S(1)}, bf16[2,128,128]{2,1,0:T(8,128)(2,1)S(1)}, u32[]{:S(2)}, u32[]{:S(2)}) collective-permute-start(bf16[2,128,128]{2,1,0:T(8,128)(2,1)S(1)} %get-tuple-element.40), channel_id=1, source_target_pairs={{0,4},{4,0},{8,12},{12,8},{16,20},{20,16},{24,28},{28,24},{1,5},{5... | collective-permute-start | bytes 196616 | tf_op jit(solution)/shard_map/ppermute | solution.py:689
  60.2 19.6 %copy-start.12 = (s32[32,128]{1,0:T(8,128)S(1)}, s32[32,128]{1,0:T(8,128)}, u32[]{:S(2)}) copy-start(s32[32,128]{1,0:T(8,128)} %get-tuple-element.26.index_any.index_ref) | copy-start | bytes 49156
